TPU v7x, 256 devices: a whole 4x4x8 slice. The times are simulated.
256 devices in a mesh: dp: 8 (over x, y_lo), hid: 32 (over y_hi, z, core).
Axes of the slice: x: 4, y: 4 (y_hi: 2, y_lo: 2; y = y_hi * 2 + y_lo), z: 8, core: 2. Of those that a mesh axis runs over, the one named last changes fastest.
Arguments:
- tokens: bfloat16 [4096, 8192], P('dp', 'hid'), may hold values from -6 to 6
- cotangent: bfloat16 [4096, 8192], P('dp', 'hid'), may hold values from -6 to 6
- right_up: bfloat16 [32, 256, 1024], P('hid'), may hold values from -0.375 to 0.375
- left_up: bfloat16 [32, 1024, 1024], P('hid'), may hold values from -0.1875 to 0.1875
- left_down: bfloat16 [32, 1024, 1024], P('hid'), may hold values from -0.1875 to 0.1875
- right_down: bfloat16 [32, 1024, 256], P('hid'), may hold values from -0.1875 to 0.1875
Outputs:
- layer_out: bfloat16 [4096, 8192], P('dp', 'hid')
- tokens_grad: bfloat16 [4096, 8192], P('dp', 'hid')
- right_up_grad: float32 [32, 256, 1024], P('hid', 'dp')
- left_up_grad: float32 [32, 1024, 1024], P('hid', 'dp')
- left_down_grad: float32 [32, 1024, 1024], P('hid', 'dp')
- right_down_grad: float32 [32, 1024, 256], P('hid', 'dp')
All inputs are finite; a program needn't handle non-finite values.
Results may differ from a plain program's by a relative error of at most 0.017.
Values may be sent and summed in bfloat16 or wider, within the bound.
No kernel may reach another device: no remote copies, remote signals or barrier semaphores. Data moves between devices by JAX's collectives and lax.ppermute only.
A program may use at most 64 MiB of HBM per device.

v0:
```python
import jax
import jax.numpy as jnp
from jax import lax
from jax.sharding import PartitionSpec as P


def swapped(value, axis, stride):
    mask = 2**stride
    pairs = [(source, source ^ mask) for source in range(lax.axis_size(axis))]
    return lax.ppermute(value, axis, pairs)


def butterfly(tile, mover):
    count_tok = tile.shape[0]
    devices = lax.axis_size("hid")
    pieces = tile.shape[1] // devices
    buffer = tile.reshape(count_tok, devices, pieces)
    sections = list(range(devices.bit_length() - 1))
    myself = lax.axis_index("hid")
    for section_bit in sections:
        span = 1 << section_bit
        view = buffer.reshape(count_tok, devices // (2 * span), 2, span, pieces)
        lower_half = view[:, :, 0]
        upper_half = view[:, :, 1]
        keep_lower = jnp.bitwise_and(jnp.right_shift(myself, section_bit), 1) == 0
        outgoing = jnp.where(keep_lower, upper_half, lower_half)
        incoming = mover(outgoing, section_bit)
        new_lower = jnp.where(keep_lower, lower_half, incoming)
        new_upper = jnp.where(keep_lower, incoming, upper_half)
        buffer = jnp.stack([new_lower, new_upper], axis=2).reshape(count_tok, devices, pieces)
    return buffer.reshape(count_tok, devices * pieces)


def contract_last(left_side, right_side):
    return lax.dot_general(
        left_side, right_side, (((1,), (1,)), ((), ())), preferred_element_type=jnp.float32
    )


def term_maker(left_side, right_side, grad_scale):
    return (
        lax.dot_general(
            left_side, right_side, (((0,), (0,)), ((), ())), preferred_element_type=jnp.float32
        )
        * grad_scale
    )


def body(tokens, cotangent, right_up, left_up, left_down, right_down):
    weight_ru = right_up[0]
    weight_lu = left_up[0]
    weight_ld = left_down[0]
    weight_rd = right_down[0]
    grad_scale = (tokens.shape[0] * lax.axis_size("dp")) ** (-0.5)
    act_up = jnp.dot(tokens, weight_ru, preferred_element_type=jnp.float32).astype(jnp.bfloat16)
    mixed_up = butterfly(
        act_up, lambda outgoing, section_bit: swapped(outgoing, "hid", section_bit)
    )
    pre = jnp.dot(mixed_up, weight_lu, preferred_element_type=jnp.float32)
    sigma = jax.nn.sigmoid(pre)
    hidden = (pre * sigma).astype(jnp.bfloat16)
    act_down = jnp.dot(hidden, weight_ld, preferred_element_type=jnp.float32).astype(jnp.bfloat16)
    mixed_down = butterfly(
        act_down, lambda outgoing, section_bit: swapped(outgoing, "hid", section_bit)
    )
    layer_out = jnp.dot(mixed_down, weight_rd, preferred_element_type=jnp.float32).astype(
        jnp.bfloat16
    )
    grad_mixed_down = contract_last(cotangent, weight_rd).astype(jnp.bfloat16)
    grad_act_down = butterfly(
        grad_mixed_down, lambda outgoing, section_bit: swapped(outgoing, "hid", section_bit)
    )
    grad_hidden = contract_last(grad_act_down, weight_ld)
    grad_pre = (grad_hidden * sigma * (1.0 + pre * (1.0 - sigma))).astype(jnp.bfloat16)
    grad_mixed_up = contract_last(grad_pre, weight_lu).astype(jnp.bfloat16)
    grad_act_up = butterfly(
        grad_mixed_up, lambda outgoing, section_bit: swapped(outgoing, "hid", section_bit)
    )
    tokens_grad = contract_last(grad_act_up, weight_ru).astype(jnp.bfloat16)
    right_up_grad = lax.psum_scatter(
        term_maker(tokens, grad_act_up, grad_scale).astype(jnp.bfloat16),
        "dp",
        scatter_dimension=0,
        tiled=True,
    ).astype(jnp.float32)
    left_up_grad = lax.psum_scatter(
        term_maker(mixed_up, grad_pre, grad_scale).astype(jnp.bfloat16),
        "dp",
        scatter_dimension=0,
        tiled=True,
    ).astype(jnp.float32)
    left_down_grad = lax.psum_scatter(
        term_maker(hidden, grad_act_down, grad_scale).astype(jnp.bfloat16),
        "dp",
        scatter_dimension=0,
        tiled=True,
    ).astype(jnp.float32)
    right_down_grad = lax.psum_scatter(
        term_maker(mixed_down, cotangent, grad_scale).astype(jnp.bfloat16),
        "dp",
        scatter_dimension=0,
        tiled=True,
    ).astype(jnp.float32)
    return (
        layer_out,
        tokens_grad,
        right_up_grad[None],
        left_up_grad[None],
        left_down_grad[None],
        right_down_grad[None],
    )


def solution(mesh):
    placed = (
        P("dp", "hid"),
        P("dp", "hid"),
        P("hid", None, None),
        P("hid", None, None),
        P("hid", None, None),
        P("hid", None, None),
    )
    return jax.shard_map(
        body,
        mesh=mesh,
        in_specs=placed,
        out_specs=(
            P("dp", "hid"),
            P("dp", "hid"),
            P("hid", "dp", None),
            P("hid", "dp", None),
            P("hid", "dp", None),
            P("hid", "dp", None),
        ),
        check_vma=False,
    )
```

profile of v0, /device:TPU:32, one launch (start us, length us, event | category | flops | bytes accessed | tf_op | source)
XLA Modules:
  0.0 510.8 jit_solution(1372710095248170037)
XLA Ops:
  7.2 2.7 convolution_convert_fusion
  12.7 2.5 convolution_convert_fusion.1
  23.0 11.2 %collective-permute-done.11 = bf16[512,8,2,32]{0,3,2,1:T(8,128)(2,1)S(1)} collective-permute-done((bf16[512,8,2,32]{0,3,2,1:T(8,128)(2,1)S(1)}, bf16[512,8,2,32]{0,3,2,1:T(8,128)(2,1)S(1)}, u32[]{:S(2)}, u32[]{:S(2)}) %collective-permute-start.11) | collective-permute-done | bytes 524320 | tf_op jit(solution)/shard_map/ppermute | solution.py:10
  34.6 3.4 collective-permute-start.12
  38.0 15.2 %collective-permute-done.1 = bf16[512,8,2,32]{0,3,2,1:T(8,128)(2,1)S(1)} collective-permute-done((bf16[512,8,2,32]{0,3,2,1:T(8,128)(2,1)S(1)}, bf16[512,8,2,32]{0,3,2,1:T(8,128)(2,1)S(1)}, u32[]{:S(2)}, u32[]{:S(2)}) %collective-permute-start.1) | collective-permute-done | bytes 524320 | tf_op jit(solution)/shard_map/ppermute | solution.py:10
  55.6 45.7 %collective-permute-done.12 = bf16[512,4,4,32]{0,3,2,1:T(8,128)(2,1)S(1)} collective-permute-done((bf16[512,4,4,32]{0,3,2,1:T(8,128)(2,1)S(1)}, bf16[512,4,4,32]{0,3,2,1:T(8,128)(2,1)S(1)}, u32[]{:S(2)}, u32[]{:S(2)}) %collective-permute-start.12) | collective-permute-done | bytes 524320 | tf_op jit(solution)/shard_map/ppermute | solution.py:10
  101.7 4.6 collective-permute-start.13
  106.3 4.2 collective-permute-done.2
  110.9 4.6 collective-permute-start.3
  115.5 22.9 %collective-permute-done.13 = bf16[512,2,8,32]{0,3,2,1:T(8,128)(2,1)S(1)} collective-permute-done((bf16[512,2,8,32]{0,3,2,1:T(8,128)(2,1)S(1)}, bf16[512,2,8,32]{0,3,2,1:T(8,128)(2,1)S(1)}, u32[]{:S(2)}, u32[]{:S(2)}) %collective-permute-start.13) | collective-permute-done | bytes 524320 | tf_op jit(solution)/shard_map/ppermute | solution.py:10
  138.9 6.2 %collective-permute-done.3 = bf16[512,2,8,32]{0,3,2,1:T(8,128)(2,1)S(1)} collective-permute-done((bf16[512,2,8,32]{0,3,2,1:T(8,128)(2,1)S(1)}, bf16[512,2,8,32]{0,3,2,1:T(8,128)(2,1)S(1)}, u32[]{:S(2)}, u32[]{:S(2)}) %collective-permute-start.3) | collective-permute-done | bytes 524320 | tf_op jit(solution)/shard_map/ppermute | solution.py:10
  145.8 8.1 %collective-permute-done.14 = bf16[512,1,16,32]{0,3,2,1:T(8,128)(2,1)S(1)} collective-permute-done((bf16[512,1,16,32]{0,3,2,1:T(8,128)(2,1)S(1)}, bf16[512,1,16,32]{0,3,2,1:T(8,128)(2,1)S(1)}, u32[]{:S(2)}, u32[]{:S(2)}) %collective-permute-start.14) | collective-permute-done | bytes 524320 | tf_op jit(solution)/shard_map/ppermute | solution.py:10
  154.1 6.7 %collective-permute-done.4 = bf16[512,1,16,32]{0,3,2,1:T(8,128)(2,1)S(1)} collective-permute-done((bf16[512,1,16,32]{0,3,2,1:T(8,128)(2,1)S(1)}, bf16[512,1,16,32]{0,3,2,1:T(8,128)(2,1)S(1)}, u32[]{:S(2)}, u32[]{:S(2)}) %collective-permute-start.4) | collective-permute-done | bytes 524320 | tf_op jit(solution)/shard_map/ppermute | solution.py:10
  170.0 4.5 fusion.13
  180.4 12.4 %collective-permute-done.16 = bf16[512,8,2,32]{0,3,2,1:T(8,128)(2,1)S(1)} collective-permute-done((bf16[512,8,2,32]{0,3,2,1:T(8,128)(2,1)S(1)}, bf16[512,8,2,32]{0,3,2,1:T(8,128)(2,1)S(1)}, u32[]{:S(2)}, u32[]{:S(2)}) %collective-permute-start.16) | collective-permute-done | bytes 524320 | tf_op jit(solution)/shard_map/ppermute | solution.py:10
  193.3 14.7 %collective-permute-done.6 = bf16[512,8,2,32]{0,3,2,1:T(8,128)(2,1)S(1)} collective-permute-done((bf16[512,8,2,32]{0,3,2,1:T(8,128)(2,1)S(1)}, bf16[512,8,2,32]{0,3,2,1:T(8,128)(2,1)S(1)}, u32[]{:S(2)}, u32[]{:S(2)}) %collective-permute-start.6) | collective-permute-done | bytes 524320 | tf_op jit(solution)/shard_map/ppermute | solution.py:10
  208.3 5.2 %collective-permute-start.7 = (bf16[512,4,4,32]{0,3,2,1:T(8,128)(2,1)S(1)}, bf16[512,4,4,32]{0,3,2,1:T(8,128)(2,1)S(1)}, u32[]{:S(2)}, u32[]{:S(2)}) collective-permute-start(bf16[512,4,4,32]{0,3,2,1:T(8,128)(2,1)S(1)} %broadcast_select_fusion.18), channel_id=1, source_target_pairs={{0,4},{1,5},{2,6},{3,7},{4,0},{5,1},{6,2},{7,3},{8,12},{9,13},{10,... | collective-permute-start | bytes 1572872 | tf_op jit(solution)/shard_map/ppermute | solution.py:10
  213.6 13.0 %collective-permute-done.17 = bf16[512,4,4,32]{0,3,2,1:T(8,128)(2,1)S(1)} collective-permute-done((bf16[512,4,4,32]{0,3,2,1:T(8,128)(2,1)S(1)}, bf16[512,4,4,32]{0,3,2,1:T(8,128)(2,1)S(1)}, u32[]{:S(2)}, u32[]{:S(2)}) %collective-permute-start.17) | collective-permute-done | bytes 524320 | tf_op jit(solution)/shard_map/ppermute | solution.py:10
  226.9 5.3 %collective-permute-start.18 = (bf16[512,2,8,32]{0,3,2,1:T(8,128)(2,1)S(1)}, bf16[512,2,8,32]{0,3,2,1:T(8,128)(2,1)S(1)}, u32[]{:S(2)}, u32[]{:S(2)}) collective-permute-start(bf16[512,2,8,32]{0,3,2,1:T(8,128)(2,1)S(1)} %broadcast_select_fusion.20), channel_id=1, source_target_pairs={{0,8},{1,9},{2,10},{3,11},{4,12},{5,13},{6,14},{7,15},{8,0},{9,1},... | collective-permute-start | bytes 1572872 | tf_op jit(solution)/shard_map/ppermute | solution.py:10
  232.2 4.7 collective-permute-done.7
  237.2 5.5 %collective-permute-start.8 = (bf16[512,2,8,32]{0,3,2,1:T(8,128)(2,1)S(1)}, bf16[512,2,8,32]{0,3,2,1:T(8,128)(2,1)S(1)}, u32[]{:S(2)}, u32[]{:S(2)}) collective-permute-start(bf16[512,2,8,32]{0,3,2,1:T(8,128)(2,1)S(1)} %broadcast_select_fusion.22), channel_id=1, source_target_pairs={{0,8},{1,9},{2,10},{3,11},{4,12},{5,13},{6,14},{7,15},{8,0},{9,1},... | collective-permute-start | bytes 1572872 | tf_op jit(solution)/shard_map/ppermute | solution.py:10
  242.8 40.2 %collective-permute-done.18 = bf16[512,2,8,32]{0,3,2,1:T(8,128)(2,1)S(1)} collective-permute-done((bf16[512,2,8,32]{0,3,2,1:T(8,128)(2,1)S(1)}, bf16[512,2,8,32]{0,3,2,1:T(8,128)(2,1)S(1)}, u32[]{:S(2)}, u32[]{:S(2)}) %collective-permute-start.18) | collective-permute-done | bytes 524320 | tf_op jit(solution)/shard_map/ppermute | solution.py:10
  283.4 5.3 %collective-permute-done.8 = bf16[512,2,8,32]{0,3,2,1:T(8,128)(2,1)S(1)} collective-permute-done((bf16[512,2,8,32]{0,3,2,1:T(8,128)(2,1)S(1)}, bf16[512,2,8,32]{0,3,2,1:T(8,128)(2,1)S(1)}, u32[]{:S(2)}, u32[]{:S(2)}) %collective-permute-start.8) | collective-permute-done | bytes 524320 | tf_op jit(solution)/shard_map/ppermute | solution.py:10
  289.9 9.5 %collective-permute-done.19 = bf16[512,1,16,32]{0,3,2,1:T(8,128)(2,1)S(1)} collective-permute-done((bf16[512,1,16,32]{0,3,2,1:T(8,128)(2,1)S(1)}, bf16[512,1,16,32]{0,3,2,1:T(8,128)(2,1)S(1)}, u32[]{:S(2)}, u32[]{:S(2)}) %collective-permute-start.19) | collective-permute-done | bytes 524320 | tf_op jit(solution)/shard_map/ppermute | solution.py:10
  302.2 3.3 collective-permute-done.9
  309.0 4.0 multiply_convert_fusion
  314.2 2.6 multiply_convert_fusion.1
  319.2 2.4 convolution_convert_fusion.3
  321.6 26.3 %reduce-scatter.13.cloned.1.call-done = bf16[32,1024]{1,0:T(8,128)(2,1)} async-done(((bf16[256,1024]{1,0:T(8,128)(2,1)}), bf16[32,1024]{1,0:T(8,128)(2,1)}) %reduce-scatter.13.cloned.1.call-update) | async-done | bytes 65552
  349.8 40.3 %reduce-scatter.11.cloned.1.call-done = bf16[128,256]{1,0:T(8,128)(2,1)} async-done(((bf16[1024,256]{1,0:T(8,128)(2,1)}), bf16[128,256]{1,0:T(8,128)(2,1)}) %reduce-scatter.11.cloned.1.call-update) | async-done | bytes 65552 | tf_op jit(solution)/shard_map/reduce_scatter | solution.py:98
  391.6 54.1 %reduce-scatter.9.cloned.1.call-done = bf16[128,1024]{1,0:T(8,128)(2,1)} async-done(((bf16[1024,1024]{1,0:T(8,128)(2,1)}), bf16[128,1024]{1,0:T(8,128)(2,1)}) %reduce-scatter.9.cloned.1.call-update) | async-done | bytes 262160 | tf_op jit(solution)/shard_map/reduce_scatter | solution.py:92
  447.5 55.0 %reduce-scatter.7.cloned.1.call-done = bf16[128,1024]{1,0:T(8,128)(2,1)} async-done(((bf16[1024,1024]{1,0:T(8,128)(2,1)}), bf16[128,1024]{1,0:T(8,128)(2,1)}) %reduce-scatter.7.cloned.1.call-update) | async-done | bytes 262160 | tf_op jit(solution)/shard_map/reduce_scatter | solution.py:86
  (147 shorter events, 49.9 us)
Async XLA Ops:
  7.2 153.8 %copy-start = (bf16[1,1024,1024]{2,1,0:T(8,128)(2,1)S(1)}, bf16[1,1024,1024]{2,1,0:T(8,128)(2,1)}, u32[]{:S(2)}) copy-start(bf16[1,1024,1024]{2,1,0:T(8,128)(2,1)} %param.9) | copy-start | bytes 6291460
  7.2 340.7 %reduce-scatter.13.cloned.1.call-start = ((), (), s32[]{:S(2)}) async-start(), calls=%async_computation.7 | async-start | bytes 589824
  10.0 2.7 copy-start.11
  12.5 5.3 %collective-permute-start.10 = (bf16[512,16,1,32]{0,3,1,2:T(8,128)(2,1)}, bf16[512,16,1,32]{0,3,1,2:T(8,128)(2,1)}, u32[]{:S(2)}, u32[]{:S(2)}) collective-permute-start(bf16[512,16,1,32]{0,3,1,2:T(8,128)(2,1)} %broadcast_select_fusion.5), channel_id=1, source_target_pairs={{0,1},{1,0},{2,3},{3,2},{4,5},{5,4},{6,7},{7,6},{8,9},{9,8},{10,11... | collective-permute-start | bytes 1572872 | tf_op jit(solution)/shard_map/ppermute | solution.py:10
  17.5 3.8 collective-permute-start
  19.4 14.8 %collective-permute-start.11 = (bf16[512,8,2,32]{0,3,2,1:T(8,128)(2,1)S(1)}, bf16[512,8,2,32]{0,3,2,1:T(8,128)(2,1)S(1)}, u32[]{:S(2)}, u32[]{:S(2)}) collective-permute-start(bf16[512,8,2,32]{0,3,2,1:T(8,128)(2,1)S(1)} %broadcast_select_fusion.13), channel_id=1, source_target_pairs={{0,2},{1,3},{2,0},{3,1},{4,6},{5,7},{6,4},{7,5},{8,10},{9,11},{10,... | collective-permute-start | bytes 1572872 | tf_op jit(solution)/shard_map/ppermute | solution.py:10
  22.6 30.6 %collective-permute-start.1 = (bf16[512,8,2,32]{0,3,2,1:T(8,128)(2,1)S(1)}, bf16[512,8,2,32]{0,3,2,1:T(8,128)(2,1)S(1)}, u32[]{:S(2)}, u32[]{:S(2)}) collective-permute-start(bf16[512,8,2,32]{0,3,2,1:T(8,128)(2,1)S(1)} %broadcast_select_fusion.15), channel_id=1, source_target_pairs={{0,2},{1,3},{2,0},{3,1},{4,6},{5,7},{6,4},{7,5},{8,10},{9,11},{10,... | collective-permute-start | bytes 1572872 | tf_op jit(solution)/shard_map/ppermute | solution.py:10
  34.6 66.7 %collective-permute-start.12 = (bf16[512,4,4,32]{0,3,2,1:T(8,128)(2,1)S(1)}, bf16[512,4,4,32]{0,3,2,1:T(8,128)(2,1)S(1)}, u32[]{:S(2)}, u32[]{:S(2)}) collective-permute-start(bf16[512,4,4,32]{0,3,2,1:T(8,128)(2,1)S(1)} %broadcast_select_fusion.17), channel_id=1, source_target_pairs={{0,4},{1,5},{2,6},{3,7},{4,0},{5,1},{6,2},{7,3},{8,12},{9,13},{10,... | collective-permute-start | bytes 1572872 | tf_op jit(solution)/shard_map/ppermute | solution.py:10
  53.6 56.9 %collective-permute-start.2 = (bf16[512,4,4,32]{0,3,2,1:T(8,128)(2,1)S(1)}, bf16[512,4,4,32]{0,3,2,1:T(8,128)(2,1)S(1)}, u32[]{:S(2)}, u32[]{:S(2)}) collective-permute-start(bf16[512,4,4,32]{0,3,2,1:T(8,128)(2,1)S(1)} %broadcast_select_fusion.19), channel_id=1, source_target_pairs={{0,4},{1,5},{2,6},{3,7},{4,0},{5,1},{6,2},{7,3},{8,12},{9,13},{10,... | collective-permute-start | bytes 1572872 | tf_op jit(solution)/shard_map/ppermute | solution.py:10
  101.7 36.7 %collective-permute-start.13 = (bf16[512,2,8,32]{0,3,2,1:T(8,128)(2,1)S(1)}, bf16[512,2,8,32]{0,3,2,1:T(8,128)(2,1)S(1)}, u32[]{:S(2)}, u32[]{:S(2)}) collective-permute-start(bf16[512,2,8,32]{0,3,2,1:T(8,128)(2,1)S(1)} %broadcast_select_fusion.21), channel_id=1, source_target_pairs={{0,8},{1,9},{2,10},{3,11},{4,12},{5,13},{6,14},{7,15},{8,0},{9,1},... | collective-permute-start | bytes 1572872 | tf_op jit(solution)/shard_map/ppermute | solution.py:10
  110.9 34.2 %collective-permute-start.3 = (bf16[512,2,8,32]{0,3,2,1:T(8,128)(2,1)S(1)}, bf16[512,2,8,32]{0,3,2,1:T(8,128)(2,1)S(1)}, u32[]{:S(2)}, u32[]{:S(2)}) collective-permute-start(bf16[512,2,8,32]{0,3,2,1:T(8,128)(2,1)S(1)} %broadcast_select_fusion.23), channel_id=1, source_target_pairs={{0,8},{1,9},{2,10},{3,11},{4,12},{5,13},{6,14},{7,15},{8,0},{9,1},... | collective-permute-start | bytes 1572872 | tf_op jit(solution)/shard_map/ppermute | solution.py:10
  138.8 15.1 %collective-permute-start.14 = (bf16[512,1,16,32]{0,3,2,1:T(8,128)(2,1)S(1)}, bf16[512,1,16,32]{0,3,2,1:T(8,128)(2,1)S(1)}, u32[]{:S(2)}, u32[]{:S(2)}) collective-permute-start(bf16[512,1,16,32]{0,3,2,1:T(8,128)(2,1)S(1)} %broadcast_select_fusion.25), channel_id=1, source_target_pairs={{0,16},{1,17},{2,18},{3,19},{4,20},{5,21},{6,22},{7,23},{8,24},{9,... | collective-permute-start | bytes 1572872 | tf_op jit(solution)/shard_map/ppermute | solution.py:10
  145.5 15.3 %collective-permute-start.4 = (bf16[512,1,16,32]{0,3,2,1:T(8,128)(2,1)S(1)}, bf16[512,1,16,32]{0,3,2,1:T(8,128)(2,1)S(1)}, u32[]{:S(2)}, u32[]{:S(2)}) collective-permute-start(bf16[512,1,16,32]{0,3,2,1:T(8,128)(2,1)S(1)} %broadcast_select_fusion.27), channel_id=1, source_target_pairs={{0,16},{1,17},{2,18},{3,19},{4,20},{5,21},{6,22},{7,23},{8,24},{9,... | collective-permute-start | bytes 1572872 | tf_op jit(solution)/shard_map/ppermute | solution.py:10
  154.0 8.3 %copy-start.5 = (bf16[512,1,2,16,32]{0,4,3,2,1:T(8,128)(2,1)}, bf16[512,1,2,16,32]{0,4,3,2,1:T(8,128)(2,1)S(1)}, u32[]{:S(2)}) copy-start(bf16[512,1,2,16,32]{0,4,3,2,1:T(8,128)(2,1)S(1)} %pad_maximum_fusion.11) | copy-start | bytes 3145732
  170.0 6.7 %collective-permute-start.15 = (bf16[512,16,1,32]{0,3,1,2:T(8,128)(2,1)}, bf16[512,16,1,32]{0,3,1,2:T(8,128)(2,1)}, u32[]{:S(2)}, u32[]{:S(2)}) collective-permute-start(bf16[512,16,1,32]{0,3,1,2:T(8,128)(2,1)} %broadcast_select_fusion.2), channel_id=1, source_target_pairs={{0,1},{1,0},{2,3},{3,2},{4,5},{5,4},{6,7},{7,6},{8,9},{9,8},{10,11... | collective-permute-start | bytes 1572872 | tf_op jit(solution)/shard_map/ppermute | solution.py:10
  176.1 2.1 collective-permute-start.5
  178.0 14.9 %collective-permute-start.16 = (bf16[512,8,2,32]{0,3,2,1:T(8,128)(2,1)S(1)}, bf16[512,8,2,32]{0,3,2,1:T(8,128)(2,1)S(1)}, u32[]{:S(2)}, u32[]{:S(2)}) collective-permute-start(bf16[512,8,2,32]{0,3,2,1:T(8,128)(2,1)S(1)} %broadcast_select_fusion.12), channel_id=1, source_target_pairs={{0,2},{1,3},{2,0},{3,1},{4,6},{5,7},{6,4},{7,5},{8,10},{9,11},{10,... | collective-permute-start | bytes 1572872 | tf_op jit(solution)/shard_map/ppermute | solution.py:10
  178.5 29.5 %collective-permute-start.6 = (bf16[512,8,2,32]{0,3,2,1:T(8,128)(2,1)S(1)}, bf16[512,8,2,32]{0,3,2,1:T(8,128)(2,1)S(1)}, u32[]{:S(2)}, u32[]{:S(2)}) collective-permute-start(bf16[512,8,2,32]{0,3,2,1:T(8,128)(2,1)S(1)} %broadcast_select_fusion.14), channel_id=1, source_target_pairs={{0,2},{1,3},{2,0},{3,1},{4,6},{5,7},{6,4},{7,5},{8,10},{9,11},{10,... | collective-permute-start | bytes 1572872 | tf_op jit(solution)/shard_map/ppermute | solution.py:10
  193.2 33.4 %collective-permute-start.17 = (bf16[512,4,4,32]{0,3,2,1:T(8,128)(2,1)S(1)}, bf16[512,4,4,32]{0,3,2,1:T(8,128)(2,1)S(1)}, u32[]{:S(2)}, u32[]{:S(2)}) collective-permute-start(bf16[512,4,4,32]{0,3,2,1:T(8,128)(2,1)S(1)} %broadcast_select_fusion.16), channel_id=1, source_target_pairs={{0,4},{1,5},{2,6},{3,7},{4,0},{5,1},{6,2},{7,3},{8,12},{9,13},{10,... | collective-permute-start | bytes 1572872 | tf_op jit(solution)/shard_map/ppermute | solution.py:10
  208.3 28.6 %collective-permute-start.7 = (bf16[512,4,4,32]{0,3,2,1:T(8,128)(2,1)S(1)}, bf16[512,4,4,32]{0,3,2,1:T(8,128)(2,1)S(1)}, u32[]{:S(2)}, u32[]{:S(2)}) collective-permute-start(bf16[512,4,4,32]{0,3,2,1:T(8,128)(2,1)S(1)} %broadcast_select_fusion.18), channel_id=1, source_target_pairs={{0,4},{1,5},{2,6},{3,7},{4,0},{5,1},{6,2},{7,3},{8,12},{9,13},{10,... | collective-permute-start | bytes 1572872 | tf_op jit(solution)/shard_map/ppermute | solution.py:10
  226.9 56.1 %collective-permute-start.18 = (bf16[512,2,8,32]{0,3,2,1:T(8,128)(2,1)S(1)}, bf16[512,2,8,32]{0,3,2,1:T(8,128)(2,1)S(1)}, u32[]{:S(2)}, u32[]{:S(2)}) collective-permute-start(bf16[512,2,8,32]{0,3,2,1:T(8,128)(2,1)S(1)} %broadcast_select_fusion.20), channel_id=1, source_target_pairs={{0,8},{1,9},{2,10},{3,11},{4,12},{5,13},{6,14},{7,15},{8,0},{9,1},... | collective-permute-start | bytes 1572872 | tf_op jit(solution)/shard_map/ppermute | solution.py:10
  237.2 51.5 %collective-permute-start.8 = (bf16[512,2,8,32]{0,3,2,1:T(8,128)(2,1)S(1)}, bf16[512,2,8,32]{0,3,2,1:T(8,128)(2,1)S(1)}, u32[]{:S(2)}, u32[]{:S(2)}) collective-permute-start(bf16[512,2,8,32]{0,3,2,1:T(8,128)(2,1)S(1)} %broadcast_select_fusion.22), channel_id=1, source_target_pairs={{0,8},{1,9},{2,10},{3,11},{4,12},{5,13},{6,14},{7,15},{8,0},{9,1},... | collective-permute-start | bytes 1572872 | tf_op jit(solution)/shard_map/ppermute | solution.py:10
  283.3 16.1 %collective-permute-start.19 = (bf16[512,1,16,32]{0,3,2,1:T(8,128)(2,1)S(1)}, bf16[512,1,16,32]{0,3,2,1:T(8,128)(2,1)S(1)}, u32[]{:S(2)}, u32[]{:S(2)}) collective-permute-start(bf16[512,1,16,32]{0,3,2,1:T(8,128)(2,1)S(1)} %broadcast_select_fusion.24), channel_id=1, source_target_pairs={{0,16},{1,17},{2,18},{3,19},{4,20},{5,21},{6,22},{7,23},{8,24},{9,... | collective-permute-start | bytes 1572872 | tf_op jit(solution)/shard_map/ppermute | solution.py:10
  289.9 15.5 %collective-permute-start.9 = (bf16[512,1,16,32]{0,3,2,1:T(8,128)(2,1)}, bf16[512,1,16,32]{0,3,2,1:T(8,128)(2,1)}, u32[]{:S(2)}, u32[]{:S(2)}) collective-permute-start(bf16[512,1,16,32]{0,3,2,1:T(8,128)(2,1)} %broadcast_select_fusion.26), channel_id=1, source_target_pairs={{0,16},{1,17},{2,18},{3,19},{4,20},{5,21},{6,22},{7,23},{8,24},{9,... | collective-permute-start | bytes 1572872 | tf_op jit(solution)/shard_map/ppermute | solution.py:10
  302.1 5.6 %copy-start.12 = (bf16[512,256]{1,0:T(8,128)(2,1)S(1)}, bf16[512,256]{1,0:T(8,128)(2,1)}, u32[]{:S(2)}) copy-start(bf16[512,256]{1,0:T(8,128)(2,1)} %param.7) | copy-start | bytes 786436
  302.1 88.0 %reduce-scatter.11.cloned.1.call-start = ((), (), s32[]{:S(2)}) async-start(), calls=%async_computation.6 | async-start | bytes 589824 | tf_op jit(solution)/shard_map/reduce_scatter | solution.py:98
  306.6 2.4 copy-start.4
  308.9 136.7 %reduce-scatter.9.cloned.1.call-start = ((), (), s32[]{:S(2)}) async-start(), calls=%async_computation.5 | async-start | bytes 2359296 | tf_op jit(solution)/shard_map/reduce_scatter | solution.py:92
  313.0 189.5 %reduce-scatter.7.cloned.1.call-start = ((), (), s32[]{:S(2)}) async-start(), calls=%async_computation.4 | async-start | bytes 2359296 | tf_op jit(solution)/shard_map/reduce_scatter | solution.py:86
  314.2 2.7 copy-start.10
  316.8 2.4 copy-start.9
  319.2 185.0 %copy-start.1 = (bf16[1,1024,1024]{2,1,0:T(8,128)(2,1)S(1)}, bf16[1,1024,1024]{2,1,0:T(8,128)(2,1)}, u32[]{:S(2)}) copy-start(bf16[1,1024,1024]{2,1,0:T(8,128)(2,1)} %param.9) | copy-start | bytes 6291460
  (8 other events, 10.3 us)
Sparse Core Ops, SparseCore 0:
  302.2 45.5 reduce-scatter.12
  351.1 38.9 reduce-scatter.10
  392.6 53.0 reduce-scatter.8
  448.1 54.3 reduce-scatter.6
where the time goes:
time: 512 us; the launch traced here: 511 us
  waiting for transfers between devices  399 us (78%)
  starting transfers between devices  36.6 us (7%)
  matrix products  26.8 us (5%)
  other arithmetic  17.7 us (3%)
  local copies, waits for them, and re-layouts  15.8 us (3%)
  between operations  14.5 us (3%)
    ppermute x20, waiting for transfers between devices, swapped(): return lax.ppermute(value, axis, pairs)  224 us
    reduce_scatter x1, waiting for transfers between devices, body(): lax.psum_scatter(term_maker(mixed_up, grad_pre, grad_scale).astype(jnp.bf...  55 us
    reduce_scatter x1, waiting for transfers between devices, body(): lax.psum_scatter(term_maker(hidden, grad_act_down, grad_scale).astype(jnp...  54.1 us
    reduce_scatter x1, waiting for transfers between devices, body(): lax.psum_scatter(term_maker(mixed_down, cotangent, grad_scale).astype(jnp...  40.3 us
    ppermute x20, starting transfers between devices, swapped(): return lax.ppermute(value, axis, pairs)  36.4 us
    unnamed x5, waiting for transfers between devices  26.3 us
  transfers between devices with their start and end apart: 24, of which 21 were waited for; matrix products, arithmetic and copies ran while one was open for 8% of the time, Pallas kernels for 0%

commit v1 on v0

v1 whole, which is shorter than its diff:
```python
import jax
import jax.numpy as jnp
from jax import lax
from jax.sharding import PartitionSpec as P


def contract(left_side, left_dim, right_side, right_dim):
    return lax.dot_general(
        left_side,
        right_side,
        (((left_dim,), (right_dim,)), ((), ())),
        preferred_element_type=jnp.float32,
    )


def exchange(tile):
    return lax.all_to_all(tile, "hid", 0, 0, tiled=True)


def summed(term, scale):
    part = (term * scale).astype(jnp.bfloat16)
    rows = part.shape[0] // lax.axis_size("dp")
    parts = lax.all_to_all(part, "dp", 0, 0, tiled=True).reshape(-1, rows, part.shape[1])
    return jnp.sum(parts.astype(jnp.float32), axis=0)


def body(tokens, cotangent, right_up, left_up, left_down, right_down):
    weight_ru = right_up[0]
    weight_lu = left_up[0]
    weight_ld = left_down[0]
    weight_rd = right_down[0]
    half = jnp.bfloat16
    scale = (tokens.shape[0] * lax.axis_size("dp")) ** (-0.5)
    act_up = contract(weight_ru, 0, tokens, 1).astype(half)
    mixed_up = exchange(act_up)
    grad_mixed_down = contract(weight_rd, 1, cotangent, 1).astype(half)
    grad_act_down = exchange(grad_mixed_down)
    pre = contract(weight_lu, 0, mixed_up, 0)
    sigma = jax.nn.sigmoid(pre)
    hidden = (pre * sigma).astype(half)
    act_down = contract(weight_ld, 0, hidden, 0).astype(half)
    mixed_down = exchange(act_down)
    grad_hidden = contract(weight_ld, 1, grad_act_down, 0)
    grad_pre = (grad_hidden * sigma * (1.0 + pre * (1.0 - sigma))).astype(half)
    grad_mixed_up = contract(weight_lu, 1, grad_pre, 0).astype(half)
    grad_act_up = exchange(grad_mixed_up)
    left_down_grad = summed(contract(hidden, 1, grad_act_down, 1), scale)
    left_up_grad = summed(contract(mixed_up, 1, grad_pre, 1), scale)
    layer_out = contract(mixed_down, 0, weight_rd, 0).astype(half)
    right_down_grad = summed(contract(mixed_down, 1, cotangent, 0), scale)
    tokens_grad = contract(grad_act_up, 0, weight_ru, 1).astype(half)
    right_up_grad = summed(contract(tokens, 0, grad_act_up, 1), scale)
    return (
        layer_out,
        tokens_grad,
        right_up_grad[None],
        left_up_grad[None],
        left_down_grad[None],
        right_down_grad[None],
    )


def solution(mesh):
    placed = (
        P("dp", "hid"),
        P("dp", "hid"),
        P("hid", None, None),
        P("hid", None, None),
        P("hid", None, None),
        P("hid", None, None),
    )
    return jax.shard_map(
        body,
        mesh=mesh,
        in_specs=placed,
        out_specs=(
            P("dp", "hid"),
            P("dp", "hid"),
            P("hid", "dp", None),
            P("hid", "dp", None),
            P("hid", "dp", None),
            P("hid", "dp", None),
        ),
        check_vma=False,
    )
```

time: 512 us -> 253 us (0.49)
  waiting for transfers between devices: 399 us -> 157 us
  between operations: 14.5 us -> 0.77 us
  local copies, waits for them, and re-layouts: 15.8 us -> 6.33 us
  other arithmetic: 17.7 us -> 8.48 us
  matrix products: 26.8 us -> 35 us
  starting transfers between devices: 36.6 us -> 43.9 us
    ppermute x20 -> x0, waiting for transfers between devices: 224 us -> none  [swapped(): return lax.ppermute(value, axis, pairs)]
    all_to_all x0 -> x8, waiting for transfers between devices: none -> 157 us  [the longest x4 104 us: exchange(): return lax.all_to_all(tile, 'hid', 0, 0, tiled=True)]
    reduce_scatter x3 -> x0, waiting for transfers between devices: 149 us -> none  [the longest x1 55 us: body(): lax.psum_scatter(term_maker(mixed_up, grad_pre, grad_scale).astype(jnp.bf...]
    all_to_all x0 -> x8, starting transfers between devices: none -> 43.9 us  [the longest x4 26.8 us: exchange(): return lax.all_to_all(tile, 'hid', 0, 0, tiled=True)]
    ppermute x20 -> x0, starting transfers between devices: 36.4 us -> none  [swapped(): return lax.ppermute(value, axis, pairs)]
    unnamed x5 -> x0, waiting for transfers between devices: 26.3 us -> none
    reduce_sum x0 -> x4, other arithmetic: none -> 8.48 us  [summed(): return jnp.sum(parts.astype(jnp.float32), axis=0)]
    select_n x24 -> x0, other arithmetic: 8.19 us -> none  [the longest x20 4.4 us: butterfly(): outgoing = jnp.where(keep_lower, upper_half, lower_half)]
  transfers between devices with their start and end apart: 24 -> 8, of which waited for: 21 -> 8; matrix products, arithmetic and copies ran while one was open for 8% -> 16% of each run, Pallas kernels for 0% -> 0%
where the time goes in v1:
time: 253 us; the launch traced here: 252 us
  waiting for transfers between devices  157 us (62%)
  starting transfers between devices  43.9 us (17%)
  matrix products  35 us (14%)
  other arithmetic  8.48 us (3%)
  local copies, waits for them, and re-layouts  6.33 us (3%)
    all_to_all x4, waiting for transfers between devices, exchange(): return lax.all_to_all(tile, 'hid', 0, 0, tiled=True)  104 us
    all_to_all x4, waiting for transfers between devices, summed(): lax.all_to_all(part, 'dp', 0, 0, tiled=True)  53.5 us
    dot_general x12, matrix products, contract(): lax.dot_general(left_side, right_side, (((left_dim,), (right_dim,)), ((),...  35 us
    all_to_all x4, starting transfers between devices, exchange(): return lax.all_to_all(tile, 'hid', 0, 0, tiled=True)  26.8 us
    all_to_all x4, starting transfers between devices, summed(): lax.all_to_all(part, 'dp', 0, 0, tiled=True)  17 us
    reduce_sum x4, other arithmetic, summed(): return jnp.sum(parts.astype(jnp.float32), axis=0)  8.48 us
  transfers between devices with their start and end apart: 8, of which 8 were waited for; matrix products, arithmetic and copies ran while one was open for 16% of the time, Pallas kernels for 0%

profile of v1, /device:TPU:32, one launch (start us, length us, event | category | flops | bytes accessed | tf_op | source)
XLA Modules:
  0.0 251.7 jit_solution(7583708203220263006)
XLA Ops:
  0.7 2.8 %convolution_convert_fusion.1 = bf16[1024,512]{1,0:T(8,128)(2,1)} fusion(bf16[512,256]{1,0:T(8,128)(2,1)} %param.6, bf16[1,256,1024]{2,1,0:T(8,128)(2,1)} %param.8), kind=kOutput, calls=%fused_computation.26 | convolution fusion | flops 268959744 | bytes 1835008 | tf_op jit(solution)/shard_map/dot_general | solution.py:8
  3.4 11.4 %all-to-all-start = ((bf16[32,32,512]{2,1,0:T(8,128)(2,1)}), bf16[32,32,512]{2,1,0:T(8,128)(2,1)S(1)}, u32[]{:S(2)}, u32[]{:S(2)}) async-start(bf16[32,32,512]{2,1,0:T(8,128)(2,1)} %bitcast.103), calls=%async_computation | async-start | bytes 2097152 | tf_op jit(solution)/shard_map/all_to_all | solution.py:17
  14.8 2.5 convolution_convert_fusion
  17.3 28.0 %all-to-all-done = bf16[32,32,512]{2,1,0:T(8,128)(2,1)S(1)} async-done(((bf16[32,32,512]{2,1,0:T(8,128)(2,1)}), bf16[32,32,512]{2,1,0:T(8,128)(2,1)S(1)}, u32[]{:S(2)}, u32[]{:S(2)}) %all-to-all-start) | async-done | bytes 1048608 | tf_op jit(solution)/shard_map/all_to_all | solution.py:17
  45.3 4.4 %all-to-all-start.2 = ((bf16[32,32,512]{2,1,0:T(8,128)(2,1)}), bf16[32,32,512]{2,1,0:T(8,128)(2,1)}, u32[]{:S(2)}, u32[]{:S(2)}) async-start(bf16[32,32,512]{2,1,0:T(8,128)(2,1)} %bitcast.102), calls=%async_computation.2 | async-start | bytes 2097152 | tf_op jit(solution)/shard_map/all_to_all | solution.py:17
  49.8 4.2 %fusion.13 = f32[512,1024]{1,0:T(8,128)} fusion(bf16[1024,512]{1,0:T(8,128)(2,1)S(1)} %bitcast.98, bf16[1,1024,1024]{2,1,0:T(8,128)(2,1)} %param.9), kind=kOutput, calls=%fused_computation.21 | convolution fusion | flops 1073741824 | bytes 5242880 | tf_op jit(solution)/shard_map/dot_general | solution.py:8
  53.9 25.9 %all-to-all-done.2 = bf16[32,32,512]{2,1,0:T(8,128)(2,1)} async-done(((bf16[32,32,512]{2,1,0:T(8,128)(2,1)}), bf16[32,32,512]{2,1,0:T(8,128)(2,1)}, u32[]{:S(2)}, u32[]{:S(2)}) %all-to-all-start.2) | async-done | bytes 1048608 | tf_op jit(solution)/shard_map/all_to_all | solution.py:17
  79.8 4.6 %multiply_convert_fusion = bf16[1024,1024]{1,0:T(8,128)(2,1)} fusion(bf16[1024,512]{1,0:T(8,128)(2,1)} %bitcast.11, f32[512,1024]{1,0:T(8,128)} %fusion.13), kind=kOutput, calls=%fused_computation.1 | convolution fusion | flops 1078460416 | bytes 5242880 | tf_op jit(solution)/shard_map/dot_general | solution.py:8
  84.4 4.4 %all-to-all-start.6 = ((bf16[8,128,1024]{2,1,0:T(8,128)(2,1)}), bf16[8,128,1024]{2,1,0:T(8,128)(2,1)}, u32[]{:S(2)}, u32[]{:S(2)}) async-start(bf16[8,128,1024]{2,1,0:T(8,128)(2,1)} %bitcast.108), calls=%async_computation.6 | async-start | bytes 4194304 | tf_op jit(solution)/shard_map/all_to_all | solution.py:23
  88.8 3.6 %fusion.1 = bf16[1024,512]{0,1:T(8,128)(2,1)S(1)} fusion(f32[512,1024]{1,0:T(8,128)} %fusion.13, bf16[1024,512]{1,0:T(8,128)(2,1)} %bitcast.11, bf16[1,1024,1024]{2,1,0:T(8,128)(2,1)S(1)} %copy-done), kind=kOutput, calls=%fused_computation.6 | convolution fusion | flops 1078460416 | bytes 6291456 | tf_op jit(solution)/shard_map/dot_general | solution.py:8
  93.5 2.6 %multiply_convert_fusion.1 = bf16[1024,1024]{1,0:T(8,128)(2,1)} fusion(bf16[1024,512]{1,0:T(8,128)(2,1)S(1)} %bitcast.99, bf16[1024,512]{0,1:T(8,128)(2,1)S(1)} %fusion.1), kind=kOutput, calls=%fused_computation.3 | convolution fusion | flops 1075838976 | bytes 4194304 | tf_op jit(solution)/shard_map/dot_general | solution.py:8
  96.1 22.7 %all-to-all-done.6 = bf16[8,128,1024]{2,1,0:T(8,128)(2,1)} async-done(((bf16[8,128,1024]{2,1,0:T(8,128)(2,1)}), bf16[8,128,1024]{2,1,0:T(8,128)(2,1)}, u32[]{:S(2)}, u32[]{:S(2)}) %all-to-all-start.6) | async-done | bytes 2097184 | tf_op jit(solution)/shard_map/all_to_all | solution.py:23
  118.8 4.3 %all-to-all-start.5 = ((bf16[8,128,1024]{2,1,0:T(8,128)(2,1)}), bf16[8,128,1024]{2,1,0:T(8,128)(2,1)}, u32[]{:S(2)}, u32[]{:S(2)}) async-start(bf16[8,128,1024]{2,1,0:T(8,128)(2,1)} %bitcast.107), calls=%async_computation.5 | async-start | bytes 4194304 | tf_op jit(solution)/shard_map/all_to_all | solution.py:23
  123.2 2.9 %fusion.23 = bf16[1024,512]{0,1:T(8,128)(2,1)S(1)} fusion(bf16[1,1024,1024]{2,1,0:T(8,128)(2,1)S(1)} %copy-done, f32[512,1024]{1,0:T(8,128)} %fusion.13), kind=kOutput, calls=%fused_computation.27 | convolution fusion | flops 1076887552 | bytes 5242880 | tf_op jit(solution)/shard_map/dot_general | solution.py:8
  126.1 1.3 copy.16
  127.4 25.2 %all-to-all-done.5 = bf16[8,128,1024]{2,1,0:T(8,128)(2,1)} async-done(((bf16[8,128,1024]{2,1,0:T(8,128)(2,1)}), bf16[8,128,1024]{2,1,0:T(8,128)(2,1)}, u32[]{:S(2)}, u32[]{:S(2)}) %all-to-all-start.5) | async-done | bytes 2097184 | tf_op jit(solution)/shard_map/all_to_all | solution.py:23
  152.6 6.6 %all-to-all-start.1 = ((bf16[32,32,512]{2,1,0:T(8,128)(2,1)}), bf16[32,32,512]{2,1,0:T(8,128)(2,1)S(1)}, u32[]{:S(2)}, u32[]{:S(2)}) async-start(bf16[32,32,512]{2,1,0:T(8,128)(2,1)} %bitcast.105), calls=%async_computation.1 | async-start | bytes 2097152 | tf_op jit(solution)/shard_map/all_to_all | solution.py:17
  159.1 4.2 %fusion.26 = bf16[1024,512]{0,1:T(8,128)(2,1)} fusion(bf16[1024,512]{0,1:T(8,128)(2,1)} %copy-done.4, bf16[1,1024,1024]{2,1,0:T(8,128)(2,1)} %param.9), kind=kOutput, calls=%fused_computation.28 | convolution fusion | flops 1074266112 | bytes 4194304 | tf_op jit(solution)/shard_map/dot_general | solution.py:8
  163.3 2.3 copy.17
  165.6 24.0 %all-to-all-done.1 = bf16[32,32,512]{2,1,0:T(8,128)(2,1)S(1)} async-done(((bf16[32,32,512]{2,1,0:T(8,128)(2,1)}), bf16[32,32,512]{2,1,0:T(8,128)(2,1)S(1)}, u32[]{:S(2)}, u32[]{:S(2)}) %all-to-all-start.1) | async-done | bytes 1048608 | tf_op jit(solution)/shard_map/all_to_all | solution.py:17
  189.6 4.4 %all-to-all-start.3 = ((bf16[32,32,512]{2,1,0:T(8,128)(2,1)}), bf16[32,32,512]{2,1,0:T(8,128)(2,1)}, u32[]{:S(2)}, u32[]{:S(2)}) async-start(bf16[32,32,512]{2,1,0:T(8,128)(2,1)} %bitcast.104), calls=%async_computation.3 | async-start | bytes 2097152 | tf_op jit(solution)/shard_map/all_to_all | solution.py:17
  194.1 2.8 %convert_reduce_fusion = f32[128,1024]{1,0:T(8,128)} fusion(bf16[8,128,1024]{2,1,0:T(8,128)(2,1)} %all-to-all-done.6), kind=kLoop, calls=%fused_computation | loop fusion | flops 1966080 | bytes 2621440 | tf_op jit(solution)/shard_map/reduce_sum | solution.py:24
  198.3 25.9 %all-to-all-done.3 = bf16[32,32,512]{2,1,0:T(8,128)(2,1)} async-done(((bf16[32,32,512]{2,1,0:T(8,128)(2,1)}), bf16[32,32,512]{2,1,0:T(8,128)(2,1)}, u32[]{:S(2)}, u32[]{:S(2)}) %all-to-all-start.3) | async-done | bytes 1048608 | tf_op jit(solution)/shard_map/all_to_all | solution.py:17
  224.2 4.1 %all-to-all-start.7 = ((bf16[8,128,256]{1,2,0:T(8,128)(2,1)}), bf16[8,128,256]{1,2,0:T(8,128)(2,1)}, u32[]{:S(2)}, u32[]{:S(2)}) async-start(bf16[8,128,256]{1,2,0:T(8,128)(2,1)} %bitcast.109), calls=%async_computation.7 | async-start | bytes 1048576 | tf_op jit(solution)/shard_map/all_to_all | solution.py:23
  228.3 2.8 %convert_reduce_fusion.1 = f32[128,1024]{1,0:T(8,128)} fusion(bf16[8,128,1024]{2,1,0:T(8,128)(2,1)} %all-to-all-done.5), kind=kLoop, calls=%fused_computation.2 | loop fusion | flops 1966080 | bytes 2621440 | tf_op jit(solution)/shard_map/reduce_sum | solution.py:24
  231.1 2.5 fusion.29
  233.6 3.7 %all-to-all-done.7 = bf16[8,128,256]{1,2,0:T(8,128)(2,1)} async-done(((bf16[8,128,256]{1,2,0:T(8,128)(2,1)}), bf16[8,128,256]{1,2,0:T(8,128)(2,1)}, u32[]{:S(2)}, u32[]{:S(2)}) %all-to-all-start.7) | async-done | bytes 524320 | tf_op jit(solution)/shard_map/all_to_all | solution.py:23
  237.3 4.1 %all-to-all-start.4 = ((bf16[8,32,1024]{2,1,0:T(8,128)(2,1)}), bf16[8,32,1024]{2,1,0:T(8,128)(2,1)}, u32[]{:S(2)}, u32[]{:S(2)}) async-start(bf16[8,32,1024]{2,1,0:T(8,128)(2,1)} %bitcast.106), calls=%async_computation.4 | async-start | bytes 1048576 | tf_op jit(solution)/shard_map/all_to_all | solution.py:23
  241.4 2.3 convolution_convert_fusion.3
  243.7 2.4 convolution_convert_fusion.2
  248.0 1.9 all-to-all-done.4
  250.0 1.8 convert_reduce_fusion.3
  (14 shorter events, 4.4 us)
Async XLA Ops:
  0.6 88.2 %copy-start = (bf16[1,1024,1024]{2,1,0:T(8,128)(2,1)S(1)}, bf16[1,1024,1024]{2,1,0:T(8,128)(2,1)}, u32[]{:S(2)}) copy-start(bf16[1,1024,1024]{2,1,0:T(8,128)(2,1)} %param.10) | copy-start | bytes 6291460
  0.6 14.2 %copy-start.1 = (bf16[512,256]{1,0:T(8,128)(2,1)S(1)}, bf16[512,256]{1,0:T(8,128)(2,1)}, u32[]{:S(2)}) copy-start(bf16[512,256]{1,0:T(8,128)(2,1)} %param.7) | copy-start | bytes 786436
  3.4 41.9 %all-to-all-start = ((bf16[32,32,512]{2,1,0:T(8,128)(2,1)}), bf16[32,32,512]{2,1,0:T(8,128)(2,1)S(1)}, u32[]{:S(2)}, u32[]{:S(2)}) async-start(bf16[32,32,512]{2,1,0:T(8,128)(2,1)} %bitcast.103), calls=%async_computation | async-start | bytes 2097152 | tf_op jit(solution)/shard_map/all_to_all | solution.py:17
  45.3 34.5 %all-to-all-start.2 = ((bf16[32,32,512]{2,1,0:T(8,128)(2,1)}), bf16[32,32,512]{2,1,0:T(8,128)(2,1)}, u32[]{:S(2)}, u32[]{:S(2)}) async-start(bf16[32,32,512]{2,1,0:T(8,128)(2,1)} %bitcast.102), calls=%async_computation.2 | async-start | bytes 2097152 | tf_op jit(solution)/shard_map/all_to_all | solution.py:17
  84.4 34.4 %all-to-all-start.6 = ((bf16[8,128,1024]{2,1,0:T(8,128)(2,1)}), bf16[8,128,1024]{2,1,0:T(8,128)(2,1)}, u32[]{:S(2)}, u32[]{:S(2)}) async-start(bf16[8,128,1024]{2,1,0:T(8,128)(2,1)} %bitcast.108), calls=%async_computation.6 | async-start | bytes 4194304 | tf_op jit(solution)/shard_map/all_to_all | solution.py:23
  92.4 1.1 copy-start.4
  118.8 33.7 %all-to-all-start.5 = ((bf16[8,128,1024]{2,1,0:T(8,128)(2,1)}), bf16[8,128,1024]{2,1,0:T(8,128)(2,1)}, u32[]{:S(2)}, u32[]{:S(2)}) async-start(bf16[8,128,1024]{2,1,0:T(8,128)(2,1)} %bitcast.107), calls=%async_computation.5 | async-start | bytes 4194304 | tf_op jit(solution)/shard_map/all_to_all | solution.py:23
  152.6 37.1 %all-to-all-start.1 = ((bf16[32,32,512]{2,1,0:T(8,128)(2,1)}), bf16[32,32,512]{2,1,0:T(8,128)(2,1)S(1)}, u32[]{:S(2)}, u32[]{:S(2)}) async-start(bf16[32,32,512]{2,1,0:T(8,128)(2,1)} %bitcast.105), calls=%async_computation.1 | async-start | bytes 2097152 | tf_op jit(solution)/shard_map/all_to_all | solution.py:17
  189.6 34.5 %all-to-all-start.3 = ((bf16[32,32,512]{2,1,0:T(8,128)(2,1)}), bf16[32,32,512]{2,1,0:T(8,128)(2,1)}, u32[]{:S(2)}, u32[]{:S(2)}) async-start(bf16[32,32,512]{2,1,0:T(8,128)(2,1)} %bitcast.104), calls=%async_computation.3 | async-start | bytes 2097152 | tf_op jit(solution)/shard_map/all_to_all | solution.py:17
  198.3 32.8 %copy-start.2 = (bf16[512,256]{1,0:T(8,128)(2,1)S(1)}, bf16[512,256]{1,0:T(8,128)(2,1)}, u32[]{:S(2)}) copy-start(bf16[512,256]{1,0:T(8,128)(2,1)} %param.6) | copy-start | bytes 786436
  224.2 13.1 %all-to-all-start.7 = ((bf16[8,128,256]{1,2,0:T(8,128)(2,1)}), bf16[8,128,256]{1,2,0:T(8,128)(2,1)}, u32[]{:S(2)}, u32[]{:S(2)}) async-start(bf16[8,128,256]{1,2,0:T(8,128)(2,1)} %bitcast.109), calls=%async_computation.7 | async-start | bytes 1048576 | tf_op jit(solution)/shard_map/all_to_all | solution.py:23
  237.3 12.7 %all-to-all-start.4 = ((bf16[8,32,1024]{2,1,0:T(8,128)(2,1)}), bf16[8,32,1024]{2,1,0:T(8,128)(2,1)}, u32[]{:S(2)}, u32[]{:S(2)}) async-start(bf16[8,32,1024]{2,1,0:T(8,128)(2,1)} %bitcast.106), calls=%async_computation.4 | async-start | bytes 1048576 | tf_op jit(solution)/shard_map/all_to_all | solution.py:23
  241.4 2.3 copy-start.3

commit v2 on v1

--- a/solution.py
+++ b/solution.py
@@ -17,11 +17,46 @@
     return lax.all_to_all(tile, "hid", 0, 0, tiled=True)
 
 
-def summed(term, scale):
-    part = (term * scale).astype(jnp.bfloat16)
+def summed(part):
     rows = part.shape[0] // lax.axis_size("dp")
     parts = lax.all_to_all(part, "dp", 0, 0, tiled=True).reshape(-1, rows, part.shape[1])
     return jnp.sum(parts.astype(jnp.float32), axis=0)
+
+
+def over_pairs(cur, axis):
+    side = jnp.bitwise_and(lax.axis_index("dp"), 1)
+    kept = lax.dynamic_index_in_dim(cur, side, axis, keepdims=False)
+    sent = lax.dynamic_index_in_dim(cur, 1 - side, axis, keepdims=False)
+    pairs = [(i, i ^ 1) for i in range(lax.axis_size("dp"))]
+    got = lax.ppermute(sent, "dp", pairs)
+    return kept.astype(jnp.float32) + got.astype(jnp.float32)
+
+
+def over_columns(cur):
+    size = lax.axis_size("dp")
+    columns = size // 2
+    column = jnp.right_shift(lax.axis_index("dp"), 1)
+    total = None
+    for step in (1, columns - 1, *range(2, columns - 1), 0):
+        place = jnp.bitwise_and(column + step, columns - 1)
+        block = lax.dynamic_index_in_dim(cur, place, 0, keepdims=False)
+        if step:
+            block = lax.ppermute(block, "dp", [(i, (i + 2 * step) % size) for i in range(size)])
+        block = block.astype(jnp.float32)
+        total = block if total is None else total + block
+    return total
+
+
+def columns_first(part):
+    size = lax.axis_size("dp")
+    cur = part.reshape(size // 2, 2, -1, part.shape[1])
+    return over_pairs(over_columns(cur).astype(part.dtype), 0)
+
+
+def pairs_first(part):
+    size = lax.axis_size("dp")
+    cur = part.reshape(size // 2, 2, -1, part.shape[1])
+    return over_columns(over_pairs(cur, 1).astype(part.dtype))
 
 
 def body(tokens, cotangent, right_up, left_up, left_down, right_down):
@@ -34,22 +69,26 @@
     act_up = contract(weight_ru, 0, tokens, 1).astype(half)
     mixed_up = exchange(act_up)
     grad_mixed_down = contract(weight_rd, 1, cotangent, 1).astype(half)
-    grad_act_down = exchange(grad_mixed_down)
+    received = exchange(grad_mixed_down)
     pre = contract(weight_lu, 0, mixed_up, 0)
     sigma = jax.nn.sigmoid(pre)
     hidden = (pre * sigma).astype(half)
     act_down = contract(weight_ld, 0, hidden, 0).astype(half)
+    grad_act_down, act_down = lax.optimization_barrier((received, act_down))
     mixed_down = exchange(act_down)
+    left_down_part = (contract(hidden, 1, grad_act_down, 1) * scale).astype(half)
+    left_down_grad = columns_first(left_down_part)
     grad_hidden = contract(weight_ld, 1, grad_act_down, 0)
     grad_pre = (grad_hidden * sigma * (1.0 + pre * (1.0 - sigma))).astype(half)
+    left_up_part = (contract(mixed_up, 1, grad_pre, 1) * scale).astype(half)
+    left_up_grad = pairs_first(left_up_part)
     grad_mixed_up = contract(weight_lu, 1, grad_pre, 0).astype(half)
     grad_act_up = exchange(grad_mixed_up)
-    left_down_grad = summed(contract(hidden, 1, grad_act_down, 1), scale)
-    left_up_grad = summed(contract(mixed_up, 1, grad_pre, 1), scale)
     layer_out = contract(mixed_down, 0, weight_rd, 0).astype(half)
-    right_down_grad = summed(contract(mixed_down, 1, cotangent, 0), scale)
+    right_down_part = (contract(mixed_down, 1, cotangent, 0) * scale).astype(half)
+    right_down_grad = columns_first(right_down_part)
     tokens_grad = contract(grad_act_up, 0, weight_ru, 1).astype(half)
-    right_up_grad = summed(contract(tokens, 0, grad_act_up, 1), scale)
+    right_up_grad = summed((contract(tokens, 0, grad_act_up, 1) * scale).astype(half))
     return (
         layer_out,
         tokens_grad,

time: 253 us -> 185 us (0.73)
  waiting for transfers between devices: 157 us -> 79.4 us
  local copies, waits for them, and re-layouts: 6.33 us -> 19.5 us
  matrix products: 35 us -> 27.8 us
  starting transfers between devices: 43.9 us -> 47.4 us
    all_to_all x4 -> x1, waiting for transfers between devices: 53.5 us -> 0.01 us  [summed(): lax.all_to_all(part, 'dp', 0, 0, tiled=True)]
    all_to_all x4, waiting for transfers between devices: 104 us -> 60.3 us  [exchange(): return lax.all_to_all(tile, 'hid', 0, 0, tiled=True)]
    ppermute x0 -> x12, waiting for transfers between devices: none -> 19.1 us  [the longest x9 12.2 us: over_columns(): lax.ppermute(block, 'dp', [(i, (i + 2 * step) % size) for i in range(size)])]
    ppermute x0 -> x12, starting transfers between devices: none -> 18.9 us  [the longest x9 14.7 us: over_columns(): lax.ppermute(block, 'dp', [(i, (i + 2 * step) % size) for i in range(size)])]
    all_to_all x4 -> x1, starting transfers between devices: 17 us -> 4.55 us  [summed(): lax.all_to_all(part, 'dp', 0, 0, tiled=True)]
    dynamic_slice x0 -> x4, local copies, waits for them, and re-layouts: none -> 7.2 us  [over_columns(): block = lax.dynamic_index_in_dim(cur, place, 0, keepdims=False)]
    dot_general x12, matrix products: 35 us -> 27.8 us  [contract(): lax.dot_general(left_side, right_side, (((left_dim,), (right_dim,)), ((),...]
    reduce_sum x4 -> x1, other arithmetic: 8.48 us -> 1.78 us  [summed(): return jnp.sum(parts.astype(jnp.float32), axis=0)]
  transfers between devices with their start and end apart: 8 -> 17, of which waited for: 8 -> 7; matrix products, arithmetic and copies ran while one was open for 16% -> 25% of each run, Pallas kernels for 0% -> 0%
where the time goes in v2:
time: 185 us; the launch traced here: 184 us
  waiting for transfers between devices  79.4 us (43%)
  starting transfers between devices  47.4 us (26%)
  matrix products  27.8 us (15%)
  local copies, waits for them, and re-layouts  19.5 us (11%)
  other arithmetic  8.87 us (5%)
    all_to_all x4, waiting for transfers between devices, exchange(): return lax.all_to_all(tile, 'hid', 0, 0, tiled=True)  60.3 us
    dot_general x12, matrix products, contract(): lax.dot_general(left_side, right_side, (((left_dim,), (right_dim,)), ((),...  27.8 us
    all_to_all x4, starting transfers between devices, exchange(): return lax.all_to_all(tile, 'hid', 0, 0, tiled=True)  24 us
    ppermute x9, starting transfers between devices, over_columns(): lax.ppermute(block, 'dp', [(i, (i + 2 * step) % size) for i in range(size)])  14.7 us
    ppermute x9, waiting for transfers between devices, over_columns(): lax.ppermute(block, 'dp', [(i, (i + 2 * step) % size) for i in range(size)])  12.2 us
    dynamic_slice x4, local copies, waits for them, and re-layouts, over_columns(): block = lax.dynamic_index_in_dim(cur, place, 0, keepdims=False)  7.2 us
    ppermute x3, waiting for transfers between devices, over_pairs(): got = lax.ppermute(sent, 'dp', pairs)  6.93 us
    all_to_all x1, starting transfers between devices, summed(): lax.all_to_all(part, 'dp', 0, 0, tiled=True)  4.55 us
  transfers between devices with their start and end apart: 17, of which 7 were waited for; matrix products, arithmetic and copies ran while one was open for 25% of the time, Pallas kernels for 0%

profile of v2, /device:TPU:32, one launch (start us, length us, event | category | flops | bytes accessed | tf_op | source)
XLA Modules:
  0.0 183.8 jit_solution(13056122680899732752)
XLA Ops:
  0.7 2.7 %convolution_convert_fusion = bf16[1024,512]{1,0:T(8,128)(2,1)} fusion(bf16[512,256]{1,0:T(8,128)(2,1)} %param.6, bf16[1,256,1024]{2,1,0:T(8,128)(2,1)} %param.8), kind=kOutput, calls=%fused_computation.25 | convolution fusion | flops 268959744 | bytes 1835008 | tf_op jit(solution)/shard_map/dot_general | solution.py:8
  3.4 11.4 %all-to-all-start.1 = ((bf16[32,32,512]{2,1,0:T(8,128)(2,1)}), bf16[32,32,512]{2,1,0:T(8,128)(2,1)S(1)}, u32[]{:S(2)}, u32[]{:S(2)}) async-start(bf16[32,32,512]{2,1,0:T(8,128)(2,1)} %bitcast.144), calls=%async_computation.1 | async-start | bytes 2097152 | tf_op jit(solution)/shard_map/all_to_all | solution.py:17
  14.8 2.5 %convolution_convert_fusion.1 = bf16[1024,512]{1,0:T(8,128)(2,1)} fusion(bf16[512,256]{1,0:T(8,128)(2,1)S(1)} %copy-done.7, bf16[1,1024,256]{2,1,0:T(8,128)(2,1)} %param.11), kind=kOutput, calls=%fused_computation.26 | convolution fusion | flops 268959744 | bytes 1835008 | tf_op jit(solution)/shard_map/dot_general | solution.py:8
  17.3 28.0 %all-to-all-done.1 = bf16[32,32,512]{2,1,0:T(8,128)(2,1)S(1)} async-done(((bf16[32,32,512]{2,1,0:T(8,128)(2,1)}), bf16[32,32,512]{2,1,0:T(8,128)(2,1)S(1)}, u32[]{:S(2)}, u32[]{:S(2)}) %all-to-all-start.1) | async-done | bytes 1048608 | tf_op jit(solution)/shard_map/all_to_all | solution.py:17
  45.3 4.4 %all-to-all-start = ((bf16[32,32,512]{2,1,0:T(8,128)(2,1)}), bf16[32,32,512]{2,1,0:T(8,128)(2,1)}, u32[]{:S(2)}, u32[]{:S(2)}) async-start(bf16[32,32,512]{2,1,0:T(8,128)(2,1)} %bitcast.143), calls=%async_computation | async-start | bytes 2097152 | tf_op jit(solution)/shard_map/all_to_all | solution.py:17
  49.7 2.9 %fusion.14 = f32[512,1024]{1,0:T(8,128)S(1)} fusion(bf16[1024,512]{1,0:T(8,128)(2,1)S(1)} %bitcast.139, bf16[1,1024,1024]{2,1,0:T(8,128)(2,1)} %param.9), kind=kOutput, calls=%fused_computation.21 | convolution fusion | flops 1073741824 | bytes 5242880 | tf_op jit(solution)/shard_map/dot_general | solution.py:8
  53.9 2.3 %fusion.24 = bf16[1024,512]{0,1:T(8,128)(2,1)} fusion(bf16[1,1024,1024]{2,1,0:T(8,128)(2,1)S(1)} %copy-done, f32[512,1024]{1,0:T(8,128)S(1)} %fusion.14), kind=kOutput, calls=%fused_computation.27 | convolution fusion | flops 1076887552 | bytes 5242880 | tf_op jit(solution)/shard_map/dot_general | solution.py:8
  56.2 23.6 %all-to-all-done = bf16[32,32,512]{2,1,0:T(8,128)(2,1)} async-done(((bf16[32,32,512]{2,1,0:T(8,128)(2,1)}), bf16[32,32,512]{2,1,0:T(8,128)(2,1)}, u32[]{:S(2)}, u32[]{:S(2)}) %all-to-all-start) | async-done | bytes 1048608 | tf_op jit(solution)/shard_map/all_to_all | solution.py:17
  79.8 2.3 %copy.18 = bf16[1024,512]{1,0:T(8,128)(2,1)} copy(bf16[1024,512]{0,1:T(8,128)(2,1)} %fusion.24) | data formatting | bytes 2097152 | tf_op jit(solution)/shard_map/optimization_barrier | solution.py:77
  82.1 4.4 %all-to-all-start.2 = ((bf16[32,32,512]{2,1,0:T(8,128)(2,1)}), bf16[32,32,512]{2,1,0:T(8,128)(2,1)}, u32[]{:S(2)}, u32[]{:S(2)}) async-start(bf16[32,32,512]{2,1,0:T(8,128)(2,1)} %bitcast.146), calls=%async_computation.2 | async-start | bytes 2097152 | tf_op jit(solution)/shard_map/all_to_all | solution.py:17
  86.5 3.6 %fusion.2 = bf16[1024,512]{0,1:T(8,128)(2,1)S(1)} fusion(f32[512,1024]{1,0:T(8,128)} %copy-done.5, bf16[1024,512]{1,0:T(8,128)(2,1)} %bitcast.2, bf16[1,1024,1024]{2,1,0:T(8,128)(2,1)S(1)} %copy-done), kind=kOutput, calls=%fused_computation.6 | convolution fusion | flops 1078460416 | bytes 6291456 | tf_op jit(solution)/shard_map/dot_general | solution.py:8
  94.6 2.6 %multiply_convert_fusion = bf16[1024,1024]{1,0:T(8,128)(2,1)S(1)} fusion(bf16[1024,512]{1,0:T(8,128)(2,1)} %bitcast.2, f32[512,1024]{1,0:T(8,128)S(1)} %copy-done.6), kind=kOutput, calls=%fused_computation | convolution fusion | flops 1078460416 | bytes 5242880 | tf_op jit(solution)/shard_map/dot_general | solution.py:8
  101.2 2.7 %collective-permute-start.6 = (bf16[2,128,1024]{2,1,0:T(8,128)(2,1)}, bf16[2,128,1024]{2,1,0:T(8,128)(2,1)}, u32[]{:S(2)}, u32[]{:S(2)}) collective-permute-start(bf16[2,128,1024]{2,1,0:T(8,128)(2,1)} %get-tuple-element.11), channel_id=1, source_target_pairs={{0,128},{32,160},{64,192},{96,224},{128,0},{160,32},{192,64},{224,... | collective-permute-start | bytes 1572872 | tf_op jit(solution)/shard_map/ppermute | solution.py:44
  108.0 8.7 %all-to-all-done.2 = bf16[32,32,512]{2,1,0:T(8,128)(2,1)} async-done(((bf16[32,32,512]{2,1,0:T(8,128)(2,1)}), bf16[32,32,512]{2,1,0:T(8,128)(2,1)}, u32[]{:S(2)}, u32[]{:S(2)}) %all-to-all-start.2) | async-done | bytes 1048608 | tf_op jit(solution)/shard_map/all_to_all | solution.py:17
  116.7 3.7 %all-to-all-start.3 = ((bf16[32,32,512]{2,1,0:T(8,128)(2,1)}), bf16[32,32,512]{2,1,0:T(8,128)(2,1)S(1)}, u32[]{:S(2)}, u32[]{:S(2)}) async-start(bf16[32,32,512]{2,1,0:T(8,128)(2,1)} %bitcast.145), calls=%async_computation.3 | async-start | bytes 2097152 | tf_op jit(solution)/shard_map/all_to_all | solution.py:17
  120.4 6.1 %collective-permute-done.6 = bf16[2,128,1024]{2,1,0:T(8,128)(2,1)} collective-permute-done((bf16[2,128,1024]{2,1,0:T(8,128)(2,1)}, bf16[2,128,1024]{2,1,0:T(8,128)(2,1)}, u32[]{:S(2)}, u32[]{:S(2)}) %collective-permute-start.6) | collective-permute-done | bytes 524320 | tf_op jit(solution)/shard_map/ppermute | solution.py:44
  126.5 1.9 %fusion.32 = bf16[2,128,1024]{2,1,0:T(8,128)(2,1)S(1)} fusion(bf16[2,128,1024]{2,1,0:T(8,128)(2,1)} %collective-permute-done.6, bf16[2,128,1024]{2,1,0:T(8,128)(2,1)} %collective-permute-done.5, bf16[2,128,1024]{2,1,0:T(8,128)(2,1)} %collective-permute-done.4, bf16[4,2,128,1024]{3,2,1,0:T(8,128)(2,1)} %bitcast.151, s32[]{:T(128)S(6)} %select_n.41), kind=kLoop, calls=%fused_computation.36 | loop fusion | flops 2097152 | bytes 2621444 | tf_op jit(solution)/shard_map/convert_element_type | solution.py:53
  133.0 2.4 %collective-permute-start.3 = (bf16[128,1024]{1,0:T(8,128)(2,1)S(1)}, bf16[128,1024]{1,0:T(8,128)(2,1)S(1)}, u32[]{:S(2)}, u32[]{:S(2)}) collective-permute-start(bf16[128,1024]{1,0:T(8,128)(2,1)S(1)} %get-tuple-element.14), channel_id=1, source_target_pairs={{0,128},{32,160},{64,192},{96,224},{128,0},{160,32},{192,64},{224,... | collective-permute-start | bytes 786440 | tf_op jit(solution)/shard_map/ppermute | solution.py:44
  137.0 3.0 %collective-permute-done.7 = bf16[128,1024]{1,0:T(8,128)(2,1)S(1)} collective-permute-done((bf16[128,1024]{1,0:T(8,128)(2,1)S(1)}, bf16[128,1024]{1,0:T(8,128)(2,1)S(1)}, u32[]{:S(2)}, u32[]{:S(2)}) %collective-permute-start.7) | collective-permute-done | bytes 262176 | tf_op jit(solution)/shard_map/ppermute | solution.py:31
  140.8 6.1 %collective-permute-done.3 = bf16[128,1024]{1,0:T(8,128)(2,1)S(1)} collective-permute-done((bf16[128,1024]{1,0:T(8,128)(2,1)S(1)}, bf16[128,1024]{1,0:T(8,128)(2,1)S(1)}, u32[]{:S(2)}, u32[]{:S(2)}) %collective-permute-start.3) | collective-permute-done | bytes 262176 | tf_op jit(solution)/shard_map/ppermute | solution.py:44
  147.9 2.5 %fusion.31 = bf16[1024,256]{0,1:T(8,128)(2,1)} fusion(bf16[1024,512]{1,0:T(8,128)(2,1)} %bitcast.11, bf16[512,256]{1,0:T(8,128)(2,1)S(1)} %copy-done.7), kind=kOutput, calls=%fused_computation.32 | convolution fusion | flops 268959744 | bytes 1835008 | tf_op jit(solution)/shard_map/dot_general | solution.py:8
  150.4 2.2 %reshape.47 = bf16[4,2,128,256]{2,1,0,3:T(2,128)(2,1)} reshape(bf16[1024,256]{0,1:T(8,128)(2,1)} %fusion.31) | data formatting | bytes 1048576 | tf_op jit(solution)/shard_map/reshape | solution.py:52
  152.6 2.2 %constant_dynamic-slice_fusion = (bf16[1,2,128,256]{2,1,0,3:T(2,128)(2,1)S(1)}, bf16[1,2,128,256]{2,1,0,3:T(2,128)(2,1)}, bf16[1,2,128,256]{2,1,0,3:T(2,128)(2,1)}, bf16[1,2,128,256]{2,1,0,3:T(2,128)(2,1)}) fusion(bf16[4,2,128,256]{2,1,0,3:T(2,128)(2,1)} %reshape.47, s32[]{:T(128)S(6)} %select_n.41, s32[]{:T(128)S(6)} %select_n.40, s32[]{:T(128)S(6)} %select_n.39, ...), kind=kLoop, calls=%fused_computation.59 | loop fusion | bytes 1048592 | tf_op jit(solution)/shard_map/jit(dynamic_index_in_dim)/dynamic_slice | solution.py:42
  156.5 1.7 copy.23
  158.2 1.7 copy.22
  160.3 2.7 %collective-permute-start.9 = (bf16[2,128,256]{2,1,0:T(8,128)(2,1)}, bf16[2,128,256]{2,1,0:T(8,128)(2,1)}, u32[]{:S(2)}, u32[]{:S(2)}) collective-permute-start(bf16[2,128,256]{2,1,0:T(8,128)(2,1)} %bitcast.154), channel_id=1, source_target_pairs={{0,192},{32,224},{64,0},{96,32},{128,64},{160,96},{192,128},{224,1... | collective-permute-start | bytes 393224 | tf_op jit(solution)/shard_map/ppermute | solution.py:44
  163.5 2.5 %convolution_convert_fusion.3 = bf16[512,256]{1,0:T(8,128)(2,1)} fusion(bf16[1024,512]{1,0:T(8,128)(2,1)} %bitcast.11, bf16[1,1024,256]{2,1,0:T(8,128)(2,1)} %param.11), kind=kOutput, calls=%fused_computation.34 | convolution fusion | flops 268566528 | bytes 1835008 | tf_op jit(solution)/shard_map/dot_general | solution.py:8
  167.4 4.6 %all-to-all-start.4 = ((bf16[8,32,1024]{2,1,0:T(8,128)(2,1)}), bf16[8,32,1024]{2,1,0:T(8,128)(2,1)}, u32[]{:S(2)}, u32[]{:S(2)}) async-start(bf16[8,32,1024]{2,1,0:T(8,128)(2,1)} %bitcast.147), calls=%async_computation.4 | async-start | bytes 1048576 | tf_op jit(solution)/shard_map/all_to_all | solution.py:22
  173.1 2.1 %collective-permute-start.11 = (bf16[128,256]{1,0:T(8,128)(2,1)S(1)}, bf16[128,256]{1,0:T(8,128)(2,1)S(1)}, u32[]{:S(2)}, u32[]{:S(2)}) collective-permute-start(bf16[128,256]{1,0:T(8,128)(2,1)S(1)} %dynamic-slice_bitcast_fusion.8), channel_id=1, source_target_pairs={{0,32},{32,0},{64,96},{96,64},{128,160},{160,128},{192,224},{224,1... | collective-permute-start | bytes 196616 | tf_op jit(solution)/shard_map/ppermute | solution.py:31
  175.2 2.2 %convolution_convert_fusion.2 = bf16[512,256]{1,0:T(8,128)(2,1)} fusion(bf16[1024,512]{1,0:T(8,128)(2,1)S(1)} %bitcast.142, bf16[1,256,1024]{2,1,0:T(8,128)(2,1)} %param.8), kind=kOutput, calls=%fused_computation.33 | convolution fusion | flops 268566528 | bytes 1835008 | tf_op jit(solution)/shard_map/dot_general | solution.py:8
  177.5 3.9 %collective-permute-done.11 = bf16[128,256]{1,0:T(8,128)(2,1)S(1)} collective-permute-done((bf16[128,256]{1,0:T(8,128)(2,1)S(1)}, bf16[128,256]{1,0:T(8,128)(2,1)S(1)}, u32[]{:S(2)}, u32[]{:S(2)}) %collective-permute-start.11) | collective-permute-done | bytes 65568 | tf_op jit(solution)/shard_map/ppermute | solution.py:31
  182.0 1.8 convert_reduce_fusion
  (52 shorter events, 27.5 us)
Async XLA Ops:
  0.6 53.3 %copy-start = (bf16[1,1024,1024]{2,1,0:T(8,128)(2,1)S(1)}, bf16[1,1024,1024]{2,1,0:T(8,128)(2,1)}, u32[]{:S(2)}) copy-start(bf16[1,1024,1024]{2,1,0:T(8,128)(2,1)} %param.10) | copy-start | bytes 6291460
  0.6 14.1 %copy-start.7 = (bf16[512,256]{1,0:T(8,128)(2,1)S(1)}, bf16[512,256]{1,0:T(8,128)(2,1)}, u32[]{:S(2)}) copy-start(bf16[512,256]{1,0:T(8,128)(2,1)} %param.7) | copy-start | bytes 786436
  3.4 41.9 %all-to-all-start.1 = ((bf16[32,32,512]{2,1,0:T(8,128)(2,1)}), bf16[32,32,512]{2,1,0:T(8,128)(2,1)S(1)}, u32[]{:S(2)}, u32[]{:S(2)}) async-start(bf16[32,32,512]{2,1,0:T(8,128)(2,1)} %bitcast.144), calls=%async_computation.1 | async-start | bytes 2097152 | tf_op jit(solution)/shard_map/all_to_all | solution.py:17
  45.3 34.5 %all-to-all-start = ((bf16[32,32,512]{2,1,0:T(8,128)(2,1)}), bf16[32,32,512]{2,1,0:T(8,128)(2,1)}, u32[]{:S(2)}, u32[]{:S(2)}) async-start(bf16[32,32,512]{2,1,0:T(8,128)(2,1)} %bitcast.143), calls=%async_computation | async-start | bytes 2097152 | tf_op jit(solution)/shard_map/all_to_all | solution.py:17
  52.6 1.3 copy-start.5
  82.1 34.6 %all-to-all-start.2 = ((bf16[32,32,512]{2,1,0:T(8,128)(2,1)}), bf16[32,32,512]{2,1,0:T(8,128)(2,1)}, u32[]{:S(2)}, u32[]{:S(2)}) async-start(bf16[32,32,512]{2,1,0:T(8,128)(2,1)} %bitcast.146), calls=%async_computation.2 | async-start | bytes 2097152 | tf_op jit(solution)/shard_map/all_to_all | solution.py:17
  91.4 1.3 copy-start.1
  91.4 3.2 %copy-start.6 = (f32[512,1024]{1,0:T(8,128)S(1)}, f32[512,1024]{1,0:T(8,128)}, u32[]{:S(2)}) copy-start(f32[512,1024]{1,0:T(8,128)} %copy-done.5) | copy-start | bytes 6291460
  93.9 36.0 %collective-permute-start = (bf16[4,128,1024]{2,1,0:T(8,128)(2,1)}, bf16[4,128,1024]{2,1,0:T(8,128)(2,1)}, u32[]{:S(2)}, u32[]{:S(2)}) collective-permute-start(bf16[4,128,1024]{2,1,0:T(8,128)(2,1)} %dynamic-slice_bitcast_fusion), channel_id=1, source_target_pairs={{0,32},{32,0},{64,96},{96,64},{128,160},{160,128},{192,224},{224,1... | collective-permute-start | bytes 3145736 | tf_op jit(solution)/shard_map/ppermute | solution.py:31
  97.2 1.3 copy-start.4
  97.2 8.1 %copy-start.3 = (bf16[1,1024,1024]{2,1,0:T(8,128)(2,1)S(1)}, bf16[1,1024,1024]{2,1,0:T(8,128)(2,1)}, u32[]{:S(2)}) copy-start(bf16[1,1024,1024]{2,1,0:T(8,128)(2,1)} %param.9) | copy-start | bytes 6291460
  99.7 20.8 %collective-permute-start.4 = (bf16[2,128,1024]{2,1,0:T(8,128)(2,1)}, bf16[2,128,1024]{2,1,0:T(8,128)(2,1)}, u32[]{:S(2)}, u32[]{:S(2)}) collective-permute-start(bf16[2,128,1024]{2,1,0:T(8,128)(2,1)} %get-tuple-element.10), channel_id=1, source_target_pairs={{0,64},{32,96},{64,128},{96,160},{128,192},{160,224},{192,0},{224,... | collective-permute-start | bytes 1572872 | tf_op jit(solution)/shard_map/ppermute | solution.py:44
  101.2 25.4 %collective-permute-start.6 = (bf16[2,128,1024]{2,1,0:T(8,128)(2,1)}, bf16[2,128,1024]{2,1,0:T(8,128)(2,1)}, u32[]{:S(2)}, u32[]{:S(2)}) collective-permute-start(bf16[2,128,1024]{2,1,0:T(8,128)(2,1)} %get-tuple-element.11), channel_id=1, source_target_pairs={{0,128},{32,160},{64,192},{96,224},{128,0},{160,32},{192,64},{224,... | collective-permute-start | bytes 1572872 | tf_op jit(solution)/shard_map/ppermute | solution.py:44
  103.9 22.6 %collective-permute-start.5 = (bf16[2,128,1024]{2,1,0:T(8,128)(2,1)}, bf16[2,128,1024]{2,1,0:T(8,128)(2,1)}, u32[]{:S(2)}, u32[]{:S(2)}) collective-permute-start(bf16[2,128,1024]{2,1,0:T(8,128)(2,1)} %get-tuple-element.12), channel_id=1, source_target_pairs={{0,192},{32,224},{64,0},{96,32},{128,64},{160,96},{192,128},{224,1... | collective-permute-start | bytes 1572872 | tf_op jit(solution)/shard_map/ppermute | solution.py:44
  116.7 49.3 %all-to-all-start.3 = ((bf16[32,32,512]{2,1,0:T(8,128)(2,1)}), bf16[32,32,512]{2,1,0:T(8,128)(2,1)S(1)}, u32[]{:S(2)}, u32[]{:S(2)}) async-start(bf16[32,32,512]{2,1,0:T(8,128)(2,1)} %bitcast.145), calls=%async_computation.3 | async-start | bytes 2097152 | tf_op jit(solution)/shard_map/all_to_all | solution.py:17
  120.4 9.5 %copy-start.2 = (bf16[1024,1024]{1,0:T(8,128)(2,1)S(1)}, bf16[1024,1024]{1,0:T(8,128)(2,1)}, u32[]{:S(2)}) copy-start(bf16[1024,1024]{1,0:T(8,128)(2,1)} %copy-done.1) | copy-start | bytes 6291460
  128.4 11.6 %collective-permute-start.7 = (bf16[128,1024]{1,0:T(8,128)(2,1)S(1)}, bf16[128,1024]{1,0:T(8,128)(2,1)S(1)}, u32[]{:S(2)}, u32[]{:S(2)}) collective-permute-start(bf16[128,1024]{1,0:T(8,128)(2,1)S(1)} %dynamic-slice_bitcast_fusion.4), channel_id=1, source_target_pairs={{0,32},{32,0},{64,96},{96,64},{128,160},{160,128},{192,224},{224,1... | collective-permute-start | bytes 786440 | tf_op jit(solution)/shard_map/ppermute | solution.py:31
  131.6 9.3 %collective-permute-start.1 = (bf16[128,1024]{1,0:T(8,128)(2,1)S(1)}, bf16[128,1024]{1,0:T(8,128)(2,1)S(1)}, u32[]{:S(2)}, u32[]{:S(2)}) collective-permute-start(bf16[128,1024]{1,0:T(8,128)(2,1)S(1)} %get-tuple-element.13), channel_id=1, source_target_pairs={{0,64},{32,96},{64,128},{96,160},{128,192},{160,224},{192,0},{224,... | collective-permute-start | bytes 786440 | tf_op jit(solution)/shard_map/ppermute | solution.py:44
  133.0 13.9 %collective-permute-start.3 = (bf16[128,1024]{1,0:T(8,128)(2,1)S(1)}, bf16[128,1024]{1,0:T(8,128)(2,1)S(1)}, u32[]{:S(2)}, u32[]{:S(2)}) collective-permute-start(bf16[128,1024]{1,0:T(8,128)(2,1)S(1)} %get-tuple-element.14), channel_id=1, source_target_pairs={{0,128},{32,160},{64,192},{96,224},{128,0},{160,32},{192,64},{224,... | collective-permute-start | bytes 786440 | tf_op jit(solution)/shard_map/ppermute | solution.py:44
  135.4 11.5 %collective-permute-start.2 = (bf16[128,1024]{1,0:T(8,128)(2,1)S(1)}, bf16[128,1024]{1,0:T(8,128)(2,1)S(1)}, u32[]{:S(2)}, u32[]{:S(2)}) collective-permute-start(bf16[128,1024]{1,0:T(8,128)(2,1)S(1)} %get-tuple-element.15), channel_id=1, source_target_pairs={{0,192},{32,224},{64,0},{96,32},{128,64},{160,96},{192,128},{224,1... | collective-permute-start | bytes 786440 | tf_op jit(solution)/shard_map/ppermute | solution.py:44
  152.6 13.4 %copy-start.8 = (bf16[512,256]{1,0:T(8,128)(2,1)S(1)}, bf16[512,256]{1,0:T(8,128)(2,1)}, u32[]{:S(2)}) copy-start(bf16[512,256]{1,0:T(8,128)(2,1)} %param.6) | copy-start | bytes 786436
  159.8 12.2 %collective-permute-start.8 = (bf16[2,128,256]{2,1,0:T(8,128)(2,1)}, bf16[2,128,256]{2,1,0:T(8,128)(2,1)}, u32[]{:S(2)}, u32[]{:S(2)}) collective-permute-start(bf16[2,128,256]{2,1,0:T(8,128)(2,1)} %bitcast.155), channel_id=1, source_target_pairs={{0,64},{32,96},{64,128},{96,160},{128,192},{160,224},{192,0},{224,... | collective-permute-start | bytes 393224 | tf_op jit(solution)/shard_map/ppermute | solution.py:44
  160.3 11.7 %collective-permute-start.9 = (bf16[2,128,256]{2,1,0:T(8,128)(2,1)}, bf16[2,128,256]{2,1,0:T(8,128)(2,1)}, u32[]{:S(2)}, u32[]{:S(2)}) collective-permute-start(bf16[2,128,256]{2,1,0:T(8,128)(2,1)} %bitcast.154), channel_id=1, source_target_pairs={{0,192},{32,224},{64,0},{96,32},{128,64},{160,96},{192,128},{224,1... | collective-permute-start | bytes 393224 | tf_op jit(solution)/shard_map/ppermute | solution.py:44
  163.1 8.9 %collective-permute-start.10 = (bf16[2,128,256]{2,1,0:T(8,128)(2,1)}, bf16[2,128,256]{2,1,0:T(8,128)(2,1)}, u32[]{:S(2)}, u32[]{:S(2)}) collective-permute-start(bf16[2,128,256]{2,1,0:T(8,128)(2,1)} %bitcast.153), channel_id=1, source_target_pairs={{0,128},{32,160},{64,192},{96,224},{128,0},{160,32},{192,64},{224,... | collective-permute-start | bytes 393224 | tf_op jit(solution)/shard_map/ppermute | solution.py:44
  167.4 14.6 %all-to-all-start.4 = ((bf16[8,32,1024]{2,1,0:T(8,128)(2,1)}), bf16[8,32,1024]{2,1,0:T(8,128)(2,1)}, u32[]{:S(2)}, u32[]{:S(2)}) async-start(bf16[8,32,1024]{2,1,0:T(8,128)(2,1)} %bitcast.147), calls=%async_computation.4 | async-start | bytes 1048576 | tf_op jit(solution)/shard_map/all_to_all | solution.py:22
  173.1 8.2 %collective-permute-start.11 = (bf16[128,256]{1,0:T(8,128)(2,1)S(1)}, bf16[128,256]{1,0:T(8,128)(2,1)S(1)}, u32[]{:S(2)}, u32[]{:S(2)}) collective-permute-start(bf16[128,256]{1,0:T(8,128)(2,1)S(1)} %dynamic-slice_bitcast_fusion.8), channel_id=1, source_target_pairs={{0,32},{32,0},{64,96},{96,64},{128,160},{160,128},{192,224},{224,1... | collective-permute-start | bytes 196616 | tf_op jit(solution)/shard_map/ppermute | solution.py:31

commit v3 on v1

--- a/solution.py
+++ b/solution.py
@@ -1,6 +1,7 @@
 import jax
 import jax.numpy as jnp
 from jax import lax
+from jax.experimental.layout import Layout, with_layout_constraint
 from jax.sharding import PartitionSpec as P
 
 
@@ -13,15 +14,63 @@
     )
 
 
+def row_major(value):
+    return with_layout_constraint(value, Layout(tuple(range(value.ndim))))
+
+
 def exchange(tile):
     return lax.all_to_all(tile, "hid", 0, 0, tiled=True)
 
 
-def summed(term, scale):
-    part = (term * scale).astype(jnp.bfloat16)
+def summed(part):
     rows = part.shape[0] // lax.axis_size("dp")
     parts = lax.all_to_all(part, "dp", 0, 0, tiled=True).reshape(-1, rows, part.shape[1])
     return jnp.sum(parts.astype(jnp.float32), axis=0)
+
+
+def pair_halves(cur, axis):
+    side = jnp.bitwise_and(lax.axis_index("dp"), 1)
+    return [
+        lax.dynamic_index_in_dim(cur, place, axis, keepdims=False) for place in (side, 1 - side)
+    ]
+
+
+def over_pairs(halves, after=()):
+    kept, sent = halves
+    pairs = [(i, i ^ 1) for i in range(lax.axis_size("dp"))]
+    got = lax.ppermute(sent, "dp", pairs)
+    got, *_ = lax.optimization_barrier((got, *after))
+    return kept.astype(jnp.float32) + got.astype(jnp.float32)
+
+
+def column_blocks(cur):
+    columns = cur.shape[0]
+    column = jnp.right_shift(lax.axis_index("dp"), 1)
+    return [
+        lax.dynamic_index_in_dim(
+            cur, jnp.bitwise_and(column + step, columns - 1), 0, keepdims=False
+        )
+        for step in column_steps(columns)
+    ]
+
+
+def column_steps(columns):
+    return (1, columns - 1, *range(2, columns - 1), 0)
+
+
+def over_columns(blocks, after=()):
+    size = lax.axis_size("dp")
+    *sent, kept = blocks
+    got = [
+        lax.ppermute(block, "dp", [(i, (i + 2 * step) % size) for i in range(size)])
+        for step, block in zip(column_steps(size // 2), sent)
+    ]
+    got = lax.optimization_barrier((*got, *after))[: len(sent)]
+    return sum((block.astype(jnp.float32) for block in got), kept.astype(jnp.float32))
+
+
+def by_place(part):
+    return part.reshape(lax.axis_size("dp") // 2, 2, -1, part.shape[1])
 
 
 def body(tokens, cotangent, right_up, left_up, left_down, right_down):
@@ -33,23 +82,41 @@
     scale = (tokens.shape[0] * lax.axis_size("dp")) ** (-0.5)
     act_up = contract(weight_ru, 0, tokens, 1).astype(half)
     mixed_up = exchange(act_up)
-    grad_mixed_down = contract(weight_rd, 1, cotangent, 1).astype(half)
-    grad_act_down = exchange(grad_mixed_down)
+    grad_mixed_down = row_major(contract(weight_rd, 1, cotangent, 1).astype(half))
+    grad_mixed_down, mixed_up = lax.optimization_barrier((grad_mixed_down, mixed_up))
+    received = exchange(grad_mixed_down)
     pre = contract(weight_lu, 0, mixed_up, 0)
     sigma = jax.nn.sigmoid(pre)
     hidden = (pre * sigma).astype(half)
     act_down = contract(weight_ld, 0, hidden, 0).astype(half)
+    act_down = row_major(act_down)
+    grad_act_down, _ = lax.optimization_barrier((received, act_down))
     mixed_down = exchange(act_down)
+    left_down_part = (contract(hidden, 1, grad_act_down, 1) * scale).astype(half)
+    grad_act_down, *blocks = lax.optimization_barrier(
+        (grad_act_down, *column_blocks(by_place(left_down_part)))
+    )
     grad_hidden = contract(weight_ld, 1, grad_act_down, 0)
     grad_pre = (grad_hidden * sigma * (1.0 + pre * (1.0 - sigma))).astype(half)
+    left_up_part = (contract(mixed_up, 1, grad_pre, 1) * scale).astype(half)
+    halves = pair_halves(by_place(left_up_part), 1)
     grad_mixed_up = contract(weight_lu, 1, grad_pre, 0).astype(half)
+    grad_mixed_up = row_major(grad_mixed_up)
+    grad_mixed_up, mixed_down, *_ = lax.optimization_barrier(
+        (grad_mixed_up, mixed_down, *halves)
+    )
+    left_down_half = over_columns(blocks).astype(half)
+    left_down_grad = over_pairs(pair_halves(left_down_half, 0))
+    left_up_half = over_pairs(halves, (left_down_half, mixed_down)).astype(half)
+    left_up_grad = over_columns(column_blocks(left_up_half))
     grad_act_up = exchange(grad_mixed_up)
-    left_down_grad = summed(contract(hidden, 1, grad_act_down, 1), scale)
-    left_up_grad = summed(contract(mixed_up, 1, grad_pre, 1), scale)
     layer_out = contract(mixed_down, 0, weight_rd, 0).astype(half)
-    right_down_grad = summed(contract(mixed_down, 1, cotangent, 0), scale)
+    later, _ = lax.optimization_barrier((mixed_down, left_up_half))
+    right_down_part = row_major((contract(later, 1, cotangent, 0) * scale).astype(half))
+    right_down_half = over_columns(column_blocks(by_place(right_down_part))).astype(half)
+    right_down_grad = over_pairs(pair_halves(right_down_half, 0))
     tokens_grad = contract(grad_act_up, 0, weight_ru, 1).astype(half)
-    right_up_grad = summed(contract(tokens, 0, grad_act_up, 1), scale)
+    right_up_grad = summed((contract(tokens, 0, grad_act_up, 1) * scale).astype(half))
     return (
         layer_out,
         tokens_grad,

time: 253 us -> 186 us (0.74)
  waiting for transfers between devices: 157 us -> 93.9 us
  matrix products: 35 us -> 28.7 us
  starting transfers between devices: 43.9 us -> 46.5 us
    all_to_all x4 -> x1, waiting for transfers between devices: 53.5 us -> 3.69 us  [summed(): lax.all_to_all(part, 'dp', 0, 0, tiled=True)]
    all_to_all x4, waiting for transfers between devices: 104 us -> 63.5 us  [exchange(): return lax.all_to_all(tile, 'hid', 0, 0, tiled=True)]
    ppermute x0 -> x12, waiting for transfers between devices: none -> 26.7 us  [the longest x3 21.7 us: over_pairs(): got = lax.ppermute(sent, 'dp', pairs)]
    ppermute x0 -> x12, starting transfers between devices: none -> 17.9 us  [the longest x9 15.4 us: over_columns(): lax.ppermute(block, 'dp', [(i, (i + 2 * step) % size) for i in range(size)])]
    all_to_all x4 -> x1, starting transfers between devices: 17 us -> 3.84 us  [summed(): lax.all_to_all(part, 'dp', 0, 0, tiled=True)]
    reduce_sum x4 -> x1, other arithmetic: 8.48 us -> 0.73 us  [summed(): return jnp.sum(parts.astype(jnp.float32), axis=0)]
    dot_general x12, matrix products: 35 us -> 28.7 us  [contract(): lax.dot_general(left_side, right_side, (((left_dim,), (right_dim,)), ((),...]
    convert_element_type x0 -> x3, other arithmetic: none -> 3.61 us  [the longest x1 1.93 us: body(): left_down_half = over_columns(blocks).astype(half)]
  transfers between devices with their start and end apart: 8 -> 17, of which waited for: 8 -> 7; matrix products, arithmetic and copies ran while one was open for 16% -> 19% of each run, Pallas kernels for 0% -> 0%
where the time goes in v3:
time: 186 us; the launch traced here: 184 us
  waiting for transfers between devices  93.9 us (50%)
  starting transfers between devices  46.5 us (25%)
  matrix products  28.7 us (15%)
  other arithmetic  7.93 us (4%)
  local copies, waits for them, and re-layouts  5.83 us (3%)
    all_to_all x4, waiting for transfers between devices, exchange(): return lax.all_to_all(tile, 'hid', 0, 0, tiled=True)  63.5 us
    dot_general x12, matrix products, contract(): lax.dot_general(left_side, right_side, (((left_dim,), (right_dim,)), ((),...  28.7 us
    all_to_all x4, starting transfers between devices, exchange(): return lax.all_to_all(tile, 'hid', 0, 0, tiled=True)  24.7 us
    ppermute x3, waiting for transfers between devices, over_pairs(): got = lax.ppermute(sent, 'dp', pairs)  21.7 us
    ppermute x9, starting transfers between devices, over_columns(): lax.ppermute(block, 'dp', [(i, (i + 2 * step) % size) for i in range(size)])  15.4 us
    ppermute x9, waiting for transfers between devices, over_columns(): lax.ppermute(block, 'dp', [(i, (i + 2 * step) % size) for i in range(size)])  5.04 us
    all_to_all x1, starting transfers between devices, summed(): lax.all_to_all(part, 'dp', 0, 0, tiled=True)  3.84 us
  transfers between devices with their start and end apart: 17, of which 7 were waited for; matrix products, arithmetic and copies ran while one was open for 19% of the time, Pallas kernels for 0%

profile of v3, /device:TPU:32, one launch (start us, length us, event | category | flops | bytes accessed | tf_op | source)
XLA Modules:
  0.0 183.7 jit_solution(2114494886493477871)
XLA Ops:
  0.7 2.7 %convolution_convert_fusion = bf16[1024,512]{1,0:T(8,128)(2,1)} fusion(bf16[512,256]{1,0:T(8,128)(2,1)} %param.6, bf16[1,256,1024]{2,1,0:T(8,128)(2,1)} %param.8), kind=kOutput, calls=%fused_computation.24 | convolution fusion | flops 268959744 | bytes 1835008 | tf_op jit(solution)/shard_map/dot_general | solution.py:9
  3.4 11.4 %all-to-all-start = ((bf16[32,32,512]{2,1,0:T(8,128)(2,1)}), bf16[32,32,512]{2,1,0:T(8,128)(2,1)S(1)}, u32[]{:S(2)}, u32[]{:S(2)}) async-start(bf16[32,32,512]{2,1,0:T(8,128)(2,1)} %bitcast.138), calls=%async_computation | async-start | bytes 2097152 | tf_op jit(solution)/shard_map/all_to_all | solution.py:22
  14.8 2.5 %convolution_convert_fusion.1 = bf16[1024,512]{1,0:T(8,128)(2,1)} fusion(bf16[512,256]{1,0:T(8,128)(2,1)S(1)} %copy-done.7, bf16[1,1024,256]{2,1,0:T(8,128)(2,1)} %param.11), kind=kOutput, calls=%fused_computation.25 | convolution fusion | flops 268959744 | bytes 1835008 | tf_op jit(solution)/shard_map/dot_general | solution.py:9
  17.3 28.0 %all-to-all-done = bf16[32,32,512]{2,1,0:T(8,128)(2,1)S(1)} async-done(((bf16[32,32,512]{2,1,0:T(8,128)(2,1)}), bf16[32,32,512]{2,1,0:T(8,128)(2,1)S(1)}, u32[]{:S(2)}, u32[]{:S(2)}) %all-to-all-start) | async-done | bytes 1048608 | tf_op jit(solution)/shard_map/all_to_all | solution.py:22
  45.2 4.4 %all-to-all-start.1 = ((bf16[32,32,512]{2,1,0:T(8,128)(2,1)}), bf16[32,32,512]{2,1,0:T(8,128)(2,1)}, u32[]{:S(2)}, u32[]{:S(2)}) async-start(bf16[32,32,512]{2,1,0:T(8,128)(2,1)} %bitcast.137), calls=%async_computation.1 | async-start | bytes 2097152 | tf_op jit(solution)/shard_map/all_to_all | solution.py:22
  49.7 2.9 %fusion.13 = f32[512,1024]{1,0:T(8,128)S(1)} fusion(bf16[1024,512]{1,0:T(8,128)(2,1)S(1)} %bitcast.135, bf16[1,1024,1024]{2,1,0:T(8,128)(2,1)} %param.9), kind=kOutput, calls=%fused_computation.19 | convolution fusion | flops 1073741824 | bytes 5242880 | tf_op jit(solution)/shard_map/dot_general | solution.py:9
  53.9 2.3 %fusion.18 = bf16[512,1024]{0,1:T(8,128)(2,1)} fusion(bf16[1,1024,1024]{2,1,0:T(8,128)(2,1)S(1)} %copy-done, f32[512,1024]{1,0:T(8,128)S(1)} %fusion.13), kind=kOutput, calls=%fused_computation.23 | convolution fusion | flops 1076887552 | bytes 5242880 | tf_op jit(solution)/shard_map/dot_general | solution.py:9
  56.3 23.5 %all-to-all-done.1 = bf16[32,32,512]{2,1,0:T(8,128)(2,1)} async-done(((bf16[32,32,512]{2,1,0:T(8,128)(2,1)}), bf16[32,32,512]{2,1,0:T(8,128)(2,1)}, u32[]{:S(2)}, u32[]{:S(2)}) %all-to-all-start.1) | async-done | bytes 1048608 | tf_op jit(solution)/shard_map/all_to_all | solution.py:22
  79.8 4.5 %all-to-all-start.2 = ((bf16[32,32,512]{2,1,0:T(8,128)(2,1)}), bf16[32,32,512]{2,1,0:T(8,128)(2,1)}, u32[]{:S(2)}, u32[]{:S(2)}) async-start(bf16[32,32,512]{2,1,0:T(8,128)(2,1)} %bitcast.142), calls=%async_computation.2 | async-start | bytes 2097152 | tf_op jit(solution)/shard_map/all_to_all | solution.py:22
  84.2 3.2 %multiply_convert_fusion.1 = bf16[1024,1024]{1,0:T(8,128)(2,1)S(1)} fusion(bf16[1024,512]{1,0:T(8,128)(2,1)} %bitcast.5, f32[512,1024]{1,0:T(8,128)} %copy-done.3), kind=kOutput, calls=%fused_computation.1 | convolution fusion | flops 1078460416 | bytes 5242880 | tf_op jit(solution)/shard_map/dot_general | solution.py:9
  88.9 1.5 collective-permute-start.1
  90.3 1.7 collective-permute-start.2
  92.1 1.8 collective-permute-start.3
  93.9 2.9 %fusion.1 = bf16[1024,512]{0,1:T(8,128)(2,1)S(1)} fusion(f32[512,1024]{1,0:T(8,128)S(1)} %copy-done.4, bf16[1024,512]{1,0:T(8,128)(2,1)} %bitcast.5, bf16[1,1024,1024]{2,1,0:T(8,128)(2,1)S(1)} %copy-done), kind=kOutput, calls=%fused_computation.4 | convolution fusion | flops 1078460416 | bytes 6291456 | tf_op jit(solution)/shard_map/dot_general | solution.py:9
  100.1 2.3 %fusion.23 = bf16[1024,512]{1,0:T(8,128)(2,1)} fusion(bf16[1024,512]{0,1:T(8,128)(2,1)S(1)} %fusion.1, bf16[1,1024,1024]{2,1,0:T(8,128)(2,1)S(1)} %copy-done.2), kind=kOutput, calls=%fused_computation.26 | convolution fusion | flops 1074266112 | bytes 4194304 | tf_op jit(solution)/shard_map/dot_general | solution.py:9
  102.4 12.0 %all-to-all-done.2 = bf16[32,32,512]{2,1,0:T(8,128)(2,1)} async-done(((bf16[32,32,512]{2,1,0:T(8,128)(2,1)}), bf16[32,32,512]{2,1,0:T(8,128)(2,1)}, u32[]{:S(2)}, u32[]{:S(2)}) %all-to-all-start.2) | async-done | bytes 1048608 | tf_op jit(solution)/shard_map/all_to_all | solution.py:22
  114.4 4.5 %all-to-all-start.3 = ((bf16[32,32,512]{2,1,0:T(8,128)(2,1)}), bf16[32,32,512]{2,1,0:T(8,128)(2,1)}, u32[]{:S(2)}, u32[]{:S(2)}) async-start(bf16[32,32,512]{2,1,0:T(8,128)(2,1)} %bitcast.141), calls=%async_computation.3 | async-start | bytes 2097152 | tf_op jit(solution)/shard_map/all_to_all | solution.py:22
  118.9 1.9 %add_convert_fusion.1 = bf16[2,128,1024]{2,1,0:T(8,128)(2,1)S(1)} fusion(bf16[2,128,1024]{2,1,0:T(8,128)(2,1)} %collective-permute-done.3, bf16[2,128,1024]{2,1,0:T(8,128)(2,1)} %collective-permute-done.2, bf16[2,128,1024]{2,1,0:T(8,128)(2,1)} %collective-permute-done.1, bf16[2,128,1024]{2,1,0:T(8,128)(2,1)} %get-tuple-element.33), kind=kLoop, calls=%fused_computation.34 | loop fusion | flops 2097152 | bytes 2621440 | tf_op jit(solution)/shard_map/convert_element_type | solution.py:108
  121.6 2.4 %convolution_convert_fusion.3 = bf16[512,256]{1,0:T(8,128)(2,1)} fusion(bf16[1024,512]{1,0:T(8,128)(2,1)} %bitcast.18, bf16[1,1024,256]{2,1,0:T(8,128)(2,1)S(1)} %copy-done.5), kind=kOutput, calls=%fused_computation.33 | convolution fusion | flops 268566528 | bytes 1835008 | tf_op jit(solution)/shard_map/dot_general | solution.py:9
  124.0 19.3 %collective-permute-done.7 = bf16[128,1024]{1,0:T(8,128)(2,1)S(1)} collective-permute-done((bf16[128,1024]{1,0:T(8,128)(2,1)S(1)}, bf16[128,1024]{1,0:T(8,128)(2,1)S(1)}, u32[]{:S(2)}, u32[]{:S(2)}) %collective-permute-start.7) | collective-permute-done | bytes 262176 | tf_op jit(solution)/shard_map/ppermute | solution.py:41
  143.3 1.6 add_convert_fusion
  145.0 2.0 %fusion.27 = bf16[1024,256]{1,0:T(8,128)(2,1)S(1)} fusion(bf16[1024,512]{1,0:T(8,128)(2,1)} %bitcast.18, bf16[512,256]{1,0:T(8,128)(2,1)S(1)} %copy-done.7), kind=kOutput, calls=%fused_computation.30 | convolution fusion | flops 268959744 | bytes 1835008 | tf_op jit(solution)/shard_map/dot_general | solution.py:9
  147.0 2.5 %collective-permute-start.10 = (bf16[2,128,256]{2,1,0:T(8,128)(2,1)S(1)}, bf16[2,128,256]{2,1,0:T(8,128)(2,1)S(1)}, u32[]{:S(2)}, u32[]{:S(2)}) collective-permute-start(bf16[2,128,256]{2,1,0:T(8,128)(2,1)S(1)} %get-tuple-element.57), channel_id=1, source_target_pairs={{0,128},{32,160},{64,192},{96,224},{128,0},{160,32},{192,64},{224,... | collective-permute-start | bytes 393224 | tf_op jit(solution)/shard_map/ppermute | solution.py:65
  149.8 2.9 %collective-permute-start.9 = (bf16[2,128,256]{2,1,0:T(8,128)(2,1)S(1)}, bf16[2,128,256]{2,1,0:T(8,128)(2,1)S(1)}, u32[]{:S(2)}, u32[]{:S(2)}) collective-permute-start(bf16[2,128,256]{2,1,0:T(8,128)(2,1)S(1)} %get-tuple-element.58), channel_id=1, source_target_pairs={{0,192},{32,224},{64,0},{96,32},{128,64},{160,96},{192,128},{224,1... | collective-permute-start | bytes 393224 | tf_op jit(solution)/shard_map/ppermute | solution.py:65
  152.9 3.2 %collective-permute-start.5 = (bf16[128,1024]{1,0:T(8,128)(2,1)S(1)}, bf16[128,1024]{1,0:T(8,128)(2,1)S(1)}, u32[]{:S(2)}, u32[]{:S(2)}) collective-permute-start(bf16[128,1024]{1,0:T(8,128)(2,1)S(1)} %get-tuple-element.55), channel_id=1, source_target_pairs={{0,192},{32,224},{64,0},{96,32},{128,64},{160,96},{192,128},{224,1... | collective-permute-start | bytes 786440 | tf_op jit(solution)/shard_map/ppermute | solution.py:65
  159.6 2.4 %collective-permute-done.11 = bf16[128,256]{1,0:T(8,128)(2,1)S(1)} collective-permute-done((bf16[128,256]{1,0:T(8,128)(2,1)S(1)}, bf16[128,256]{1,0:T(8,128)(2,1)S(1)}, u32[]{:S(2)}, u32[]{:S(2)}) %collective-permute-start.11) | collective-permute-done | bytes 65568 | tf_op jit(solution)/shard_map/ppermute | solution.py:41
  162.6 5.0 %collective-permute-done.4 = bf16[128,1024]{1,0:T(8,128)(2,1)S(1)} collective-permute-done((bf16[128,1024]{1,0:T(8,128)(2,1)S(1)}, bf16[128,1024]{1,0:T(8,128)(2,1)S(1)}, u32[]{:S(2)}, u32[]{:S(2)}) %collective-permute-start.4) | collective-permute-done | bytes 262176 | tf_op jit(solution)/shard_map/ppermute | solution.py:65
  168.3 1.7 fusion.28
  171.0 3.8 %all-to-all-start.4 = ((bf16[8,32,1024]{2,1,0:T(8,128)(2,1)}), bf16[8,32,1024]{2,1,0:T(8,128)(2,1)S(1)}, u32[]{:S(2)}, u32[]{:S(2)}) async-start(bf16[8,32,1024]{2,1,0:T(8,128)(2,1)} %bitcast.25), calls=%async_computation.4 | async-start | bytes 1048576 | tf_op jit(solution)/shard_map/all_to_all | solution.py:27
  174.8 2.1 %fusion.32 = f32[1,128,1024]{2,1,0:T(8,128)} fusion(bf16[128,1024]{1,0:T(8,128)(2,1)} %collective-permute-done.6, bf16[128,1024]{1,0:T(8,128)(2,1)} %copy-done.9, bf16[128,1024]{1,0:T(8,128)(2,1)S(1)} %collective-permute-done.4, bf16[4,128,1024]{2,1,0:T(8,128)(2,1)} %copy-done.1, s32[]{:T(128)S(6)} %select_n.39), kind=kLoop, calls=%fused_computation.43 | loop fusion | flops 917504 | bytes 1572868 | tf_op jit(solution)/shard_map/broadcast_in_dim | solution.py:124
  176.9 2.4 %convolution_convert_fusion.2 = bf16[512,256]{1,0:T(8,128)(2,1)} fusion(bf16[1024,512]{1,0:T(8,128)(2,1)} %bitcast.23, bf16[1,256,1024]{2,1,0:T(8,128)(2,1)S(1)} %copy-done.6), kind=kOutput, calls=%fused_computation.32 | convolution fusion | flops 268566528 | bytes 1835008 | tf_op jit(solution)/shard_map/dot_general | solution.py:9
  179.3 3.7 %all-to-all-done.4 = bf16[8,32,1024]{2,1,0:T(8,128)(2,1)S(1)} async-done(((bf16[8,32,1024]{2,1,0:T(8,128)(2,1)}), bf16[8,32,1024]{2,1,0:T(8,128)(2,1)S(1)}, u32[]{:S(2)}, u32[]{:S(2)}) %all-to-all-start.4) | async-done | bytes 524320 | tf_op jit(solution)/shard_map/all_to_all | solution.py:27
  (48 shorter events, 13.7 us)
Async XLA Ops:
  0.6 53.3 %copy-start = (bf16[1,1024,1024]{2,1,0:T(8,128)(2,1)S(1)}, bf16[1,1024,1024]{2,1,0:T(8,128)(2,1)}, u32[]{:S(2)}) copy-start(bf16[1,1024,1024]{2,1,0:T(8,128)(2,1)} %param.10) | copy-start | bytes 6291460
  0.6 14.1 %copy-start.7 = (bf16[512,256]{1,0:T(8,128)(2,1)S(1)}, bf16[512,256]{1,0:T(8,128)(2,1)}, u32[]{:S(2)}) copy-start(bf16[512,256]{1,0:T(8,128)(2,1)} %param.7) | copy-start | bytes 786436
  3.4 41.9 %all-to-all-start = ((bf16[32,32,512]{2,1,0:T(8,128)(2,1)}), bf16[32,32,512]{2,1,0:T(8,128)(2,1)S(1)}, u32[]{:S(2)}, u32[]{:S(2)}) async-start(bf16[32,32,512]{2,1,0:T(8,128)(2,1)} %bitcast.138), calls=%async_computation | async-start | bytes 2097152 | tf_op jit(solution)/shard_map/all_to_all | solution.py:22
  45.2 34.5 %all-to-all-start.1 = ((bf16[32,32,512]{2,1,0:T(8,128)(2,1)}), bf16[32,32,512]{2,1,0:T(8,128)(2,1)}, u32[]{:S(2)}, u32[]{:S(2)}) async-start(bf16[32,32,512]{2,1,0:T(8,128)(2,1)} %bitcast.137), calls=%async_computation.1 | async-start | bytes 2097152 | tf_op jit(solution)/shard_map/all_to_all | solution.py:22
  52.6 1.3 copy-start.3
  79.8 34.6 %all-to-all-start.2 = ((bf16[32,32,512]{2,1,0:T(8,128)(2,1)}), bf16[32,32,512]{2,1,0:T(8,128)(2,1)}, u32[]{:S(2)}, u32[]{:S(2)}) async-start(bf16[32,32,512]{2,1,0:T(8,128)(2,1)} %bitcast.142), calls=%async_computation.2 | async-start | bytes 2097152 | tf_op jit(solution)/shard_map/all_to_all | solution.py:22
  87.5 6.4 %copy-start.4 = (f32[512,1024]{1,0:T(8,128)S(1)}, f32[512,1024]{1,0:T(8,128)}, u32[]{:S(2)}) copy-start(f32[512,1024]{1,0:T(8,128)} %copy-done.3) | copy-start | bytes 6291460
  88.9 30.0 %collective-permute-start.1 = (bf16[2,128,1024]{2,1,0:T(8,128)(2,1)}, bf16[2,128,1024]{2,1,0:T(8,128)(2,1)}, u32[]{:S(2)}, u32[]{:S(2)}) collective-permute-start(bf16[2,128,1024]{2,1,0:T(8,128)(2,1)} %get-tuple-element.34), channel_id=1, source_target_pairs={{0,64},{32,96},{64,128},{96,160},{128,192},{160,224},{192,0},{224,... | collective-permute-start | bytes 1572872 | tf_op jit(solution)/shard_map/ppermute | solution.py:65
  90.3 28.5 %collective-permute-start.2 = (bf16[2,128,1024]{2,1,0:T(8,128)(2,1)}, bf16[2,128,1024]{2,1,0:T(8,128)(2,1)}, u32[]{:S(2)}, u32[]{:S(2)}) collective-permute-start(bf16[2,128,1024]{2,1,0:T(8,128)(2,1)} %get-tuple-element.35), channel_id=1, source_target_pairs={{0,192},{32,224},{64,0},{96,32},{128,64},{160,96},{192,128},{224,1... | collective-permute-start | bytes 1572872 | tf_op jit(solution)/shard_map/ppermute | solution.py:65
  92.1 26.8 %collective-permute-start.3 = (bf16[2,128,1024]{2,1,0:T(8,128)(2,1)}, bf16[2,128,1024]{2,1,0:T(8,128)(2,1)}, u32[]{:S(2)}, u32[]{:S(2)}) collective-permute-start(bf16[2,128,1024]{2,1,0:T(8,128)(2,1)} %get-tuple-element.36), channel_id=1, source_target_pairs={{0,128},{32,160},{64,192},{96,224},{128,0},{160,32},{192,64},{224,... | collective-permute-start | bytes 1572872 | tf_op jit(solution)/shard_map/ppermute | solution.py:65
  98.1 2.0 %copy-start.2 = (bf16[1,1024,1024]{2,1,0:T(8,128)(2,1)S(1)}, bf16[1,1024,1024]{2,1,0:T(8,128)(2,1)}, u32[]{:S(2)}) copy-start(bf16[1,1024,1024]{2,1,0:T(8,128)(2,1)} %param.9) | copy-start | bytes 6291460
  99.3 44.0 %collective-permute-start = (bf16[4,128,1024]{2,1,0:T(8,128)(2,1)}, bf16[4,128,1024]{2,1,0:T(8,128)(2,1)}, u32[]{:S(2)}, u32[]{:S(2)}) collective-permute-start(bf16[4,128,1024]{2,1,0:T(8,128)(2,1)} %get-tuple-element.48), channel_id=1, source_target_pairs={{0,32},{32,0},{64,96},{96,64},{128,160},{160,128},{192,224},{224,1... | collective-permute-start | bytes 3145736 | tf_op jit(solution)/shard_map/ppermute | solution.py:41
  114.4 53.2 %all-to-all-start.3 = ((bf16[32,32,512]{2,1,0:T(8,128)(2,1)}), bf16[32,32,512]{2,1,0:T(8,128)(2,1)}, u32[]{:S(2)}, u32[]{:S(2)}) async-start(bf16[32,32,512]{2,1,0:T(8,128)(2,1)} %bitcast.141), calls=%async_computation.3 | async-start | bytes 2097152 | tf_op jit(solution)/shard_map/all_to_all | solution.py:22
  118.9 2.8 %copy-start.5 = (bf16[1,1024,256]{2,1,0:T(8,128)(2,1)S(1)}, bf16[1,1024,256]{2,1,0:T(8,128)(2,1)}, u32[]{:S(2)}) copy-start(bf16[1,1024,256]{2,1,0:T(8,128)(2,1)} %param.11) | copy-start | bytes 1572868
  120.9 22.5 %collective-permute-start.7 = (bf16[128,1024]{1,0:T(8,128)(2,1)S(1)}, bf16[128,1024]{1,0:T(8,128)(2,1)S(1)}, u32[]{:S(2)}, u32[]{:S(2)}) collective-permute-start(bf16[128,1024]{1,0:T(8,128)(2,1)S(1)} %dynamic-slice_bitcast_fusion.6), channel_id=1, source_target_pairs={{0,32},{32,0},{64,96},{96,64},{128,160},{160,128},{192,224},{224,1... | collective-permute-start | bytes 786440 | tf_op jit(solution)/shard_map/ppermute | solution.py:41
  144.9 7.9 %copy-start.1 = (bf16[4,128,1024]{2,1,0:T(8,128)(2,1)}, bf16[4,128,1024]{2,1,0:T(8,128)(2,1)S(1)}, u32[]{:S(2)}) copy-start(bf16[4,128,1024]{2,1,0:T(8,128)(2,1)S(1)} %add_convert_fusion) | copy-start | bytes 3145732
  147.0 21.3 %copy-start.8 = (bf16[512,256]{1,0:T(8,128)(2,1)S(1)}, bf16[512,256]{1,0:T(8,128)(2,1)}, u32[]{:S(2)}) copy-start(bf16[512,256]{1,0:T(8,128)(2,1)} %param.6) | copy-start | bytes 786436
  147.0 9.1 %collective-permute-start.10 = (bf16[2,128,256]{2,1,0:T(8,128)(2,1)S(1)}, bf16[2,128,256]{2,1,0:T(8,128)(2,1)S(1)}, u32[]{:S(2)}, u32[]{:S(2)}) collective-permute-start(bf16[2,128,256]{2,1,0:T(8,128)(2,1)S(1)} %get-tuple-element.57), channel_id=1, source_target_pairs={{0,128},{32,160},{64,192},{96,224},{128,0},{160,32},{192,64},{224,... | collective-permute-start | bytes 393224 | tf_op jit(solution)/shard_map/ppermute | solution.py:65
  149.5 8.0 %collective-permute-start.8 = (bf16[2,128,256]{2,1,0:T(8,128)(2,1)S(1)}, bf16[2,128,256]{2,1,0:T(8,128)(2,1)S(1)}, u32[]{:S(2)}, u32[]{:S(2)}) collective-permute-start(bf16[2,128,256]{2,1,0:T(8,128)(2,1)S(1)} %get-tuple-element.59), channel_id=1, source_target_pairs={{0,64},{32,96},{64,128},{96,160},{128,192},{160,224},{192,0},{224,... | collective-permute-start | bytes 393224 | tf_op jit(solution)/shard_map/ppermute | solution.py:65
  149.8 7.7 %collective-permute-start.9 = (bf16[2,128,256]{2,1,0:T(8,128)(2,1)S(1)}, bf16[2,128,256]{2,1,0:T(8,128)(2,1)S(1)}, u32[]{:S(2)}, u32[]{:S(2)}) collective-permute-start(bf16[2,128,256]{2,1,0:T(8,128)(2,1)S(1)} %get-tuple-element.58), channel_id=1, source_target_pairs={{0,192},{32,224},{64,0},{96,32},{128,64},{160,96},{192,128},{224,1... | collective-permute-start | bytes 393224 | tf_op jit(solution)/shard_map/ppermute | solution.py:65
  152.8 14.8 %collective-permute-start.4 = (bf16[128,1024]{1,0:T(8,128)(2,1)S(1)}, bf16[128,1024]{1,0:T(8,128)(2,1)S(1)}, u32[]{:S(2)}, u32[]{:S(2)}) collective-permute-start(bf16[128,1024]{1,0:T(8,128)(2,1)S(1)} %get-tuple-element.56), channel_id=1, source_target_pairs={{0,64},{32,96},{64,128},{96,160},{128,192},{160,224},{192,0},{224,... | collective-permute-start | bytes 786440 | tf_op jit(solution)/shard_map/ppermute | solution.py:65
  152.9 14.7 %collective-permute-start.5 = (bf16[128,1024]{1,0:T(8,128)(2,1)S(1)}, bf16[128,1024]{1,0:T(8,128)(2,1)S(1)}, u32[]{:S(2)}, u32[]{:S(2)}) collective-permute-start(bf16[128,1024]{1,0:T(8,128)(2,1)S(1)} %get-tuple-element.55), channel_id=1, source_target_pairs={{0,192},{32,224},{64,0},{96,32},{128,64},{160,96},{192,128},{224,1... | collective-permute-start | bytes 786440 | tf_op jit(solution)/shard_map/ppermute | solution.py:65
  156.1 11.5 %collective-permute-start.6 = (bf16[128,1024]{1,0:T(8,128)(2,1)S(1)}, bf16[128,1024]{1,0:T(8,128)(2,1)}, u32[]{:S(2)}, u32[]{:S(2)}) collective-permute-start(bf16[128,1024]{1,0:T(8,128)(2,1)S(1)} %get-tuple-element.54), channel_id=1, source_target_pairs={{0,128},{32,160},{64,192},{96,224},{128,0},{160,32},{192,64},{224,... | collective-permute-start | bytes 786440 | tf_op jit(solution)/shard_map/ppermute | solution.py:65
  157.6 4.4 %collective-permute-start.11 = (bf16[128,256]{1,0:T(8,128)(2,1)S(1)}, bf16[128,256]{1,0:T(8,128)(2,1)S(1)}, u32[]{:S(2)}, u32[]{:S(2)}) collective-permute-start(bf16[128,256]{1,0:T(8,128)(2,1)S(1)} %dynamic-slice_bitcast_fusion.13), channel_id=1, source_target_pairs={{0,32},{32,0},{64,96},{96,64},{128,160},{160,128},{192,224},{224,1... | collective-permute-start | bytes 196616 | tf_op jit(solution)/shard_map/ppermute | solution.py:41
  167.6 0.7 copy-start.9
  170.0 6.9 %copy-start.6 = (bf16[1,256,1024]{2,1,0:T(8,128)(2,1)S(1)}, bf16[1,256,1024]{2,1,0:T(8,128)(2,1)}, u32[]{:S(2)}) copy-start(bf16[1,256,1024]{2,1,0:T(8,128)(2,1)} %param.8) | copy-start | bytes 1572868
  171.0 12.0 %all-to-all-start.4 = ((bf16[8,32,1024]{2,1,0:T(8,128)(2,1)}), bf16[8,32,1024]{2,1,0:T(8,128)(2,1)S(1)}, u32[]{:S(2)}, u32[]{:S(2)}) async-start(bf16[8,32,1024]{2,1,0:T(8,128)(2,1)} %bitcast.25), calls=%async_computation.4 | async-start | bytes 1048576 | tf_op jit(solution)/shard_map/all_to_all | solution.py:27

commit v4 on v3

--- a/solution.py
+++ b/solution.py
@@ -44,29 +44,39 @@
 
 
 def column_blocks(cur):
-    columns = cur.shape[0]
     column = jnp.right_shift(lax.axis_index("dp"), 1)
-    return [
+    own, ahead, back, far = (
         lax.dynamic_index_in_dim(
-            cur, jnp.bitwise_and(column + step, columns - 1), 0, keepdims=False
+            cur, jnp.bitwise_and(column + step, cur.shape[0] - 1), 0, keepdims=False
         )
-        for step in column_steps(columns)
-    ]
+        for step in (0, 1, 3, 2)
+    )
+    return [own, ahead, back, far[0], far[1]]
 
 
-def column_steps(columns):
-    return (1, columns - 1, *range(2, columns - 1), 0)
+def shifted(value, step):
+    size = lax.axis_size("dp")
+    return lax.ppermute(value, "dp", [(i, (i + 2 * step) % size) for i in range(size)])
 
 
-def over_columns(blocks, after=()):
-    size = lax.axis_size("dp")
-    *sent, kept = blocks
-    got = [
-        lax.ppermute(block, "dp", [(i, (i + 2 * step) % size) for i in range(size)])
-        for step, block in zip(column_steps(size // 2), sent)
-    ]
-    got = lax.optimization_barrier((*got, *after))[: len(sent)]
-    return sum((block.astype(jnp.float32) for block in got), kept.astype(jnp.float32))
+def added(*terms):
+    return sum((term.astype(jnp.float32) for term in terms[1:]), terms[0].astype(jnp.float32))
+
+
+def first_leg(blocks):
+    own, ahead, back, far_ahead, far_back = blocks
+    from_back, from_ahead = shifted(far_ahead, 1), shifted(far_back, -1)
+    half = own.dtype
+    ahead = jnp.stack([added(ahead[0], from_back).astype(half), ahead[1]])
+    back = jnp.stack([back[0], added(back[1], from_ahead).astype(half)])
+    return [own, ahead, back]
+
+
+def second_leg(blocks, after=()):
+    own, ahead, back = blocks
+    got = (shifted(ahead, 1), shifted(back, -1))
+    got = lax.optimization_barrier((*got, *after))[:2]
+    return added(own, *got)
 
 
 def by_place(part):
@@ -93,30 +103,32 @@
     grad_act_down, _ = lax.optimization_barrier((received, act_down))
     mixed_down = exchange(act_down)
     left_down_part = (contract(hidden, 1, grad_act_down, 1) * scale).astype(half)
-    grad_act_down, *blocks = lax.optimization_barrier(
+    grad_act_down, *down_blocks = lax.optimization_barrier(
         (grad_act_down, *column_blocks(by_place(left_down_part)))
     )
+    down_blocks = first_leg(down_blocks)
     grad_hidden = contract(weight_ld, 1, grad_act_down, 0)
     grad_pre = (grad_hidden * sigma * (1.0 + pre * (1.0 - sigma))).astype(half)
     left_up_part = (contract(mixed_up, 1, grad_pre, 1) * scale).astype(half)
-    halves = pair_halves(by_place(left_up_part), 1)
-    grad_mixed_up = contract(weight_lu, 1, grad_pre, 0).astype(half)
-    grad_mixed_up = row_major(grad_mixed_up)
+    up_blocks = first_leg(column_blocks(by_place(left_up_part)))
+    grad_mixed_up = row_major(contract(weight_lu, 1, grad_pre, 0).astype(half))
     grad_mixed_up, mixed_down, *_ = lax.optimization_barrier(
-        (grad_mixed_up, mixed_down, *halves)
+        (grad_mixed_up, mixed_down, *down_blocks, *up_blocks)
     )
-    left_down_half = over_columns(blocks).astype(half)
+    grad_act_up = exchange(grad_mixed_up)
+    left_down_half = second_leg(down_blocks, (mixed_down,)).astype(half)
     left_down_grad = over_pairs(pair_halves(left_down_half, 0))
-    left_up_half = over_pairs(halves, (left_down_half, mixed_down)).astype(half)
-    left_up_grad = over_columns(column_blocks(left_up_half))
-    grad_act_up = exchange(grad_mixed_up)
+    later, _ = lax.optimization_barrier((mixed_down, mixed_down))
+    right_down_part = row_major((contract(later, 1, cotangent, 0) * scale).astype(half))
+    right_blocks = column_blocks(by_place(right_down_part))
     layer_out = contract(mixed_down, 0, weight_rd, 0).astype(half)
-    later, _ = lax.optimization_barrier((mixed_down, left_up_half))
-    right_down_part = row_major((contract(later, 1, cotangent, 0) * scale).astype(half))
-    right_down_half = over_columns(column_blocks(by_place(right_down_part))).astype(half)
+    left_up_half = second_leg(up_blocks, (mixed_down,)).astype(half)
+    right_up_part = (contract(tokens, 0, grad_act_up, 1) * scale).astype(half)
+    left_up_grad = over_pairs(pair_halves(left_up_half, 0))
+    right_up_grad = summed(right_up_part)
+    right_down_half = second_leg(first_leg(right_blocks), (right_up_part,)).astype(half)
     right_down_grad = over_pairs(pair_halves(right_down_half, 0))
     tokens_grad = contract(grad_act_up, 0, weight_ru, 1).astype(half)
-    right_up_grad = summed((contract(tokens, 0, grad_act_up, 1) * scale).astype(half))
     return (
         layer_out,
         tokens_grad,

time: 186 us -> 177 us (0.952)
  waiting for transfers between devices: 93.9 us -> 73.1 us
  starting transfers between devices: 46.5 us -> 55.1 us
  other arithmetic: 7.93 us -> 12.4 us
    all_to_all x4, waiting for transfers between devices: 63.5 us -> 51.9 us  [exchange(): return lax.all_to_all(tile, 'hid', 0, 0, tiled=True)]
    ppermute x3, waiting for transfers between devices: 21.7 us -> 15.7 us  [over_pairs(): got = lax.ppermute(sent, 'dp', pairs)]
    all_to_all x4, starting transfers between devices: 24.7 us -> 30.2 us  [exchange(): return lax.all_to_all(tile, 'hid', 0, 0, tiled=True)]
    another operation x0 -> x10, other arithmetic: none -> 5.16 us  [the longest x6 2.7 us: first_leg(): back = jnp.stack([back[0], added(back[1], from_ahead).astype(half)])]
    all_to_all x1, waiting for transfers between devices: 3.69 us -> 0.01 us  [summed(): lax.all_to_all(part, 'dp', 0, 0, tiled=True)]
    ppermute x9 -> x12, starting transfers between devices: 15.4 us -> 17.2 us  [shifted(): lax.ppermute(value, 'dp', [(i, (i + 2 * step) % size) for i in range(size)])]
    ppermute x9 -> x12, waiting for transfers between devices: 5.04 us -> 5.46 us  [shifted(): lax.ppermute(value, 'dp', [(i, (i + 2 * step) % size) for i in range(size)])]
  transfers between devices with their start and end apart: 17 -> 20, of which waited for: 7 -> 7; matrix products, arithmetic and copies ran while one was open for 19% -> 23% of each run, Pallas kernels for 0% -> 0%
where the time goes in v4:
time: 177 us; the launch traced here: 175 us
  waiting for transfers between devices  73.1 us (41%)
  starting transfers between devices  55.1 us (31%)
  matrix products  28.1 us (16%)
  other arithmetic  12.4 us (7%)
  local copies, waits for them, and re-layouts  5.57 us (3%)
    all_to_all x4, waiting for transfers between devices, exchange(): return lax.all_to_all(tile, 'hid', 0, 0, tiled=True)  51.9 us
    all_to_all x4, starting transfers between devices, exchange(): return lax.all_to_all(tile, 'hid', 0, 0, tiled=True)  30.2 us
    dot_general x12, matrix products, contract(): lax.dot_general(left_side, right_side, (((left_dim,), (right_dim,)), ((),...  28.1 us
    ppermute x12, starting transfers between devices, shifted(): lax.ppermute(value, 'dp', [(i, (i + 2 * step) % size) for i in range(size)])  17.2 us
    ppermute x3, waiting for transfers between devices, over_pairs(): got = lax.ppermute(sent, 'dp', pairs)  15.7 us
    ppermute x12, waiting for transfers between devices, shifted(): lax.ppermute(value, 'dp', [(i, (i + 2 * step) % size) for i in range(size)])  5.46 us
    ppermute x3, starting transfers between devices, over_pairs(): got = lax.ppermute(sent, 'dp', pairs)  4.19 us
  transfers between devices with their start and end apart: 20, of which 7 were waited for; matrix products, arithmetic and copies ran while one was open for 23% of the time, Pallas kernels for 0%

profile of v4, /device:TPU:32, one launch (start us, length us, event | category | flops | bytes accessed | tf_op | source)
XLA Modules:
  0.0 175.2 jit_solution(7382613174375320899)
XLA Ops:
  0.7 2.7 %convolution_convert_fusion = bf16[1024,512]{1,0:T(8,128)(2,1)} fusion(bf16[512,256]{1,0:T(8,128)(2,1)} %param.6, bf16[1,256,1024]{2,1,0:T(8,128)(2,1)} %param.8), kind=kOutput, calls=%fused_computation.23 | convolution fusion | flops 268959744 | bytes 1835008 | tf_op jit(solution)/shard_map/dot_general | solution.py:9
  3.4 11.4 %all-to-all-start = ((bf16[32,32,512]{2,1,0:T(8,128)(2,1)}), bf16[32,32,512]{2,1,0:T(8,128)(2,1)S(1)}, u32[]{:S(2)}, u32[]{:S(2)}) async-start(bf16[32,32,512]{2,1,0:T(8,128)(2,1)} %bitcast.184), calls=%async_computation | async-start | bytes 2097152 | tf_op jit(solution)/shard_map/all_to_all | solution.py:22
  14.8 2.5 %convolution_convert_fusion.1 = bf16[1024,512]{1,0:T(8,128)(2,1)} fusion(bf16[512,256]{1,0:T(8,128)(2,1)S(1)} %copy-done.9, bf16[1,1024,256]{2,1,0:T(8,128)(2,1)} %param.11), kind=kOutput, calls=%fused_computation.24 | convolution fusion | flops 268959744 | bytes 1835008 | tf_op jit(solution)/shard_map/dot_general | solution.py:9
  17.3 28.0 %all-to-all-done = bf16[32,32,512]{2,1,0:T(8,128)(2,1)S(1)} async-done(((bf16[32,32,512]{2,1,0:T(8,128)(2,1)}), bf16[32,32,512]{2,1,0:T(8,128)(2,1)S(1)}, u32[]{:S(2)}, u32[]{:S(2)}) %all-to-all-start) | async-done | bytes 1048608 | tf_op jit(solution)/shard_map/all_to_all | solution.py:22
  45.3 4.5 %all-to-all-start.1 = ((bf16[32,32,512]{2,1,0:T(8,128)(2,1)}), bf16[32,32,512]{2,1,0:T(8,128)(2,1)}, u32[]{:S(2)}, u32[]{:S(2)}) async-start(bf16[32,32,512]{2,1,0:T(8,128)(2,1)} %bitcast.183), calls=%async_computation.1 | async-start | bytes 2097152 | tf_op jit(solution)/shard_map/all_to_all | solution.py:22
  49.7 2.9 %fusion.13 = f32[512,1024]{1,0:T(8,128)S(1)} fusion(bf16[1024,512]{1,0:T(8,128)(2,1)S(1)} %bitcast.181, bf16[1,1024,1024]{2,1,0:T(8,128)(2,1)} %param.9), kind=kOutput, calls=%fused_computation.19 | convolution fusion | flops 1073741824 | bytes 5242880 | tf_op jit(solution)/shard_map/dot_general | solution.py:9
  54.0 2.4 %fusion.18 = bf16[512,1024]{0,1:T(8,128)(2,1)} fusion(bf16[1,1024,1024]{2,1,0:T(8,128)(2,1)S(1)} %copy-done, f32[512,1024]{1,0:T(8,128)S(1)} %fusion.13), kind=kOutput, calls=%fused_computation.22 | convolution fusion | flops 1076887552 | bytes 5242880 | tf_op jit(solution)/shard_map/dot_general | solution.py:9
  56.4 23.4 %all-to-all-done.1 = bf16[32,32,512]{2,1,0:T(8,128)(2,1)} async-done(((bf16[32,32,512]{2,1,0:T(8,128)(2,1)}), bf16[32,32,512]{2,1,0:T(8,128)(2,1)}, u32[]{:S(2)}, u32[]{:S(2)}) %all-to-all-start.1) | async-done | bytes 1048608 | tf_op jit(solution)/shard_map/all_to_all | solution.py:22
  79.8 4.5 %all-to-all-start.2 = ((bf16[32,32,512]{2,1,0:T(8,128)(2,1)}), bf16[32,32,512]{2,1,0:T(8,128)(2,1)}, u32[]{:S(2)}, u32[]{:S(2)}) async-start(bf16[32,32,512]{2,1,0:T(8,128)(2,1)} %bitcast.192), calls=%async_computation.2 | async-start | bytes 2097152 | tf_op jit(solution)/shard_map/all_to_all | solution.py:22
  84.2 3.2 %multiply_convert_fusion.1 = bf16[1024,1024]{1,0:T(8,128)(2,1)S(1)} fusion(bf16[1024,512]{1,0:T(8,128)(2,1)} %bitcast.5, f32[512,1024]{1,0:T(8,128)} %copy-done.3), kind=kOutput, calls=%fused_computation.1 | convolution fusion | flops 1078460416 | bytes 5242880 | tf_op jit(solution)/shard_map/dot_general | solution.py:9
  89.3 2.9 %fusion.1 = bf16[1024,512]{0,1:T(8,128)(2,1)S(1)} fusion(f32[512,1024]{1,0:T(8,128)S(1)} %copy-done.4, bf16[1024,512]{1,0:T(8,128)(2,1)} %bitcast.5, bf16[1,1024,1024]{2,1,0:T(8,128)(2,1)S(1)} %copy-done), kind=kOutput, calls=%fused_computation.4 | convolution fusion | flops 1078460416 | bytes 6291456 | tf_op jit(solution)/shard_map/dot_general | solution.py:9
  92.2 1.6 collective-permute-start
  93.8 1.7 collective-permute-start.1
  97.0 1.6 collective-permute-start.3
  99.2 2.3 %fusion.23 = bf16[1024,512]{1,0:T(8,128)(2,1)} fusion(bf16[1024,512]{0,1:T(8,128)(2,1)S(1)} %fusion.1, bf16[1,1024,1024]{2,1,0:T(8,128)(2,1)S(1)} %copy-done.2), kind=kOutput, calls=%fused_computation.25 | convolution fusion | flops 1074266112 | bytes 4194304 | tf_op jit(solution)/shard_map/dot_general | solution.py:9
  101.5 5.4 %collective-permute-done.3 = bf16[128,1024]{1,0:T(8,128)(2,1)S(1)} collective-permute-done((bf16[128,1024]{1,0:T(8,128)(2,1)S(1)}, bf16[128,1024]{1,0:T(8,128)(2,1)S(1)}, u32[]{:S(2)}, u32[]{:S(2)}) %collective-permute-start.3) | collective-permute-done | bytes 262176 | tf_op jit(solution)/shard_map/ppermute | solution.py:59
  108.0 1.5 collective-permute-start.4
  110.3 1.7 collective-permute-start.5
  114.2 2.9 %collective-permute-start.8 = (bf16[2,128,1024]{2,1,0:T(8,128)(2,1)}, bf16[2,128,1024]{2,1,0:T(8,128)(2,1)}, u32[]{:S(2)}, u32[]{:S(2)}) collective-permute-start(bf16[2,128,1024]{2,1,0:T(8,128)(2,1)} %pad_maximum_fusion.1), channel_id=1, source_target_pairs={{0,192},{32,224},{64,0},{96,32},{128,64},{160,96},{192,128},{224,1... | collective-permute-start | bytes 1572872 | tf_op jit(solution)/shard_map/ppermute | solution.py:59
  117.2 9.9 %all-to-all-start.3 = ((bf16[32,32,512]{2,1,0:T(8,128)(2,1)}), bf16[32,32,512]{2,1,0:T(8,128)(2,1)S(1)}, u32[]{:S(2)}, u32[]{:S(2)}) async-start(bf16[32,32,512]{2,1,0:T(8,128)(2,1)} %bitcast.34), calls=%async_computation.3 | async-start | bytes 2097152 | tf_op jit(solution)/shard_map/all_to_all | solution.py:22
  127.1 1.7 fusion.27
  129.5 2.4 %convolution_convert_fusion.3 = bf16[512,256]{1,0:T(8,128)(2,1)} fusion(bf16[1024,512]{1,0:T(8,128)(2,1)} %bitcast.19, bf16[1,1024,256]{2,1,0:T(8,128)(2,1)S(1)} %copy-done.7), kind=kOutput, calls=%fused_computation.32 | convolution fusion | flops 268566528 | bytes 1835008 | tf_op jit(solution)/shard_map/dot_general | solution.py:9
  131.9 1.5 collective-permute-start.10
  133.4 1.6 add_convert_fusion.1
  140.3 3.2 %collective-permute-start.13 = (bf16[2,128,256]{2,1,0:T(8,128)(2,1)}, bf16[2,128,256]{2,1,0:T(8,128)(2,1)}, u32[]{:S(2)}, u32[]{:S(2)}) collective-permute-start(bf16[2,128,256]{2,1,0:T(8,128)(2,1)} %pad_maximum_fusion.5), channel_id=1, source_target_pairs={{0,192},{32,224},{64,0},{96,32},{128,64},{160,96},{192,128},{224,1... | collective-permute-start | bytes 393224 | tf_op jit(solution)/shard_map/ppermute | solution.py:59
  143.5 6.0 %collective-permute-done.6 = bf16[128,1024]{1,0:T(8,128)(2,1)S(1)} collective-permute-done((bf16[128,1024]{1,0:T(8,128)(2,1)S(1)}, bf16[128,1024]{1,0:T(8,128)(2,1)S(1)}, u32[]{:S(2)}, u32[]{:S(2)}) %collective-permute-start.6) | collective-permute-done | bytes 262176 | tf_op jit(solution)/shard_map/ppermute | solution.py:41
  149.5 6.0 %collective-permute-done.9 = bf16[128,1024]{1,0:T(8,128)(2,1)S(1)} collective-permute-done((bf16[128,1024]{1,0:T(8,128)(2,1)S(1)}, bf16[128,1024]{1,0:T(8,128)(2,1)S(1)}, u32[]{:S(2)}, u32[]{:S(2)}) %collective-permute-start.9) | collective-permute-done | bytes 262176 | tf_op jit(solution)/shard_map/ppermute | solution.py:41
  159.0 2.0 %copy.14 = bf16[256,1024]{1,0:T(8,128)(2,1)} copy(bf16[256,1024]{0,1:T(8,128)(2,1)} %fusion.28) | data formatting | bytes 1048576 | tf_op jit(solution)/shard_map/convert_element_type | solution.py:126
  161.0 3.5 %all-to-all-start.4 = ((bf16[8,32,1024]{2,1,0:T(8,128)(2,1)}), bf16[8,32,1024]{2,1,0:T(8,128)(2,1)S(1)}, u32[]{:S(2)}, u32[]{:S(2)}) async-start(bf16[8,32,1024]{2,1,0:T(8,128)(2,1)} %bitcast.37), calls=%async_computation.4 | async-start | bytes 1048576 | tf_op jit(solution)/shard_map/all_to_all | solution.py:27
  165.6 2.0 %collective-permute-start.14 = (bf16[128,256]{1,0:T(8,128)(2,1)S(1)}, bf16[128,256]{1,0:T(8,128)(2,1)S(1)}, u32[]{:S(2)}, u32[]{:S(2)}) collective-permute-start(bf16[128,256]{1,0:T(8,128)(2,1)S(1)} %dynamic-slice_bitcast_fusion.20), channel_id=1, source_target_pairs={{0,32},{32,0},{64,96},{96,64},{128,160},{160,128},{192,224},{224,1... | collective-permute-start | bytes 196616 | tf_op jit(solution)/shard_map/ppermute | solution.py:41
  167.6 2.5 %convolution_convert_fusion.2 = bf16[512,256]{1,0:T(8,128)(2,1)} fusion(bf16[1024,512]{1,0:T(8,128)(2,1)} %bitcast.191, bf16[1,256,1024]{2,1,0:T(8,128)(2,1)} %param.8), kind=kOutput, calls=%fused_computation.31 | convolution fusion | flops 268566528 | bytes 1835008 | tf_op jit(solution)/shard_map/dot_general | solution.py:9
  170.1 3.7 %collective-permute-done.14 = bf16[128,256]{1,0:T(8,128)(2,1)S(1)} collective-permute-done((bf16[128,256]{1,0:T(8,128)(2,1)S(1)}, bf16[128,256]{1,0:T(8,128)(2,1)S(1)}, u32[]{:S(2)}, u32[]{:S(2)}) %collective-permute-start.14) | collective-permute-done | bytes 65568 | tf_op jit(solution)/shard_map/ppermute | solution.py:41
  (69 shorter events, 20.9 us)
Async XLA Ops:
  0.6 53.3 %copy-start = (bf16[1,1024,1024]{2,1,0:T(8,128)(2,1)S(1)}, bf16[1,1024,1024]{2,1,0:T(8,128)(2,1)}, u32[]{:S(2)}) copy-start(bf16[1,1024,1024]{2,1,0:T(8,128)(2,1)} %param.10) | copy-start | bytes 6291460
  0.6 14.1 %copy-start.9 = (bf16[512,256]{1,0:T(8,128)(2,1)S(1)}, bf16[512,256]{1,0:T(8,128)(2,1)}, u32[]{:S(2)}) copy-start(bf16[512,256]{1,0:T(8,128)(2,1)} %param.7) | copy-start | bytes 786436
  3.4 41.9 %all-to-all-start = ((bf16[32,32,512]{2,1,0:T(8,128)(2,1)}), bf16[32,32,512]{2,1,0:T(8,128)(2,1)S(1)}, u32[]{:S(2)}, u32[]{:S(2)}) async-start(bf16[32,32,512]{2,1,0:T(8,128)(2,1)} %bitcast.184), calls=%async_computation | async-start | bytes 2097152 | tf_op jit(solution)/shard_map/all_to_all | solution.py:22
  45.3 34.5 %all-to-all-start.1 = ((bf16[32,32,512]{2,1,0:T(8,128)(2,1)}), bf16[32,32,512]{2,1,0:T(8,128)(2,1)}, u32[]{:S(2)}, u32[]{:S(2)}) async-start(bf16[32,32,512]{2,1,0:T(8,128)(2,1)} %bitcast.183), calls=%async_computation.1 | async-start | bytes 2097152 | tf_op jit(solution)/shard_map/all_to_all | solution.py:22
  52.6 1.4 copy-start.3
  79.8 37.4 %all-to-all-start.2 = ((bf16[32,32,512]{2,1,0:T(8,128)(2,1)}), bf16[32,32,512]{2,1,0:T(8,128)(2,1)}, u32[]{:S(2)}, u32[]{:S(2)}) async-start(bf16[32,32,512]{2,1,0:T(8,128)(2,1)} %bitcast.192), calls=%async_computation.2 | async-start | bytes 2097152 | tf_op jit(solution)/shard_map/all_to_all | solution.py:22
  87.5 1.8 %copy-start.4 = (f32[512,1024]{1,0:T(8,128)S(1)}, f32[512,1024]{1,0:T(8,128)}, u32[]{:S(2)}) copy-start(f32[512,1024]{1,0:T(8,128)} %copy-done.3) | copy-start | bytes 6291460
  92.2 19.8 %collective-permute-start = (bf16[128,1024]{1,0:T(8,128)(2,1)S(1)}, bf16[128,1024]{1,0:T(8,128)(2,1)S(1)}, u32[]{:S(2)}, u32[]{:S(2)}) collective-permute-start(bf16[128,1024]{1,0:T(8,128)(2,1)S(1)} %get-tuple-element.30), channel_id=1, source_target_pairs={{0,64},{32,96},{64,128},{96,160},{128,192},{160,224},{192,0},{224,... | collective-permute-start | bytes 786440 | tf_op jit(solution)/shard_map/ppermute | solution.py:59
  93.8 19.5 %collective-permute-start.1 = (bf16[128,1024]{1,0:T(8,128)(2,1)S(1)}, bf16[128,1024]{1,0:T(8,128)(2,1)S(1)}, u32[]{:S(2)}, u32[]{:S(2)}) collective-permute-start(bf16[128,1024]{1,0:T(8,128)(2,1)S(1)} %get-tuple-element.32), channel_id=1, source_target_pairs={{0,192},{32,224},{64,0},{96,32},{128,64},{160,96},{192,128},{224,1... | collective-permute-start | bytes 786440 | tf_op jit(solution)/shard_map/ppermute | solution.py:59
  96.9 10.1 %copy-start.1 = (bf16[1024,1024]{1,0:T(8,128)(2,1)}, bf16[1024,1024]{1,0:T(8,128)(2,1)S(1)}, u32[]{:S(2)}) copy-start(bf16[1024,1024]{1,0:T(8,128)(2,1)S(1)} %multiply_convert_fusion) | copy-start | bytes 6291460
  96.9 2.4 %copy-start.2 = (bf16[1,1024,1024]{2,1,0:T(8,128)(2,1)S(1)}, bf16[1,1024,1024]{2,1,0:T(8,128)(2,1)}, u32[]{:S(2)}) copy-start(bf16[1,1024,1024]{2,1,0:T(8,128)(2,1)} %param.9) | copy-start | bytes 6291460
  97.0 9.9 %collective-permute-start.3 = (bf16[128,1024]{1,0:T(8,128)(2,1)S(1)}, bf16[128,1024]{1,0:T(8,128)(2,1)S(1)}, u32[]{:S(2)}, u32[]{:S(2)}) collective-permute-start(bf16[128,1024]{1,0:T(8,128)(2,1)S(1)} %get-tuple-element.44), channel_id=1, source_target_pairs={{0,192},{32,224},{64,0},{96,32},{128,64},{160,96},{192,128},{224,1... | collective-permute-start | bytes 786440 | tf_op jit(solution)/shard_map/ppermute | solution.py:59
  98.6 8.3 %collective-permute-start.2 = (bf16[128,1024]{1,0:T(8,128)(2,1)S(1)}, bf16[128,1024]{1,0:T(8,128)(2,1)S(1)}, u32[]{:S(2)}, u32[]{:S(2)}) collective-permute-start(bf16[128,1024]{1,0:T(8,128)(2,1)S(1)} %get-tuple-element.43), channel_id=1, source_target_pairs={{0,64},{32,96},{64,128},{96,160},{128,192},{160,224},{192,0},{224,... | collective-permute-start | bytes 786440 | tf_op jit(solution)/shard_map/ppermute | solution.py:59
  108.0 24.0 %collective-permute-start.4 = (bf16[2,128,1024]{2,1,0:T(8,128)(2,1)}, bf16[2,128,1024]{2,1,0:T(8,128)(2,1)}, u32[]{:S(2)}, u32[]{:S(2)}) collective-permute-start(bf16[2,128,1024]{2,1,0:T(8,128)(2,1)} %pad_maximum_fusion.2), channel_id=1, source_target_pairs={{0,64},{32,96},{64,128},{96,160},{128,192},{160,224},{192,0},{224,... | collective-permute-start | bytes 1572872 | tf_op jit(solution)/shard_map/ppermute | solution.py:59
  110.3 23.1 %collective-permute-start.5 = (bf16[2,128,1024]{2,1,0:T(8,128)(2,1)}, bf16[2,128,1024]{2,1,0:T(8,128)(2,1)}, u32[]{:S(2)}, u32[]{:S(2)}) collective-permute-start(bf16[2,128,1024]{2,1,0:T(8,128)(2,1)} %pad_maximum_fusion.3), channel_id=1, source_target_pairs={{0,192},{32,224},{64,0},{96,32},{128,64},{160,96},{192,128},{224,1... | collective-permute-start | bytes 1572872 | tf_op jit(solution)/shard_map/ppermute | solution.py:59
  113.0 22.9 %collective-permute-start.7 = (bf16[2,128,1024]{2,1,0:T(8,128)(2,1)}, bf16[2,128,1024]{2,1,0:T(8,128)(2,1)}, u32[]{:S(2)}, u32[]{:S(2)}) collective-permute-start(bf16[2,128,1024]{2,1,0:T(8,128)(2,1)} %pad_maximum_fusion), channel_id=1, source_target_pairs={{0,64},{32,96},{64,128},{96,160},{128,192},{160,224},{192,0},{224,... | collective-permute-start | bytes 1572872 | tf_op jit(solution)/shard_map/ppermute | solution.py:59
  114.2 21.6 %collective-permute-start.8 = (bf16[2,128,1024]{2,1,0:T(8,128)(2,1)}, bf16[2,128,1024]{2,1,0:T(8,128)(2,1)}, u32[]{:S(2)}, u32[]{:S(2)}) collective-permute-start(bf16[2,128,1024]{2,1,0:T(8,128)(2,1)} %pad_maximum_fusion.1), channel_id=1, source_target_pairs={{0,192},{32,224},{64,0},{96,32},{128,64},{160,96},{192,128},{224,1... | collective-permute-start | bytes 1572872 | tf_op jit(solution)/shard_map/ppermute | solution.py:59
  117.2 40.5 %all-to-all-start.3 = ((bf16[32,32,512]{2,1,0:T(8,128)(2,1)}), bf16[32,32,512]{2,1,0:T(8,128)(2,1)S(1)}, u32[]{:S(2)}, u32[]{:S(2)}) async-start(bf16[32,32,512]{2,1,0:T(8,128)(2,1)} %bitcast.34), calls=%async_computation.3 | async-start | bytes 2097152 | tf_op jit(solution)/shard_map/all_to_all | solution.py:22
  127.1 2.4 %copy-start.7 = (bf16[1,1024,256]{2,1,0:T(8,128)(2,1)S(1)}, bf16[1,1024,256]{2,1,0:T(8,128)(2,1)}, u32[]{:S(2)}) copy-start(bf16[1,1024,256]{2,1,0:T(8,128)(2,1)} %param.11) | copy-start | bytes 1572868
  128.9 10.0 %copy-start.8 = (bf16[1024,256]{1,0:T(8,128)(2,1)}, bf16[1024,256]{1,0:T(8,128)(2,1)S(1)}, u32[]{:S(2)}) copy-start(bf16[1024,256]{1,0:T(8,128)(2,1)S(1)} %fusion.27) | copy-start | bytes 1572868
  128.9 7.0 %copy-start.5 = (bf16[2,128,1024]{2,1,0:T(8,128)(2,1)S(1)}, bf16[2,128,1024]{2,1,0:T(8,128)(2,1)}, u32[]{:S(2)}) copy-start(bf16[2,128,1024]{2,1,0:T(8,128)(2,1)} %get-tuple-element.28) | copy-start | bytes 1572868
  128.9 9.9 %collective-permute-start.12 = (bf16[128,256]{1,0:T(8,128)(2,1)S(1)}, bf16[128,256]{1,0:T(8,128)(2,1)S(1)}, u32[]{:S(2)}, u32[]{:S(2)}) collective-permute-start(bf16[128,256]{1,0:T(8,128)(2,1)S(1)} %get-tuple-element.55), channel_id=1, source_target_pairs={{0,192},{32,224},{64,0},{96,32},{128,64},{160,96},{192,128},{224,1... | collective-permute-start | bytes 196616 | tf_op jit(solution)/shard_map/ppermute | solution.py:59
  131.9 6.9 %collective-permute-start.10 = (bf16[128,256]{1,0:T(8,128)(2,1)S(1)}, bf16[128,256]{1,0:T(8,128)(2,1)S(1)}, u32[]{:S(2)}, u32[]{:S(2)}) collective-permute-start(bf16[128,256]{1,0:T(8,128)(2,1)S(1)} %get-tuple-element.54), channel_id=1, source_target_pairs={{0,64},{32,96},{64,128},{96,160},{128,192},{160,224},{192,0},{224,... | collective-permute-start | bytes 196616 | tf_op jit(solution)/shard_map/ppermute | solution.py:59
  135.1 14.4 %collective-permute-start.6 = (bf16[128,1024]{1,0:T(8,128)(2,1)S(1)}, bf16[128,1024]{1,0:T(8,128)(2,1)S(1)}, u32[]{:S(2)}, u32[]{:S(2)}) collective-permute-start(bf16[128,1024]{1,0:T(8,128)(2,1)S(1)} %dynamic-slice_bitcast_fusion.13), channel_id=1, source_target_pairs={{0,32},{32,0},{64,96},{96,64},{128,160},{160,128},{192,224},{224,1... | collective-permute-start | bytes 786440 | tf_op jit(solution)/shard_map/ppermute | solution.py:41
  137.4 20.4 %copy-start.10 = (bf16[512,256]{1,0:T(8,128)(2,1)S(1)}, bf16[512,256]{1,0:T(8,128)(2,1)}, u32[]{:S(2)}) copy-start(bf16[512,256]{1,0:T(8,128)(2,1)} %param.6) | copy-start | bytes 786436
  137.4 18.1 %collective-permute-start.9 = (bf16[128,1024]{1,0:T(8,128)(2,1)S(1)}, bf16[128,1024]{1,0:T(8,128)(2,1)S(1)}, u32[]{:S(2)}, u32[]{:S(2)}) collective-permute-start(bf16[128,1024]{1,0:T(8,128)(2,1)S(1)} %dynamic-slice_bitcast_fusion.12), channel_id=1, source_target_pairs={{0,32},{32,0},{64,96},{96,64},{128,160},{160,128},{192,224},{224,1... | collective-permute-start | bytes 786440 | tf_op jit(solution)/shard_map/ppermute | solution.py:41
  139.6 24.9 %collective-permute-start.11 = (bf16[2,128,256]{2,1,0:T(8,128)(2,1)}, bf16[2,128,256]{2,1,0:T(8,128)(2,1)S(1)}, u32[]{:S(2)}, u32[]{:S(2)}) collective-permute-start(bf16[2,128,256]{2,1,0:T(8,128)(2,1)} %pad_maximum_fusion.4), channel_id=1, source_target_pairs={{0,64},{32,96},{64,128},{96,160},{128,192},{160,224},{192,0},{224,... | collective-permute-start | bytes 393224 | tf_op jit(solution)/shard_map/ppermute | solution.py:59
  140.3 24.3 %collective-permute-start.13 = (bf16[2,128,256]{2,1,0:T(8,128)(2,1)}, bf16[2,128,256]{2,1,0:T(8,128)(2,1)}, u32[]{:S(2)}, u32[]{:S(2)}) collective-permute-start(bf16[2,128,256]{2,1,0:T(8,128)(2,1)} %pad_maximum_fusion.5), channel_id=1, source_target_pairs={{0,192},{32,224},{64,0},{96,32},{128,64},{160,96},{192,128},{224,1... | collective-permute-start | bytes 393224 | tf_op jit(solution)/shard_map/ppermute | solution.py:59
  157.7 3.3 %copy-start.6 = (bf16[32,32,512]{2,1,0:T(8,128)(2,1)}, bf16[32,32,512]{2,1,0:T(8,128)(2,1)S(1)}, u32[]{:S(2)}) copy-start(bf16[32,32,512]{2,1,0:T(8,128)(2,1)S(1)} %all-to-all-done.3) | copy-start | bytes 3145732
  161.0 13.5 %all-to-all-start.4 = ((bf16[8,32,1024]{2,1,0:T(8,128)(2,1)}), bf16[8,32,1024]{2,1,0:T(8,128)(2,1)S(1)}, u32[]{:S(2)}, u32[]{:S(2)}) async-start(bf16[8,32,1024]{2,1,0:T(8,128)(2,1)} %bitcast.37), calls=%async_computation.4 | async-start | bytes 1048576 | tf_op jit(solution)/shard_map/all_to_all | solution.py:27
  165.6 8.2 %collective-permute-start.14 = (bf16[128,256]{1,0:T(8,128)(2,1)S(1)}, bf16[128,256]{1,0:T(8,128)(2,1)S(1)}, u32[]{:S(2)}, u32[]{:S(2)}) collective-permute-start(bf16[128,256]{1,0:T(8,128)(2,1)S(1)} %dynamic-slice_bitcast_fusion.20), channel_id=1, source_target_pairs={{0,32},{32,0},{64,96},{96,64},{128,160},{160,128},{192,224},{224,1... | collective-permute-start | bytes 196616 | tf_op jit(solution)/shard_map/ppermute | solution.py:41

commit v5 on v4

--- a/solution.py
+++ b/solution.py
@@ -67,8 +67,8 @@
     own, ahead, back, far_ahead, far_back = blocks
     from_back, from_ahead = shifted(far_ahead, 1), shifted(far_back, -1)
     half = own.dtype
-    ahead = jnp.stack([added(ahead[0], from_back).astype(half), ahead[1]])
-    back = jnp.stack([back[0], added(back[1], from_ahead).astype(half)])
+    ahead = ahead.at[0].set(added(ahead[0], from_back).astype(half))
+    back = back.at[1].set(added(back[1], from_ahead).astype(half))
     return [own, ahead, back]
 
 
@@ -100,7 +100,11 @@
     hidden = (pre * sigma).astype(half)
     act_down = contract(weight_ld, 0, hidden, 0).astype(half)
     act_down = row_major(act_down)
-    grad_act_down, _ = lax.optimization_barrier((received, act_down))
+    slope = sigma * (1.0 + pre * (1.0 - sigma))
+    tokens_turned = row_major(tokens.T)
+    grad_act_down, hidden, slope, tokens_turned, _ = lax.optimization_barrier(
+        (received, hidden, slope, tokens_turned, act_down)
+    )
     mixed_down = exchange(act_down)
     left_down_part = (contract(hidden, 1, grad_act_down, 1) * scale).astype(half)
     grad_act_down, *down_blocks = lax.optimization_barrier(
@@ -108,7 +112,7 @@
     )
     down_blocks = first_leg(down_blocks)
     grad_hidden = contract(weight_ld, 1, grad_act_down, 0)
-    grad_pre = (grad_hidden * sigma * (1.0 + pre * (1.0 - sigma))).astype(half)
+    grad_pre = (grad_hidden * slope).astype(half)
     left_up_part = (contract(mixed_up, 1, grad_pre, 1) * scale).astype(half)
     up_blocks = first_leg(column_blocks(by_place(left_up_part)))
     grad_mixed_up = row_major(contract(weight_lu, 1, grad_pre, 0).astype(half))
@@ -118,12 +122,11 @@
     grad_act_up = exchange(grad_mixed_up)
     left_down_half = second_leg(down_blocks, (mixed_down,)).astype(half)
     left_down_grad = over_pairs(pair_halves(left_down_half, 0))
-    later, _ = lax.optimization_barrier((mixed_down, mixed_down))
-    right_down_part = row_major((contract(later, 1, cotangent, 0) * scale).astype(half))
+    right_down_part = row_major((contract(mixed_down, 1, cotangent, 0) * scale).astype(half))
     right_blocks = column_blocks(by_place(right_down_part))
     layer_out = contract(mixed_down, 0, weight_rd, 0).astype(half)
     left_up_half = second_leg(up_blocks, (mixed_down,)).astype(half)
-    right_up_part = (contract(tokens, 0, grad_act_up, 1) * scale).astype(half)
+    right_up_part = row_major((contract(tokens_turned, 1, grad_act_up, 1) * scale).astype(half))
     left_up_grad = over_pairs(pair_halves(left_up_half, 0))
     right_up_grad = summed(right_up_part)
     right_down_half = second_leg(first_leg(right_blocks), (right_up_part,)).astype(half)

time: 177 us -> 177 us (level)
  local copies, waits for them, and re-layouts: 5.57 us -> 8.88 us
    another operation x10 -> x0, other arithmetic: 5.16 us -> none  [the longest x6 2.7 us: first_leg(): back = jnp.stack([back[0], added(back[1], from_ahead).astype(half)])]
    scatter x0 -> x4, other arithmetic: none -> 3.23 us  [the longest x3 2.47 us: first_leg(): back = back.at[1].set(added(back[1], from_ahead).astype(half))]
    ppermute x12, waiting for transfers between devices: 5.46 us -> 3.12 us  [shifted(): lax.ppermute(value, 'dp', [(i, (i + 2 * step) % size) for i in range(size)])]
    squeeze x1 -> x3, local copies, waits for them, and re-layouts: 0.97 us -> 3.06 us  [column_blocks(): lax.dynamic_index_in_dim(cur, jnp.bitwise_and(column + step, cur.shape[0]...]
    convert_element_type x1 -> x0, local copies, waits for them, and re-layouts: 2.04 us -> none  [body(): right_up_part = (contract(tokens, 0, grad_act_up, 1) * scale).astype(half)]
    unnamed x22 -> x29, local copies, waits for them, and re-layouts: 2.28 us -> 3.71 us
  transfers between devices with their start and end apart: 20 -> 20, of which waited for: 7 -> 8; matrix products, arithmetic and copies ran while one was open for 23% -> 23% of each run, Pallas kernels for 0% -> 0%
where the time goes in v5:
time: 177 us; the launch traced here: 176 us
  waiting for transfers between devices  71.8 us (41%)
  starting transfers between devices  55.4 us (31%)
  matrix products  27.9 us (16%)
  other arithmetic  11.3 us (6%)
  local copies, waits for them, and re-layouts  8.88 us (5%)
    all_to_all x4, waiting for transfers between devices, exchange(): return lax.all_to_all(tile, 'hid', 0, 0, tiled=True)  52.8 us
    all_to_all x4, starting transfers between devices, exchange(): return lax.all_to_all(tile, 'hid', 0, 0, tiled=True)  29.1 us
    dot_general x12, matrix products, contract(): lax.dot_general(left_side, right_side, (((left_dim,), (right_dim,)), ((),...  27.9 us
    ppermute x12, starting transfers between devices, shifted(): lax.ppermute(value, 'dp', [(i, (i + 2 * step) % size) for i in range(size)])  18 us
    ppermute x3, waiting for transfers between devices, over_pairs(): got = lax.ppermute(sent, 'dp', pairs)  15.9 us
    ppermute x3, starting transfers between devices, over_pairs(): got = lax.ppermute(sent, 'dp', pairs)  4.2 us
    all_to_all x1, starting transfers between devices, summed(): lax.all_to_all(part, 'dp', 0, 0, tiled=True)  4.14 us
    unnamed x29, local copies, waits for them, and re-layouts  3.71 us
  transfers between devices with their start and end apart: 20, of which 8 were waited for; matrix products, arithmetic and copies ran while one was open for 23% of the time, Pallas kernels for 0%

profile of v5, /device:TPU:32, one launch (start us, length us, event | category | flops | bytes accessed | tf_op | source)
XLA Modules:
  0.0 176.3 jit_solution(6532604594492577909)
XLA Ops:
  0.7 2.7 %convolution_convert_fusion = bf16[1024,512]{1,0:T(8,128)(2,1)} fusion(bf16[512,256]{1,0:T(8,128)(2,1)} %param.18, bf16[1,256,1024]{2,1,0:T(8,128)(2,1)} %param.20), kind=kOutput, calls=%fused_computation.23 | convolution fusion | flops 268959744 | bytes 1835008 | tf_op jit(solution)/shard_map/dot_general | solution.py:9
  3.4 11.4 %all-to-all-start = ((bf16[32,32,512]{2,1,0:T(8,128)(2,1)}), bf16[32,32,512]{2,1,0:T(8,128)(2,1)}, u32[]{:S(2)}, u32[]{:S(2)}) async-start(bf16[32,32,512]{2,1,0:T(8,128)(2,1)} %bitcast.2), calls=%async_computation | async-start | bytes 2097152 | tf_op jit(solution)/shard_map/all_to_all | solution.py:22
  14.9 1.5 convolution_convert_fusion.1
  16.3 29.1 %all-to-all-done = bf16[32,32,512]{2,1,0:T(8,128)(2,1)} async-done(((bf16[32,32,512]{2,1,0:T(8,128)(2,1)}), bf16[32,32,512]{2,1,0:T(8,128)(2,1)}, u32[]{:S(2)}, u32[]{:S(2)}) %all-to-all-start) | async-done | bytes 1048608 | tf_op jit(solution)/shard_map/all_to_all | solution.py:22
  45.4 4.5 %all-to-all-start.1 = ((bf16[32,32,512]{2,1,0:T(8,128)(2,1)}), bf16[32,32,512]{2,1,0:T(8,128)(2,1)}, u32[]{:S(2)}, u32[]{:S(2)}) async-start(bf16[32,32,512]{2,1,0:T(8,128)(2,1)} %bitcast.4), calls=%async_computation.1 | async-start | bytes 2097152 | tf_op jit(solution)/shard_map/all_to_all | solution.py:22
  50.0 4.6 %fusion.10 = (f32[1024,512]{0,1:T(8,128)}, bf16[1024,512]{0,1:T(8,128)(2,1)S(1)}) fusion(bf16[1024,512]{1,0:T(8,128)(2,1)} %bitcast.3, bf16[1,1024,1024]{2,1,0:T(8,128)(2,1)S(1)} %copy-done), kind=kOutput, calls=%fused_computation.16 | convolution fusion | flops 1078460416 | bytes 6291456 | tf_op jit(solution)/shard_map/dot_general | solution.py:9
  55.6 2.3 %fusion.18 = bf16[512,1024]{0,1:T(8,128)(2,1)} fusion(bf16[1024,512]{0,1:T(8,128)(2,1)S(1)} %get-tuple-element.101, bf16[1,1024,1024]{2,1,0:T(8,128)(2,1)S(1)} %copy-done.10), kind=kOutput, calls=%fused_computation.22 | convolution fusion | flops 1074266112 | bytes 4194304 | tf_op jit(solution)/shard_map/dot_general | solution.py:9
  57.9 22.0 %all-to-all-done.1 = bf16[32,32,512]{2,1,0:T(8,128)(2,1)} async-done(((bf16[32,32,512]{2,1,0:T(8,128)(2,1)}), bf16[32,32,512]{2,1,0:T(8,128)(2,1)}, u32[]{:S(2)}, u32[]{:S(2)}) %all-to-all-start.1) | async-done | bytes 1048608 | tf_op jit(solution)/shard_map/all_to_all | solution.py:22
  79.9 3.7 %all-to-all-start.2 = ((bf16[32,32,512]{2,1,0:T(8,128)(2,1)}), bf16[32,32,512]{2,1,0:T(8,128)(2,1)S(1)}, u32[]{:S(2)}, u32[]{:S(2)}) async-start(bf16[32,32,512]{2,1,0:T(8,128)(2,1)} %bitcast.202), calls=%async_computation.2 | async-start | bytes 2097152 | tf_op jit(solution)/shard_map/all_to_all | solution.py:22
  83.6 2.8 %multiply_convert_fusion.1 = bf16[1024,1024]{1,0:T(8,128)(2,1)S(1)} fusion(bf16[1024,512]{0,1:T(8,128)(2,1)} %copy-done.13, bf16[1024,512]{1,0:T(8,128)(2,1)} %bitcast.5), kind=kOutput, calls=%fused_computation.1 | convolution fusion | flops 1075838976 | bytes 4194304 | tf_op jit(solution)/shard_map/dot_general | solution.py:9
  89.3 2.6 %fusion = bf16[1024,512]{0,1:T(8,128)(2,1)S(1)} fusion(f32[1024,512]{0,1:T(8,128)S(1)} %copy-done.12, bf16[1024,512]{1,0:T(8,128)(2,1)} %bitcast.5, bf16[1,1024,1024]{2,1,0:T(8,128)(2,1)S(1)} %copy-done.11), kind=kOutput, calls=%fused_computation.3 | convolution fusion | flops 1074790400 | bytes 6291456 | tf_op jit(solution)/shard_map/dot_general | solution.py:9
  91.9 2.5 %multiply_convert_fusion = bf16[1024,1024]{1,0:T(8,128)(2,1)S(1)} fusion(bf16[1024,512]{1,0:T(8,128)(2,1)} %bitcast.3, bf16[1024,512]{0,1:T(8,128)(2,1)S(1)} %fusion), kind=kOutput, calls=%fused_computation | convolution fusion | flops 1075838976 | bytes 4194304 | tf_op jit(solution)/shard_map/dot_general | solution.py:9
  94.4 2.8 %collective-permute-start.3 = (bf16[128,1024]{1,0:T(8,128)(2,1)S(1)}, bf16[128,1024]{1,0:T(8,128)(2,1)S(1)}, u32[]{:S(2)}, u32[]{:S(2)}) collective-permute-start(bf16[128,1024]{1,0:T(8,128)(2,1)S(1)} %get-tuple-element.120), channel_id=1, source_target_pairs={{0,192},{32,224},{64,0},{96,32},{128,64},{160,96},{192,128},{224,1... | collective-permute-start | bytes 786440 | tf_op jit(solution)/shard_map/ppermute | solution.py:59
  97.2 2.3 %fusion.23 = bf16[1024,512]{1,0:T(8,128)(2,1)} fusion(bf16[1024,512]{0,1:T(8,128)(2,1)S(1)} %fusion, bf16[1,1024,1024]{2,1,0:T(8,128)(2,1)S(1)} %copy-done), kind=kOutput, calls=%fused_computation.25 | convolution fusion | flops 1074266112 | bytes 4194304 | tf_op jit(solution)/shard_map/dot_general | solution.py:9
  102.4 2.6 %collective-permute-start.1 = (bf16[128,1024]{1,0:T(8,128)(2,1)S(1)}, bf16[128,1024]{1,0:T(8,128)(2,1)S(1)}, u32[]{:S(2)}, u32[]{:S(2)}) collective-permute-start(bf16[128,1024]{1,0:T(8,128)(2,1)S(1)} %get-tuple-element.108), channel_id=1, source_target_pairs={{0,192},{32,224},{64,0},{96,32},{128,64},{160,96},{192,128},{224,1... | collective-permute-start | bytes 786440 | tf_op jit(solution)/shard_map/ppermute | solution.py:59
  106.0 1.7 collective-permute-done.2
  108.7 3.2 %collective-permute-start.5 = (bf16[2,128,1024]{2,1,0:T(8,128)(2,1)}, bf16[2,128,1024]{2,1,0:T(8,128)(2,1)}, u32[]{:S(2)}, u32[]{:S(2)}) collective-permute-start(bf16[2,128,1024]{2,1,0:T(8,128)(2,1)} %get-tuple-element.118), channel_id=1, source_target_pairs={{0,192},{32,224},{64,0},{96,32},{128,64},{160,96},{192,128},{224,1... | collective-permute-start | bytes 1572872 | tf_op jit(solution)/shard_map/ppermute | solution.py:59
  114.8 3.2 %collective-permute-start.8 = (bf16[2,128,1024]{2,1,0:T(8,128)(2,1)}, bf16[2,128,1024]{2,1,0:T(8,128)(2,1)}, u32[]{:S(2)}, u32[]{:S(2)}) collective-permute-start(bf16[2,128,1024]{2,1,0:T(8,128)(2,1)} %fusion.41), channel_id=1, source_target_pairs={{0,192},{32,224},{64,0},{96,32},{128,64},{160,96},{192,128},{224,1... | collective-permute-start | bytes 1572872 | tf_op jit(solution)/shard_map/ppermute | solution.py:59
  119.1 9.5 %all-to-all-start.3 = ((bf16[32,32,512]{2,1,0:T(8,128)(2,1)}), bf16[32,32,512]{2,1,0:T(8,128)(2,1)S(1)}, u32[]{:S(2)}, u32[]{:S(2)}) async-start(bf16[32,32,512]{2,1,0:T(8,128)(2,1)} %bitcast.199), calls=%async_computation.3 | async-start | bytes 2097152 | tf_op jit(solution)/shard_map/all_to_all | solution.py:22
  128.6 2.7 %convolution_convert_fusion.3 = bf16[512,256]{1,0:T(8,128)(2,1)} fusion(bf16[1024,512]{1,0:T(8,128)(2,1)} %bitcast.200, bf16[1,1024,256]{2,1,0:T(8,128)(2,1)} %param.23), kind=kOutput, calls=%fused_computation.31 | convolution fusion | flops 268566528 | bytes 1835008 | tf_op jit(solution)/shard_map/dot_general | solution.py:9
  131.9 2.0 %collective-permute-start.10 = (bf16[128,256]{1,0:T(8,128)(2,1)S(1)}, bf16[128,256]{1,0:T(8,128)(2,1)S(1)}, u32[]{:S(2)}, u32[]{:S(2)}) collective-permute-start(bf16[128,256]{1,0:T(8,128)(2,1)S(1)} %get-tuple-element.135), channel_id=1, source_target_pairs={{0,64},{32,96},{64,128},{96,160},{128,192},{160,224},{192,0},{224,... | collective-permute-start | bytes 196616 | tf_op jit(solution)/shard_map/ppermute | solution.py:59
  133.9 1.5 add_convert_fusion.1
  136.2 1.5 add_convert_fusion
  140.5 3.2 %collective-permute-start.13 = (bf16[2,128,256]{2,1,0:T(8,128)(2,1)}, bf16[2,128,256]{2,1,0:T(8,128)(2,1)}, u32[]{:S(2)}, u32[]{:S(2)}) collective-permute-start(bf16[2,128,256]{2,1,0:T(8,128)(2,1)} %get-tuple-element.132), channel_id=1, source_target_pairs={{0,192},{32,224},{64,0},{96,32},{128,64},{160,96},{192,128},{224,1... | collective-permute-start | bytes 393224 | tf_op jit(solution)/shard_map/ppermute | solution.py:59
  143.8 5.4 %collective-permute-done.6 = bf16[128,1024]{1,0:T(8,128)(2,1)S(1)} collective-permute-done((bf16[128,1024]{1,0:T(8,128)(2,1)S(1)}, bf16[128,1024]{1,0:T(8,128)(2,1)S(1)}, u32[]{:S(2)}, u32[]{:S(2)}) %collective-permute-start.6) | collective-permute-done | bytes 262176 | tf_op jit(solution)/shard_map/ppermute | solution.py:41
  149.2 6.5 %collective-permute-done.9 = bf16[128,1024]{1,0:T(8,128)(2,1)S(1)} collective-permute-done((bf16[128,1024]{1,0:T(8,128)(2,1)S(1)}, bf16[128,1024]{1,0:T(8,128)(2,1)S(1)}, u32[]{:S(2)}, u32[]{:S(2)}) %collective-permute-start.9) | collective-permute-done | bytes 262176 | tf_op jit(solution)/shard_map/ppermute | solution.py:41
  157.4 1.7 all-to-all-done.3
  160.4 4.1 %all-to-all-start.4 = ((bf16[8,32,1024]{2,1,0:T(8,128)(2,1)}), bf16[8,32,1024]{2,1,0:T(8,128)(2,1)}, u32[]{:S(2)}, u32[]{:S(2)}) async-start(bf16[8,32,1024]{2,1,0:T(8,128)(2,1)} %bitcast.197), calls=%async_computation.4 | async-start | bytes 1048576 | tf_op jit(solution)/shard_map/all_to_all | solution.py:27
  165.6 2.0 %collective-permute-start.14 = (bf16[128,256]{1,0:T(8,128)(2,1)S(1)}, bf16[128,256]{1,0:T(8,128)(2,1)S(1)}, u32[]{:S(2)}, u32[]{:S(2)}) collective-permute-start(bf16[128,256]{1,0:T(8,128)(2,1)S(1)} %dynamic-slice_bitcast_fusion.20), channel_id=1, source_target_pairs={{0,32},{32,0},{64,96},{96,64},{128,160},{160,128},{192,224},{224,1... | collective-permute-start | bytes 196616 | tf_op jit(solution)/shard_map/ppermute | solution.py:41
  167.6 2.2 %convolution_convert_fusion.2 = bf16[512,256]{1,0:T(8,128)(2,1)} fusion(bf16[1024,512]{1,0:T(8,128)(2,1)S(1)} %bitcast.191, bf16[1,256,1024]{2,1,0:T(8,128)(2,1)} %param.20), kind=kOutput, calls=%fused_computation.30 | convolution fusion | flops 268566528 | bytes 1835008 | tf_op jit(solution)/shard_map/dot_general | solution.py:9
  169.8 4.0 %collective-permute-done.14 = bf16[128,256]{1,0:T(8,128)(2,1)S(1)} collective-permute-done((bf16[128,256]{1,0:T(8,128)(2,1)S(1)}, bf16[128,256]{1,0:T(8,128)(2,1)S(1)}, u32[]{:S(2)}, u32[]{:S(2)}) %collective-permute-start.14) | collective-permute-done | bytes 65568 | tf_op jit(solution)/shard_map/ppermute | solution.py:41
  174.5 1.8 %convert_reduce_fusion = f32[32,1024]{1,0:T(8,128)} fusion(bf16[8,32,1024]{2,1,0:T(8,128)(2,1)} %all-to-all-done.4), kind=kLoop, calls=%fused_computation.34 | loop fusion | flops 491520 | bytes 655360 | tf_op jit(solution)/shard_map/reduce_sum | solution.py:28
  (71 shorter events, 21.7 us)
Async XLA Ops:
  0.6 49.4 %copy-start = (bf16[1,1024,1024]{2,1,0:T(8,128)(2,1)S(1)}, bf16[1,1024,1024]{2,1,0:T(8,128)(2,1)}, u32[]{:S(2)}) copy-start(bf16[1,1024,1024]{2,1,0:T(8,128)(2,1)} %param.21) | copy-start | bytes 6291460
  0.6 14.2 %copy-start.8 = (bf16[512,256]{1,0:T(8,128)(2,1)S(1)}, bf16[512,256]{1,0:T(8,128)(2,1)}, u32[]{:S(2)}) copy-start(bf16[512,256]{1,0:T(8,128)(2,1)} %param.19) | copy-start | bytes 786436
  0.7 14.2 %copy-start.7 = (bf16[1,1024,256]{2,1,0:T(8,128)(2,1)S(1)}, bf16[1,1024,256]{2,1,0:T(8,128)(2,1)}, u32[]{:S(2)}) copy-start(bf16[1,1024,256]{2,1,0:T(8,128)(2,1)} %param.23) | copy-start | bytes 1572868
  3.4 42.0 %all-to-all-start = ((bf16[32,32,512]{2,1,0:T(8,128)(2,1)}), bf16[32,32,512]{2,1,0:T(8,128)(2,1)}, u32[]{:S(2)}, u32[]{:S(2)}) async-start(bf16[32,32,512]{2,1,0:T(8,128)(2,1)} %bitcast.2), calls=%async_computation | async-start | bytes 2097152 | tf_op jit(solution)/shard_map/all_to_all | solution.py:22
  14.9 35.0 %copy-start.3 = (bf16[512,256]{1,0:T(8,128)(2,1)S(1)}, bf16[512,256]{1,0:T(8,128)(2,1)}, u32[]{:S(2)}) copy-start(bf16[512,256]{1,0:T(8,128)(2,1)} %param.18) | copy-start | bytes 786436
  45.4 34.5 %all-to-all-start.1 = ((bf16[32,32,512]{2,1,0:T(8,128)(2,1)}), bf16[32,32,512]{2,1,0:T(8,128)(2,1)}, u32[]{:S(2)}, u32[]{:S(2)}) async-start(bf16[32,32,512]{2,1,0:T(8,128)(2,1)} %bitcast.4), calls=%async_computation.1 | async-start | bytes 2097152 | tf_op jit(solution)/shard_map/all_to_all | solution.py:22
  50.0 5.6 %copy-start.10 = (bf16[1,1024,1024]{2,1,0:T(8,128)(2,1)S(1)}, bf16[1,1024,1024]{2,1,0:T(8,128)(2,1)}, u32[]{:S(2)}) copy-start(bf16[1,1024,1024]{2,1,0:T(8,128)(2,1)} %param.22) | copy-start | bytes 6291460
  79.9 38.2 %all-to-all-start.2 = ((bf16[32,32,512]{2,1,0:T(8,128)(2,1)}), bf16[32,32,512]{2,1,0:T(8,128)(2,1)S(1)}, u32[]{:S(2)}, u32[]{:S(2)}) async-start(bf16[32,32,512]{2,1,0:T(8,128)(2,1)} %bitcast.202), calls=%async_computation.2 | async-start | bytes 2097152 | tf_op jit(solution)/shard_map/all_to_all | solution.py:22
  86.5 2.2 %copy-start.11 = (bf16[1,1024,1024]{2,1,0:T(8,128)(2,1)S(1)}, bf16[1,1024,1024]{2,1,0:T(8,128)(2,1)}, u32[]{:S(2)}) copy-start(bf16[1,1024,1024]{2,1,0:T(8,128)(2,1)} %param.22) | copy-start | bytes 6291460
  86.5 2.8 %copy-start.12 = (f32[1024,512]{0,1:T(8,128)S(1)}, f32[1024,512]{0,1:T(8,128)}, u32[]{:S(2)}) copy-start(f32[1024,512]{0,1:T(8,128)} %get-tuple-element.103) | copy-start | bytes 6291460
  94.4 11.6 %collective-permute-start.3 = (bf16[128,1024]{1,0:T(8,128)(2,1)S(1)}, bf16[128,1024]{1,0:T(8,128)(2,1)S(1)}, u32[]{:S(2)}, u32[]{:S(2)}) collective-permute-start(bf16[128,1024]{1,0:T(8,128)(2,1)S(1)} %get-tuple-element.120), channel_id=1, source_target_pairs={{0,192},{32,224},{64,0},{96,32},{128,64},{160,96},{192,128},{224,1... | collective-permute-start | bytes 786440 | tf_op jit(solution)/shard_map/ppermute | solution.py:59
  97.2 10.4 %collective-permute-start.2 = (bf16[128,1024]{1,0:T(8,128)(2,1)S(1)}, bf16[128,1024]{1,0:T(8,128)(2,1)S(1)}, u32[]{:S(2)}, u32[]{:S(2)}) collective-permute-start(bf16[128,1024]{1,0:T(8,128)(2,1)S(1)} %get-tuple-element.121), channel_id=1, source_target_pairs={{0,64},{32,96},{64,128},{96,160},{128,192},{160,224},{192,0},{224,... | collective-permute-start | bytes 786440 | tf_op jit(solution)/shard_map/ppermute | solution.py:59
  99.5 13.8 %collective-permute-start = (bf16[128,1024]{1,0:T(8,128)(2,1)S(1)}, bf16[128,1024]{1,0:T(8,128)(2,1)S(1)}, u32[]{:S(2)}, u32[]{:S(2)}) collective-permute-start(bf16[128,1024]{1,0:T(8,128)(2,1)S(1)} %get-tuple-element.106), channel_id=1, source_target_pairs={{0,64},{32,96},{64,128},{96,160},{128,192},{160,224},{192,0},{224,... | collective-permute-start | bytes 786440 | tf_op jit(solution)/shard_map/ppermute | solution.py:59
  102.4 11.6 %collective-permute-start.1 = (bf16[128,1024]{1,0:T(8,128)(2,1)S(1)}, bf16[128,1024]{1,0:T(8,128)(2,1)S(1)}, u32[]{:S(2)}, u32[]{:S(2)}) collective-permute-start(bf16[128,1024]{1,0:T(8,128)(2,1)S(1)} %get-tuple-element.108), channel_id=1, source_target_pairs={{0,192},{32,224},{64,0},{96,32},{128,64},{160,96},{192,128},{224,1... | collective-permute-start | bytes 786440 | tf_op jit(solution)/shard_map/ppermute | solution.py:59
  108.7 23.2 %collective-permute-start.4 = (bf16[2,128,1024]{2,1,0:T(8,128)(2,1)}, bf16[2,128,1024]{2,1,0:T(8,128)(2,1)}, u32[]{:S(2)}, u32[]{:S(2)}) collective-permute-start(bf16[2,128,1024]{2,1,0:T(8,128)(2,1)} %get-tuple-element.119), channel_id=1, source_target_pairs={{0,64},{32,96},{64,128},{96,160},{128,192},{160,224},{192,0},{224,... | collective-permute-start | bytes 1572872 | tf_op jit(solution)/shard_map/ppermute | solution.py:59
  108.7 25.2 %collective-permute-start.5 = (bf16[2,128,1024]{2,1,0:T(8,128)(2,1)}, bf16[2,128,1024]{2,1,0:T(8,128)(2,1)}, u32[]{:S(2)}, u32[]{:S(2)}) collective-permute-start(bf16[2,128,1024]{2,1,0:T(8,128)(2,1)} %get-tuple-element.118), channel_id=1, source_target_pairs={{0,192},{32,224},{64,0},{96,32},{128,64},{160,96},{192,128},{224,1... | collective-permute-start | bytes 1572872 | tf_op jit(solution)/shard_map/ppermute | solution.py:59
  114.1 22.1 %collective-permute-start.7 = (bf16[2,128,1024]{2,1,0:T(8,128)(2,1)}, bf16[2,128,1024]{2,1,0:T(8,128)(2,1)}, u32[]{:S(2)}, u32[]{:S(2)}) collective-permute-start(bf16[2,128,1024]{2,1,0:T(8,128)(2,1)} %fusion.39), channel_id=1, source_target_pairs={{0,64},{32,96},{64,128},{96,160},{128,192},{160,224},{192,0},{224,... | collective-permute-start | bytes 1572872 | tf_op jit(solution)/shard_map/ppermute | solution.py:59
  114.8 21.3 %collective-permute-start.8 = (bf16[2,128,1024]{2,1,0:T(8,128)(2,1)}, bf16[2,128,1024]{2,1,0:T(8,128)(2,1)}, u32[]{:S(2)}, u32[]{:S(2)}) collective-permute-start(bf16[2,128,1024]{2,1,0:T(8,128)(2,1)} %fusion.41), channel_id=1, source_target_pairs={{0,192},{32,224},{64,0},{96,32},{128,64},{160,96},{192,128},{224,1... | collective-permute-start | bytes 1572872 | tf_op jit(solution)/shard_map/ppermute | solution.py:59
  119.1 40.0 %all-to-all-start.3 = ((bf16[32,32,512]{2,1,0:T(8,128)(2,1)}), bf16[32,32,512]{2,1,0:T(8,128)(2,1)S(1)}, u32[]{:S(2)}, u32[]{:S(2)}) async-start(bf16[32,32,512]{2,1,0:T(8,128)(2,1)} %bitcast.199), calls=%async_computation.3 | async-start | bytes 2097152 | tf_op jit(solution)/shard_map/all_to_all | solution.py:22
  128.6 2.7 %copy-start.5 = (bf16[32,32,512]{2,1,0:T(8,128)(2,1)S(1)}, bf16[32,32,512]{2,1,0:T(8,128)(2,1)}, u32[]{:S(2)}) copy-start(bf16[32,32,512]{2,1,0:T(8,128)(2,1)} %copy-done.4) | copy-start | bytes 3145732
  128.6 2.7 %copy-start.9 = (bf16[512,256]{1,0:T(8,128)(2,1)S(1)}, bf16[512,256]{1,0:T(8,128)(2,1)}, u32[]{:S(2)}) copy-start(bf16[512,256]{1,0:T(8,128)(2,1)} %param.19) | copy-start | bytes 786436
  128.6 5.3 %copy-start.2 = (bf16[2,128,1024]{2,1,0:T(8,128)(2,1)S(1)}, bf16[2,128,1024]{2,1,0:T(8,128)(2,1)}, u32[]{:S(2)}) copy-start(bf16[2,128,1024]{2,1,0:T(8,128)(2,1)} %get-tuple-element.124) | copy-start | bytes 1572868
  131.3 4.9 %copy-start.1 = (bf16[2,128,1024]{2,1,0:T(8,128)(2,1)S(1)}, bf16[2,128,1024]{2,1,0:T(8,128)(2,1)}, u32[]{:S(2)}) copy-start(bf16[2,128,1024]{2,1,0:T(8,128)(2,1)} %get-tuple-element.104) | copy-start | bytes 1572868
  131.7 8.1 %copy-start.6 = (bf16[1024,256]{1,0:T(8,128)(2,1)}, bf16[1024,256]{1,0:T(8,128)(2,1)S(1)}, u32[]{:S(2)}) copy-start(bf16[1024,256]{1,0:T(8,128)(2,1)S(1)} %fusion.27) | copy-start | bytes 1572868
  131.8 8.1 %collective-permute-start.12 = (bf16[128,256]{1,0:T(8,128)(2,1)S(1)}, bf16[128,256]{1,0:T(8,128)(2,1)S(1)}, u32[]{:S(2)}, u32[]{:S(2)}) collective-permute-start(bf16[128,256]{1,0:T(8,128)(2,1)S(1)} %get-tuple-element.134), channel_id=1, source_target_pairs={{0,192},{32,224},{64,0},{96,32},{128,64},{160,96},{192,128},{224,1... | collective-permute-start | bytes 196616 | tf_op jit(solution)/shard_map/ppermute | solution.py:59
  131.9 8.0 %collective-permute-start.10 = (bf16[128,256]{1,0:T(8,128)(2,1)S(1)}, bf16[128,256]{1,0:T(8,128)(2,1)S(1)}, u32[]{:S(2)}, u32[]{:S(2)}) collective-permute-start(bf16[128,256]{1,0:T(8,128)(2,1)S(1)} %get-tuple-element.135), channel_id=1, source_target_pairs={{0,64},{32,96},{64,128},{96,160},{128,192},{160,224},{192,0},{224,... | collective-permute-start | bytes 196616 | tf_op jit(solution)/shard_map/ppermute | solution.py:59
  135.4 13.8 %collective-permute-start.6 = (bf16[128,1024]{1,0:T(8,128)(2,1)S(1)}, bf16[128,1024]{1,0:T(8,128)(2,1)S(1)}, u32[]{:S(2)}, u32[]{:S(2)}) collective-permute-start(bf16[128,1024]{1,0:T(8,128)(2,1)S(1)} %dynamic-slice_bitcast_fusion.13), channel_id=1, source_target_pairs={{0,32},{32,0},{64,96},{96,64},{128,160},{160,128},{192,224},{224,1... | collective-permute-start | bytes 786440 | tf_op jit(solution)/shard_map/ppermute | solution.py:41
  137.7 18.0 %collective-permute-start.9 = (bf16[128,1024]{1,0:T(8,128)(2,1)S(1)}, bf16[128,1024]{1,0:T(8,128)(2,1)S(1)}, u32[]{:S(2)}, u32[]{:S(2)}) collective-permute-start(bf16[128,1024]{1,0:T(8,128)(2,1)S(1)} %dynamic-slice_bitcast_fusion.12), channel_id=1, source_target_pairs={{0,32},{32,0},{64,96},{96,64},{128,160},{160,128},{192,224},{224,1... | collective-permute-start | bytes 786440 | tf_op jit(solution)/shard_map/ppermute | solution.py:41
  140.5 24.0 %collective-permute-start.11 = (bf16[2,128,256]{2,1,0:T(8,128)(2,1)}, bf16[2,128,256]{2,1,0:T(8,128)(2,1)S(1)}, u32[]{:S(2)}, u32[]{:S(2)}) collective-permute-start(bf16[2,128,256]{2,1,0:T(8,128)(2,1)} %get-tuple-element.133), channel_id=1, source_target_pairs={{0,64},{32,96},{64,128},{96,160},{128,192},{160,224},{192,0},{224,... | collective-permute-start | bytes 393224 | tf_op jit(solution)/shard_map/ppermute | solution.py:59
  140.5 24.0 %collective-permute-start.13 = (bf16[2,128,256]{2,1,0:T(8,128)(2,1)}, bf16[2,128,256]{2,1,0:T(8,128)(2,1)}, u32[]{:S(2)}, u32[]{:S(2)}) collective-permute-start(bf16[2,128,256]{2,1,0:T(8,128)(2,1)} %get-tuple-element.132), channel_id=1, source_target_pairs={{0,192},{32,224},{64,0},{96,32},{128,64},{160,96},{192,128},{224,1... | collective-permute-start | bytes 393224 | tf_op jit(solution)/shard_map/ppermute | solution.py:59
  160.4 14.1 %all-to-all-start.4 = ((bf16[8,32,1024]{2,1,0:T(8,128)(2,1)}), bf16[8,32,1024]{2,1,0:T(8,128)(2,1)}, u32[]{:S(2)}, u32[]{:S(2)}) async-start(bf16[8,32,1024]{2,1,0:T(8,128)(2,1)} %bitcast.197), calls=%async_computation.4 | async-start | bytes 1048576 | tf_op jit(solution)/shard_map/all_to_all | solution.py:27
  165.6 8.2 %collective-permute-start.14 = (bf16[128,256]{1,0:T(8,128)(2,1)S(1)}, bf16[128,256]{1,0:T(8,128)(2,1)S(1)}, u32[]{:S(2)}, u32[]{:S(2)}) collective-permute-start(bf16[128,256]{1,0:T(8,128)(2,1)S(1)} %dynamic-slice_bitcast_fusion.20), channel_id=1, source_target_pairs={{0,32},{32,0},{64,96},{96,64},{128,160},{160,128},{192,224},{224,1... | collective-permute-start | bytes 196616 | tf_op jit(solution)/shard_map/ppermute | solution.py:41
  (2 other events, 2.0 us)

commit v6 on v5

--- a/solution.py
+++ b/solution.py
@@ -107,21 +107,17 @@
     )
     mixed_down = exchange(act_down)
     left_down_part = (contract(hidden, 1, grad_act_down, 1) * scale).astype(half)
-    grad_act_down, *down_blocks = lax.optimization_barrier(
-        (grad_act_down, *column_blocks(by_place(left_down_part)))
-    )
-    down_blocks = first_leg(down_blocks)
+    left_down_sum = lax.psum_scatter(left_down_part, "dp", scatter_dimension=0, tiled=True)
+    grad_act_down, _ = lax.optimization_barrier((grad_act_down, left_down_part))
     grad_hidden = contract(weight_ld, 1, grad_act_down, 0)
     grad_pre = (grad_hidden * slope).astype(half)
     left_up_part = (contract(mixed_up, 1, grad_pre, 1) * scale).astype(half)
     up_blocks = first_leg(column_blocks(by_place(left_up_part)))
     grad_mixed_up = row_major(contract(weight_lu, 1, grad_pre, 0).astype(half))
     grad_mixed_up, mixed_down, *_ = lax.optimization_barrier(
-        (grad_mixed_up, mixed_down, *down_blocks, *up_blocks)
+        (grad_mixed_up, mixed_down, *up_blocks)
     )
     grad_act_up = exchange(grad_mixed_up)
-    left_down_half = second_leg(down_blocks, (mixed_down,)).astype(half)
-    left_down_grad = over_pairs(pair_halves(left_down_half, 0))
     right_down_part = row_major((contract(mixed_down, 1, cotangent, 0) * scale).astype(half))
     right_blocks = column_blocks(by_place(right_down_part))
     layer_out = contract(mixed_down, 0, weight_rd, 0).astype(half)
@@ -137,7 +133,7 @@
         tokens_grad,
         right_up_grad[None],
         left_up_grad[None],
-        left_down_grad[None],
+        left_down_sum.astype(jnp.float32)[None],
         right_down_grad[None],
     )
 

time: 177 us -> 195 us (1.10)
  waiting for transfers between devices: 71.8 us -> 93.3 us
  between operations: 0.99 us -> 14.3 us
  starting transfers between devices: 55.4 us -> 44.4 us
  local copies, waits for them, and re-layouts: 8.88 us -> 3.21 us
  other arithmetic: 11.3 us -> 8.08 us
  matrix products: 27.9 us -> 30 us
    ppermute x12 -> x8, waiting for transfers between devices: 3.12 us -> 14.2 us  [shifted(): lax.ppermute(value, 'dp', [(i, (i + 2 * step) % size) for i in range(size)])]
    ppermute x12 -> x8, starting transfers between devices: 18 us -> 10.9 us  [shifted(): lax.ppermute(value, 'dp', [(i, (i + 2 * step) % size) for i in range(size)])]
    all_to_all x4, waiting for transfers between devices: 52.8 us -> 59.6 us  [exchange(): return lax.all_to_all(tile, 'hid', 0, 0, tiled=True)]
    all_to_all x4, starting transfers between devices: 29.1 us -> 24 us  [exchange(): return lax.all_to_all(tile, 'hid', 0, 0, tiled=True)]
    ppermute x3 -> x2, waiting for transfers between devices: 15.9 us -> 19.5 us  [over_pairs(): got = lax.ppermute(sent, 'dp', pairs)]
    unnamed x29 -> x21, local copies, waits for them, and re-layouts: 3.71 us -> 1.22 us
    dot_general x12, matrix products: 27.9 us -> 30 us  [contract(): lax.dot_general(left_side, right_side, (((left_dim,), (right_dim,)), ((),...]
    ppermute x3 -> x2, starting transfers between devices: 4.2 us -> 5.36 us  [over_pairs(): got = lax.ppermute(sent, 'dp', pairs)]
  transfers between devices with their start and end apart: 20 -> 16, of which waited for: 8 -> 8; matrix products, arithmetic and copies ran while one was open for 23% -> 18% of each run, Pallas kernels for 0% -> 0%
where the time goes in v6:
time: 195 us; the launch traced here: 193 us
  waiting for transfers between devices  93.3 us (48%)
  starting transfers between devices  44.4 us (23%)
  matrix products  30 us (15%)
  between operations  14.3 us (7%)
  other arithmetic  8.08 us (4%)
  local copies, waits for them, and re-layouts  3.21 us (2%)
    all_to_all x4, waiting for transfers between devices, exchange(): return lax.all_to_all(tile, 'hid', 0, 0, tiled=True)  59.6 us
    dot_general x12, matrix products, contract(): lax.dot_general(left_side, right_side, (((left_dim,), (right_dim,)), ((),...  30 us
    all_to_all x4, starting transfers between devices, exchange(): return lax.all_to_all(tile, 'hid', 0, 0, tiled=True)  24 us
    ppermute x2, waiting for transfers between devices, over_pairs(): got = lax.ppermute(sent, 'dp', pairs)  19.5 us
    ppermute x8, waiting for transfers between devices, shifted(): lax.ppermute(value, 'dp', [(i, (i + 2 * step) % size) for i in range(size)])  14.2 us
    ppermute x8, starting transfers between devices, shifted(): lax.ppermute(value, 'dp', [(i, (i + 2 * step) % size) for i in range(size)])  10.9 us
    ppermute x2, starting transfers between devices, over_pairs(): got = lax.ppermute(sent, 'dp', pairs)  5.36 us
    all_to_all x1, starting transfers between devices, summed(): lax.all_to_all(part, 'dp', 0, 0, tiled=True)  4.15 us
  transfers between devices with their start and end apart: 16, of which 8 were waited for; matrix products, arithmetic and copies ran while one was open for 18% of the time, Pallas kernels for 0%

profile of v6, /device:TPU:32, one launch (start us, length us, event | category | flops | bytes accessed | tf_op | source)
XLA Modules:
  0.0 193.3 jit_solution(8668395256328293024)
XLA Ops:
  7.2 2.7 %convolution_convert_fusion = bf16[1024,512]{1,0:T(8,128)(2,1)} fusion(bf16[512,256]{1,0:T(8,128)(2,1)} %param.14, bf16[1,256,1024]{2,1,0:T(8,128)(2,1)} %param.16), kind=kOutput, calls=%fused_computation.23 | convolution fusion | flops 268959744 | bytes 1835008 | tf_op jit(solution)/shard_map/dot_general | solution.py:9
  9.9 11.4 %all-to-all-start = ((bf16[32,32,512]{2,1,0:T(8,128)(2,1)}), bf16[32,32,512]{2,1,0:T(8,128)(2,1)S(1)}, u32[]{:S(2)}, u32[]{:S(2)}) async-start(bf16[32,32,512]{2,1,0:T(8,128)(2,1)} %bitcast.2), calls=%async_computation | async-start | bytes 2097152 | tf_op jit(solution)/shard_map/all_to_all | solution.py:22
  21.3 2.5 %convolution_convert_fusion.1 = bf16[1024,512]{1,0:T(8,128)(2,1)} fusion(bf16[512,256]{1,0:T(8,128)(2,1)S(1)} %copy-done.7, bf16[1,1024,256]{2,1,0:T(8,128)(2,1)} %param.19), kind=kOutput, calls=%fused_computation.24 | convolution fusion | flops 268959744 | bytes 1835008 | tf_op jit(solution)/shard_map/dot_general | solution.py:9
  23.8 28.0 %all-to-all-done = bf16[32,32,512]{2,1,0:T(8,128)(2,1)S(1)} async-done(((bf16[32,32,512]{2,1,0:T(8,128)(2,1)}), bf16[32,32,512]{2,1,0:T(8,128)(2,1)S(1)}, u32[]{:S(2)}, u32[]{:S(2)}) %all-to-all-start) | async-done | bytes 1048608 | tf_op jit(solution)/shard_map/all_to_all | solution.py:22
  51.8 4.5 %all-to-all-start.1 = ((bf16[32,32,512]{2,1,0:T(8,128)(2,1)}), bf16[32,32,512]{2,1,0:T(8,128)(2,1)}, u32[]{:S(2)}, u32[]{:S(2)}) async-start(bf16[32,32,512]{2,1,0:T(8,128)(2,1)} %bitcast.4), calls=%async_computation.1 | async-start | bytes 2097152 | tf_op jit(solution)/shard_map/all_to_all | solution.py:22
  56.3 3.2 %fusion.10 = (f32[1024,512]{0,1:T(8,128)}, bf16[1024,512]{0,1:T(8,128)(2,1)S(1)}) fusion(bf16[1024,512]{1,0:T(8,128)(2,1)S(1)} %bitcast.170, bf16[1,1024,1024]{2,1,0:T(8,128)(2,1)S(1)} %copy-done), kind=kOutput, calls=%fused_computation.16 | convolution fusion | flops 1078460416 | bytes 6291456 | tf_op jit(solution)/shard_map/dot_general | solution.py:9
  60.5 2.3 %fusion.18 = bf16[512,1024]{0,1:T(8,128)(2,1)} fusion(bf16[1024,512]{0,1:T(8,128)(2,1)S(1)} %get-tuple-element.70, bf16[1,1024,1024]{2,1,0:T(8,128)(2,1)S(1)} %copy-done.8), kind=kOutput, calls=%fused_computation.22 | convolution fusion | flops 1074266112 | bytes 4194304 | tf_op jit(solution)/shard_map/dot_general | solution.py:9
  62.8 23.5 %all-to-all-done.1 = bf16[32,32,512]{2,1,0:T(8,128)(2,1)} async-done(((bf16[32,32,512]{2,1,0:T(8,128)(2,1)}), bf16[32,32,512]{2,1,0:T(8,128)(2,1)}, u32[]{:S(2)}, u32[]{:S(2)}) %all-to-all-start.1) | async-done | bytes 1048608 | tf_op jit(solution)/shard_map/all_to_all | solution.py:22
  86.3 4.5 %all-to-all-start.2 = ((bf16[32,32,512]{2,1,0:T(8,128)(2,1)}), bf16[32,32,512]{2,1,0:T(8,128)(2,1)}, u32[]{:S(2)}, u32[]{:S(2)}) async-start(bf16[32,32,512]{2,1,0:T(8,128)(2,1)} %bitcast.169), calls=%async_computation.2 | async-start | bytes 2097152 | tf_op jit(solution)/shard_map/all_to_all | solution.py:22
  91.0 4.2 %multiply_convert_fusion.1 = bf16[1024,1024]{1,0:T(8,128)(2,1)} fusion(bf16[1024,512]{0,1:T(8,128)(2,1)} %copy-done.9, bf16[1024,512]{1,0:T(8,128)(2,1)} %bitcast.5), kind=kOutput, calls=%fused_computation.1 | convolution fusion | flops 1075838976 | bytes 4194304 | tf_op jit(solution)/shard_map/dot_general | solution.py:9
  95.2 3.9 %fusion = bf16[1024,512]{0,1:T(8,128)(2,1)S(1)} fusion(f32[1024,512]{0,1:T(8,128)} %get-tuple-element.72, bf16[1024,512]{1,0:T(8,128)(2,1)} %bitcast.5, bf16[1,1024,1024]{2,1,0:T(8,128)(2,1)} %param.18), kind=kOutput, calls=%fused_computation.3 | convolution fusion | flops 1074790400 | bytes 6291456 | tf_op jit(solution)/shard_map/dot_general | solution.py:9
  99.2 1.3 multiply_convert_fusion
  100.5 2.8 %collective-permute-start.1 = (bf16[128,1024]{1,0:T(8,128)(2,1)S(1)}, bf16[128,1024]{1,0:T(8,128)(2,1)S(1)}, u32[]{:S(2)}, u32[]{:S(2)}) collective-permute-start(bf16[128,1024]{1,0:T(8,128)(2,1)S(1)} %get-tuple-element.82), channel_id=1, source_target_pairs={{0,192},{32,224},{64,0},{96,32},{128,64},{160,96},{192,128},{224,1... | collective-permute-start | bytes 786440 | tf_op jit(solution)/shard_map/ppermute | solution.py:59
  104.5 2.3 %fusion.23 = bf16[1024,512]{1,0:T(8,128)(2,1)} fusion(bf16[1024,512]{0,1:T(8,128)(2,1)S(1)} %fusion, bf16[1,1024,1024]{2,1,0:T(8,128)(2,1)S(1)} %copy-done), kind=kOutput, calls=%fused_computation.25 | convolution fusion | flops 1074266112 | bytes 4194304 | tf_op jit(solution)/shard_map/dot_general | solution.py:9
  106.8 4.7 %collective-permute-done.1 = bf16[128,1024]{1,0:T(8,128)(2,1)S(1)} collective-permute-done((bf16[128,1024]{1,0:T(8,128)(2,1)S(1)}, bf16[128,1024]{1,0:T(8,128)(2,1)S(1)}, u32[]{:S(2)}, u32[]{:S(2)}) %collective-permute-start.1) | collective-permute-done | bytes 262176 | tf_op jit(solution)/shard_map/ppermute | solution.py:59
  113.0 8.1 %all-to-all-done.2 = bf16[32,32,512]{2,1,0:T(8,128)(2,1)} async-done(((bf16[32,32,512]{2,1,0:T(8,128)(2,1)}), bf16[32,32,512]{2,1,0:T(8,128)(2,1)}, u32[]{:S(2)}, u32[]{:S(2)}) %all-to-all-start.2) | async-done | bytes 1048608 | tf_op jit(solution)/shard_map/all_to_all | solution.py:22
  121.1 3.7 %all-to-all-start.3 = ((bf16[32,32,512]{2,1,0:T(8,128)(2,1)}), bf16[32,32,512]{2,1,0:T(8,128)(2,1)S(1)}, u32[]{:S(2)}, u32[]{:S(2)}) async-start(bf16[32,32,512]{2,1,0:T(8,128)(2,1)} %bitcast.168), calls=%async_computation.3 | async-start | bytes 2097152 | tf_op jit(solution)/shard_map/all_to_all | solution.py:22
  124.8 2.7 %collective-permute-start.3 = (bf16[2,128,1024]{2,1,0:T(8,128)(2,1)}, bf16[2,128,1024]{2,1,0:T(8,128)(2,1)S(1)}, u32[]{:S(2)}, u32[]{:S(2)}) collective-permute-start(bf16[2,128,1024]{2,1,0:T(8,128)(2,1)} %get-tuple-element.80), channel_id=1, source_target_pairs={{0,192},{32,224},{64,0},{96,32},{128,64},{160,96},{192,128},{224,1... | collective-permute-start | bytes 1572872 | tf_op jit(solution)/shard_map/ppermute | solution.py:59
  127.6 1.7 fusion.27
  129.3 3.3 %collective-permute-start.7 = (bf16[128,256]{1,0:T(8,128)(2,1)S(1)}, bf16[128,256]{1,0:T(8,128)(2,1)S(1)}, u32[]{:S(2)}, u32[]{:S(2)}) collective-permute-start(bf16[128,256]{1,0:T(8,128)(2,1)S(1)} %get-tuple-element.91), channel_id=1, source_target_pairs={{0,192},{32,224},{64,0},{96,32},{128,64},{160,96},{192,128},{224,1... | collective-permute-start | bytes 196616 | tf_op jit(solution)/shard_map/ppermute | solution.py:59
  132.6 2.4 %convolution_convert_fusion.3 = bf16[512,256]{1,0:T(8,128)(2,1)} fusion(bf16[1024,512]{1,0:T(8,128)(2,1)} %bitcast.14, bf16[1,1024,256]{2,1,0:T(8,128)(2,1)S(1)} %copy-done.6), kind=kOutput, calls=%fused_computation.31 | convolution fusion | flops 268566528 | bytes 1835008 | tf_op jit(solution)/shard_map/dot_general | solution.py:9
  135.0 8.9 %collective-permute-done.3 = bf16[2,128,1024]{2,1,0:T(8,128)(2,1)S(1)} collective-permute-done((bf16[2,128,1024]{2,1,0:T(8,128)(2,1)}, bf16[2,128,1024]{2,1,0:T(8,128)(2,1)S(1)}, u32[]{:S(2)}, u32[]{:S(2)}) %collective-permute-start.3) | collective-permute-done | bytes 524320 | tf_op jit(solution)/shard_map/ppermute | solution.py:59
  144.3 3.4 %collective-permute-start.4 = (bf16[128,1024]{1,0:T(8,128)(2,1)S(1)}, bf16[128,1024]{1,0:T(8,128)(2,1)S(1)}, u32[]{:S(2)}, u32[]{:S(2)}) collective-permute-start(bf16[128,1024]{1,0:T(8,128)(2,1)S(1)} %dynamic-slice_bitcast_fusion.7), channel_id=1, source_target_pairs={{0,32},{32,0},{64,96},{96,64},{128,160},{160,128},{192,224},{224,1... | collective-permute-start | bytes 786440 | tf_op jit(solution)/shard_map/ppermute | solution.py:41
  149.8 1.4 collective-permute-start.6
  151.1 15.5 %collective-permute-done.4 = bf16[128,1024]{1,0:T(8,128)(2,1)S(1)} collective-permute-done((bf16[128,1024]{1,0:T(8,128)(2,1)S(1)}, bf16[128,1024]{1,0:T(8,128)(2,1)S(1)}, u32[]{:S(2)}, u32[]{:S(2)}) %collective-permute-start.4) | collective-permute-done | bytes 262176 | tf_op jit(solution)/shard_map/ppermute | solution.py:41
  167.5 1.3 fusion.26
  168.8 4.2 %all-to-all-start.4 = ((bf16[8,32,1024]{2,1,0:T(8,128)(2,1)}), bf16[8,32,1024]{2,1,0:T(8,128)(2,1)}, u32[]{:S(2)}, u32[]{:S(2)}) async-start(bf16[8,32,1024]{2,1,0:T(8,128)(2,1)} %bitcast.166), calls=%async_computation.4 | async-start | bytes 1048576 | tf_op jit(solution)/shard_map/all_to_all | solution.py:27
  174.0 2.0 %collective-permute-start.9 = (bf16[128,256]{1,0:T(8,128)(2,1)S(1)}, bf16[128,256]{1,0:T(8,128)(2,1)S(1)}, u32[]{:S(2)}, u32[]{:S(2)}) collective-permute-start(bf16[128,256]{1,0:T(8,128)(2,1)S(1)} %dynamic-slice_bitcast_fusion.14), channel_id=1, source_target_pairs={{0,32},{32,0},{64,96},{96,64},{128,160},{160,128},{192,224},{224,1... | collective-permute-start | bytes 196616 | tf_op jit(solution)/shard_map/ppermute | solution.py:41
  176.0 2.2 %convolution_convert_fusion.2 = bf16[512,256]{1,0:T(8,128)(2,1)} fusion(bf16[1024,512]{1,0:T(8,128)(2,1)S(1)} %bitcast.162, bf16[1,256,1024]{2,1,0:T(8,128)(2,1)} %param.16), kind=kOutput, calls=%fused_computation.30 | convolution fusion | flops 268566528 | bytes 1835008 | tf_op jit(solution)/shard_map/dot_general | solution.py:9
  178.3 4.0 %collective-permute-done.9 = bf16[128,256]{1,0:T(8,128)(2,1)S(1)} collective-permute-done((bf16[128,256]{1,0:T(8,128)(2,1)S(1)}, bf16[128,256]{1,0:T(8,128)(2,1)S(1)}, u32[]{:S(2)}, u32[]{:S(2)}) %collective-permute-start.9) | collective-permute-done | bytes 65568 | tf_op jit(solution)/shard_map/ppermute | solution.py:41
  182.9 1.8 convert_reduce_fusion
  184.7 1.8 bitcast_convert_fusion
  (48 shorter events, 9.0 us)
Async XLA Ops:
  7.2 49.1 %copy-start = (bf16[1,1024,1024]{2,1,0:T(8,128)(2,1)S(1)}, bf16[1,1024,1024]{2,1,0:T(8,128)(2,1)}, u32[]{:S(2)}) copy-start(bf16[1,1024,1024]{2,1,0:T(8,128)(2,1)} %param.17) | copy-start | bytes 6291460
  7.2 14.1 %copy-start.7 = (bf16[512,256]{1,0:T(8,128)(2,1)S(1)}, bf16[512,256]{1,0:T(8,128)(2,1)}, u32[]{:S(2)}) copy-start(bf16[512,256]{1,0:T(8,128)(2,1)} %param.15) | copy-start | bytes 786436
  9.9 41.9 %all-to-all-start = ((bf16[32,32,512]{2,1,0:T(8,128)(2,1)}), bf16[32,32,512]{2,1,0:T(8,128)(2,1)S(1)}, u32[]{:S(2)}, u32[]{:S(2)}) async-start(bf16[32,32,512]{2,1,0:T(8,128)(2,1)} %bitcast.2), calls=%async_computation | async-start | bytes 2097152 | tf_op jit(solution)/shard_map/all_to_all | solution.py:22
  51.8 7.7 %copy-start.3 = (bf16[32,32,512]{2,1,0:T(8,128)(2,1)}, bf16[32,32,512]{2,1,0:T(8,128)(2,1)S(1)}, u32[]{:S(2)}) copy-start(bf16[32,32,512]{2,1,0:T(8,128)(2,1)S(1)} %all-to-all-done) | copy-start | bytes 3145732
  51.8 34.5 %all-to-all-start.1 = ((bf16[32,32,512]{2,1,0:T(8,128)(2,1)}), bf16[32,32,512]{2,1,0:T(8,128)(2,1)}, u32[]{:S(2)}, u32[]{:S(2)}) async-start(bf16[32,32,512]{2,1,0:T(8,128)(2,1)} %bitcast.4), calls=%async_computation.1 | async-start | bytes 2097152 | tf_op jit(solution)/shard_map/all_to_all | solution.py:22
  56.3 4.3 %copy-start.8 = (bf16[1,1024,1024]{2,1,0:T(8,128)(2,1)S(1)}, bf16[1,1024,1024]{2,1,0:T(8,128)(2,1)}, u32[]{:S(2)}) copy-start(bf16[1,1024,1024]{2,1,0:T(8,128)(2,1)} %param.18) | copy-start | bytes 6291460
  59.5 1.0 copy-start.9
  62.8 28.1 %copy-start.2 = (bf16[512,256]{1,0:T(8,128)(2,1)S(1)}, bf16[512,256]{1,0:T(8,128)(2,1)}, u32[]{:S(2)}) copy-start(bf16[512,256]{1,0:T(8,128)(2,1)} %param.14) | copy-start | bytes 786436
  86.3 34.8 %all-to-all-start.2 = ((bf16[32,32,512]{2,1,0:T(8,128)(2,1)}), bf16[32,32,512]{2,1,0:T(8,128)(2,1)}, u32[]{:S(2)}, u32[]{:S(2)}) async-start(bf16[32,32,512]{2,1,0:T(8,128)(2,1)} %bitcast.169), calls=%async_computation.2 | async-start | bytes 2097152 | tf_op jit(solution)/shard_map/all_to_all | solution.py:22
  90.8 93.9 %reduce-scatter.2.cloned.1.call-start = ((), (), s32[]{:S(2)}) async-start(), calls=%async_computation.6 | async-start | bytes 2359296 | tf_op jit(solution)/shard_map/reduce_scatter | solution.py:110
  95.2 3.9 %copy-start.4 = (bf16[32,32,512]{2,1,0:T(8,128)(2,1)S(1)}, bf16[32,32,512]{2,1,0:T(8,128)(2,1)}, u32[]{:S(2)}) copy-start(bf16[32,32,512]{2,1,0:T(8,128)(2,1)} %copy-done.3) | copy-start | bytes 3145732
  100.5 11.0 %collective-permute-start.1 = (bf16[128,1024]{1,0:T(8,128)(2,1)S(1)}, bf16[128,1024]{1,0:T(8,128)(2,1)S(1)}, u32[]{:S(2)}, u32[]{:S(2)}) collective-permute-start(bf16[128,1024]{1,0:T(8,128)(2,1)S(1)} %get-tuple-element.82), channel_id=1, source_target_pairs={{0,192},{32,224},{64,0},{96,32},{128,64},{160,96},{192,128},{224,1... | collective-permute-start | bytes 786440 | tf_op jit(solution)/shard_map/ppermute | solution.py:59
  103.3 8.7 %collective-permute-start = (bf16[128,1024]{1,0:T(8,128)(2,1)S(1)}, bf16[128,1024]{1,0:T(8,128)(2,1)S(1)}, u32[]{:S(2)}, u32[]{:S(2)}) collective-permute-start(bf16[128,1024]{1,0:T(8,128)(2,1)S(1)} %get-tuple-element.83), channel_id=1, source_target_pairs={{0,64},{32,96},{64,128},{96,160},{128,192},{160,224},{192,0},{224,... | collective-permute-start | bytes 786440 | tf_op jit(solution)/shard_map/ppermute | solution.py:59
  121.1 46.4 %all-to-all-start.3 = ((bf16[32,32,512]{2,1,0:T(8,128)(2,1)}), bf16[32,32,512]{2,1,0:T(8,128)(2,1)S(1)}, u32[]{:S(2)}, u32[]{:S(2)}) async-start(bf16[32,32,512]{2,1,0:T(8,128)(2,1)} %bitcast.168), calls=%async_computation.3 | async-start | bytes 2097152 | tf_op jit(solution)/shard_map/all_to_all | solution.py:22
  124.8 7.8 %copy-start.6 = (bf16[1,1024,256]{2,1,0:T(8,128)(2,1)S(1)}, bf16[1,1024,256]{2,1,0:T(8,128)(2,1)}, u32[]{:S(2)}) copy-start(bf16[1,1024,256]{2,1,0:T(8,128)(2,1)} %param.19) | copy-start | bytes 1572868
  124.8 19.2 %copy-start.1 = (bf16[2,128,1024]{2,1,0:T(8,128)(2,1)S(1)}, bf16[2,128,1024]{2,1,0:T(8,128)(2,1)}, u32[]{:S(2)}) copy-start(bf16[2,128,1024]{2,1,0:T(8,128)(2,1)} %get-tuple-element.86) | copy-start | bytes 1572868
  124.8 19.2 %collective-permute-start.3 = (bf16[2,128,1024]{2,1,0:T(8,128)(2,1)}, bf16[2,128,1024]{2,1,0:T(8,128)(2,1)S(1)}, u32[]{:S(2)}, u32[]{:S(2)}) collective-permute-start(bf16[2,128,1024]{2,1,0:T(8,128)(2,1)} %get-tuple-element.80), channel_id=1, source_target_pairs={{0,192},{32,224},{64,0},{96,32},{128,64},{160,96},{192,128},{224,1... | collective-permute-start | bytes 1572872 | tf_op jit(solution)/shard_map/ppermute | solution.py:59
  127.6 16.4 %collective-permute-start.2 = (bf16[2,128,1024]{2,1,0:T(8,128)(2,1)}, bf16[2,128,1024]{2,1,0:T(8,128)(2,1)S(1)}, u32[]{:S(2)}, u32[]{:S(2)}) collective-permute-start(bf16[2,128,1024]{2,1,0:T(8,128)(2,1)} %get-tuple-element.81), channel_id=1, source_target_pairs={{0,64},{32,96},{64,128},{96,160},{128,192},{160,224},{192,0},{224,... | collective-permute-start | bytes 1572872 | tf_op jit(solution)/shard_map/ppermute | solution.py:59
  129.3 19.1 %copy-start.5 = (bf16[1024,256]{1,0:T(8,128)(2,1)}, bf16[1024,256]{1,0:T(8,128)(2,1)S(1)}, u32[]{:S(2)}) copy-start(bf16[1024,256]{1,0:T(8,128)(2,1)S(1)} %fusion.27) | copy-start | bytes 1572868
  129.3 19.1 %collective-permute-start.7 = (bf16[128,256]{1,0:T(8,128)(2,1)S(1)}, bf16[128,256]{1,0:T(8,128)(2,1)S(1)}, u32[]{:S(2)}, u32[]{:S(2)}) collective-permute-start(bf16[128,256]{1,0:T(8,128)(2,1)S(1)} %get-tuple-element.91), channel_id=1, source_target_pairs={{0,192},{32,224},{64,0},{96,32},{128,64},{160,96},{192,128},{224,1... | collective-permute-start | bytes 196616 | tf_op jit(solution)/shard_map/ppermute | solution.py:59
  132.6 15.8 %collective-permute-start.5 = (bf16[128,256]{1,0:T(8,128)(2,1)S(1)}, bf16[128,256]{1,0:T(8,128)(2,1)S(1)}, u32[]{:S(2)}, u32[]{:S(2)}) collective-permute-start(bf16[128,256]{1,0:T(8,128)(2,1)S(1)} %get-tuple-element.92), channel_id=1, source_target_pairs={{0,64},{32,96},{64,128},{96,160},{128,192},{160,224},{192,0},{224,... | collective-permute-start | bytes 196616 | tf_op jit(solution)/shard_map/ppermute | solution.py:59
  144.3 22.4 %collective-permute-start.4 = (bf16[128,1024]{1,0:T(8,128)(2,1)S(1)}, bf16[128,1024]{1,0:T(8,128)(2,1)S(1)}, u32[]{:S(2)}, u32[]{:S(2)}) collective-permute-start(bf16[128,1024]{1,0:T(8,128)(2,1)S(1)} %dynamic-slice_bitcast_fusion.7), channel_id=1, source_target_pairs={{0,32},{32,0},{64,96},{96,64},{128,160},{160,128},{192,224},{224,1... | collective-permute-start | bytes 786440 | tf_op jit(solution)/shard_map/ppermute | solution.py:41
  149.1 23.9 %collective-permute-start.8 = (bf16[2,128,256]{2,1,0:T(8,128)(2,1)}, bf16[2,128,256]{2,1,0:T(8,128)(2,1)S(1)}, u32[]{:S(2)}, u32[]{:S(2)}) collective-permute-start(bf16[2,128,256]{2,1,0:T(8,128)(2,1)} %get-tuple-element.89), channel_id=1, source_target_pairs={{0,192},{32,224},{64,0},{96,32},{128,64},{160,96},{192,128},{224,1... | collective-permute-start | bytes 393224 | tf_op jit(solution)/shard_map/ppermute | solution.py:59
  149.8 23.2 %collective-permute-start.6 = (bf16[2,128,256]{2,1,0:T(8,128)(2,1)}, bf16[2,128,256]{2,1,0:T(8,128)(2,1)}, u32[]{:S(2)}, u32[]{:S(2)}) collective-permute-start(bf16[2,128,256]{2,1,0:T(8,128)(2,1)} %get-tuple-element.90), channel_id=1, source_target_pairs={{0,64},{32,96},{64,128},{96,160},{128,192},{160,224},{192,0},{224,... | collective-permute-start | bytes 393224 | tf_op jit(solution)/shard_map/ppermute | solution.py:59
  168.8 14.1 %all-to-all-start.4 = ((bf16[8,32,1024]{2,1,0:T(8,128)(2,1)}), bf16[8,32,1024]{2,1,0:T(8,128)(2,1)}, u32[]{:S(2)}, u32[]{:S(2)}) async-start(bf16[8,32,1024]{2,1,0:T(8,128)(2,1)} %bitcast.166), calls=%async_computation.4 | async-start | bytes 1048576 | tf_op jit(solution)/shard_map/all_to_all | solution.py:27
  174.0 8.2 %collective-permute-start.9 = (bf16[128,256]{1,0:T(8,128)(2,1)S(1)}, bf16[128,256]{1,0:T(8,128)(2,1)S(1)}, u32[]{:S(2)}, u32[]{:S(2)}) collective-permute-start(bf16[128,256]{1,0:T(8,128)(2,1)S(1)} %dynamic-slice_bitcast_fusion.14), channel_id=1, source_target_pairs={{0,32},{32,0},{64,96},{96,64},{128,160},{160,128},{192,224},{224,1... | collective-permute-start | bytes 196616 | tf_op jit(solution)/shard_map/ppermute | solution.py:41
Sparse Core Ops, SparseCore 0:
  95.4 75.8 reduce-scatter.1

commit v7 on v5

--- a/solution.py
+++ b/solution.py
@@ -63,9 +63,10 @@
     return sum((term.astype(jnp.float32) for term in terms[1:]), terms[0].astype(jnp.float32))
 
 
-def first_leg(blocks):
+def first_leg(blocks, after=()):
     own, ahead, back, far_ahead, far_back = blocks
-    from_back, from_ahead = shifted(far_ahead, 1), shifted(far_back, -1)
+    got = (shifted(far_ahead, 1), shifted(far_back, -1))
+    from_back, from_ahead = lax.optimization_barrier((*got, *after))[:2]
     half = own.dtype
     ahead = ahead.at[0].set(added(ahead[0], from_back).astype(half))
     back = back.at[1].set(added(back[1], from_ahead).astype(half))
@@ -114,23 +115,26 @@
     grad_hidden = contract(weight_ld, 1, grad_act_down, 0)
     grad_pre = (grad_hidden * slope).astype(half)
     left_up_part = (contract(mixed_up, 1, grad_pre, 1) * scale).astype(half)
-    up_blocks = first_leg(column_blocks(by_place(left_up_part)))
+    up_blocks = column_blocks(by_place(left_up_part))
     grad_mixed_up = row_major(contract(weight_lu, 1, grad_pre, 0).astype(half))
     grad_mixed_up, mixed_down, *_ = lax.optimization_barrier(
         (grad_mixed_up, mixed_down, *down_blocks, *up_blocks)
     )
     grad_act_up = exchange(grad_mixed_up)
     left_down_half = second_leg(down_blocks, (mixed_down,)).astype(half)
-    left_down_grad = over_pairs(pair_halves(left_down_half, 0))
+    down_halves = pair_halves(left_down_half, 0)
     right_down_part = row_major((contract(mixed_down, 1, cotangent, 0) * scale).astype(half))
     right_blocks = column_blocks(by_place(right_down_part))
     layer_out = contract(mixed_down, 0, weight_rd, 0).astype(half)
-    left_up_half = second_leg(up_blocks, (mixed_down,)).astype(half)
+    left_up_half = second_leg(first_leg(up_blocks, (mixed_down,)), down_halves).astype(half)
     right_up_part = row_major((contract(tokens_turned, 1, grad_act_up, 1) * scale).astype(half))
-    left_up_grad = over_pairs(pair_halves(left_up_half, 0))
+    up_halves = pair_halves(left_up_half, 0)
+    left_down_grad = over_pairs(down_halves, up_halves)
+    left_up_grad = over_pairs(up_halves, (right_up_part,))
     right_up_grad = summed(right_up_part)
     right_down_half = second_leg(first_leg(right_blocks), (right_up_part,)).astype(half)
     right_down_grad = over_pairs(pair_halves(right_down_half, 0))
+    grad_act_up, _ = lax.optimization_barrier((grad_act_up, left_up_grad))
     tokens_grad = contract(grad_act_up, 0, weight_ru, 1).astype(half)
     return (
         layer_out,

time: 177 us -> 176 us (level)
  starting transfers between devices: 55.4 us -> 49.2 us
  waiting for transfers between devices: 71.8 us -> 73.9 us
    ppermute x12, waiting for transfers between devices: 3.12 us -> 17.3 us  [shifted(): lax.ppermute(value, 'dp', [(i, (i + 2 * step) % size) for i in range(size)])]
    ppermute x3, waiting for transfers between devices: 15.9 us -> 2.02 us  [over_pairs(): got = lax.ppermute(sent, 'dp', pairs)]
    all_to_all x4, starting transfers between devices: 29.1 us -> 25.7 us  [exchange(): return lax.all_to_all(tile, 'hid', 0, 0, tiled=True)]
    unnamed x29 -> x37, local copies, waits for them, and re-layouts: 3.71 us -> 2.23 us
  transfers between devices with their start and end apart: 20 -> 20, of which waited for: 8 -> 6; matrix products, arithmetic and copies ran while one was open for 23% -> 26% of each run, Pallas kernels for 0% -> 0%
where the time goes in v7:
time: 176 us; the launch traced here: 174 us
  waiting for transfers between devices  73.9 us (42%)
  starting transfers between devices  49.2 us (28%)
  matrix products  27.6 us (16%)
  other arithmetic  12.4 us (7%)
  local copies, waits for them, and re-layouts  9.95 us (6%)
    all_to_all x4, waiting for transfers between devices, exchange(): return lax.all_to_all(tile, 'hid', 0, 0, tiled=True)  54.5 us
    dot_general x12, matrix products, contract(): lax.dot_general(left_side, right_side, (((left_dim,), (right_dim,)), ((),...  27.6 us
    all_to_all x4, starting transfers between devices, exchange(): return lax.all_to_all(tile, 'hid', 0, 0, tiled=True)  25.7 us
    ppermute x12, waiting for transfers between devices, shifted(): lax.ppermute(value, 'dp', [(i, (i + 2 * step) % size) for i in range(size)])  17.3 us
    ppermute x12, starting transfers between devices, shifted(): lax.ppermute(value, 'dp', [(i, (i + 2 * step) % size) for i in range(size)])  16.4 us
    scatter x3, other arithmetic, first_leg(): back = back.at[1].set(added(back[1], from_ahead).astype(half))  3.76 us
    all_to_all x1, starting transfers between devices, summed(): lax.all_to_all(part, 'dp', 0, 0, tiled=True)  3.69 us
  transfers between devices with their start and end apart: 20, of which 6 were waited for; matrix products, arithmetic and copies ran while one was open for 26% of the time, Pallas kernels for 0%

profile of v7, /device:TPU:32, one launch (start us, length us, event | category | flops | bytes accessed | tf_op | source)
XLA Modules:
  0.0 174.0 jit_solution(2966017809065970009)
XLA Ops:
  0.7 2.7 %convolution_convert_fusion = bf16[1024,512]{1,0:T(8,128)(2,1)} fusion(bf16[512,256]{1,0:T(8,128)(2,1)} %param.18, bf16[1,256,1024]{2,1,0:T(8,128)(2,1)} %param.20), kind=kOutput, calls=%fused_computation.23 | convolution fusion | flops 268959744 | bytes 1835008 | tf_op jit(solution)/shard_map/dot_general | solution.py:9
  3.4 11.4 %all-to-all-start = ((bf16[32,32,512]{2,1,0:T(8,128)(2,1)}), bf16[32,32,512]{2,1,0:T(8,128)(2,1)}, u32[]{:S(2)}, u32[]{:S(2)}) async-start(bf16[32,32,512]{2,1,0:T(8,128)(2,1)} %bitcast.2), calls=%async_computation | async-start | bytes 2097152 | tf_op jit(solution)/shard_map/all_to_all | solution.py:22
  14.9 1.5 convolution_convert_fusion.1
  16.3 29.1 %all-to-all-done = bf16[32,32,512]{2,1,0:T(8,128)(2,1)} async-done(((bf16[32,32,512]{2,1,0:T(8,128)(2,1)}), bf16[32,32,512]{2,1,0:T(8,128)(2,1)}, u32[]{:S(2)}, u32[]{:S(2)}) %all-to-all-start) | async-done | bytes 1048608 | tf_op jit(solution)/shard_map/all_to_all | solution.py:22
  45.4 4.5 %all-to-all-start.1 = ((bf16[32,32,512]{2,1,0:T(8,128)(2,1)}), bf16[32,32,512]{2,1,0:T(8,128)(2,1)}, u32[]{:S(2)}, u32[]{:S(2)}) async-start(bf16[32,32,512]{2,1,0:T(8,128)(2,1)} %bitcast.4), calls=%async_computation.1 | async-start | bytes 2097152 | tf_op jit(solution)/shard_map/all_to_all | solution.py:22
  50.0 4.6 %fusion.10 = (f32[1024,512]{0,1:T(8,128)}, bf16[1024,512]{0,1:T(8,128)(2,1)S(1)}) fusion(bf16[1024,512]{1,0:T(8,128)(2,1)} %bitcast.3, bf16[1,1024,1024]{2,1,0:T(8,128)(2,1)S(1)} %copy-done), kind=kOutput, calls=%fused_computation.16 | convolution fusion | flops 1078460416 | bytes 6291456 | tf_op jit(solution)/shard_map/dot_general | solution.py:9
  55.6 2.3 %fusion.18 = bf16[512,1024]{0,1:T(8,128)(2,1)} fusion(bf16[1024,512]{0,1:T(8,128)(2,1)S(1)} %get-tuple-element.110, bf16[1,1024,1024]{2,1,0:T(8,128)(2,1)S(1)} %copy-done.14), kind=kOutput, calls=%fused_computation.22 | convolution fusion | flops 1074266112 | bytes 4194304 | tf_op jit(solution)/shard_map/dot_general | solution.py:9
  57.9 22.0 %all-to-all-done.1 = bf16[32,32,512]{2,1,0:T(8,128)(2,1)} async-done(((bf16[32,32,512]{2,1,0:T(8,128)(2,1)}), bf16[32,32,512]{2,1,0:T(8,128)(2,1)}, u32[]{:S(2)}, u32[]{:S(2)}) %all-to-all-start.1) | async-done | bytes 1048608 | tf_op jit(solution)/shard_map/all_to_all | solution.py:22
  79.9 3.7 %all-to-all-start.2 = ((bf16[32,32,512]{2,1,0:T(8,128)(2,1)}), bf16[32,32,512]{2,1,0:T(8,128)(2,1)S(1)}, u32[]{:S(2)}, u32[]{:S(2)}) async-start(bf16[32,32,512]{2,1,0:T(8,128)(2,1)} %bitcast.201), calls=%async_computation.2 | async-start | bytes 2097152 | tf_op jit(solution)/shard_map/all_to_all | solution.py:22
  83.6 2.8 %multiply_convert_fusion.1 = bf16[1024,1024]{1,0:T(8,128)(2,1)S(1)} fusion(bf16[1024,512]{0,1:T(8,128)(2,1)} %copy-done.17, bf16[1024,512]{1,0:T(8,128)(2,1)} %bitcast.5), kind=kOutput, calls=%fused_computation.1 | convolution fusion | flops 1075838976 | bytes 4194304 | tf_op jit(solution)/shard_map/dot_general | solution.py:9
  87.8 1.5 collective-permute-start
  89.3 1.7 %collective-permute-start.1 = (bf16[128,1024]{1,0:T(8,128)(2,1)S(1)}, bf16[128,1024]{1,0:T(8,128)(2,1)S(1)}, u32[]{:S(2)}, u32[]{:S(2)}) collective-permute-start(bf16[128,1024]{1,0:T(8,128)(2,1)S(1)} %get-tuple-element.116), channel_id=1, source_target_pairs={{0,192},{32,224},{64,0},{96,32},{128,64},{160,96},{192,128},{224,1... | collective-permute-start | bytes 786440 | tf_op jit(solution)/shard_map/ppermute | solution.py:59
  93.0 2.6 %fusion = bf16[1024,512]{0,1:T(8,128)(2,1)S(1)} fusion(f32[1024,512]{0,1:T(8,128)S(1)} %copy-done.16, bf16[1024,512]{1,0:T(8,128)(2,1)} %bitcast.5, bf16[1,1024,1024]{2,1,0:T(8,128)(2,1)S(1)} %copy-done.15), kind=kOutput, calls=%fused_computation.3 | convolution fusion | flops 1074790400 | bytes 6291456 | tf_op jit(solution)/shard_map/dot_general | solution.py:9
  95.6 2.5 %multiply_convert_fusion = bf16[1024,1024]{1,0:T(8,128)(2,1)S(1)} fusion(bf16[1024,512]{1,0:T(8,128)(2,1)} %bitcast.3, bf16[1024,512]{0,1:T(8,128)(2,1)S(1)} %fusion), kind=kOutput, calls=%fused_computation | convolution fusion | flops 1075838976 | bytes 4194304 | tf_op jit(solution)/shard_map/dot_general | solution.py:9
  99.2 3.0 %collective-permute-start.3 = (bf16[128,1024]{1,0:T(8,128)(2,1)}, bf16[128,1024]{1,0:T(8,128)(2,1)}, u32[]{:S(2)}, u32[]{:S(2)}) collective-permute-start(bf16[128,1024]{1,0:T(8,128)(2,1)} %get-tuple-element.140), channel_id=1, source_target_pairs={{0,192},{32,224},{64,0},{96,32},{128,64},{160,96},{192,128},{224,1... | collective-permute-start | bytes 786440 | tf_op jit(solution)/shard_map/ppermute | solution.py:59
  103.4 2.2 %fusion.23 = bf16[1024,512]{1,0:T(8,128)(2,1)} fusion(bf16[1024,512]{0,1:T(8,128)(2,1)S(1)} %fusion, bf16[1,1024,1024]{2,1,0:T(8,128)(2,1)S(1)} %copy-done), kind=kOutput, calls=%fused_computation.25 | convolution fusion | flops 1074266112 | bytes 4194304 | tf_op jit(solution)/shard_map/dot_general | solution.py:9
  107.2 3.2 %collective-permute-start.7 = (bf16[2,128,1024]{2,1,0:T(8,128)(2,1)}, bf16[2,128,1024]{2,1,0:T(8,128)(2,1)}, u32[]{:S(2)}, u32[]{:S(2)}) collective-permute-start(bf16[2,128,1024]{2,1,0:T(8,128)(2,1)} %fusion.39), channel_id=1, source_target_pairs={{0,192},{32,224},{64,0},{96,32},{128,64},{160,96},{192,128},{224,1... | collective-permute-start | bytes 1572872 | tf_op jit(solution)/shard_map/ppermute | solution.py:59
  110.5 3.4 %all-to-all-done.2 = bf16[32,32,512]{2,1,0:T(8,128)(2,1)S(1)} async-done(((bf16[32,32,512]{2,1,0:T(8,128)(2,1)}), bf16[32,32,512]{2,1,0:T(8,128)(2,1)S(1)}, u32[]{:S(2)}, u32[]{:S(2)}) %all-to-all-start.2) | async-done | bytes 1048608 | tf_op jit(solution)/shard_map/all_to_all | solution.py:22
  114.9 6.1 %all-to-all-start.3 = ((bf16[32,32,512]{2,1,0:T(8,128)(2,1)}), bf16[32,32,512]{2,1,0:T(8,128)(2,1)S(1)}, u32[]{:S(2)}, u32[]{:S(2)}) async-start(bf16[32,32,512]{2,1,0:T(8,128)(2,1)} %bitcast.198), calls=%async_computation.3 | async-start | bytes 2097152 | tf_op jit(solution)/shard_map/all_to_all | solution.py:22
  121.0 2.3 %fusion.43 = (bf16[2,128,1024]{2,1,0:T(8,128)(2,1)}, bf16[2,128,1024]{2,1,0:T(8,128)(2,1)}) fusion(bf16[2,128,1024]{2,1,0:T(8,128)(2,1)} %get-tuple-element.142, bf16[128,1024]{1,0:T(8,128)(2,1)} %collective-permute-done.3, bf16[4,2,128,1024]{3,2,1,0:T(8,128)(2,1)} %bitcast.193, s32[]{:T(128)S(6)} %select_n.36, s32[]{:T(128)S(6)} %add.155, ...), kind=kLoop, calls=%fused_computation.62 | loop fusion | flops 1048576 | bytes 1572876 | tf_op jit(solution)/shard_map/scatter | solution.py:72
  123.3 1.7 fusion.27
  125.7 2.8 %collective-permute-start.11 = (bf16[128,256]{1,0:T(8,128)(2,1)S(1)}, bf16[128,256]{1,0:T(8,128)(2,1)S(1)}, u32[]{:S(2)}, u32[]{:S(2)}) collective-permute-start(bf16[128,256]{1,0:T(8,128)(2,1)S(1)} %get-tuple-element.156), channel_id=1, source_target_pairs={{0,192},{32,224},{64,0},{96,32},{128,64},{160,96},{192,128},{224,1... | collective-permute-start | bytes 196616 | tf_op jit(solution)/shard_map/ppermute | solution.py:59
  130.4 9.7 %collective-permute-done.10 = bf16[128,256]{1,0:T(8,128)(2,1)S(1)} collective-permute-done((bf16[128,256]{1,0:T(8,128)(2,1)S(1)}, bf16[128,256]{1,0:T(8,128)(2,1)S(1)}, u32[]{:S(2)}, u32[]{:S(2)}) %collective-permute-start.10) | collective-permute-done | bytes 65568 | tf_op jit(solution)/shard_map/ppermute | solution.py:59
  140.8 2.0 %collective-permute-start.12 = (bf16[2,128,256]{2,1,0:T(8,128)(2,1)}, bf16[2,128,256]{2,1,0:T(8,128)(2,1)S(1)}, u32[]{:S(2)}, u32[]{:S(2)}) collective-permute-start(bf16[2,128,256]{2,1,0:T(8,128)(2,1)} %get-tuple-element.153), channel_id=1, source_target_pairs={{0,64},{32,96},{64,128},{96,160},{128,192},{160,224},{192,0},{224,... | collective-permute-start | bytes 393224 | tf_op jit(solution)/shard_map/ppermute | solution.py:59
  144.1 1.5 add_convert_fusion.1
  147.1 7.6 %collective-permute-done.5 = bf16[2,128,1024]{2,1,0:T(8,128)(2,1)S(1)} collective-permute-done((bf16[2,128,1024]{2,1,0:T(8,128)(2,1)S(1)}, bf16[2,128,1024]{2,1,0:T(8,128)(2,1)S(1)}, u32[]{:S(2)}, u32[]{:S(2)}) %collective-permute-start.5) | collective-permute-done | bytes 524320 | tf_op jit(solution)/shard_map/ppermute | solution.py:59
  156.5 2.2 %convolution_convert_fusion.2 = bf16[512,256]{1,0:T(8,128)(2,1)} fusion(bf16[1024,512]{1,0:T(8,128)(2,1)S(1)} %bitcast.189, bf16[1,256,1024]{2,1,0:T(8,128)(2,1)} %param.20), kind=kOutput, calls=%fused_computation.30 | convolution fusion | flops 268566528 | bytes 1835008 | tf_op jit(solution)/shard_map/dot_general | solution.py:9
  160.0 3.7 %all-to-all-start.4 = ((bf16[8,32,1024]{2,1,0:T(8,128)(2,1)}), bf16[8,32,1024]{2,1,0:T(8,128)(2,1)S(1)}, u32[]{:S(2)}, u32[]{:S(2)}) async-start(bf16[8,32,1024]{2,1,0:T(8,128)(2,1)} %bitcast.196), calls=%async_computation.4 | async-start | bytes 1048576 | tf_op jit(solution)/shard_map/all_to_all | solution.py:27
  163.7 1.9 %fusion.53 = f32[1,128,1024]{2,1,0:T(8,128)} fusion(bf16[128,1024]{1,0:T(8,128)(2,1)} %collective-permute-done.8, bf16[2,128,1024]{2,1,0:T(8,128)(2,1)} %copy-done.4, s32[]{:T(128)S(6)} %select_n.38), kind=kLoop, calls=%fused_computation.93 | loop fusion | flops 393216 | bytes 1048580 | tf_op jit(solution)/shard_map/broadcast_in_dim | solution.py:143
  166.7 2.1 %collective-permute-start.14 = (bf16[128,256]{1,0:T(8,128)(2,1)S(1)}, bf16[128,256]{1,0:T(8,128)(2,1)S(1)}, u32[]{:S(2)}, u32[]{:S(2)}) collective-permute-start(bf16[128,256]{1,0:T(8,128)(2,1)S(1)} %dynamic-slice_bitcast_fusion.22), channel_id=1, source_target_pairs={{0,32},{32,0},{64,96},{96,64},{128,160},{160,128},{192,224},{224,1... | collective-permute-start | bytes 196616 | tf_op jit(solution)/shard_map/ppermute | solution.py:41
  168.8 1.8 %add_bitcast_fusion = f32[1,128,1024]{2,1,0:T(8,128)} fusion(bf16[128,1024]{1,0:T(8,128)(2,1)} %collective-permute-done.9, bf16[128,1024]{1,0:T(8,128)(2,1)S(1)} %copy-done.8), kind=kLoop, calls=%fused_computation.47 | loop fusion | flops 393216 | bytes 1048576 | tf_op jit(solution)/shard_map/broadcast_in_dim | solution.py:144
  170.6 2.0 %collective-permute-done.14 = bf16[128,256]{1,0:T(8,128)(2,1)S(1)} collective-permute-done((bf16[128,256]{1,0:T(8,128)(2,1)S(1)}, bf16[128,256]{1,0:T(8,128)(2,1)S(1)}, u32[]{:S(2)}, u32[]{:S(2)}) %collective-permute-start.14) | collective-permute-done | bytes 65568 | tf_op jit(solution)/shard_map/ppermute | solution.py:41
  (79 shorter events, 20.9 us)
Async XLA Ops:
  0.6 49.4 %copy-start = (bf16[1,1024,1024]{2,1,0:T(8,128)(2,1)S(1)}, bf16[1,1024,1024]{2,1,0:T(8,128)(2,1)}, u32[]{:S(2)}) copy-start(bf16[1,1024,1024]{2,1,0:T(8,128)(2,1)} %param.21) | copy-start | bytes 6291460
  0.6 14.2 %copy-start.13 = (bf16[512,256]{1,0:T(8,128)(2,1)S(1)}, bf16[512,256]{1,0:T(8,128)(2,1)}, u32[]{:S(2)}) copy-start(bf16[512,256]{1,0:T(8,128)(2,1)} %param.19) | copy-start | bytes 786436
  0.7 14.2 %copy-start.10 = (bf16[1,1024,256]{2,1,0:T(8,128)(2,1)S(1)}, bf16[1,1024,256]{2,1,0:T(8,128)(2,1)}, u32[]{:S(2)}) copy-start(bf16[1,1024,256]{2,1,0:T(8,128)(2,1)} %param.23) | copy-start | bytes 1572868
  3.4 42.0 %all-to-all-start = ((bf16[32,32,512]{2,1,0:T(8,128)(2,1)}), bf16[32,32,512]{2,1,0:T(8,128)(2,1)}, u32[]{:S(2)}, u32[]{:S(2)}) async-start(bf16[32,32,512]{2,1,0:T(8,128)(2,1)} %bitcast.2), calls=%async_computation | async-start | bytes 2097152 | tf_op jit(solution)/shard_map/all_to_all | solution.py:22
  14.9 35.0 %copy-start.5 = (bf16[512,256]{1,0:T(8,128)(2,1)S(1)}, bf16[512,256]{1,0:T(8,128)(2,1)}, u32[]{:S(2)}) copy-start(bf16[512,256]{1,0:T(8,128)(2,1)} %param.18) | copy-start | bytes 786436
  45.4 34.5 %all-to-all-start.1 = ((bf16[32,32,512]{2,1,0:T(8,128)(2,1)}), bf16[32,32,512]{2,1,0:T(8,128)(2,1)}, u32[]{:S(2)}, u32[]{:S(2)}) async-start(bf16[32,32,512]{2,1,0:T(8,128)(2,1)} %bitcast.4), calls=%async_computation.1 | async-start | bytes 2097152 | tf_op jit(solution)/shard_map/all_to_all | solution.py:22
  79.9 34.0 %all-to-all-start.2 = ((bf16[32,32,512]{2,1,0:T(8,128)(2,1)}), bf16[32,32,512]{2,1,0:T(8,128)(2,1)S(1)}, u32[]{:S(2)}, u32[]{:S(2)}) async-start(bf16[32,32,512]{2,1,0:T(8,128)(2,1)} %bitcast.201), calls=%async_computation.2 | async-start | bytes 2097152 | tf_op jit(solution)/shard_map/all_to_all | solution.py:22
  86.6 6.4 %copy-start.15 = (bf16[1,1024,1024]{2,1,0:T(8,128)(2,1)S(1)}, bf16[1,1024,1024]{2,1,0:T(8,128)(2,1)}, u32[]{:S(2)}) copy-start(bf16[1,1024,1024]{2,1,0:T(8,128)(2,1)} %param.22) | copy-start | bytes 6291460
  87.8 17.8 %collective-permute-start = (bf16[128,1024]{1,0:T(8,128)(2,1)S(1)}, bf16[128,1024]{1,0:T(8,128)(2,1)S(1)}, u32[]{:S(2)}, u32[]{:S(2)}) collective-permute-start(bf16[128,1024]{1,0:T(8,128)(2,1)S(1)} %get-tuple-element.115), channel_id=1, source_target_pairs={{0,64},{32,96},{64,128},{96,160},{128,192},{160,224},{192,0},{224,... | collective-permute-start | bytes 786440 | tf_op jit(solution)/shard_map/ppermute | solution.py:59
  89.3 16.4 %collective-permute-start.1 = (bf16[128,1024]{1,0:T(8,128)(2,1)S(1)}, bf16[128,1024]{1,0:T(8,128)(2,1)S(1)}, u32[]{:S(2)}, u32[]{:S(2)}) collective-permute-start(bf16[128,1024]{1,0:T(8,128)(2,1)S(1)} %get-tuple-element.116), channel_id=1, source_target_pairs={{0,192},{32,224},{64,0},{96,32},{128,64},{160,96},{192,128},{224,1... | collective-permute-start | bytes 786440 | tf_op jit(solution)/shard_map/ppermute | solution.py:59
  99.0 22.1 %collective-permute-start.2 = (bf16[128,1024]{1,0:T(8,128)(2,1)}, bf16[128,1024]{1,0:T(8,128)(2,1)}, u32[]{:S(2)}, u32[]{:S(2)}) collective-permute-start(bf16[128,1024]{1,0:T(8,128)(2,1)} %get-tuple-element.141), channel_id=1, source_target_pairs={{0,64},{32,96},{64,128},{96,160},{128,192},{160,224},{192,0},{224,... | collective-permute-start | bytes 786440 | tf_op jit(solution)/shard_map/ppermute | solution.py:59
  99.2 21.8 %collective-permute-start.3 = (bf16[128,1024]{1,0:T(8,128)(2,1)}, bf16[128,1024]{1,0:T(8,128)(2,1)}, u32[]{:S(2)}, u32[]{:S(2)}) collective-permute-start(bf16[128,1024]{1,0:T(8,128)(2,1)} %get-tuple-element.140), channel_id=1, source_target_pairs={{0,192},{32,224},{64,0},{96,32},{128,64},{160,96},{192,128},{224,1... | collective-permute-start | bytes 786440 | tf_op jit(solution)/shard_map/ppermute | solution.py:59
  106.4 36.4 %collective-permute-start.6 = (bf16[2,128,1024]{2,1,0:T(8,128)(2,1)}, bf16[2,128,1024]{2,1,0:T(8,128)(2,1)}, u32[]{:S(2)}, u32[]{:S(2)}) collective-permute-start(bf16[2,128,1024]{2,1,0:T(8,128)(2,1)} %fusion.37), channel_id=1, source_target_pairs={{0,64},{32,96},{64,128},{96,160},{128,192},{160,224},{192,0},{224,... | collective-permute-start | bytes 1572872 | tf_op jit(solution)/shard_map/ppermute | solution.py:59
  107.2 36.9 %collective-permute-start.7 = (bf16[2,128,1024]{2,1,0:T(8,128)(2,1)}, bf16[2,128,1024]{2,1,0:T(8,128)(2,1)}, u32[]{:S(2)}, u32[]{:S(2)}) collective-permute-start(bf16[2,128,1024]{2,1,0:T(8,128)(2,1)} %fusion.39), channel_id=1, source_target_pairs={{0,192},{32,224},{64,0},{96,32},{128,64},{160,96},{192,128},{224,1... | collective-permute-start | bytes 1572872 | tf_op jit(solution)/shard_map/ppermute | solution.py:59
  114.9 41.7 %all-to-all-start.3 = ((bf16[32,32,512]{2,1,0:T(8,128)(2,1)}), bf16[32,32,512]{2,1,0:T(8,128)(2,1)S(1)}, u32[]{:S(2)}, u32[]{:S(2)}) async-start(bf16[32,32,512]{2,1,0:T(8,128)(2,1)} %bitcast.198), calls=%async_computation.3 | async-start | bytes 2097152 | tf_op jit(solution)/shard_map/all_to_all | solution.py:22
  121.0 7.5 %copy-start.7 = (bf16[32,32,512]{2,1,0:T(8,128)(2,1)S(1)}, bf16[32,32,512]{2,1,0:T(8,128)(2,1)}, u32[]{:S(2)}) copy-start(bf16[32,32,512]{2,1,0:T(8,128)(2,1)} %copy-done.6) | copy-start | bytes 3145732
  121.0 7.5 %copy-start.11 = (bf16[1,1024,256]{2,1,0:T(8,128)(2,1)S(1)}, bf16[1,1024,256]{2,1,0:T(8,128)(2,1)}, u32[]{:S(2)}) copy-start(bf16[1,1024,256]{2,1,0:T(8,128)(2,1)} %param.23) | copy-start | bytes 1572868
  123.3 23.8 %collective-permute-start.4 = (bf16[2,128,1024]{2,1,0:T(8,128)(2,1)}, bf16[2,128,1024]{2,1,0:T(8,128)(2,1)S(1)}, u32[]{:S(2)}, u32[]{:S(2)}) collective-permute-start(bf16[2,128,1024]{2,1,0:T(8,128)(2,1)} %get-tuple-element.139), channel_id=1, source_target_pairs={{0,64},{32,96},{64,128},{96,160},{128,192},{160,224},{192,0},{224,... | collective-permute-start | bytes 1572872 | tf_op jit(solution)/shard_map/ppermute | solution.py:59
  125.0 19.0 %copy-start.9 = (bf16[1024,256]{1,0:T(8,128)(2,1)}, bf16[1024,256]{1,0:T(8,128)(2,1)S(1)}, u32[]{:S(2)}) copy-start(bf16[1024,256]{1,0:T(8,128)(2,1)S(1)} %fusion.27) | copy-start | bytes 1572868
  125.1 15.1 %copy-start.12 = (bf16[2,128,1024]{2,1,0:T(8,128)(2,1)S(1)}, bf16[2,128,1024]{2,1,0:T(8,128)(2,1)}, u32[]{:S(2)}) copy-start(bf16[2,128,1024]{2,1,0:T(8,128)(2,1)} %get-tuple-element.138) | copy-start | bytes 1572868
  125.1 19.0 %copy-start.2 = (bf16[2,128,1024]{2,1,0:T(8,128)(2,1)S(1)}, bf16[2,128,1024]{2,1,0:T(8,128)(2,1)}, u32[]{:S(2)}) copy-start(bf16[2,128,1024]{2,1,0:T(8,128)(2,1)} %get-tuple-element.113) | copy-start | bytes 1572868
  125.1 15.0 %collective-permute-start.10 = (bf16[128,256]{1,0:T(8,128)(2,1)S(1)}, bf16[128,256]{1,0:T(8,128)(2,1)S(1)}, u32[]{:S(2)}, u32[]{:S(2)}) collective-permute-start(bf16[128,256]{1,0:T(8,128)(2,1)S(1)} %get-tuple-element.157), channel_id=1, source_target_pairs={{0,64},{32,96},{64,128},{96,160},{128,192},{160,224},{192,0},{224,... | collective-permute-start | bytes 196616 | tf_op jit(solution)/shard_map/ppermute | solution.py:59
  125.7 14.4 %collective-permute-start.11 = (bf16[128,256]{1,0:T(8,128)(2,1)S(1)}, bf16[128,256]{1,0:T(8,128)(2,1)S(1)}, u32[]{:S(2)}, u32[]{:S(2)}) collective-permute-start(bf16[128,256]{1,0:T(8,128)(2,1)S(1)} %get-tuple-element.156), channel_id=1, source_target_pairs={{0,192},{32,224},{64,0},{96,32},{128,64},{160,96},{192,128},{224,1... | collective-permute-start | bytes 196616 | tf_op jit(solution)/shard_map/ppermute | solution.py:59
  129.7 25.0 %copy-start.3 = (bf16[2,128,1024]{2,1,0:T(8,128)(2,1)S(1)}, bf16[2,128,1024]{2,1,0:T(8,128)(2,1)}, u32[]{:S(2)}) copy-start(bf16[2,128,1024]{2,1,0:T(8,128)(2,1)} %get-tuple-element.144) | copy-start | bytes 1572868
  140.1 14.6 %collective-permute-start.5 = (bf16[2,128,1024]{2,1,0:T(8,128)(2,1)S(1)}, bf16[2,128,1024]{2,1,0:T(8,128)(2,1)S(1)}, u32[]{:S(2)}, u32[]{:S(2)}) collective-permute-start(bf16[2,128,1024]{2,1,0:T(8,128)(2,1)S(1)} %copy-done.12), channel_id=1, source_target_pairs={{0,192},{32,224},{64,0},{96,32},{128,64},{160,96},{192,128},{224,1... | collective-permute-start | bytes 1572872 | tf_op jit(solution)/shard_map/ppermute | solution.py:59
  140.8 24.8 %collective-permute-start.12 = (bf16[2,128,256]{2,1,0:T(8,128)(2,1)}, bf16[2,128,256]{2,1,0:T(8,128)(2,1)S(1)}, u32[]{:S(2)}, u32[]{:S(2)}) collective-permute-start(bf16[2,128,256]{2,1,0:T(8,128)(2,1)} %get-tuple-element.153), channel_id=1, source_target_pairs={{0,64},{32,96},{64,128},{96,160},{128,192},{160,224},{192,0},{224,... | collective-permute-start | bytes 393224 | tf_op jit(solution)/shard_map/ppermute | solution.py:59
  142.9 22.8 %collective-permute-start.13 = (bf16[2,128,256]{2,1,0:T(8,128)(2,1)}, bf16[2,128,256]{2,1,0:T(8,128)(2,1)}, u32[]{:S(2)}, u32[]{:S(2)}) collective-permute-start(bf16[2,128,256]{2,1,0:T(8,128)(2,1)} %get-tuple-element.152), channel_id=1, source_target_pairs={{0,192},{32,224},{64,0},{96,32},{128,64},{160,96},{192,128},{224,1... | collective-permute-start | bytes 393224 | tf_op jit(solution)/shard_map/ppermute | solution.py:59
  146.4 19.2 %collective-permute-start.9 = (bf16[128,1024]{1,0:T(8,128)(2,1)}, bf16[128,1024]{1,0:T(8,128)(2,1)}, u32[]{:S(2)}, u32[]{:S(2)}) collective-permute-start(bf16[128,1024]{1,0:T(8,128)(2,1)} %get-tuple-element.158), channel_id=1, source_target_pairs={{0,32},{32,0},{64,96},{96,64},{128,160},{160,128},{192,224},{224,1... | collective-permute-start | bytes 786440 | tf_op jit(solution)/shard_map/ppermute | solution.py:41
  155.9 7.9 %collective-permute-start.8 = (bf16[128,1024]{1,0:T(8,128)(2,1)}, bf16[128,1024]{1,0:T(8,128)(2,1)}, u32[]{:S(2)}, u32[]{:S(2)}) collective-permute-start(bf16[128,1024]{1,0:T(8,128)(2,1)} %dynamic-slice_bitcast_fusion.12), channel_id=1, source_target_pairs={{0,32},{32,0},{64,96},{96,64},{128,160},{160,128},{192,224},{224,1... | collective-permute-start | bytes 786440 | tf_op jit(solution)/shard_map/ppermute | solution.py:41
  160.0 8.8 %copy-start.8 = (bf16[128,1024]{1,0:T(8,128)(2,1)S(1)}, bf16[128,1024]{1,0:T(8,128)(2,1)}, u32[]{:S(2)}) copy-start(bf16[128,1024]{1,0:T(8,128)(2,1)} %get-tuple-element.159) | copy-start | bytes 786436
  160.0 13.2 %all-to-all-start.4 = ((bf16[8,32,1024]{2,1,0:T(8,128)(2,1)}), bf16[8,32,1024]{2,1,0:T(8,128)(2,1)S(1)}, u32[]{:S(2)}, u32[]{:S(2)}) async-start(bf16[8,32,1024]{2,1,0:T(8,128)(2,1)} %bitcast.196), calls=%async_computation.4 | async-start | bytes 1048576 | tf_op jit(solution)/shard_map/all_to_all | solution.py:27
  166.7 5.9 %collective-permute-start.14 = (bf16[128,256]{1,0:T(8,128)(2,1)S(1)}, bf16[128,256]{1,0:T(8,128)(2,1)S(1)}, u32[]{:S(2)}, u32[]{:S(2)}) collective-permute-start(bf16[128,256]{1,0:T(8,128)(2,1)S(1)} %dynamic-slice_bitcast_fusion.22), channel_id=1, source_target_pairs={{0,32},{32,0},{64,96},{96,64},{128,160},{160,128},{192,224},{224,1... | collective-permute-start | bytes 196616 | tf_op jit(solution)/shard_map/ppermute | solution.py:41
  (6 other events, 20.2 us)

commit v8 on v7

--- a/solution.py
+++ b/solution.py
@@ -28,16 +28,16 @@
     return jnp.sum(parts.astype(jnp.float32), axis=0)
 
 
-def pair_halves(cur, axis):
-    side = jnp.bitwise_and(lax.axis_index("dp"), 1)
+def pair_halves(cur, axis, bit=0):
+    side = jnp.bitwise_and(jnp.right_shift(lax.axis_index("dp"), bit), 1)
     return [
         lax.dynamic_index_in_dim(cur, place, axis, keepdims=False) for place in (side, 1 - side)
     ]
 
 
-def over_pairs(halves, after=()):
+def over_pairs(halves, after=(), bit=0):
     kept, sent = halves
-    pairs = [(i, i ^ 1) for i in range(lax.axis_size("dp"))]
+    pairs = [(i, i ^ (1 << bit)) for i in range(lax.axis_size("dp"))]
     got = lax.ppermute(sent, "dp", pairs)
     got, *_ = lax.optimization_barrier((got, *after))
     return kept.astype(jnp.float32) + got.astype(jnp.float32)
@@ -121,19 +121,23 @@
         (grad_mixed_up, mixed_down, *down_blocks, *up_blocks)
     )
     grad_act_up = exchange(grad_mixed_up)
+    up_blocks = first_leg(up_blocks, (mixed_down,))
+    later, *up_blocks = lax.optimization_barrier((mixed_down, *up_blocks))
     left_down_half = second_leg(down_blocks, (mixed_down,)).astype(half)
     down_halves = pair_halves(left_down_half, 0)
-    right_down_part = row_major((contract(mixed_down, 1, cotangent, 0) * scale).astype(half))
-    right_blocks = column_blocks(by_place(right_down_part))
+    right_down_part = row_major((contract(later, 1, cotangent, 0) * scale).astype(half))
+    right_cur = right_down_part.reshape(2, 2, 2, -1, right_down_part.shape[1])
+    right_halves = pair_halves(right_cur, 0, 2)
     layer_out = contract(mixed_down, 0, weight_rd, 0).astype(half)
-    left_up_half = second_leg(first_leg(up_blocks, (mixed_down,)), down_halves).astype(half)
+    left_up_half = second_leg(up_blocks, down_halves).astype(half)
     right_up_part = row_major((contract(tokens_turned, 1, grad_act_up, 1) * scale).astype(half))
     up_halves = pair_halves(left_up_half, 0)
     left_down_grad = over_pairs(down_halves, up_halves)
     left_up_grad = over_pairs(up_halves, (right_up_part,))
     right_up_grad = summed(right_up_part)
-    right_down_half = second_leg(first_leg(right_blocks), (right_up_part,)).astype(half)
-    right_down_grad = over_pairs(pair_halves(right_down_half, 0))
+    right_cur = over_pairs(right_halves, down_halves, 2).astype(half)
+    right_cur = over_pairs(pair_halves(right_cur, 0, 1), (right_up_part,), 1).astype(half)
+    right_down_grad = over_pairs(pair_halves(right_cur, 0), ())
     grad_act_up, _ = lax.optimization_barrier((grad_act_up, left_up_grad))
     tokens_grad = contract(grad_act_up, 0, weight_ru, 1).astype(half)
     return (

time: 176 us -> 173 us (0.983)
  starting transfers between devices: 49.2 us -> 44.7 us
    ppermute x12 -> x8, waiting for transfers between devices: 17.3 us -> 10.3 us  [shifted(): lax.ppermute(value, 'dp', [(i, (i + 2 * step) % size) for i in range(size)])]
    ppermute x12 -> x8, starting transfers between devices: 16.4 us -> 11.7 us  [shifted(): lax.ppermute(value, 'dp', [(i, (i + 2 * step) % size) for i in range(size)])]
    all_to_all x4, waiting for transfers between devices: 54.5 us -> 58.6 us  [exchange(): return lax.all_to_all(tile, 'hid', 0, 0, tiled=True)]
    all_to_all x1, waiting for transfers between devices: 0.01 us -> 3.14 us  [summed(): lax.all_to_all(part, 'dp', 0, 0, tiled=True)]
    ppermute x3 -> x5, starting transfers between devices: 3.45 us -> 4.41 us  [over_pairs(): got = lax.ppermute(sent, 'dp', pairs)]
    scatter x3 -> x2, other arithmetic: 3.76 us -> 3.07 us  [first_leg(): back = back.at[1].set(added(back[1], from_ahead).astype(half))]
  transfers between devices with their start and end apart: 20 -> 18, of which waited for: 6 -> 9; matrix products, arithmetic and copies ran while one was open for 26% -> 26% of each run, Pallas kernels for 0% -> 0%
where the time goes in v8:
time: 173 us; the launch traced here: 171 us
  waiting for transfers between devices  74.4 us (43%)
  starting transfers between devices  44.7 us (26%)
  matrix products  27.7 us (16%)
  other arithmetic  13.6 us (8%)
  local copies, waits for them, and re-layouts  9.87 us (6%)
    all_to_all x4, waiting for transfers between devices, exchange(): return lax.all_to_all(tile, 'hid', 0, 0, tiled=True)  58.6 us
    dot_general x12, matrix products, contract(): lax.dot_general(left_side, right_side, (((left_dim,), (right_dim,)), ((),...  27.7 us
    all_to_all x4, starting transfers between devices, exchange(): return lax.all_to_all(tile, 'hid', 0, 0, tiled=True)  24.5 us
    ppermute x8, starting transfers between devices, shifted(): lax.ppermute(value, 'dp', [(i, (i + 2 * step) % size) for i in range(size)])  11.7 us
    ppermute x8, waiting for transfers between devices, shifted(): lax.ppermute(value, 'dp', [(i, (i + 2 * step) % size) for i in range(size)])  10.3 us
    ppermute x5, starting transfers between devices, over_pairs(): got = lax.ppermute(sent, 'dp', pairs)  4.41 us
    all_to_all x1, starting transfers between devices, summed(): lax.all_to_all(part, 'dp', 0, 0, tiled=True)  4.14 us
  transfers between devices with their start and end apart: 18, of which 9 were waited for; matrix products, arithmetic and copies ran while one was open for 26% of the time, Pallas kernels for 0%

profile of v8, /device:TPU:32, one launch (start us, length us, event | category | flops | bytes accessed | tf_op | source)
XLA Modules:
  0.0 171.3 jit_solution(12401652338321968133)
XLA Ops:
  0.7 2.8 %convolution_convert_fusion = bf16[1024,512]{1,0:T(8,128)(2,1)} fusion(bf16[512,256]{1,0:T(8,128)(2,1)} %param.14, bf16[1,256,1024]{2,1,0:T(8,128)(2,1)} %param.16), kind=kOutput, calls=%fused_computation.23 | convolution fusion | flops 268959744 | bytes 1835008 | tf_op jit(solution)/shard_map/dot_general | solution.py:9
  3.4 11.4 %all-to-all-start = ((bf16[32,32,512]{2,1,0:T(8,128)(2,1)}), bf16[32,32,512]{2,1,0:T(8,128)(2,1)}, u32[]{:S(2)}, u32[]{:S(2)}) async-start(bf16[32,32,512]{2,1,0:T(8,128)(2,1)} %bitcast.2), calls=%async_computation | async-start | bytes 2097152 | tf_op jit(solution)/shard_map/all_to_all | solution.py:22
  16.3 29.1 %all-to-all-done = bf16[32,32,512]{2,1,0:T(8,128)(2,1)} async-done(((bf16[32,32,512]{2,1,0:T(8,128)(2,1)}), bf16[32,32,512]{2,1,0:T(8,128)(2,1)}, u32[]{:S(2)}, u32[]{:S(2)}) %all-to-all-start) | async-done | bytes 1048608 | tf_op jit(solution)/shard_map/all_to_all | solution.py:22
  45.4 4.4 %all-to-all-start.1 = ((bf16[32,32,512]{2,1,0:T(8,128)(2,1)}), bf16[32,32,512]{2,1,0:T(8,128)(2,1)}, u32[]{:S(2)}, u32[]{:S(2)}) async-start(bf16[32,32,512]{2,1,0:T(8,128)(2,1)} %bitcast.4), calls=%async_computation.1 | async-start | bytes 2097152 | tf_op jit(solution)/shard_map/all_to_all | solution.py:22
  50.0 4.6 %fusion.10 = (f32[1024,512]{0,1:T(8,128)}, bf16[1024,512]{0,1:T(8,128)(2,1)S(1)}) fusion(bf16[1024,512]{1,0:T(8,128)(2,1)} %bitcast.3, bf16[1,1024,1024]{2,1,0:T(8,128)(2,1)S(1)} %copy-done), kind=kOutput, calls=%fused_computation.16 | convolution fusion | flops 1078460416 | bytes 6291456 | tf_op jit(solution)/shard_map/dot_general | solution.py:9
  55.6 2.3 %fusion.18 = bf16[512,1024]{0,1:T(8,128)(2,1)} fusion(bf16[1024,512]{0,1:T(8,128)(2,1)S(1)} %get-tuple-element.88, bf16[1,1024,1024]{2,1,0:T(8,128)(2,1)S(1)} %copy-done.16), kind=kOutput, calls=%fused_computation.22 | convolution fusion | flops 1074266112 | bytes 4194304 | tf_op jit(solution)/shard_map/dot_general | solution.py:9
  57.9 22.0 %all-to-all-done.1 = bf16[32,32,512]{2,1,0:T(8,128)(2,1)} async-done(((bf16[32,32,512]{2,1,0:T(8,128)(2,1)}), bf16[32,32,512]{2,1,0:T(8,128)(2,1)}, u32[]{:S(2)}, u32[]{:S(2)}) %all-to-all-start.1) | async-done | bytes 1048608 | tf_op jit(solution)/shard_map/all_to_all | solution.py:22
  79.9 3.7 %all-to-all-start.2 = ((bf16[32,32,512]{2,1,0:T(8,128)(2,1)}), bf16[32,32,512]{2,1,0:T(8,128)(2,1)S(1)}, u32[]{:S(2)}, u32[]{:S(2)}) async-start(bf16[32,32,512]{2,1,0:T(8,128)(2,1)} %bitcast.182), calls=%async_computation.2 | async-start | bytes 2097152 | tf_op jit(solution)/shard_map/all_to_all | solution.py:22
  83.6 2.8 %multiply_convert_fusion.1 = bf16[1024,1024]{1,0:T(8,128)(2,1)S(1)} fusion(bf16[1024,512]{0,1:T(8,128)(2,1)} %copy-done.19, bf16[1024,512]{1,0:T(8,128)(2,1)} %bitcast.5), kind=kOutput, calls=%fused_computation.1 | convolution fusion | flops 1075838976 | bytes 4194304 | tf_op jit(solution)/shard_map/dot_general | solution.py:9
  87.8 1.5 collective-permute-start
  89.3 1.7 %collective-permute-start.1 = (bf16[128,1024]{1,0:T(8,128)(2,1)S(1)}, bf16[128,1024]{1,0:T(8,128)(2,1)S(1)}, u32[]{:S(2)}, u32[]{:S(2)}) collective-permute-start(bf16[128,1024]{1,0:T(8,128)(2,1)S(1)} %get-tuple-element.94), channel_id=1, source_target_pairs={{0,192},{32,224},{64,0},{96,32},{128,64},{160,96},{192,128},{224,1... | collective-permute-start | bytes 786440 | tf_op jit(solution)/shard_map/ppermute | solution.py:59
  93.0 2.6 %fusion = bf16[1024,512]{0,1:T(8,128)(2,1)S(1)} fusion(f32[1024,512]{0,1:T(8,128)S(1)} %copy-done.18, bf16[1024,512]{1,0:T(8,128)(2,1)} %bitcast.5, bf16[1,1024,1024]{2,1,0:T(8,128)(2,1)S(1)} %copy-done.17), kind=kOutput, calls=%fused_computation.3 | convolution fusion | flops 1074790400 | bytes 6291456 | tf_op jit(solution)/shard_map/dot_general | solution.py:9
  95.5 2.5 %multiply_convert_fusion = bf16[1024,1024]{1,0:T(8,128)(2,1)S(1)} fusion(bf16[1024,512]{1,0:T(8,128)(2,1)} %bitcast.3, bf16[1024,512]{0,1:T(8,128)(2,1)S(1)} %fusion), kind=kOutput, calls=%fused_computation | convolution fusion | flops 1075838976 | bytes 4194304 | tf_op jit(solution)/shard_map/dot_general | solution.py:9
  99.2 3.0 %collective-permute-start.3 = (bf16[128,1024]{1,0:T(8,128)(2,1)}, bf16[128,1024]{1,0:T(8,128)(2,1)}, u32[]{:S(2)}, u32[]{:S(2)}) collective-permute-start(bf16[128,1024]{1,0:T(8,128)(2,1)} %get-tuple-element.120), channel_id=1, source_target_pairs={{0,192},{32,224},{64,0},{96,32},{128,64},{160,96},{192,128},{224,1... | collective-permute-start | bytes 786440 | tf_op jit(solution)/shard_map/ppermute | solution.py:59
  103.4 2.3 %fusion.23 = bf16[1024,512]{1,0:T(8,128)(2,1)} fusion(bf16[1024,512]{0,1:T(8,128)(2,1)S(1)} %fusion, bf16[1,1024,1024]{2,1,0:T(8,128)(2,1)S(1)} %copy-done), kind=kOutput, calls=%fused_computation.25 | convolution fusion | flops 1074266112 | bytes 4194304 | tf_op jit(solution)/shard_map/dot_general | solution.py:9
  107.5 1.7 collective-permute-start.6
  109.2 4.7 %all-to-all-done.2 = bf16[32,32,512]{2,1,0:T(8,128)(2,1)S(1)} async-done(((bf16[32,32,512]{2,1,0:T(8,128)(2,1)}), bf16[32,32,512]{2,1,0:T(8,128)(2,1)S(1)}, u32[]{:S(2)}, u32[]{:S(2)}) %all-to-all-start.2) | async-done | bytes 1048608 | tf_op jit(solution)/shard_map/all_to_all | solution.py:22
  114.9 4.9 %all-to-all-start.3 = ((bf16[32,32,512]{2,1,0:T(8,128)(2,1)}), bf16[32,32,512]{2,1,0:T(8,128)(2,1)S(1)}, u32[]{:S(2)}, u32[]{:S(2)}) async-start(bf16[32,32,512]{2,1,0:T(8,128)(2,1)} %bitcast.179), calls=%async_computation.3 | async-start | bytes 2097152 | tf_op jit(solution)/shard_map/all_to_all | solution.py:22
  119.8 2.3 %fusion.44 = (bf16[2,128,1024]{2,1,0:T(8,128)(2,1)}, bf16[2,128,1024]{2,1,0:T(8,128)(2,1)}) fusion(bf16[2,128,1024]{2,1,0:T(8,128)(2,1)} %get-tuple-element.122, bf16[128,1024]{1,0:T(8,128)(2,1)} %collective-permute-done.3, bf16[4,2,128,1024]{3,2,1,0:T(8,128)(2,1)} %bitcast.174, s32[]{:T(128)S(6)} %select_n.45, s32[]{:T(128)S(6)} %add.147, ...), kind=kLoop, calls=%fused_computation.64 | loop fusion | flops 1048576 | bytes 1572876 | tf_op jit(solution)/shard_map/scatter | solution.py:72
  122.1 1.8 %fusion.27 = bf16[1024,256]{1,0:T(8,128)(2,1)S(1)} fusion(bf16[1024,512]{1,0:T(8,128)(2,1)} %bitcast.180, bf16[512,256]{1,0:T(8,128)(2,1)} %param.15), kind=kOutput, calls=%fused_computation.29 | convolution fusion | flops 268959744 | bytes 1835008 | tf_op jit(solution)/shard_map/dot_general | solution.py:9
  123.9 1.9 %collective-permute-start.10 = (bf16[2,2,128,256]{3,2,1,0:T(8,128)(2,1)S(1)}, bf16[2,2,128,256]{3,2,1,0:T(8,128)(2,1)S(1)}, u32[]{:S(2)}, u32[]{:S(2)}) collective-permute-start(bf16[2,2,128,256]{3,2,1,0:T(8,128)(2,1)S(1)} %dynamic-slice_bitcast_fusion.12), channel_id=1, source_target_pairs={{0,128},{32,160},{64,192},{96,224},{128,0},{160,32},{192,64},{224,... | collective-permute-start | bytes 786440 | tf_op jit(solution)/shard_map/ppermute | solution.py:41
  127.2 1.9 %collective-permute-start.5 = (bf16[2,128,1024]{2,1,0:T(8,128)(2,1)S(1)}, bf16[2,128,1024]{2,1,0:T(8,128)(2,1)S(1)}, u32[]{:S(2)}, u32[]{:S(2)}) collective-permute-start(bf16[2,128,1024]{2,1,0:T(8,128)(2,1)S(1)} %copy-done.13), channel_id=1, source_target_pairs={{0,192},{32,224},{64,0},{96,32},{128,64},{160,96},{192,128},{224,1... | collective-permute-start | bytes 1572872 | tf_op jit(solution)/shard_map/ppermute | solution.py:59
  130.3 1.5 add_convert_fusion.1
  135.3 9.8 %collective-permute-done.4 = bf16[2,128,1024]{2,1,0:T(8,128)(2,1)S(1)} collective-permute-done((bf16[2,128,1024]{2,1,0:T(8,128)(2,1)S(1)}, bf16[2,128,1024]{2,1,0:T(8,128)(2,1)S(1)}, u32[]{:S(2)}, u32[]{:S(2)}) %collective-permute-start.4) | collective-permute-done | bytes 524320 | tf_op jit(solution)/shard_map/ppermute | solution.py:59
  147.4 2.8 %all-to-all-done.3 = bf16[32,32,512]{2,1,0:T(8,128)(2,1)S(1)} async-done(((bf16[32,32,512]{2,1,0:T(8,128)(2,1)}), bf16[32,32,512]{2,1,0:T(8,128)(2,1)S(1)}, u32[]{:S(2)}, u32[]{:S(2)}) %all-to-all-start.3) | async-done | bytes 1048608 | tf_op jit(solution)/shard_map/all_to_all | solution.py:22
  154.8 1.8 %fusion.47 = f32[1,128,1024]{2,1,0:T(8,128)} fusion(bf16[128,1024]{1,0:T(8,128)(2,1)} %collective-permute-done.8, bf16[2,128,1024]{2,1,0:T(8,128)(2,1)S(1)} %copy-done.5, s32[]{:T(128)S(6)} %select_n.47), kind=kLoop, calls=%fused_computation.82 | loop fusion | flops 393216 | bytes 1048580 | tf_op jit(solution)/shard_map/broadcast_in_dim | solution.py:147
  156.7 4.1 %all-to-all-start.4 = ((bf16[8,32,1024]{2,1,0:T(8,128)(2,1)}), bf16[8,32,1024]{2,1,0:T(8,128)(2,1)}, u32[]{:S(2)}, u32[]{:S(2)}) async-start(bf16[8,32,1024]{2,1,0:T(8,128)(2,1)} %bitcast.177), calls=%async_computation.4 | async-start | bytes 1048576 | tf_op jit(solution)/shard_map/all_to_all | solution.py:27
  160.8 2.2 %convolution_convert_fusion.2 = bf16[512,256]{1,0:T(8,128)(2,1)} fusion(bf16[1024,512]{1,0:T(8,128)(2,1)S(1)} %bitcast.171, bf16[1,256,1024]{2,1,0:T(8,128)(2,1)} %param.16), kind=kOutput, calls=%fused_computation.30 | convolution fusion | flops 268566528 | bytes 1835008 | tf_op jit(solution)/shard_map/dot_general | solution.py:9
  163.0 1.8 %add_bitcast_fusion = f32[1,128,1024]{2,1,0:T(8,128)} fusion(bf16[128,1024]{1,0:T(8,128)(2,1)} %collective-permute-done.9, bf16[128,1024]{1,0:T(8,128)(2,1)S(1)} %copy-done.9), kind=kLoop, calls=%fused_computation.49 | loop fusion | flops 393216 | bytes 1048576 | tf_op jit(solution)/shard_map/broadcast_in_dim | solution.py:148
  164.8 1.5 fusion.46
  166.4 3.1 %all-to-all-done.4 = bf16[8,32,1024]{2,1,0:T(8,128)(2,1)} async-done(((bf16[8,32,1024]{2,1,0:T(8,128)(2,1)}), bf16[8,32,1024]{2,1,0:T(8,128)(2,1)}, u32[]{:S(2)}, u32[]{:S(2)}) %all-to-all-start.4) | async-done | bytes 524320 | tf_op jit(solution)/shard_map/all_to_all | solution.py:27
  169.5 1.8 %convert_reduce_fusion = f32[32,1024]{1,0:T(8,128)} fusion(bf16[8,32,1024]{2,1,0:T(8,128)(2,1)} %all-to-all-done.4), kind=kLoop, calls=%fused_computation.32 | loop fusion | flops 491520 | bytes 655360 | tf_op jit(solution)/shard_map/reduce_sum | solution.py:28
  (79 shorter events, 23.9 us)
Async XLA Ops:
  0.6 49.4 %copy-start = (bf16[1,1024,1024]{2,1,0:T(8,128)(2,1)S(1)}, bf16[1,1024,1024]{2,1,0:T(8,128)(2,1)}, u32[]{:S(2)}) copy-start(bf16[1,1024,1024]{2,1,0:T(8,128)(2,1)} %param.17) | copy-start | bytes 6291460
  0.6 14.2 %copy-start.15 = (bf16[512,256]{1,0:T(8,128)(2,1)S(1)}, bf16[512,256]{1,0:T(8,128)(2,1)}, u32[]{:S(2)}) copy-start(bf16[512,256]{1,0:T(8,128)(2,1)} %param.15) | copy-start | bytes 786436
  0.7 14.2 %copy-start.11 = (bf16[1,1024,256]{2,1,0:T(8,128)(2,1)S(1)}, bf16[1,1024,256]{2,1,0:T(8,128)(2,1)}, u32[]{:S(2)}) copy-start(bf16[1,1024,256]{2,1,0:T(8,128)(2,1)} %param.19) | copy-start | bytes 1572868
  3.4 42.0 %all-to-all-start = ((bf16[32,32,512]{2,1,0:T(8,128)(2,1)}), bf16[32,32,512]{2,1,0:T(8,128)(2,1)}, u32[]{:S(2)}, u32[]{:S(2)}) async-start(bf16[32,32,512]{2,1,0:T(8,128)(2,1)} %bitcast.2), calls=%async_computation | async-start | bytes 2097152 | tf_op jit(solution)/shard_map/all_to_all | solution.py:22
  14.9 35.0 %copy-start.6 = (bf16[512,256]{1,0:T(8,128)(2,1)S(1)}, bf16[512,256]{1,0:T(8,128)(2,1)}, u32[]{:S(2)}) copy-start(bf16[512,256]{1,0:T(8,128)(2,1)} %param.14) | copy-start | bytes 786436
  45.4 34.5 %all-to-all-start.1 = ((bf16[32,32,512]{2,1,0:T(8,128)(2,1)}), bf16[32,32,512]{2,1,0:T(8,128)(2,1)}, u32[]{:S(2)}, u32[]{:S(2)}) async-start(bf16[32,32,512]{2,1,0:T(8,128)(2,1)} %bitcast.4), calls=%async_computation.1 | async-start | bytes 2097152 | tf_op jit(solution)/shard_map/all_to_all | solution.py:22
  50.0 5.6 %copy-start.16 = (bf16[1,1024,1024]{2,1,0:T(8,128)(2,1)S(1)}, bf16[1,1024,1024]{2,1,0:T(8,128)(2,1)}, u32[]{:S(2)}) copy-start(bf16[1,1024,1024]{2,1,0:T(8,128)(2,1)} %param.18) | copy-start | bytes 6291460
  79.9 34.0 %all-to-all-start.2 = ((bf16[32,32,512]{2,1,0:T(8,128)(2,1)}), bf16[32,32,512]{2,1,0:T(8,128)(2,1)S(1)}, u32[]{:S(2)}, u32[]{:S(2)}) async-start(bf16[32,32,512]{2,1,0:T(8,128)(2,1)} %bitcast.182), calls=%async_computation.2 | async-start | bytes 2097152 | tf_op jit(solution)/shard_map/all_to_all | solution.py:22
  86.5 6.4 %copy-start.17 = (bf16[1,1024,1024]{2,1,0:T(8,128)(2,1)S(1)}, bf16[1,1024,1024]{2,1,0:T(8,128)(2,1)}, u32[]{:S(2)}) copy-start(bf16[1,1024,1024]{2,1,0:T(8,128)(2,1)} %param.18) | copy-start | bytes 6291460
  86.6 6.4 %copy-start.18 = (f32[1024,512]{0,1:T(8,128)S(1)}, f32[1024,512]{0,1:T(8,128)}, u32[]{:S(2)}) copy-start(f32[1024,512]{0,1:T(8,128)} %get-tuple-element.90) | copy-start | bytes 6291460
  87.8 17.8 %collective-permute-start = (bf16[128,1024]{1,0:T(8,128)(2,1)S(1)}, bf16[128,1024]{1,0:T(8,128)(2,1)S(1)}, u32[]{:S(2)}, u32[]{:S(2)}) collective-permute-start(bf16[128,1024]{1,0:T(8,128)(2,1)S(1)} %get-tuple-element.93), channel_id=1, source_target_pairs={{0,64},{32,96},{64,128},{96,160},{128,192},{160,224},{192,0},{224,... | collective-permute-start | bytes 786440 | tf_op jit(solution)/shard_map/ppermute | solution.py:59
  89.3 16.4 %collective-permute-start.1 = (bf16[128,1024]{1,0:T(8,128)(2,1)S(1)}, bf16[128,1024]{1,0:T(8,128)(2,1)S(1)}, u32[]{:S(2)}, u32[]{:S(2)}) collective-permute-start(bf16[128,1024]{1,0:T(8,128)(2,1)S(1)} %get-tuple-element.94), channel_id=1, source_target_pairs={{0,192},{32,224},{64,0},{96,32},{128,64},{160,96},{192,128},{224,1... | collective-permute-start | bytes 786440 | tf_op jit(solution)/shard_map/ppermute | solution.py:59
  98.0 5.3 %copy-start.1 = (bf16[1024,1024]{1,0:T(8,128)(2,1)}, bf16[1024,1024]{1,0:T(8,128)(2,1)S(1)}, u32[]{:S(2)}) copy-start(bf16[1024,1024]{1,0:T(8,128)(2,1)S(1)} %multiply_convert_fusion) | copy-start | bytes 6291460
  99.0 14.9 %collective-permute-start.2 = (bf16[128,1024]{1,0:T(8,128)(2,1)}, bf16[128,1024]{1,0:T(8,128)(2,1)}, u32[]{:S(2)}, u32[]{:S(2)}) collective-permute-start(bf16[128,1024]{1,0:T(8,128)(2,1)} %get-tuple-element.121), channel_id=1, source_target_pairs={{0,64},{32,96},{64,128},{96,160},{128,192},{160,224},{192,0},{224,... | collective-permute-start | bytes 786440 | tf_op jit(solution)/shard_map/ppermute | solution.py:59
  99.2 14.6 %collective-permute-start.3 = (bf16[128,1024]{1,0:T(8,128)(2,1)}, bf16[128,1024]{1,0:T(8,128)(2,1)}, u32[]{:S(2)}, u32[]{:S(2)}) collective-permute-start(bf16[128,1024]{1,0:T(8,128)(2,1)} %get-tuple-element.120), channel_id=1, source_target_pairs={{0,192},{32,224},{64,0},{96,32},{128,64},{160,96},{192,128},{224,1... | collective-permute-start | bytes 786440 | tf_op jit(solution)/shard_map/ppermute | solution.py:59
  106.4 23.9 %collective-permute-start.7 = (bf16[2,128,1024]{2,1,0:T(8,128)(2,1)}, bf16[2,128,1024]{2,1,0:T(8,128)(2,1)}, u32[]{:S(2)}, u32[]{:S(2)}) collective-permute-start(bf16[2,128,1024]{2,1,0:T(8,128)(2,1)} %fusion.40), channel_id=1, source_target_pairs={{0,192},{32,224},{64,0},{96,32},{128,64},{160,96},{192,128},{224,1... | collective-permute-start | bytes 1572872 | tf_op jit(solution)/shard_map/ppermute | solution.py:59
  107.5 22.8 %collective-permute-start.6 = (bf16[2,128,1024]{2,1,0:T(8,128)(2,1)}, bf16[2,128,1024]{2,1,0:T(8,128)(2,1)}, u32[]{:S(2)}, u32[]{:S(2)}) collective-permute-start(bf16[2,128,1024]{2,1,0:T(8,128)(2,1)} %fusion.38), channel_id=1, source_target_pairs={{0,64},{32,96},{64,128},{96,160},{128,192},{160,224},{192,0},{224,... | collective-permute-start | bytes 1572872 | tf_op jit(solution)/shard_map/ppermute | solution.py:59
  114.9 35.4 %all-to-all-start.3 = ((bf16[32,32,512]{2,1,0:T(8,128)(2,1)}), bf16[32,32,512]{2,1,0:T(8,128)(2,1)S(1)}, u32[]{:S(2)}, u32[]{:S(2)}) async-start(bf16[32,32,512]{2,1,0:T(8,128)(2,1)} %bitcast.179), calls=%async_computation.3 | async-start | bytes 2097152 | tf_op jit(solution)/shard_map/all_to_all | solution.py:22
  119.8 9.4 %copy-start.8 = (bf16[32,32,512]{2,1,0:T(8,128)(2,1)S(1)}, bf16[32,32,512]{2,1,0:T(8,128)(2,1)}, u32[]{:S(2)}) copy-start(bf16[32,32,512]{2,1,0:T(8,128)(2,1)} %copy-done.7) | copy-start | bytes 3145732
  119.8 9.4 %copy-start.12 = (bf16[1,1024,256]{2,1,0:T(8,128)(2,1)S(1)}, bf16[1,1024,256]{2,1,0:T(8,128)(2,1)}, u32[]{:S(2)}) copy-start(bf16[1,1024,256]{2,1,0:T(8,128)(2,1)} %param.19) | copy-start | bytes 1572868
  122.1 8.2 %copy-start.2 = (bf16[2,128,1024]{2,1,0:T(8,128)(2,1)S(1)}, bf16[2,128,1024]{2,1,0:T(8,128)(2,1)}, u32[]{:S(2)}) copy-start(bf16[2,128,1024]{2,1,0:T(8,128)(2,1)} %get-tuple-element.91) | copy-start | bytes 1572868
  123.9 10.8 %collective-permute-start.10 = (bf16[2,2,128,256]{3,2,1,0:T(8,128)(2,1)S(1)}, bf16[2,2,128,256]{3,2,1,0:T(8,128)(2,1)S(1)}, u32[]{:S(2)}, u32[]{:S(2)}) collective-permute-start(bf16[2,2,128,256]{3,2,1,0:T(8,128)(2,1)S(1)} %dynamic-slice_bitcast_fusion.12), channel_id=1, source_target_pairs={{0,128},{32,160},{64,192},{96,224},{128,0},{160,32},{192,64},{224,... | collective-permute-start | bytes 786440 | tf_op jit(solution)/shard_map/ppermute | solution.py:41
  125.9 19.2 %collective-permute-start.4 = (bf16[2,128,1024]{2,1,0:T(8,128)(2,1)S(1)}, bf16[2,128,1024]{2,1,0:T(8,128)(2,1)S(1)}, u32[]{:S(2)}, u32[]{:S(2)}) collective-permute-start(bf16[2,128,1024]{2,1,0:T(8,128)(2,1)S(1)} %copy-done.14), channel_id=1, source_target_pairs={{0,64},{32,96},{64,128},{96,160},{128,192},{160,224},{192,0},{224,... | collective-permute-start | bytes 1572872 | tf_op jit(solution)/shard_map/ppermute | solution.py:59
  127.2 18.4 %collective-permute-start.5 = (bf16[2,128,1024]{2,1,0:T(8,128)(2,1)S(1)}, bf16[2,128,1024]{2,1,0:T(8,128)(2,1)S(1)}, u32[]{:S(2)}, u32[]{:S(2)}) collective-permute-start(bf16[2,128,1024]{2,1,0:T(8,128)(2,1)S(1)} %copy-done.13), channel_id=1, source_target_pairs={{0,192},{32,224},{64,0},{96,32},{128,64},{160,96},{192,128},{224,1... | collective-permute-start | bytes 1572872 | tf_op jit(solution)/shard_map/ppermute | solution.py:59
  130.3 15.3 %copy-start.3 = (bf16[2,128,1024]{2,1,0:T(8,128)(2,1)S(1)}, bf16[2,128,1024]{2,1,0:T(8,128)(2,1)}, u32[]{:S(2)}) copy-start(bf16[2,128,1024]{2,1,0:T(8,128)(2,1)} %get-tuple-element.102) | copy-start | bytes 1572868
  132.7 23.9 %collective-permute-start.9 = (bf16[128,1024]{1,0:T(8,128)(2,1)}, bf16[128,1024]{1,0:T(8,128)(2,1)}, u32[]{:S(2)}, u32[]{:S(2)}) collective-permute-start(bf16[128,1024]{1,0:T(8,128)(2,1)} %get-tuple-element.132), channel_id=1, source_target_pairs={{0,32},{32,0},{64,96},{96,64},{128,160},{160,128},{192,224},{224,1... | collective-permute-start | bytes 786440 | tf_op jit(solution)/shard_map/ppermute | solution.py:41
  134.8 10.3 %copy-start.10 = (bf16[2,2,128,256]{3,2,1,0:T(8,128)(2,1)}, bf16[2,2,128,256]{3,2,1,0:T(8,128)(2,1)S(1)}, u32[]{:S(2)}) copy-start(bf16[2,2,128,256]{3,2,1,0:T(8,128)(2,1)S(1)} %fusion.28) | copy-start | bytes 786436
  134.8 16.7 %collective-permute-start.11 = (bf16[2,128,256]{2,1,0:T(8,128)(2,1)S(1)}, bf16[2,128,256]{2,1,0:T(8,128)(2,1)}, u32[]{:S(2)}, u32[]{:S(2)}) collective-permute-start(bf16[2,128,256]{2,1,0:T(8,128)(2,1)S(1)} %dynamic-slice_bitcast_fusion.17), channel_id=1, source_target_pairs={{0,64},{32,96},{64,0},{96,32},{128,192},{160,224},{192,128},{224,1... | collective-permute-start | bytes 393224 | tf_op jit(solution)/shard_map/ppermute | solution.py:41
  146.8 8.1 %collective-permute-start.8 = (bf16[128,1024]{1,0:T(8,128)(2,1)}, bf16[128,1024]{1,0:T(8,128)(2,1)}, u32[]{:S(2)}, u32[]{:S(2)}) collective-permute-start(bf16[128,1024]{1,0:T(8,128)(2,1)} %dynamic-slice_bitcast_fusion.13), channel_id=1, source_target_pairs={{0,32},{32,0},{64,96},{96,64},{128,160},{160,128},{192,224},{224,1... | collective-permute-start | bytes 786440 | tf_op jit(solution)/shard_map/ppermute | solution.py:41
  152.5 10.5 %copy-start.9 = (bf16[128,1024]{1,0:T(8,128)(2,1)S(1)}, bf16[128,1024]{1,0:T(8,128)(2,1)}, u32[]{:S(2)}) copy-start(bf16[128,1024]{1,0:T(8,128)(2,1)} %get-tuple-element.133) | copy-start | bytes 786436
  153.2 11.7 %collective-permute-start.12 = (bf16[128,256]{1,0:T(8,128)(2,1)}, bf16[128,256]{1,0:T(8,128)(2,1)}, u32[]{:S(2)}, u32[]{:S(2)}) collective-permute-start(bf16[128,256]{1,0:T(8,128)(2,1)} %dynamic-slice_bitcast_fusion.18), channel_id=1, source_target_pairs={{0,32},{32,0},{64,96},{96,64},{128,160},{160,128},{192,224},{224,1... | collective-permute-start | bytes 196616 | tf_op jit(solution)/shard_map/ppermute | solution.py:41
  156.7 12.8 %all-to-all-start.4 = ((bf16[8,32,1024]{2,1,0:T(8,128)(2,1)}), bf16[8,32,1024]{2,1,0:T(8,128)(2,1)}, u32[]{:S(2)}, u32[]{:S(2)}) async-start(bf16[8,32,1024]{2,1,0:T(8,128)(2,1)} %bitcast.177), calls=%async_computation.4 | async-start | bytes 1048576 | tf_op jit(solution)/shard_map/all_to_all | solution.py:27
  (6 other events, 16.4 us)

commit v9 on v8

--- a/solution.py
+++ b/solution.py
@@ -22,10 +22,9 @@
     return lax.all_to_all(tile, "hid", 0, 0, tiled=True)
 
 
-def summed(part):
+def collected(part):
     rows = part.shape[0] // lax.axis_size("dp")
-    parts = lax.all_to_all(part, "dp", 0, 0, tiled=True).reshape(-1, rows, part.shape[1])
-    return jnp.sum(parts.astype(jnp.float32), axis=0)
+    return lax.all_to_all(part, "dp", 0, 0, tiled=True).reshape(-1, rows, part.shape[1])
 
 
 def pair_halves(cur, axis, bit=0):
@@ -35,12 +34,8 @@
     ]
 
 
-def over_pairs(halves, after=(), bit=0):
-    kept, sent = halves
-    pairs = [(i, i ^ (1 << bit)) for i in range(lax.axis_size("dp"))]
-    got = lax.ppermute(sent, "dp", pairs)
-    got, *_ = lax.optimization_barrier((got, *after))
-    return kept.astype(jnp.float32) + got.astype(jnp.float32)
+def paired(value, bit=0):
+    return lax.ppermute(value, "dp", [(i, i ^ (1 << bit)) for i in range(lax.axis_size("dp"))])
 
 
 def column_blocks(cur):
@@ -132,13 +127,22 @@
     left_up_half = second_leg(up_blocks, down_halves).astype(half)
     right_up_part = row_major((contract(tokens_turned, 1, grad_act_up, 1) * scale).astype(half))
     up_halves = pair_halves(left_up_half, 0)
-    left_down_grad = over_pairs(down_halves, up_halves)
-    left_up_grad = over_pairs(up_halves, (right_up_part,))
-    right_up_grad = summed(right_up_part)
-    right_cur = over_pairs(right_halves, down_halves, 2).astype(half)
-    right_cur = over_pairs(pair_halves(right_cur, 0, 1), (right_up_part,), 1).astype(half)
-    right_down_grad = over_pairs(pair_halves(right_cur, 0), ())
-    grad_act_up, _ = lax.optimization_barrier((grad_act_up, left_up_grad))
+    right_kept, right_sent = right_halves
+    right_got, *_ = lax.optimization_barrier((paired(right_sent, 2), *down_halves))
+    right_cur = added(right_kept, right_got).astype(half)
+    right_kept, right_sent = pair_halves(right_cur, 0, 1)
+    right_got = paired(right_sent, 1)
+    right_kept, right_sent = pair_halves(added(right_kept, right_got).astype(half), 0)
+    right_got = paired(right_sent)
+    down_got, up_got = paired(down_halves[1]), paired(up_halves[1])
+    right_up_parts = collected(right_up_part)
+    down_got, up_got, right_got, right_up_parts = lax.optimization_barrier(
+        (down_got, up_got, right_got, right_up_parts)
+    )
+    left_down_grad = added(down_halves[0], down_got)
+    left_up_grad = added(up_halves[0], up_got)
+    right_up_grad = added(*right_up_parts)
+    right_down_grad = added(right_kept, right_got)
     tokens_grad = contract(grad_act_up, 0, weight_ru, 1).astype(half)
     return (
         layer_out,

time: 173 us -> 172 us (level)
  starting transfers between devices: 44.7 us -> 47.5 us
    all_to_all x1, waiting for transfers between devices: 3.14 us -> 0.01 us  [collected(): lax.all_to_all(part, 'dp', 0, 0, tiled=True)]
    ppermute x5, starting transfers between devices: 4.41 us -> 7.19 us  [paired(): lax.ppermute(value, 'dp', [(i, i ^ 1 << bit) for i in range(lax.axis_size...]
    broadcast_in_dim x1 -> x0, other arithmetic: 1.81 us -> none  [body(): left_down_grad[None]]
    add x0 -> x1, other arithmetic: none -> 1.79 us  [added(): sum((term.astype(jnp.float32) for term in terms[1:]), terms[0].astype(jnp...]
    reduce_sum x1 -> x0, other arithmetic: 1.78 us -> none  [summed(): return jnp.sum(parts.astype(jnp.float32), axis=0)]
  transfers between devices with their start and end apart: 18 -> 18, of which waited for: 9 -> 7; matrix products, arithmetic and copies ran while one was open for 26% -> 23% of each run, Pallas kernels for 0% -> 0%
where the time goes in v9:
time: 172 us; the launch traced here: 171 us
  waiting for transfers between devices  72.9 us (42%)
  starting transfers between devices  47.5 us (28%)
  matrix products  28.4 us (17%)
  other arithmetic  12.2 us (7%)
  local copies, waits for them, and re-layouts  9.45 us (5%)
    all_to_all x4, waiting for transfers between devices, exchange(): return lax.all_to_all(tile, 'hid', 0, 0, tiled=True)  59.2 us
    dot_general x12, matrix products, contract(): lax.dot_general(left_side, right_side, (((left_dim,), (right_dim,)), ((),...  28.4 us
    all_to_all x4, starting transfers between devices, exchange(): return lax.all_to_all(tile, 'hid', 0, 0, tiled=True)  24 us
    ppermute x8, starting transfers between devices, shifted(): lax.ppermute(value, 'dp', [(i, (i + 2 * step) % size) for i in range(size)])  11.8 us
    ppermute x8, waiting for transfers between devices, shifted(): lax.ppermute(value, 'dp', [(i, (i + 2 * step) % size) for i in range(size)])  9.66 us
    ppermute x5, starting transfers between devices, paired(): lax.ppermute(value, 'dp', [(i, i ^ 1 << bit) for i in range(lax.axis_size...  7.19 us
    all_to_all x1, starting transfers between devices, collected(): lax.all_to_all(part, 'dp', 0, 0, tiled=True)  4.52 us
    ppermute x5, waiting for transfers between devices, paired(): lax.ppermute(value, 'dp', [(i, i ^ 1 << bit) for i in range(lax.axis_size...  4.02 us
  transfers between devices with their start and end apart: 18, of which 7 were waited for; matrix products, arithmetic and copies ran while one was open for 23% of the time, Pallas kernels for 0%

profile of v9, /device:TPU:32, one launch (start us, length us, event | category | flops | bytes accessed | tf_op | source)
XLA Modules:
  0.0 171.4 jit_solution(1365787714024528545)
XLA Ops:
  0.6 2.8 %convolution_convert_fusion = bf16[1024,512]{1,0:T(8,128)(2,1)} fusion(bf16[512,256]{1,0:T(8,128)(2,1)} %param.14, bf16[1,256,1024]{2,1,0:T(8,128)(2,1)} %param.16), kind=kOutput, calls=%fused_computation.23 | convolution fusion | flops 268959744 | bytes 1835008 | tf_op jit(solution)/shard_map/dot_general | solution.py:9
  3.4 11.4 %all-to-all-start = ((bf16[32,32,512]{2,1,0:T(8,128)(2,1)}), bf16[32,32,512]{2,1,0:T(8,128)(2,1)S(1)}, u32[]{:S(2)}, u32[]{:S(2)}) async-start(bf16[32,32,512]{2,1,0:T(8,128)(2,1)} %bitcast.2), calls=%async_computation | async-start | bytes 2097152 | tf_op jit(solution)/shard_map/all_to_all | solution.py:22
  14.8 2.6 %convolution_convert_fusion.1 = bf16[1024,512]{1,0:T(8,128)(2,1)} fusion(bf16[512,256]{1,0:T(8,128)(2,1)} %param.15, bf16[1,1024,256]{2,1,0:T(8,128)(2,1)} %param.19), kind=kOutput, calls=%fused_computation.24 | convolution fusion | flops 268959744 | bytes 1835008 | tf_op jit(solution)/shard_map/dot_general | solution.py:9
  17.4 27.9 %all-to-all-done = bf16[32,32,512]{2,1,0:T(8,128)(2,1)S(1)} async-done(((bf16[32,32,512]{2,1,0:T(8,128)(2,1)}), bf16[32,32,512]{2,1,0:T(8,128)(2,1)S(1)}, u32[]{:S(2)}, u32[]{:S(2)}) %all-to-all-start) | async-done | bytes 1048608 | tf_op jit(solution)/shard_map/all_to_all | solution.py:22
  45.3 4.5 %all-to-all-start.1 = ((bf16[32,32,512]{2,1,0:T(8,128)(2,1)}), bf16[32,32,512]{2,1,0:T(8,128)(2,1)}, u32[]{:S(2)}, u32[]{:S(2)}) async-start(bf16[32,32,512]{2,1,0:T(8,128)(2,1)} %bitcast.4), calls=%async_computation.1 | async-start | bytes 2097152 | tf_op jit(solution)/shard_map/all_to_all | solution.py:22
  50.6 3.2 %fusion.10 = (f32[1024,512]{0,1:T(8,128)}, bf16[1024,512]{0,1:T(8,128)(2,1)S(1)}) fusion(bf16[1024,512]{1,0:T(8,128)(2,1)S(1)} %bitcast.178, bf16[1,1024,1024]{2,1,0:T(8,128)(2,1)S(1)} %copy-done), kind=kOutput, calls=%fused_computation.16 | convolution fusion | flops 1078460416 | bytes 6291456 | tf_op jit(solution)/shard_map/dot_general | solution.py:9
  54.8 2.3 %fusion.18 = bf16[512,1024]{0,1:T(8,128)(2,1)} fusion(bf16[1024,512]{0,1:T(8,128)(2,1)S(1)} %get-tuple-element.88, bf16[1,1024,1024]{2,1,0:T(8,128)(2,1)S(1)} %copy-done.14), kind=kOutput, calls=%fused_computation.22 | convolution fusion | flops 1074266112 | bytes 4194304 | tf_op jit(solution)/shard_map/dot_general | solution.py:9
  57.1 22.7 %all-to-all-done.1 = bf16[32,32,512]{2,1,0:T(8,128)(2,1)} async-done(((bf16[32,32,512]{2,1,0:T(8,128)(2,1)}), bf16[32,32,512]{2,1,0:T(8,128)(2,1)}, u32[]{:S(2)}, u32[]{:S(2)}) %all-to-all-start.1) | async-done | bytes 1048608 | tf_op jit(solution)/shard_map/all_to_all | solution.py:22
  79.8 4.5 %all-to-all-start.2 = ((bf16[32,32,512]{2,1,0:T(8,128)(2,1)}), bf16[32,32,512]{2,1,0:T(8,128)(2,1)}, u32[]{:S(2)}, u32[]{:S(2)}) async-start(bf16[32,32,512]{2,1,0:T(8,128)(2,1)} %bitcast.181), calls=%async_computation.2 | async-start | bytes 2097152 | tf_op jit(solution)/shard_map/all_to_all | solution.py:22
  84.3 2.8 %multiply_convert_fusion.1 = bf16[1024,1024]{1,0:T(8,128)(2,1)S(1)} fusion(bf16[1024,512]{0,1:T(8,128)(2,1)} %copy-done.17, bf16[1024,512]{1,0:T(8,128)(2,1)} %bitcast.5), kind=kOutput, calls=%fused_computation.1 | convolution fusion | flops 1075838976 | bytes 4194304 | tf_op jit(solution)/shard_map/dot_general | solution.py:9
  89.9 1.7 %collective-permute-start.1 = (bf16[128,1024]{1,0:T(8,128)(2,1)S(1)}, bf16[128,1024]{1,0:T(8,128)(2,1)S(1)}, u32[]{:S(2)}, u32[]{:S(2)}) collective-permute-start(bf16[128,1024]{1,0:T(8,128)(2,1)S(1)} %get-tuple-element.94), channel_id=1, source_target_pairs={{0,192},{32,224},{64,0},{96,32},{128,64},{160,96},{192,128},{224,1... | collective-permute-start | bytes 786440 | tf_op jit(solution)/shard_map/ppermute | solution.py:54
  93.6 2.6 %fusion = bf16[1024,512]{0,1:T(8,128)(2,1)S(1)} fusion(f32[1024,512]{0,1:T(8,128)S(1)} %copy-done.16, bf16[1024,512]{1,0:T(8,128)(2,1)} %bitcast.5, bf16[1,1024,1024]{2,1,0:T(8,128)(2,1)S(1)} %copy-done.15), kind=kOutput, calls=%fused_computation.3 | convolution fusion | flops 1074790400 | bytes 6291456 | tf_op jit(solution)/shard_map/dot_general | solution.py:9
  97.9 3.0 %collective-permute-start.6 = (bf16[128,1024]{1,0:T(8,128)(2,1)S(1)}, bf16[128,1024]{1,0:T(8,128)(2,1)S(1)}, u32[]{:S(2)}, u32[]{:S(2)}) collective-permute-start(bf16[128,1024]{1,0:T(8,128)(2,1)S(1)} %get-tuple-element.118), channel_id=1, source_target_pairs={{0,192},{32,224},{64,0},{96,32},{128,64},{160,96},{192,128},{224,1... | collective-permute-start | bytes 786440 | tf_op jit(solution)/shard_map/ppermute | solution.py:54
  102.0 2.3 %fusion.23 = bf16[1024,512]{1,0:T(8,128)(2,1)} fusion(bf16[1024,512]{0,1:T(8,128)(2,1)S(1)} %fusion, bf16[1,1024,1024]{2,1,0:T(8,128)(2,1)S(1)} %copy-done), kind=kOutput, calls=%fused_computation.25 | convolution fusion | flops 1074266112 | bytes 4194304 | tf_op jit(solution)/shard_map/dot_general | solution.py:9
  106.2 1.7 collective-permute-start.2
  107.9 6.5 %all-to-all-done.2 = bf16[32,32,512]{2,1,0:T(8,128)(2,1)} async-done(((bf16[32,32,512]{2,1,0:T(8,128)(2,1)}), bf16[32,32,512]{2,1,0:T(8,128)(2,1)}, u32[]{:S(2)}, u32[]{:S(2)}) %all-to-all-start.2) | async-done | bytes 1048608 | tf_op jit(solution)/shard_map/all_to_all | solution.py:22
  115.1 3.7 %all-to-all-start.3 = ((bf16[32,32,512]{2,1,0:T(8,128)(2,1)}), bf16[32,32,512]{2,1,0:T(8,128)(2,1)S(1)}, u32[]{:S(2)}, u32[]{:S(2)}) async-start(bf16[32,32,512]{2,1,0:T(8,128)(2,1)} %bitcast.180), calls=%async_computation.3 | async-start | bytes 2097152 | tf_op jit(solution)/shard_map/all_to_all | solution.py:22
  118.8 2.2 %fusion.45 = (bf16[2,128,1024]{2,1,0:T(8,128)(2,1)}, bf16[2,128,1024]{2,1,0:T(8,128)(2,1)}) fusion(bf16[2,128,1024]{2,1,0:T(8,128)(2,1)} %get-tuple-element.120, bf16[128,1024]{1,0:T(8,128)(2,1)} %copy-done.12, bf16[4,2,128,1024]{3,2,1,0:T(8,128)(2,1)} %bitcast.173, s32[]{:T(128)S(6)} %select_n.45, s32[]{:T(128)S(6)} %add.182, ...), kind=kLoop, calls=%fused_computation.64 | loop fusion | flops 1048576 | bytes 1572876 | tf_op jit(solution)/shard_map/scatter | solution.py:67
  121.1 1.8 %fusion.26 = bf16[1024,256]{1,0:T(8,128)(2,1)S(1)} fusion(bf16[1024,512]{1,0:T(8,128)(2,1)} %bitcast.20, bf16[512,256]{1,0:T(8,128)(2,1)S(1)} %copy-done.10), kind=kOutput, calls=%fused_computation.28 | convolution fusion | flops 268959744 | bytes 1835008 | tf_op jit(solution)/shard_map/dot_general | solution.py:9
  122.9 3.1 %collective-permute-start.10 = (bf16[2,2,128,256]{3,2,1,0:T(8,128)(2,1)S(1)}, bf16[2,2,128,256]{3,2,1,0:T(8,128)(2,1)S(1)}, u32[]{:S(2)}, u32[]{:S(2)}) collective-permute-start(bf16[2,2,128,256]{3,2,1,0:T(8,128)(2,1)S(1)} %dynamic-slice_bitcast_fusion.12), channel_id=1, source_target_pairs={{0,128},{32,160},{64,192},{96,224},{128,0},{160,32},{192,64},{224,... | collective-permute-start | bytes 786440 | tf_op jit(solution)/shard_map/ppermute | solution.py:38
  126.6 2.6 %collective-permute-start.8 = (bf16[2,128,1024]{2,1,0:T(8,128)(2,1)S(1)}, bf16[2,128,1024]{2,1,0:T(8,128)(2,1)S(1)}, u32[]{:S(2)}, u32[]{:S(2)}) collective-permute-start(bf16[2,128,1024]{2,1,0:T(8,128)(2,1)S(1)} %copy-done.8), channel_id=1, source_target_pairs={{0,192},{32,224},{64,0},{96,32},{128,64},{160,96},{192,128},{224,1... | collective-permute-start | bytes 1572872 | tf_op jit(solution)/shard_map/ppermute | solution.py:54
  129.3 2.4 %convolution_convert_fusion.3 = bf16[512,256]{1,0:T(8,128)(2,1)} fusion(bf16[1024,512]{1,0:T(8,128)(2,1)} %bitcast.20, bf16[1,1024,256]{2,1,0:T(8,128)(2,1)S(1)} %copy-done.7), kind=kOutput, calls=%fused_computation.31 | convolution fusion | flops 268566528 | bytes 1835008 | tf_op jit(solution)/shard_map/dot_general | solution.py:9
  131.7 1.5 add_convert_fusion.1
  135.4 8.6 %collective-permute-done.7 = bf16[2,128,1024]{2,1,0:T(8,128)(2,1)S(1)} collective-permute-done((bf16[2,128,1024]{2,1,0:T(8,128)(2,1)S(1)}, bf16[2,128,1024]{2,1,0:T(8,128)(2,1)S(1)}, u32[]{:S(2)}, u32[]{:S(2)}) %collective-permute-start.7) | collective-permute-done | bytes 524320 | tf_op jit(solution)/shard_map/ppermute | solution.py:54
  146.9 2.1 %all-to-all-done.3 = bf16[32,32,512]{2,1,0:T(8,128)(2,1)S(1)} async-done(((bf16[32,32,512]{2,1,0:T(8,128)(2,1)}), bf16[32,32,512]{2,1,0:T(8,128)(2,1)S(1)}, u32[]{:S(2)}, u32[]{:S(2)}) %all-to-all-start.3) | async-done | bytes 1048608 | tf_op jit(solution)/shard_map/all_to_all | solution.py:22
  149.1 2.2 %fusion.27 = bf16[256,1024]{1,0:T(8,128)(2,1)} fusion(bf16[256,512]{1,0:T(8,128)(2,1)} %bitcast.177, bf16[1024,512]{1,0:T(8,128)(2,1)S(1)} %bitcast.169), kind=kOutput, calls=%fused_computation.29 | convolution fusion | flops 268959744 | bytes 1835008 | tf_op jit(solution)/shard_map/dot_general | solution.py:9
  151.3 4.5 %all-to-all-start.4 = ((bf16[8,32,1024]{2,1,0:T(8,128)(2,1)}), bf16[8,32,1024]{2,1,0:T(8,128)(2,1)}, u32[]{:S(2)}, u32[]{:S(2)}) async-start(bf16[8,32,1024]{2,1,0:T(8,128)(2,1)} %bitcast.176), calls=%async_computation.4 | async-start | bytes 1048576 | tf_op jit(solution)/shard_map/all_to_all | solution.py:27
  156.8 2.1 %collective-permute-start.12 = (bf16[128,256]{1,0:T(8,128)(2,1)S(1)}, bf16[128,256]{1,0:T(8,128)(2,1)S(1)}, u32[]{:S(2)}, u32[]{:S(2)}) collective-permute-start(bf16[128,256]{1,0:T(8,128)(2,1)S(1)} %dynamic-slice_bitcast_fusion.17), channel_id=1, source_target_pairs={{0,32},{32,0},{64,96},{96,64},{128,160},{160,128},{192,224},{224,1... | collective-permute-start | bytes 196616 | tf_op jit(solution)/shard_map/ppermute | solution.py:38
  158.9 2.2 %convolution_convert_fusion.2 = bf16[512,256]{1,0:T(8,128)(2,1)} fusion(bf16[1024,512]{1,0:T(8,128)(2,1)S(1)} %bitcast.170, bf16[1,256,1024]{2,1,0:T(8,128)(2,1)} %param.16), kind=kOutput, calls=%fused_computation.30 | convolution fusion | flops 268566528 | bytes 1835008 | tf_op jit(solution)/shard_map/dot_general | solution.py:9
  161.2 4.0 %collective-permute-done.12 = bf16[128,256]{1,0:T(8,128)(2,1)S(1)} collective-permute-done((bf16[128,256]{1,0:T(8,128)(2,1)S(1)}, bf16[128,256]{1,0:T(8,128)(2,1)S(1)}, u32[]{:S(2)}, u32[]{:S(2)}) %collective-permute-start.12) | collective-permute-done | bytes 65568 | tf_op jit(solution)/shard_map/ppermute | solution.py:38
  167.3 1.8 %convert_add_fusion.8 = f32[1,32,1024]{2,1,0:T(8,128)} fusion(bf16[8,32,1024]{2,1,0:T(8,128)(2,1)} %all-to-all-done.4), kind=kLoop, calls=%fused_computation.79 | loop fusion | flops 491520 | bytes 655360 | tf_op jit(solution)/shard_map/add | solution.py:58
  169.1 2.3 %fusion.28 = (f32[1,128,1024]{2,1,0:T(8,128)}, f32[1,128,1024]{2,1,0:T(8,128)}) fusion(bf16[128,1024]{1,0:T(8,128)(2,1)} %collective-permute-done.9, bf16[2,128,1024]{2,1,0:T(8,128)(2,1)} %copy-done.4, s32[]{:T(128)S(6)} %select_n.48, bf16[128,1024]{1,0:T(8,128)(2,1)} %collective-permute-done.4, bf16[128,1024]{1,0:T(8,128)(2,1)S(1)} %get-tuple-element.130), kind=kLoop, calls=%fused_computation.35 | loop fusion | flops 786432 | bytes 2097156 | tf_op jit(solution)/shard_map/broadcast_in_dim | solution.py:151
  (74 shorter events, 21.0 us)
Async XLA Ops:
  0.6 50.0 %copy-start = (bf16[1,1024,1024]{2,1,0:T(8,128)(2,1)S(1)}, bf16[1,1024,1024]{2,1,0:T(8,128)(2,1)}, u32[]{:S(2)}) copy-start(bf16[1,1024,1024]{2,1,0:T(8,128)(2,1)} %param.17) | copy-start | bytes 6291460
  3.4 41.9 %all-to-all-start = ((bf16[32,32,512]{2,1,0:T(8,128)(2,1)}), bf16[32,32,512]{2,1,0:T(8,128)(2,1)S(1)}, u32[]{:S(2)}, u32[]{:S(2)}) async-start(bf16[32,32,512]{2,1,0:T(8,128)(2,1)} %bitcast.2), calls=%async_computation | async-start | bytes 2097152 | tf_op jit(solution)/shard_map/all_to_all | solution.py:22
  14.8 35.0 %copy-start.5 = (bf16[512,256]{1,0:T(8,128)(2,1)S(1)}, bf16[512,256]{1,0:T(8,128)(2,1)}, u32[]{:S(2)}) copy-start(bf16[512,256]{1,0:T(8,128)(2,1)} %param.14) | copy-start | bytes 786436
  45.3 34.5 %all-to-all-start.1 = ((bf16[32,32,512]{2,1,0:T(8,128)(2,1)}), bf16[32,32,512]{2,1,0:T(8,128)(2,1)}, u32[]{:S(2)}, u32[]{:S(2)}) async-start(bf16[32,32,512]{2,1,0:T(8,128)(2,1)} %bitcast.4), calls=%async_computation.1 | async-start | bytes 2097152 | tf_op jit(solution)/shard_map/all_to_all | solution.py:22
  50.6 4.2 %copy-start.14 = (bf16[1,1024,1024]{2,1,0:T(8,128)(2,1)S(1)}, bf16[1,1024,1024]{2,1,0:T(8,128)(2,1)}, u32[]{:S(2)}) copy-start(bf16[1,1024,1024]{2,1,0:T(8,128)(2,1)} %param.18) | copy-start | bytes 6291460
  53.8 1.0 copy-start.17
  79.8 34.5 %all-to-all-start.2 = ((bf16[32,32,512]{2,1,0:T(8,128)(2,1)}), bf16[32,32,512]{2,1,0:T(8,128)(2,1)}, u32[]{:S(2)}, u32[]{:S(2)}) async-start(bf16[32,32,512]{2,1,0:T(8,128)(2,1)} %bitcast.181), calls=%async_computation.2 | async-start | bytes 2097152 | tf_op jit(solution)/shard_map/all_to_all | solution.py:22
  87.2 6.4 %copy-start.15 = (bf16[1,1024,1024]{2,1,0:T(8,128)(2,1)S(1)}, bf16[1,1024,1024]{2,1,0:T(8,128)(2,1)}, u32[]{:S(2)}) copy-start(bf16[1,1024,1024]{2,1,0:T(8,128)(2,1)} %param.18) | copy-start | bytes 6291460
  87.2 6.4 %copy-start.16 = (f32[1024,512]{0,1:T(8,128)S(1)}, f32[1024,512]{0,1:T(8,128)}, u32[]{:S(2)}) copy-start(f32[1024,512]{0,1:T(8,128)} %get-tuple-element.90) | copy-start | bytes 6291460
  88.4 15.9 %collective-permute-start = (bf16[128,1024]{1,0:T(8,128)(2,1)S(1)}, bf16[128,1024]{1,0:T(8,128)(2,1)S(1)}, u32[]{:S(2)}, u32[]{:S(2)}) collective-permute-start(bf16[128,1024]{1,0:T(8,128)(2,1)S(1)} %get-tuple-element.93), channel_id=1, source_target_pairs={{0,64},{32,96},{64,128},{96,160},{128,192},{160,224},{192,0},{224,... | collective-permute-start | bytes 786440 | tf_op jit(solution)/shard_map/ppermute | solution.py:54
  89.9 14.4 %collective-permute-start.1 = (bf16[128,1024]{1,0:T(8,128)(2,1)S(1)}, bf16[128,1024]{1,0:T(8,128)(2,1)S(1)}, u32[]{:S(2)}, u32[]{:S(2)}) collective-permute-start(bf16[128,1024]{1,0:T(8,128)(2,1)S(1)} %get-tuple-element.94), channel_id=1, source_target_pairs={{0,192},{32,224},{64,0},{96,32},{128,64},{160,96},{192,128},{224,1... | collective-permute-start | bytes 786440 | tf_op jit(solution)/shard_map/ppermute | solution.py:54
  97.4 4.6 %copy-start.1 = (bf16[1024,1024]{1,0:T(8,128)(2,1)}, bf16[1024,1024]{1,0:T(8,128)(2,1)S(1)}, u32[]{:S(2)}) copy-start(bf16[1024,1024]{1,0:T(8,128)(2,1)S(1)} %multiply_convert_fusion) | copy-start | bytes 6291460
  97.5 16.8 %collective-permute-start.5 = (bf16[128,1024]{1,0:T(8,128)(2,1)S(1)}, bf16[128,1024]{1,0:T(8,128)(2,1)S(1)}, u32[]{:S(2)}, u32[]{:S(2)}) collective-permute-start(bf16[128,1024]{1,0:T(8,128)(2,1)S(1)} %get-tuple-element.119), channel_id=1, source_target_pairs={{0,64},{32,96},{64,128},{96,160},{128,192},{160,224},{192,0},{224,... | collective-permute-start | bytes 786440 | tf_op jit(solution)/shard_map/ppermute | solution.py:54
  97.9 16.5 %collective-permute-start.6 = (bf16[128,1024]{1,0:T(8,128)(2,1)S(1)}, bf16[128,1024]{1,0:T(8,128)(2,1)S(1)}, u32[]{:S(2)}, u32[]{:S(2)}) collective-permute-start(bf16[128,1024]{1,0:T(8,128)(2,1)S(1)} %get-tuple-element.118), channel_id=1, source_target_pairs={{0,192},{32,224},{64,0},{96,32},{128,64},{160,96},{192,128},{224,1... | collective-permute-start | bytes 786440 | tf_op jit(solution)/shard_map/ppermute | solution.py:54
  105.1 16.0 %copy-start.10 = (bf16[512,256]{1,0:T(8,128)(2,1)S(1)}, bf16[512,256]{1,0:T(8,128)(2,1)}, u32[]{:S(2)}) copy-start(bf16[512,256]{1,0:T(8,128)(2,1)} %param.15) | copy-start | bytes 786436
  105.1 26.6 %collective-permute-start.3 = (bf16[2,128,1024]{2,1,0:T(8,128)(2,1)}, bf16[2,128,1024]{2,1,0:T(8,128)(2,1)}, u32[]{:S(2)}, u32[]{:S(2)}) collective-permute-start(bf16[2,128,1024]{2,1,0:T(8,128)(2,1)} %fusion.41), channel_id=1, source_target_pairs={{0,192},{32,224},{64,0},{96,32},{128,64},{160,96},{192,128},{224,1... | collective-permute-start | bytes 1572872 | tf_op jit(solution)/shard_map/ppermute | solution.py:54
  106.2 25.5 %collective-permute-start.2 = (bf16[2,128,1024]{2,1,0:T(8,128)(2,1)}, bf16[2,128,1024]{2,1,0:T(8,128)(2,1)}, u32[]{:S(2)}, u32[]{:S(2)}) collective-permute-start(bf16[2,128,1024]{2,1,0:T(8,128)(2,1)} %fusion.39), channel_id=1, source_target_pairs={{0,64},{32,96},{64,128},{96,160},{128,192},{160,224},{192,0},{224,... | collective-permute-start | bytes 1572872 | tf_op jit(solution)/shard_map/ppermute | solution.py:54
  115.1 34.0 %all-to-all-start.3 = ((bf16[32,32,512]{2,1,0:T(8,128)(2,1)}), bf16[32,32,512]{2,1,0:T(8,128)(2,1)S(1)}, u32[]{:S(2)}, u32[]{:S(2)}) async-start(bf16[32,32,512]{2,1,0:T(8,128)(2,1)} %bitcast.180), calls=%async_computation.3 | async-start | bytes 2097152 | tf_op jit(solution)/shard_map/all_to_all | solution.py:22
  118.8 10.4 %copy-start.7 = (bf16[1,1024,256]{2,1,0:T(8,128)(2,1)S(1)}, bf16[1,1024,256]{2,1,0:T(8,128)(2,1)}, u32[]{:S(2)}) copy-start(bf16[1,1024,256]{2,1,0:T(8,128)(2,1)} %param.19) | copy-start | bytes 1572868
  121.1 4.9 %copy-start.9 = (bf16[2,128,1024]{2,1,0:T(8,128)(2,1)S(1)}, bf16[2,128,1024]{2,1,0:T(8,128)(2,1)}, u32[]{:S(2)}) copy-start(bf16[2,128,1024]{2,1,0:T(8,128)(2,1)} %get-tuple-element.105) | copy-start | bytes 1572868
  121.1 5.5 %copy-start.8 = (bf16[2,128,1024]{2,1,0:T(8,128)(2,1)S(1)}, bf16[2,128,1024]{2,1,0:T(8,128)(2,1)}, u32[]{:S(2)}) copy-start(bf16[2,128,1024]{2,1,0:T(8,128)(2,1)} %get-tuple-element.106) | copy-start | bytes 1572868
  121.1 10.6 %copy-start.2 = (bf16[2,128,1024]{2,1,0:T(8,128)(2,1)S(1)}, bf16[2,128,1024]{2,1,0:T(8,128)(2,1)}, u32[]{:S(2)}) copy-start(bf16[2,128,1024]{2,1,0:T(8,128)(2,1)} %get-tuple-element.91) | copy-start | bytes 1572868
  122.9 11.8 %collective-permute-start.10 = (bf16[2,2,128,256]{3,2,1,0:T(8,128)(2,1)S(1)}, bf16[2,2,128,256]{3,2,1,0:T(8,128)(2,1)S(1)}, u32[]{:S(2)}, u32[]{:S(2)}) collective-permute-start(bf16[2,2,128,256]{3,2,1,0:T(8,128)(2,1)S(1)} %dynamic-slice_bitcast_fusion.12), channel_id=1, source_target_pairs={{0,128},{32,160},{64,192},{96,224},{128,0},{160,32},{192,64},{224,... | collective-permute-start | bytes 786440 | tf_op jit(solution)/shard_map/ppermute | solution.py:38
  126.0 17.9 %collective-permute-start.7 = (bf16[2,128,1024]{2,1,0:T(8,128)(2,1)S(1)}, bf16[2,128,1024]{2,1,0:T(8,128)(2,1)S(1)}, u32[]{:S(2)}, u32[]{:S(2)}) collective-permute-start(bf16[2,128,1024]{2,1,0:T(8,128)(2,1)S(1)} %copy-done.9), channel_id=1, source_target_pairs={{0,64},{32,96},{64,128},{96,160},{128,192},{160,224},{192,0},{224,... | collective-permute-start | bytes 1572872 | tf_op jit(solution)/shard_map/ppermute | solution.py:54
  126.6 18.4 %collective-permute-start.8 = (bf16[2,128,1024]{2,1,0:T(8,128)(2,1)S(1)}, bf16[2,128,1024]{2,1,0:T(8,128)(2,1)S(1)}, u32[]{:S(2)}, u32[]{:S(2)}) collective-permute-start(bf16[2,128,1024]{2,1,0:T(8,128)(2,1)S(1)} %copy-done.8), channel_id=1, source_target_pairs={{0,192},{32,224},{64,0},{96,32},{128,64},{160,96},{192,128},{224,1... | collective-permute-start | bytes 1572872 | tf_op jit(solution)/shard_map/ppermute | solution.py:54
  131.7 13.4 %copy-start.3 = (bf16[2,128,1024]{2,1,0:T(8,128)(2,1)S(1)}, bf16[2,128,1024]{2,1,0:T(8,128)(2,1)}, u32[]{:S(2)}) copy-start(bf16[2,128,1024]{2,1,0:T(8,128)(2,1)} %get-tuple-element.104) | copy-start | bytes 1572868
  134.0 31.8 %collective-permute-start.4 = (bf16[128,1024]{1,0:T(8,128)(2,1)}, bf16[128,1024]{1,0:T(8,128)(2,1)}, u32[]{:S(2)}, u32[]{:S(2)}) collective-permute-start(bf16[128,1024]{1,0:T(8,128)(2,1)} %get-tuple-element.131), channel_id=1, source_target_pairs={{0,32},{32,0},{64,96},{96,64},{128,160},{160,128},{192,224},{224,1... | collective-permute-start | bytes 786440 | tf_op jit(solution)/shard_map/ppermute | solution.py:38
  134.8 9.2 %copy-start.6 = (bf16[2,2,128,256]{3,2,1,0:T(8,128)(2,1)}, bf16[2,2,128,256]{3,2,1,0:T(8,128)(2,1)S(1)}, u32[]{:S(2)}) copy-start(bf16[2,2,128,256]{3,2,1,0:T(8,128)(2,1)S(1)} %fusion.29) | copy-start | bytes 786436
  134.8 21.0 %collective-permute-start.11 = (bf16[2,128,256]{2,1,0:T(8,128)(2,1)S(1)}, bf16[2,128,256]{2,1,0:T(8,128)(2,1)}, u32[]{:S(2)}, u32[]{:S(2)}) collective-permute-start(bf16[2,128,256]{2,1,0:T(8,128)(2,1)S(1)} %dynamic-slice_bitcast_fusion.16), channel_id=1, source_target_pairs={{0,64},{32,96},{64,0},{96,32},{128,192},{160,224},{192,128},{224,1... | collective-permute-start | bytes 393224 | tf_op jit(solution)/shard_map/ppermute | solution.py:38
  146.3 19.6 %collective-permute-start.9 = (bf16[128,1024]{1,0:T(8,128)(2,1)}, bf16[128,1024]{1,0:T(8,128)(2,1)}, u32[]{:S(2)}, u32[]{:S(2)}) collective-permute-start(bf16[128,1024]{1,0:T(8,128)(2,1)} %dynamic-slice_bitcast_fusion.13), channel_id=1, source_target_pairs={{0,32},{32,0},{64,96},{96,64},{128,160},{160,128},{192,224},{224,1... | collective-permute-start | bytes 786440 | tf_op jit(solution)/shard_map/ppermute | solution.py:38
  151.3 14.5 %all-to-all-start.4 = ((bf16[8,32,1024]{2,1,0:T(8,128)(2,1)}), bf16[8,32,1024]{2,1,0:T(8,128)(2,1)}, u32[]{:S(2)}, u32[]{:S(2)}) async-start(bf16[8,32,1024]{2,1,0:T(8,128)(2,1)} %bitcast.176), calls=%async_computation.4 | async-start | bytes 1048576 | tf_op jit(solution)/shard_map/all_to_all | solution.py:27
  156.8 8.3 %collective-permute-start.12 = (bf16[128,256]{1,0:T(8,128)(2,1)S(1)}, bf16[128,256]{1,0:T(8,128)(2,1)S(1)}, u32[]{:S(2)}, u32[]{:S(2)}) collective-permute-start(bf16[128,256]{1,0:T(8,128)(2,1)S(1)} %dynamic-slice_bitcast_fusion.17), channel_id=1, source_target_pairs={{0,32},{32,0},{64,96},{96,64},{128,160},{160,128},{192,224},{224,1... | collective-permute-start | bytes 196616 | tf_op jit(solution)/shard_map/ppermute | solution.py:38
  (4 other events, 3.0 us)

commit v10 on v9

--- a/solution.py
+++ b/solution.py
@@ -2,6 +2,8 @@
 import jax.numpy as jnp
 from jax import lax
 from jax.experimental.layout import Layout, with_layout_constraint
+from jax.experimental import pallas as pl
+from jax.experimental.pallas import tpu as pltpu
 from jax.sharding import PartitionSpec as P
 
 
@@ -77,6 +79,32 @@
 
 def by_place(part):
     return part.reshape(lax.axis_size("dp") // 2, 2, -1, part.shape[1])
+
+
+def final_kernel(parts, *refs):
+    wide = jnp.float32
+    *pairs, parts_out, first_out, second_out, third_out = refs
+    total = parts[0].astype(wide)
+    for place in range(1, parts.shape[0]):
+        total = total + parts[place].astype(wide)
+    parts_out[...] = total
+    for place, out in enumerate((first_out, second_out, third_out)):
+        kept, got = pairs[2 * place], pairs[2 * place + 1]
+        out[...] = kept[...].astype(wide) + got[...].astype(wide)
+
+
+def final_sums(parts, *pairs):
+    shapes = [parts.shape[1:]] + [kept.shape for kept, _ in pairs]
+    reads = sum(value.size for pair in pairs for value in pair) + parts.size
+    writes = sum(shape[0] * shape[1] for shape in shapes)
+    return pl.pallas_call(
+        final_kernel,
+        out_shape=[jax.ShapeDtypeStruct(shape, jnp.float32) for shape in shapes],
+        compiler_params=pltpu.CompilerParams(vmem_limit_bytes=16 * 1024 * 1024),
+        cost_estimate=pl.CostEstimate(
+            flops=reads, bytes_accessed=2 * reads + 4 * writes, transcendentals=0
+        ),
+    )(parts, *(value for pair in pairs for value in pair))
 
 
 def body(tokens, cotangent, right_up, left_up, left_down, right_down):
@@ -136,13 +164,9 @@
     right_got = paired(right_sent)
     down_got, up_got = paired(down_halves[1]), paired(up_halves[1])
     right_up_parts = collected(right_up_part)
-    down_got, up_got, right_got, right_up_parts = lax.optimization_barrier(
-        (down_got, up_got, right_got, right_up_parts)
-    )
-    left_down_grad = added(down_halves[0], down_got)
-    left_up_grad = added(up_halves[0], up_got)
-    right_up_grad = added(*right_up_parts)
-    right_down_grad = added(right_kept, right_got)
+    right_up_grad, left_up_grad, left_down_grad, right_down_grad = final_sums(
+        right_up_parts, (up_halves[0], up_got), (down_halves[0], down_got), (right_kept, right_got)
+    )
     tokens_grad = contract(grad_act_up, 0, weight_ru, 1).astype(half)
     return (
         layer_out,

time: 172 us -> 168 us (0.977)
  other arithmetic: 12.2 us -> 6.54 us
  Pallas kernels: 0 us -> 2.05 us
  local copies, waits for them, and re-layouts: 9.45 us -> 7.6 us
  matrix products: 28.4 us -> 30.2 us
    broadcast_in_dim x2 -> x0, other arithmetic: 3.77 us -> none  [the longest x1 2.25 us: body(): left_up_grad[None]]
    unnamed x37 -> x25, local copies, waits for them, and re-layouts: 3.38 us -> 0.21 us
    pallas_call x0 -> x1, Pallas kernels: none -> 2.05 us  [final_sums(): pl.pallas_call(final_kernel, out_shape=[jax.ShapeDtypeStruct(shape, jnp.f...]
    add x1 -> x0, other arithmetic: 1.79 us -> none  [added(): sum((term.astype(jnp.float32) for term in terms[1:]), terms[0].astype(jnp...]
    dot_general x12, matrix products: 28.4 us -> 30.2 us  [contract(): lax.dot_general(left_side, right_side, (((left_dim,), (right_dim,)), ((),...]
  transfers between devices with their start and end apart: 18 -> 18, of which waited for: 7 -> 7; matrix products, arithmetic and copies ran while one was open for 23% -> 25% of each run, Pallas kernels for 0% -> 0%
where the time goes in v10:
time: 168 us; the launch traced here: 167 us
  waiting for transfers between devices  71.8 us (43%)
  starting transfers between devices  48.2 us (29%)
  matrix products  30.2 us (18%)
  local copies, waits for them, and re-layouts  7.6 us (5%)
  other arithmetic  6.54 us (4%)
  Pallas kernels  2.05 us (1%)
    all_to_all x4, waiting for transfers between devices, exchange(): return lax.all_to_all(tile, 'hid', 0, 0, tiled=True)  59 us
    dot_general x12, matrix products, contract(): lax.dot_general(left_side, right_side, (((left_dim,), (right_dim,)), ((),...  30.2 us
    all_to_all x4, starting transfers between devices, exchange(): return lax.all_to_all(tile, 'hid', 0, 0, tiled=True)  24.7 us
    ppermute x8, starting transfers between devices, shifted(): lax.ppermute(value, 'dp', [(i, (i + 2 * step) % size) for i in range(size)])  11.7 us
    ppermute x8, waiting for transfers between devices, shifted(): lax.ppermute(value, 'dp', [(i, (i + 2 * step) % size) for i in range(size)])  9 us
    ppermute x5, starting transfers between devices, paired(): lax.ppermute(value, 'dp', [(i, i ^ 1 << bit) for i in range(lax.axis_size...  7.24 us
    all_to_all x1, starting transfers between devices, collected(): lax.all_to_all(part, 'dp', 0, 0, tiled=True)  4.52 us
    ppermute x5, waiting for transfers between devices, paired(): lax.ppermute(value, 'dp', [(i, i ^ 1 << bit) for i in range(lax.axis_size...  3.77 us
  transfers between devices with their start and end apart: 18, of which 7 were waited for; matrix products, arithmetic and copies ran while one was open for 25% of the time, Pallas kernels for 0%

profile of v10, /device:TPU:32, one launch (start us, length us, event | category | flops | bytes accessed | tf_op | source)
XLA Modules:
  0.0 167.3 jit_solution(16759553464180009609)
XLA Ops:
  0.6 2.7 %convolution_convert_fusion = bf16[1024,512]{1,0:T(8,128)(2,1)} fusion(bf16[512,256]{1,0:T(8,128)(2,1)} %param.14, bf16[1,256,1024]{2,1,0:T(8,128)(2,1)} %param.16), kind=kOutput, calls=%fused_computation.23 | convolution fusion | flops 268959744 | bytes 1835008 | tf_op jit(solution)/shard_map/dot_general | solution.py:11
  3.4 11.4 %all-to-all-start = ((bf16[32,32,512]{2,1,0:T(8,128)(2,1)}), bf16[32,32,512]{2,1,0:T(8,128)(2,1)S(1)}, u32[]{:S(2)}, u32[]{:S(2)}) async-start(bf16[32,32,512]{2,1,0:T(8,128)(2,1)} %bitcast.2), calls=%async_computation | async-start | bytes 2097152 | tf_op jit(solution)/shard_map/all_to_all | solution.py:24
  14.8 2.6 %convolution_convert_fusion.1 = bf16[1024,512]{1,0:T(8,128)(2,1)} fusion(bf16[512,256]{1,0:T(8,128)(2,1)} %param.15, bf16[1,1024,256]{2,1,0:T(8,128)(2,1)} %param.19), kind=kOutput, calls=%fused_computation.24 | convolution fusion | flops 268959744 | bytes 1835008 | tf_op jit(solution)/shard_map/dot_general | solution.py:11
  17.4 27.9 %all-to-all-done = bf16[32,32,512]{2,1,0:T(8,128)(2,1)S(1)} async-done(((bf16[32,32,512]{2,1,0:T(8,128)(2,1)}), bf16[32,32,512]{2,1,0:T(8,128)(2,1)S(1)}, u32[]{:S(2)}, u32[]{:S(2)}) %all-to-all-start) | async-done | bytes 1048608 | tf_op jit(solution)/shard_map/all_to_all | solution.py:24
  45.2 4.5 %all-to-all-start.1 = ((bf16[32,32,512]{2,1,0:T(8,128)(2,1)}), bf16[32,32,512]{2,1,0:T(8,128)(2,1)}, u32[]{:S(2)}, u32[]{:S(2)}) async-start(bf16[32,32,512]{2,1,0:T(8,128)(2,1)} %bitcast.4), calls=%async_computation.1 | async-start | bytes 2097152 | tf_op jit(solution)/shard_map/all_to_all | solution.py:24
  49.9 4.6 %fusion.10 = (f32[1024,512]{0,1:T(8,128)}, bf16[1024,512]{0,1:T(8,128)(2,1)S(1)}) fusion(bf16[1024,512]{1,0:T(8,128)(2,1)} %bitcast.172, bf16[1,1024,1024]{2,1,0:T(8,128)(2,1)S(1)} %copy-done), kind=kOutput, calls=%fused_computation.16 | convolution fusion | flops 1078460416 | bytes 6291456 | tf_op jit(solution)/shard_map/dot_general | solution.py:11
  54.5 2.3 %fusion.18 = bf16[512,1024]{0,1:T(8,128)(2,1)} fusion(bf16[1024,512]{0,1:T(8,128)(2,1)S(1)} %get-tuple-element.88, bf16[1,1024,1024]{2,1,0:T(8,128)(2,1)S(1)} %copy-done.9), kind=kOutput, calls=%fused_computation.22 | convolution fusion | flops 1074266112 | bytes 4194304 | tf_op jit(solution)/shard_map/dot_general | solution.py:11
  56.8 23.0 %all-to-all-done.1 = bf16[32,32,512]{2,1,0:T(8,128)(2,1)} async-done(((bf16[32,32,512]{2,1,0:T(8,128)(2,1)}), bf16[32,32,512]{2,1,0:T(8,128)(2,1)}, u32[]{:S(2)}, u32[]{:S(2)}) %all-to-all-start.1) | async-done | bytes 1048608 | tf_op jit(solution)/shard_map/all_to_all | solution.py:24
  79.8 4.5 %all-to-all-start.2 = ((bf16[32,32,512]{2,1,0:T(8,128)(2,1)}), bf16[32,32,512]{2,1,0:T(8,128)(2,1)}, u32[]{:S(2)}, u32[]{:S(2)}) async-start(bf16[32,32,512]{2,1,0:T(8,128)(2,1)} %bitcast.19), calls=%async_computation.2 | async-start | bytes 2097152 | tf_op jit(solution)/shard_map/all_to_all | solution.py:24
  84.2 2.5 %multiply_convert_fusion.1 = bf16[1024,1024]{1,0:T(8,128)(2,1)S(1)} fusion(bf16[1024,512]{0,1:T(8,128)(2,1)S(1)} %get-tuple-element.88, bf16[1024,512]{1,0:T(8,128)(2,1)} %bitcast.5), kind=kOutput, calls=%fused_computation.1 | convolution fusion | flops 1075838976 | bytes 4194304 | tf_op jit(solution)/shard_map/dot_general | solution.py:11
  88.0 1.5 collective-permute-start
  89.5 1.7 %collective-permute-start.1 = (bf16[128,1024]{1,0:T(8,128)(2,1)S(1)}, bf16[128,1024]{1,0:T(8,128)(2,1)S(1)}, u32[]{:S(2)}, u32[]{:S(2)}) collective-permute-start(bf16[128,1024]{1,0:T(8,128)(2,1)S(1)} %get-tuple-element.94), channel_id=1, source_target_pairs={{0,192},{32,224},{64,0},{96,32},{128,64},{160,96},{192,128},{224,1... | collective-permute-start | bytes 786440 | tf_op jit(solution)/shard_map/ppermute | solution.py:56
  93.2 2.6 %fusion = bf16[1024,512]{0,1:T(8,128)(2,1)S(1)} fusion(f32[1024,512]{0,1:T(8,128)S(1)} %copy-done.11, bf16[1024,512]{1,0:T(8,128)(2,1)} %bitcast.5, bf16[1,1024,1024]{2,1,0:T(8,128)(2,1)S(1)} %copy-done.10), kind=kOutput, calls=%fused_computation.3 | convolution fusion | flops 1074790400 | bytes 6291456 | tf_op jit(solution)/shard_map/dot_general | solution.py:11
  98.3 3.0 %collective-permute-start.3 = (bf16[128,1024]{1,0:T(8,128)(2,1)}, bf16[128,1024]{1,0:T(8,128)(2,1)}, u32[]{:S(2)}, u32[]{:S(2)}) collective-permute-start(bf16[128,1024]{1,0:T(8,128)(2,1)} %get-tuple-element.118), channel_id=1, source_target_pairs={{0,192},{32,224},{64,0},{96,32},{128,64},{160,96},{192,128},{224,1... | collective-permute-start | bytes 786440 | tf_op jit(solution)/shard_map/ppermute | solution.py:56
  102.4 2.3 %fusion.23 = bf16[1024,512]{1,0:T(8,128)(2,1)} fusion(bf16[1024,512]{0,1:T(8,128)(2,1)S(1)} %fusion, bf16[1,1024,1024]{2,1,0:T(8,128)(2,1)S(1)} %copy-done), kind=kOutput, calls=%fused_computation.25 | convolution fusion | flops 1074266112 | bytes 4194304 | tf_op jit(solution)/shard_map/dot_general | solution.py:11
  106.6 1.7 %collective-permute-start.6 = (bf16[2,128,1024]{2,1,0:T(8,128)(2,1)}, bf16[2,128,1024]{2,1,0:T(8,128)(2,1)}, u32[]{:S(2)}, u32[]{:S(2)}) collective-permute-start(bf16[2,128,1024]{2,1,0:T(8,128)(2,1)} %fusion.38), channel_id=1, source_target_pairs={{0,64},{32,96},{64,128},{96,160},{128,192},{160,224},{192,0},{224,... | collective-permute-start | bytes 1572872 | tf_op jit(solution)/shard_map/ppermute | solution.py:56
  108.2 6.1 %all-to-all-done.2 = bf16[32,32,512]{2,1,0:T(8,128)(2,1)} async-done(((bf16[32,32,512]{2,1,0:T(8,128)(2,1)}), bf16[32,32,512]{2,1,0:T(8,128)(2,1)}, u32[]{:S(2)}, u32[]{:S(2)}) %all-to-all-start.2) | async-done | bytes 1048608 | tf_op jit(solution)/shard_map/all_to_all | solution.py:24
  114.3 4.5 %all-to-all-start.3 = ((bf16[32,32,512]{2,1,0:T(8,128)(2,1)}), bf16[32,32,512]{2,1,0:T(8,128)(2,1)}, u32[]{:S(2)}, u32[]{:S(2)}) async-start(bf16[32,32,512]{2,1,0:T(8,128)(2,1)} %bitcast.174), calls=%async_computation.3 | async-start | bytes 2097152 | tf_op jit(solution)/shard_map/all_to_all | solution.py:24
  118.8 2.2 %fusion.44 = (bf16[2,128,1024]{2,1,0:T(8,128)(2,1)}, bf16[2,128,1024]{2,1,0:T(8,128)(2,1)}) fusion(bf16[2,128,1024]{2,1,0:T(8,128)(2,1)} %get-tuple-element.120, bf16[128,1024]{1,0:T(8,128)(2,1)} %collective-permute-done.3, bf16[4,2,128,1024]{3,2,1,0:T(8,128)(2,1)} %bitcast.167, s32[]{:T(128)S(6)} %select_n.45, s32[]{:T(128)S(6)} %add.135, ...), kind=kLoop, calls=%fused_computation.61 | loop fusion | flops 1048576 | bytes 1572876 | tf_op jit(solution)/shard_map/scatter | solution.py:69
  121.0 1.8 %fusion.27 = bf16[1024,256]{1,0:T(8,128)(2,1)S(1)} fusion(bf16[1024,512]{1,0:T(8,128)(2,1)} %bitcast.20, bf16[512,256]{1,0:T(8,128)(2,1)} %param.15), kind=kOutput, calls=%fused_computation.29 | convolution fusion | flops 268959744 | bytes 1835008 | tf_op jit(solution)/shard_map/dot_general | solution.py:11
  122.9 3.1 %collective-permute-start.10 = (bf16[2,2,128,256]{3,2,1,0:T(8,128)(2,1)S(1)}, bf16[2,2,128,256]{3,2,1,0:T(8,128)(2,1)S(1)}, u32[]{:S(2)}, u32[]{:S(2)}) collective-permute-start(bf16[2,2,128,256]{3,2,1,0:T(8,128)(2,1)S(1)} %dynamic-slice_bitcast_fusion.12), channel_id=1, source_target_pairs={{0,128},{32,160},{64,192},{96,224},{128,0},{160,32},{192,64},{224,... | collective-permute-start | bytes 786440 | tf_op jit(solution)/shard_map/ppermute | solution.py:40
  126.6 2.6 %collective-permute-start.5 = (bf16[2,128,1024]{2,1,0:T(8,128)(2,1)S(1)}, bf16[2,128,1024]{2,1,0:T(8,128)(2,1)S(1)}, u32[]{:S(2)}, u32[]{:S(2)}) collective-permute-start(bf16[2,128,1024]{2,1,0:T(8,128)(2,1)S(1)} %copy-done.7), channel_id=1, source_target_pairs={{0,192},{32,224},{64,0},{96,32},{128,64},{160,96},{192,128},{224,1... | collective-permute-start | bytes 1572872 | tf_op jit(solution)/shard_map/ppermute | solution.py:56
  129.2 2.4 %convolution_convert_fusion.3 = bf16[512,256]{1,0:T(8,128)(2,1)} fusion(bf16[1024,512]{1,0:T(8,128)(2,1)} %bitcast.20, bf16[1,1024,256]{2,1,0:T(8,128)(2,1)S(1)} %copy-done.6), kind=kOutput, calls=%fused_computation.31 | convolution fusion | flops 268566528 | bytes 1835008 | tf_op jit(solution)/shard_map/dot_general | solution.py:11
  131.6 1.5 add_convert_fusion.1
  136.0 7.9 %collective-permute-done.4 = bf16[2,128,1024]{2,1,0:T(8,128)(2,1)S(1)} collective-permute-done((bf16[2,128,1024]{2,1,0:T(8,128)(2,1)S(1)}, bf16[2,128,1024]{2,1,0:T(8,128)(2,1)S(1)}, u32[]{:S(2)}, u32[]{:S(2)}) %collective-permute-start.4) | collective-permute-done | bytes 524320 | tf_op jit(solution)/shard_map/ppermute | solution.py:56
  146.7 2.1 %all-to-all-done.3 = bf16[32,32,512]{2,1,0:T(8,128)(2,1)} async-done(((bf16[32,32,512]{2,1,0:T(8,128)(2,1)}), bf16[32,32,512]{2,1,0:T(8,128)(2,1)}, u32[]{:S(2)}, u32[]{:S(2)}) %all-to-all-start.3) | async-done | bytes 1048608 | tf_op jit(solution)/shard_map/all_to_all | solution.py:24
  148.9 2.5 %fusion.26 = bf16[256,1024]{1,0:T(8,128)(2,1)} fusion(bf16[256,512]{1,0:T(8,128)(2,1)S(1)} %bitcast.171, bf16[1024,512]{1,0:T(8,128)(2,1)} %bitcast.32), kind=kOutput, calls=%fused_computation.28 | convolution fusion | flops 268959744 | bytes 1835008 | tf_op jit(solution)/shard_map/dot_general | solution.py:11
  151.3 4.5 %all-to-all-start.4 = ((bf16[8,32,1024]{2,1,0:T(8,128)(2,1)}), bf16[8,32,1024]{2,1,0:T(8,128)(2,1)S(1)}, u32[]{:S(2)}, u32[]{:S(2)}) async-start(bf16[8,32,1024]{2,1,0:T(8,128)(2,1)} %bitcast.170), calls=%async_computation.4 | async-start | bytes 1048576 | tf_op jit(solution)/shard_map/all_to_all | solution.py:29
  156.8 2.1 %collective-permute-start.12 = (bf16[128,256]{1,0:T(8,128)(2,1)S(1)}, bf16[128,256]{1,0:T(8,128)(2,1)S(1)}, u32[]{:S(2)}, u32[]{:S(2)}) collective-permute-start(bf16[128,256]{1,0:T(8,128)(2,1)S(1)} %get-tuple-element.134), channel_id=1, source_target_pairs={{0,32},{32,0},{64,96},{96,64},{128,160},{160,128},{192,224},{224,1... | collective-permute-start | bytes 196616 | tf_op jit(solution)/shard_map/ppermute | solution.py:40
  158.9 2.5 %convolution_convert_fusion.2 = bf16[512,256]{1,0:T(8,128)(2,1)} fusion(bf16[1024,512]{1,0:T(8,128)(2,1)} %bitcast.32, bf16[1,256,1024]{2,1,0:T(8,128)(2,1)} %param.16), kind=kOutput, calls=%fused_computation.30 | convolution fusion | flops 268566528 | bytes 1835008 | tf_op jit(solution)/shard_map/dot_general | solution.py:11
  161.5 3.8 %collective-permute-done.12.refs_5_ = bf16[128,256]{1,0:T(8,128)(2,1)S(1)} collective-permute-done((bf16[128,256]{1,0:T(8,128)(2,1)S(1)}, bf16[128,256]{1,0:T(8,128)(2,1)S(1)}, u32[]{:S(2)}, u32[]{:S(2)}) %collective-permute-start.12) | collective-permute-done | bytes 65568 | tf_op jit(solution)/shard_map/ppermute | solution.py:40
  165.3 2.1 %shard_map.109 = (f32[32,1024]{1,0:T(8,128)}, f32[128,1024]{1,0:T(8,128)}, f32[128,1024]{1,0:T(8,128)}, f32[128,256]{1,0:T(8,128)}) custom-call(bf16[8,32,1024]{2,1,0:T(8,128)(2,1)S(1)} %all-to-all-done.4.parts, bf16[128,1024]{1,0:T(8,128)(2,1)S(1)} %get-tuple-element.131.refs_0_, bf16[128,1024]{1,0:T(8,128)(2,1)} %collective-permute-done.8.refs_1_, ...), custom_call_target="tpu_custom_call" | custom-call | flops 851968 | bytes 3014656 | tf_op jit(solution)/shard_map/pallas_call | solution.py:100
  (60 shorter events, 16.0 us)
Async XLA Ops:
  0.6 49.3 %copy-start = (bf16[1,1024,1024]{2,1,0:T(8,128)(2,1)S(1)}, bf16[1,1024,1024]{2,1,0:T(8,128)(2,1)}, u32[]{:S(2)}) copy-start(bf16[1,1024,1024]{2,1,0:T(8,128)(2,1)} %param.17) | copy-start | bytes 6291460
  3.4 41.9 %all-to-all-start = ((bf16[32,32,512]{2,1,0:T(8,128)(2,1)}), bf16[32,32,512]{2,1,0:T(8,128)(2,1)S(1)}, u32[]{:S(2)}, u32[]{:S(2)}) async-start(bf16[32,32,512]{2,1,0:T(8,128)(2,1)} %bitcast.2), calls=%async_computation | async-start | bytes 2097152 | tf_op jit(solution)/shard_map/all_to_all | solution.py:24
  14.7 35.0 %copy-start.2 = (bf16[512,256]{1,0:T(8,128)(2,1)S(1)}, bf16[512,256]{1,0:T(8,128)(2,1)}, u32[]{:S(2)}) copy-start(bf16[512,256]{1,0:T(8,128)(2,1)} %param.14) | copy-start | bytes 786436
  45.2 4.5 %copy-start.3 = (bf16[32,32,512]{2,1,0:T(8,128)(2,1)}, bf16[32,32,512]{2,1,0:T(8,128)(2,1)S(1)}, u32[]{:S(2)}) copy-start(bf16[32,32,512]{2,1,0:T(8,128)(2,1)S(1)} %all-to-all-done) | copy-start | bytes 3145732
  45.2 34.5 %all-to-all-start.1 = ((bf16[32,32,512]{2,1,0:T(8,128)(2,1)}), bf16[32,32,512]{2,1,0:T(8,128)(2,1)}, u32[]{:S(2)}, u32[]{:S(2)}) async-start(bf16[32,32,512]{2,1,0:T(8,128)(2,1)} %bitcast.4), calls=%async_computation.1 | async-start | bytes 2097152 | tf_op jit(solution)/shard_map/all_to_all | solution.py:24
  49.9 4.6 %copy-start.9 = (bf16[1,1024,1024]{2,1,0:T(8,128)(2,1)S(1)}, bf16[1,1024,1024]{2,1,0:T(8,128)(2,1)}, u32[]{:S(2)}) copy-start(bf16[1,1024,1024]{2,1,0:T(8,128)(2,1)} %param.18) | copy-start | bytes 6291460
  79.8 34.5 %all-to-all-start.2 = ((bf16[32,32,512]{2,1,0:T(8,128)(2,1)}), bf16[32,32,512]{2,1,0:T(8,128)(2,1)}, u32[]{:S(2)}, u32[]{:S(2)}) async-start(bf16[32,32,512]{2,1,0:T(8,128)(2,1)} %bitcast.19), calls=%async_computation.2 | async-start | bytes 2097152 | tf_op jit(solution)/shard_map/all_to_all | solution.py:24
  86.8 6.3 %copy-start.10 = (bf16[1,1024,1024]{2,1,0:T(8,128)(2,1)S(1)}, bf16[1,1024,1024]{2,1,0:T(8,128)(2,1)}, u32[]{:S(2)}) copy-start(bf16[1,1024,1024]{2,1,0:T(8,128)(2,1)} %param.18) | copy-start | bytes 6291460
  86.8 6.3 %copy-start.11 = (f32[1024,512]{0,1:T(8,128)S(1)}, f32[1024,512]{0,1:T(8,128)}, u32[]{:S(2)}) copy-start(f32[1024,512]{0,1:T(8,128)} %get-tuple-element.90) | copy-start | bytes 6291460
  88.0 16.7 %collective-permute-start = (bf16[128,1024]{1,0:T(8,128)(2,1)S(1)}, bf16[128,1024]{1,0:T(8,128)(2,1)S(1)}, u32[]{:S(2)}, u32[]{:S(2)}) collective-permute-start(bf16[128,1024]{1,0:T(8,128)(2,1)S(1)} %get-tuple-element.93), channel_id=1, source_target_pairs={{0,64},{32,96},{64,128},{96,160},{128,192},{160,224},{192,0},{224,... | collective-permute-start | bytes 786440 | tf_op jit(solution)/shard_map/ppermute | solution.py:56
  89.5 15.2 %collective-permute-start.1 = (bf16[128,1024]{1,0:T(8,128)(2,1)S(1)}, bf16[128,1024]{1,0:T(8,128)(2,1)S(1)}, u32[]{:S(2)}, u32[]{:S(2)}) collective-permute-start(bf16[128,1024]{1,0:T(8,128)(2,1)S(1)} %get-tuple-element.94), channel_id=1, source_target_pairs={{0,192},{32,224},{64,0},{96,32},{128,64},{160,96},{192,128},{224,1... | collective-permute-start | bytes 786440 | tf_op jit(solution)/shard_map/ppermute | solution.py:56
  93.2 2.7 %copy-start.4 = (bf16[32,32,512]{2,1,0:T(8,128)(2,1)S(1)}, bf16[32,32,512]{2,1,0:T(8,128)(2,1)}, u32[]{:S(2)}) copy-start(bf16[32,32,512]{2,1,0:T(8,128)(2,1)} %copy-done.3) | copy-start | bytes 3145732
  97.1 5.3 %copy-start.1 = (bf16[1024,1024]{1,0:T(8,128)(2,1)}, bf16[1024,1024]{1,0:T(8,128)(2,1)S(1)}, u32[]{:S(2)}) copy-start(bf16[1024,1024]{1,0:T(8,128)(2,1)S(1)} %multiply_convert_fusion) | copy-start | bytes 6291460
  98.0 16.3 %collective-permute-start.2 = (bf16[128,1024]{1,0:T(8,128)(2,1)}, bf16[128,1024]{1,0:T(8,128)(2,1)}, u32[]{:S(2)}, u32[]{:S(2)}) collective-permute-start(bf16[128,1024]{1,0:T(8,128)(2,1)} %get-tuple-element.119), channel_id=1, source_target_pairs={{0,64},{32,96},{64,128},{96,160},{128,192},{160,224},{192,0},{224,... | collective-permute-start | bytes 786440 | tf_op jit(solution)/shard_map/ppermute | solution.py:56
  98.3 16.0 %collective-permute-start.3 = (bf16[128,1024]{1,0:T(8,128)(2,1)}, bf16[128,1024]{1,0:T(8,128)(2,1)}, u32[]{:S(2)}, u32[]{:S(2)}) collective-permute-start(bf16[128,1024]{1,0:T(8,128)(2,1)} %get-tuple-element.118), channel_id=1, source_target_pairs={{0,192},{32,224},{64,0},{96,32},{128,64},{160,96},{192,128},{224,1... | collective-permute-start | bytes 786440 | tf_op jit(solution)/shard_map/ppermute | solution.py:56
  105.4 26.2 %collective-permute-start.7 = (bf16[2,128,1024]{2,1,0:T(8,128)(2,1)}, bf16[2,128,1024]{2,1,0:T(8,128)(2,1)}, u32[]{:S(2)}, u32[]{:S(2)}) collective-permute-start(bf16[2,128,1024]{2,1,0:T(8,128)(2,1)} %fusion.40), channel_id=1, source_target_pairs={{0,192},{32,224},{64,0},{96,32},{128,64},{160,96},{192,128},{224,1... | collective-permute-start | bytes 1572872 | tf_op jit(solution)/shard_map/ppermute | solution.py:56
  106.6 25.1 %collective-permute-start.6 = (bf16[2,128,1024]{2,1,0:T(8,128)(2,1)}, bf16[2,128,1024]{2,1,0:T(8,128)(2,1)}, u32[]{:S(2)}, u32[]{:S(2)}) collective-permute-start(bf16[2,128,1024]{2,1,0:T(8,128)(2,1)} %fusion.38), channel_id=1, source_target_pairs={{0,64},{32,96},{64,128},{96,160},{128,192},{160,224},{192,0},{224,... | collective-permute-start | bytes 1572872 | tf_op jit(solution)/shard_map/ppermute | solution.py:56
  114.3 34.5 %all-to-all-start.3 = ((bf16[32,32,512]{2,1,0:T(8,128)(2,1)}), bf16[32,32,512]{2,1,0:T(8,128)(2,1)}, u32[]{:S(2)}, u32[]{:S(2)}) async-start(bf16[32,32,512]{2,1,0:T(8,128)(2,1)} %bitcast.174), calls=%async_computation.3 | async-start | bytes 2097152 | tf_op jit(solution)/shard_map/all_to_all | solution.py:24
  118.8 10.4 %copy-start.6 = (bf16[1,1024,256]{2,1,0:T(8,128)(2,1)S(1)}, bf16[1,1024,256]{2,1,0:T(8,128)(2,1)}, u32[]{:S(2)}) copy-start(bf16[1,1024,256]{2,1,0:T(8,128)(2,1)} %param.19) | copy-start | bytes 1572868
  121.0 4.9 %copy-start.8 = (bf16[2,128,1024]{2,1,0:T(8,128)(2,1)S(1)}, bf16[2,128,1024]{2,1,0:T(8,128)(2,1)}, u32[]{:S(2)}) copy-start(bf16[2,128,1024]{2,1,0:T(8,128)(2,1)} %get-tuple-element.104) | copy-start | bytes 1572868
  121.0 5.5 %copy-start.7 = (bf16[2,128,1024]{2,1,0:T(8,128)(2,1)S(1)}, bf16[2,128,1024]{2,1,0:T(8,128)(2,1)}, u32[]{:S(2)}) copy-start(bf16[2,128,1024]{2,1,0:T(8,128)(2,1)} %get-tuple-element.105) | copy-start | bytes 1572868
  122.9 11.7 %collective-permute-start.10 = (bf16[2,2,128,256]{3,2,1,0:T(8,128)(2,1)S(1)}, bf16[2,2,128,256]{3,2,1,0:T(8,128)(2,1)S(1)}, u32[]{:S(2)}, u32[]{:S(2)}) collective-permute-start(bf16[2,2,128,256]{3,2,1,0:T(8,128)(2,1)S(1)} %dynamic-slice_bitcast_fusion.12), channel_id=1, source_target_pairs={{0,128},{32,160},{64,192},{96,224},{128,0},{160,32},{192,64},{224,... | collective-permute-start | bytes 786440 | tf_op jit(solution)/shard_map/ppermute | solution.py:40
  126.0 18.0 %collective-permute-start.4 = (bf16[2,128,1024]{2,1,0:T(8,128)(2,1)S(1)}, bf16[2,128,1024]{2,1,0:T(8,128)(2,1)S(1)}, u32[]{:S(2)}, u32[]{:S(2)}) collective-permute-start(bf16[2,128,1024]{2,1,0:T(8,128)(2,1)S(1)} %copy-done.8), channel_id=1, source_target_pairs={{0,64},{32,96},{64,128},{96,160},{128,192},{160,224},{192,0},{224,... | collective-permute-start | bytes 1572872 | tf_op jit(solution)/shard_map/ppermute | solution.py:56
  126.6 18.4 %collective-permute-start.5 = (bf16[2,128,1024]{2,1,0:T(8,128)(2,1)S(1)}, bf16[2,128,1024]{2,1,0:T(8,128)(2,1)S(1)}, u32[]{:S(2)}, u32[]{:S(2)}) collective-permute-start(bf16[2,128,1024]{2,1,0:T(8,128)(2,1)S(1)} %copy-done.7), channel_id=1, source_target_pairs={{0,192},{32,224},{64,0},{96,32},{128,64},{160,96},{192,128},{224,1... | collective-permute-start | bytes 1572872 | tf_op jit(solution)/shard_map/ppermute | solution.py:56
  133.9 31.4 %collective-permute-start.9 = (bf16[128,1024]{1,0:T(8,128)(2,1)}, bf16[128,1024]{1,0:T(8,128)(2,1)S(1)}, u32[]{:S(2)}, u32[]{:S(2)}) collective-permute-start(bf16[128,1024]{1,0:T(8,128)(2,1)} %get-tuple-element.132), channel_id=1, source_target_pairs={{0,32},{32,0},{64,96},{96,64},{128,160},{160,128},{192,224},{224,1... | collective-permute-start | bytes 786440 | tf_op jit(solution)/shard_map/ppermute | solution.py:40
  134.6 9.3 %copy-start.5 = (bf16[2,2,128,256]{3,2,1,0:T(8,128)(2,1)}, bf16[2,2,128,256]{3,2,1,0:T(8,128)(2,1)S(1)}, u32[]{:S(2)}) copy-start(bf16[2,2,128,256]{3,2,1,0:T(8,128)(2,1)S(1)} %fusion.28) | copy-start | bytes 786436
  135.4 20.5 %collective-permute-start.11 = (bf16[2,128,256]{2,1,0:T(8,128)(2,1)}, bf16[2,128,256]{2,1,0:T(8,128)(2,1)S(1)}, u32[]{:S(2)}, u32[]{:S(2)}) collective-permute-start(bf16[2,128,256]{2,1,0:T(8,128)(2,1)} %dynamic-slice_bitcast_fusion.17), channel_id=1, source_target_pairs={{0,64},{32,96},{64,0},{96,32},{128,192},{160,224},{192,128},{224,1... | collective-permute-start | bytes 393224 | tf_op jit(solution)/shard_map/ppermute | solution.py:40
  146.1 19.2 %collective-permute-start.8 = (bf16[128,1024]{1,0:T(8,128)(2,1)}, bf16[128,1024]{1,0:T(8,128)(2,1)}, u32[]{:S(2)}, u32[]{:S(2)}) collective-permute-start(bf16[128,1024]{1,0:T(8,128)(2,1)} %get-tuple-element.130), channel_id=1, source_target_pairs={{0,32},{32,0},{64,96},{96,64},{128,160},{160,128},{192,224},{224,1... | collective-permute-start | bytes 786440 | tf_op jit(solution)/shard_map/ppermute | solution.py:40
  151.3 13.9 %all-to-all-start.4 = ((bf16[8,32,1024]{2,1,0:T(8,128)(2,1)}), bf16[8,32,1024]{2,1,0:T(8,128)(2,1)S(1)}, u32[]{:S(2)}, u32[]{:S(2)}) async-start(bf16[8,32,1024]{2,1,0:T(8,128)(2,1)} %bitcast.170), calls=%async_computation.4 | async-start | bytes 1048576 | tf_op jit(solution)/shard_map/all_to_all | solution.py:29
  156.8 8.4 %collective-permute-start.12 = (bf16[128,256]{1,0:T(8,128)(2,1)S(1)}, bf16[128,256]{1,0:T(8,128)(2,1)S(1)}, u32[]{:S(2)}, u32[]{:S(2)}) collective-permute-start(bf16[128,256]{1,0:T(8,128)(2,1)S(1)} %get-tuple-element.134), channel_id=1, source_target_pairs={{0,32},{32,0},{64,96},{96,64},{128,160},{160,128},{192,224},{224,1... | collective-permute-start | bytes 196616 | tf_op jit(solution)/shard_map/ppermute | solution.py:40

commit v11 on v10

--- a/solution.py
+++ b/solution.py
@@ -105,6 +105,30 @@
             flops=reads, bytes_accessed=2 * reads + 4 * writes, transcendentals=0
         ),
     )(parts, *(value for pair in pairs for value in pair))
+
+
+def scaled_product(left_side, right_side, scale):
+    def kernel(left, right, out):
+        term = lax.dot_general(
+            left[...],
+            right[...],
+            (((1,), (1,)), ((), ())),
+            preferred_element_type=jnp.float32,
+        )
+        out[...] = (term * scale).astype(out.dtype)
+
+    rows, depth = left_side.shape
+    columns = right_side.shape[0]
+    return pl.pallas_call(
+        kernel,
+        out_shape=jax.ShapeDtypeStruct((rows, columns), left_side.dtype),
+        compiler_params=pltpu.CompilerParams(vmem_limit_bytes=16 * 1024 * 1024),
+        cost_estimate=pl.CostEstimate(
+            flops=2 * rows * columns * depth,
+            bytes_accessed=2 * (rows * depth + columns * depth + rows * columns),
+            transcendentals=0,
+        ),
+    )(left_side, right_side)
 
 
 def body(tokens, cotangent, right_up, left_up, left_down, right_down):
@@ -153,7 +177,7 @@
     right_halves = pair_halves(right_cur, 0, 2)
     layer_out = contract(mixed_down, 0, weight_rd, 0).astype(half)
     left_up_half = second_leg(up_blocks, down_halves).astype(half)
-    right_up_part = row_major((contract(tokens_turned, 1, grad_act_up, 1) * scale).astype(half))
+    right_up_part = scaled_product(tokens_turned, grad_act_up, scale)
     up_halves = pair_halves(left_up_half, 0)
     right_kept, right_sent = right_halves
     right_got, *_ = lax.optimization_barrier((paired(right_sent, 2), *down_halves))

time: 168 us -> 169 us (level)
  local copies, waits for them, and re-layouts: 7.6 us -> 11.7 us
  matrix products: 30.2 us -> 26.4 us
  starting transfers between devices: 48.2 us -> 46.1 us
  waiting for transfers between devices: 71.8 us -> 73.8 us
    dot_general x12 -> x11, matrix products: 30.2 us -> 26.4 us  [contract(): lax.dot_general(left_side, right_side, (((left_dim,), (right_dim,)), ((),...]
    unnamed x25 -> x41, local copies, waits for them, and re-layouts: 0.21 us -> 3.89 us
    ppermute x5, starting transfers between devices: 7.24 us -> 5.54 us  [paired(): lax.ppermute(value, 'dp', [(i, i ^ 1 << bit) for i in range(lax.axis_size...]
  transfers between devices with their start and end apart: 18 -> 18, of which waited for: 7 -> 8; matrix products, arithmetic and copies ran while one was open for 25% -> 23% of each run, Pallas kernels for 0% -> 0%
where the time goes in v11:
time: 169 us; the launch traced here: 168 us
  waiting for transfers between devices  73.8 us (44%)
  starting transfers between devices  46.1 us (27%)
  matrix products  26.4 us (16%)
  local copies, waits for them, and re-layouts  11.7 us (7%)
  other arithmetic  6.67 us (4%)
  Pallas kernels  2.75 us (2%)
    all_to_all x4, waiting for transfers between devices, exchange(): return lax.all_to_all(tile, 'hid', 0, 0, tiled=True)  58.6 us
    dot_general x11, matrix products, contract(): lax.dot_general(left_side, right_side, (((left_dim,), (right_dim,)), ((),...  26.4 us
    all_to_all x4, starting transfers between devices, exchange(): return lax.all_to_all(tile, 'hid', 0, 0, tiled=True)  24.5 us
    ppermute x8, starting transfers between devices, shifted(): lax.ppermute(value, 'dp', [(i, (i + 2 * step) % size) for i in range(size)])  11.7 us
    ppermute x8, waiting for transfers between devices, shifted(): lax.ppermute(value, 'dp', [(i, (i + 2 * step) % size) for i in range(size)])  9.74 us
    ppermute x5, starting transfers between devices, paired(): lax.ppermute(value, 'dp', [(i, i ^ 1 << bit) for i in range(lax.axis_size...  5.54 us
    ppermute x5, waiting for transfers between devices, paired(): lax.ppermute(value, 'dp', [(i, i ^ 1 << bit) for i in range(lax.axis_size...  5.44 us
    all_to_all x1, starting transfers between devices, collected(): lax.all_to_all(part, 'dp', 0, 0, tiled=True)  4.28 us
  transfers between devices with their start and end apart: 18, of which 8 were waited for; matrix products, arithmetic and copies ran while one was open for 23% of the time, Pallas kernels for 0%

profile of v11, /device:TPU:32, one launch (start us, length us, event | category | flops | bytes accessed | tf_op | source)
XLA Modules:
  0.0 168.4 jit_solution(16500434496422417051)
XLA Ops:
  0.7 2.8 %convolution_convert_fusion = bf16[1024,512]{1,0:T(8,128)(2,1)} fusion(bf16[512,256]{1,0:T(8,128)(2,1)} %param.14, bf16[1,256,1024]{2,1,0:T(8,128)(2,1)} %param.16), kind=kOutput, calls=%fused_computation.23 | convolution fusion | flops 268959744 | bytes 1835008 | tf_op jit(solution)/shard_map/dot_general | solution.py:11
  3.4 11.4 %all-to-all-start = ((bf16[32,32,512]{2,1,0:T(8,128)(2,1)}), bf16[32,32,512]{2,1,0:T(8,128)(2,1)}, u32[]{:S(2)}, u32[]{:S(2)}) async-start(bf16[32,32,512]{2,1,0:T(8,128)(2,1)} %bitcast.2), calls=%async_computation | async-start | bytes 2097152 | tf_op jit(solution)/shard_map/all_to_all | solution.py:24
  14.9 1.5 convolution_convert_fusion.1
  16.3 29.1 %all-to-all-done = bf16[32,32,512]{2,1,0:T(8,128)(2,1)} async-done(((bf16[32,32,512]{2,1,0:T(8,128)(2,1)}), bf16[32,32,512]{2,1,0:T(8,128)(2,1)}, u32[]{:S(2)}, u32[]{:S(2)}) %all-to-all-start) | async-done | bytes 1048608 | tf_op jit(solution)/shard_map/all_to_all | solution.py:24
  45.4 4.5 %all-to-all-start.1 = ((bf16[32,32,512]{2,1,0:T(8,128)(2,1)}), bf16[32,32,512]{2,1,0:T(8,128)(2,1)}, u32[]{:S(2)}, u32[]{:S(2)}) async-start(bf16[32,32,512]{2,1,0:T(8,128)(2,1)} %bitcast.4), calls=%async_computation.1 | async-start | bytes 2097152 | tf_op jit(solution)/shard_map/all_to_all | solution.py:24
  50.1 4.6 %fusion.10 = (f32[1024,512]{0,1:T(8,128)}, bf16[1024,512]{0,1:T(8,128)(2,1)S(1)}) fusion(bf16[1024,512]{1,0:T(8,128)(2,1)} %bitcast.3, bf16[1,1024,1024]{2,1,0:T(8,128)(2,1)S(1)} %copy-done), kind=kOutput, calls=%fused_computation.16 | convolution fusion | flops 1078460416 | bytes 6291456 | tf_op jit(solution)/shard_map/dot_general | solution.py:11
  55.6 2.3 %fusion.18 = bf16[512,1024]{0,1:T(8,128)(2,1)} fusion(bf16[1024,512]{0,1:T(8,128)(2,1)S(1)} %get-tuple-element.88, bf16[1,1024,1024]{2,1,0:T(8,128)(2,1)S(1)} %copy-done.16), kind=kOutput, calls=%fused_computation.22 | convolution fusion | flops 1074266112 | bytes 4194304 | tf_op jit(solution)/shard_map/dot_general | solution.py:11
  57.9 22.0 %all-to-all-done.1 = bf16[32,32,512]{2,1,0:T(8,128)(2,1)} async-done(((bf16[32,32,512]{2,1,0:T(8,128)(2,1)}), bf16[32,32,512]{2,1,0:T(8,128)(2,1)}, u32[]{:S(2)}, u32[]{:S(2)}) %all-to-all-start.1) | async-done | bytes 1048608 | tf_op jit(solution)/shard_map/all_to_all | solution.py:24
  79.9 3.7 %all-to-all-start.2 = ((bf16[32,32,512]{2,1,0:T(8,128)(2,1)}), bf16[32,32,512]{2,1,0:T(8,128)(2,1)S(1)}, u32[]{:S(2)}, u32[]{:S(2)}) async-start(bf16[32,32,512]{2,1,0:T(8,128)(2,1)} %bitcast.175), calls=%async_computation.2 | async-start | bytes 2097152 | tf_op jit(solution)/shard_map/all_to_all | solution.py:24
  83.6 2.8 %multiply_convert_fusion.1 = bf16[1024,1024]{1,0:T(8,128)(2,1)S(1)} fusion(bf16[1024,512]{0,1:T(8,128)(2,1)} %copy-done.19, bf16[1024,512]{1,0:T(8,128)(2,1)} %bitcast.5), kind=kOutput, calls=%fused_computation.1 | convolution fusion | flops 1075838976 | bytes 4194304 | tf_op jit(solution)/shard_map/dot_general | solution.py:11
  87.8 1.5 collective-permute-start
  89.3 1.7 %collective-permute-start.1 = (bf16[128,1024]{1,0:T(8,128)(2,1)S(1)}, bf16[128,1024]{1,0:T(8,128)(2,1)S(1)}, u32[]{:S(2)}, u32[]{:S(2)}) collective-permute-start(bf16[128,1024]{1,0:T(8,128)(2,1)S(1)} %get-tuple-element.94), channel_id=1, source_target_pairs={{0,192},{32,224},{64,0},{96,32},{128,64},{160,96},{192,128},{224,1... | collective-permute-start | bytes 786440 | tf_op jit(solution)/shard_map/ppermute | solution.py:56
  93.0 2.6 %fusion = bf16[1024,512]{0,1:T(8,128)(2,1)S(1)} fusion(f32[1024,512]{0,1:T(8,128)S(1)} %copy-done.18, bf16[1024,512]{1,0:T(8,128)(2,1)} %bitcast.5, bf16[1,1024,1024]{2,1,0:T(8,128)(2,1)S(1)} %copy-done.17), kind=kOutput, calls=%fused_computation.3 | convolution fusion | flops 1074790400 | bytes 6291456 | tf_op jit(solution)/shard_map/dot_general | solution.py:11
  95.6 2.5 %multiply_convert_fusion = bf16[1024,1024]{1,0:T(8,128)(2,1)S(1)} fusion(bf16[1024,512]{1,0:T(8,128)(2,1)} %bitcast.3, bf16[1024,512]{0,1:T(8,128)(2,1)S(1)} %fusion), kind=kOutput, calls=%fused_computation | convolution fusion | flops 1075838976 | bytes 4194304 | tf_op jit(solution)/shard_map/dot_general | solution.py:11
  99.3 3.0 %collective-permute-start.3 = (bf16[128,1024]{1,0:T(8,128)(2,1)}, bf16[128,1024]{1,0:T(8,128)(2,1)}, u32[]{:S(2)}, u32[]{:S(2)}) collective-permute-start(bf16[128,1024]{1,0:T(8,128)(2,1)} %get-tuple-element.118), channel_id=1, source_target_pairs={{0,192},{32,224},{64,0},{96,32},{128,64},{160,96},{192,128},{224,1... | collective-permute-start | bytes 786440 | tf_op jit(solution)/shard_map/ppermute | solution.py:56
  103.4 2.3 %fusion.23 = bf16[1024,512]{1,0:T(8,128)(2,1)} fusion(bf16[1024,512]{0,1:T(8,128)(2,1)S(1)} %fusion, bf16[1,1024,1024]{2,1,0:T(8,128)(2,1)S(1)} %copy-done), kind=kOutput, calls=%fused_computation.25 | convolution fusion | flops 1074266112 | bytes 4194304 | tf_op jit(solution)/shard_map/dot_general | solution.py:11
  107.6 1.7 collective-permute-start.6
  109.3 4.6 %all-to-all-done.2 = bf16[32,32,512]{2,1,0:T(8,128)(2,1)S(1)} async-done(((bf16[32,32,512]{2,1,0:T(8,128)(2,1)}), bf16[32,32,512]{2,1,0:T(8,128)(2,1)S(1)}, u32[]{:S(2)}, u32[]{:S(2)}) %all-to-all-start.2) | async-done | bytes 1048608 | tf_op jit(solution)/shard_map/all_to_all | solution.py:24
  114.8 4.9 %all-to-all-start.3 = ((bf16[32,32,512]{2,1,0:T(8,128)(2,1)}), bf16[32,32,512]{2,1,0:T(8,128)(2,1)S(1)}, u32[]{:S(2)}, u32[]{:S(2)}) async-start(bf16[32,32,512]{2,1,0:T(8,128)(2,1)} %bitcast.172), calls=%async_computation.3 | async-start | bytes 2097152 | tf_op jit(solution)/shard_map/all_to_all | solution.py:24
  119.8 2.3 %fusion.43 = (bf16[2,128,1024]{2,1,0:T(8,128)(2,1)}, bf16[2,128,1024]{2,1,0:T(8,128)(2,1)}) fusion(bf16[2,128,1024]{2,1,0:T(8,128)(2,1)} %get-tuple-element.120, bf16[128,1024]{1,0:T(8,128)(2,1)} %collective-permute-done.3, bf16[4,2,128,1024]{3,2,1,0:T(8,128)(2,1)} %bitcast.169, s32[]{:T(128)S(6)} %select_n.45, s32[]{:T(128)S(6)} %add.135, ...), kind=kLoop, calls=%fused_computation.59 | loop fusion | flops 1048576 | bytes 1572876 | tf_op jit(solution)/shard_map/scatter | solution.py:69
  122.1 1.8 %fusion.26 = bf16[1024,256]{1,0:T(8,128)(2,1)S(1)} fusion(bf16[1024,512]{1,0:T(8,128)(2,1)} %bitcast.173, bf16[512,256]{1,0:T(8,128)(2,1)} %param.15), kind=kOutput, calls=%fused_computation.27 | convolution fusion | flops 268959744 | bytes 1835008 | tf_op jit(solution)/shard_map/dot_general | solution.py:11
  124.0 1.9 %collective-permute-start.10 = (bf16[2,2,128,256]{3,2,1,0:T(8,128)(2,1)S(1)}, bf16[2,2,128,256]{3,2,1,0:T(8,128)(2,1)S(1)}, u32[]{:S(2)}, u32[]{:S(2)}) collective-permute-start(bf16[2,2,128,256]{3,2,1,0:T(8,128)(2,1)S(1)} %dynamic-slice_bitcast_fusion.12), channel_id=1, source_target_pairs={{0,128},{32,160},{64,192},{96,224},{128,0},{160,32},{192,64},{224,... | collective-permute-start | bytes 786440 | tf_op jit(solution)/shard_map/ppermute | solution.py:40
  127.2 1.9 %collective-permute-start.5 = (bf16[2,128,1024]{2,1,0:T(8,128)(2,1)S(1)}, bf16[2,128,1024]{2,1,0:T(8,128)(2,1)S(1)}, u32[]{:S(2)}, u32[]{:S(2)}) collective-permute-start(bf16[2,128,1024]{2,1,0:T(8,128)(2,1)S(1)} %copy-done.13), channel_id=1, source_target_pairs={{0,192},{32,224},{64,0},{96,32},{128,64},{160,96},{192,128},{224,1... | collective-permute-start | bytes 1572872 | tf_op jit(solution)/shard_map/ppermute | solution.py:56
  130.3 1.5 add_convert_fusion.1
  133.4 1.4 collective-permute-done.10
  135.9 9.3 %collective-permute-done.4 = bf16[2,128,1024]{2,1,0:T(8,128)(2,1)S(1)} collective-permute-done((bf16[2,128,1024]{2,1,0:T(8,128)(2,1)S(1)}, bf16[2,128,1024]{2,1,0:T(8,128)(2,1)S(1)}, u32[]{:S(2)}, u32[]{:S(2)}) %collective-permute-start.4) | collective-permute-done | bytes 524320 | tf_op jit(solution)/shard_map/ppermute | solution.py:56
  147.4 2.9 %all-to-all-done.3 = bf16[32,32,512]{2,1,0:T(8,128)(2,1)S(1)} async-done(((bf16[32,32,512]{2,1,0:T(8,128)(2,1)}), bf16[32,32,512]{2,1,0:T(8,128)(2,1)S(1)}, u32[]{:S(2)}, u32[]{:S(2)}) %all-to-all-start.3) | async-done | bytes 1048608 | tf_op jit(solution)/shard_map/all_to_all | solution.py:24
  151.6 4.3 %all-to-all-start.4 = ((bf16[8,32,1024]{2,1,0:T(8,128)(2,1)}), bf16[8,32,1024]{2,1,0:T(8,128)(2,1)}, u32[]{:S(2)}, u32[]{:S(2)}) async-start(bf16[8,32,1024]{2,1,0:T(8,128)(2,1)} %bitcast.165), calls=%async_computation.4 | async-start | bytes 1048576 | tf_op jit(solution)/shard_map/all_to_all | solution.py:29
  156.8 2.0 %collective-permute-start.12 = (bf16[128,256]{1,0:T(8,128)(2,1)S(1)}, bf16[128,256]{1,0:T(8,128)(2,1)S(1)}, u32[]{:S(2)}, u32[]{:S(2)}) collective-permute-start(bf16[128,256]{1,0:T(8,128)(2,1)S(1)} %get-tuple-element.134), channel_id=1, source_target_pairs={{0,32},{32,0},{64,96},{96,64},{128,160},{160,128},{192,224},{224,1... | collective-permute-start | bytes 196616 | tf_op jit(solution)/shard_map/ppermute | solution.py:40
  158.8 2.2 %convolution_convert_fusion.2 = bf16[512,256]{1,0:T(8,128)(2,1)} fusion(bf16[1024,512]{1,0:T(8,128)(2,1)S(1)} %bitcast.164, bf16[1,256,1024]{2,1,0:T(8,128)(2,1)} %param.16), kind=kOutput, calls=%fused_computation.28 | convolution fusion | flops 268566528 | bytes 1835008 | tf_op jit(solution)/shard_map/dot_general | solution.py:11
  161.0 4.1 %collective-permute-done.12.refs_5_ = bf16[128,256]{1,0:T(8,128)(2,1)S(1)} collective-permute-done((bf16[128,256]{1,0:T(8,128)(2,1)S(1)}, bf16[128,256]{1,0:T(8,128)(2,1)S(1)}, u32[]{:S(2)}, u32[]{:S(2)}) %collective-permute-start.12) | collective-permute-done | bytes 65568 | tf_op jit(solution)/shard_map/ppermute | solution.py:40
  166.1 2.3 %shard_map.110 = (f32[32,1024]{1,0:T(8,128)}, f32[128,1024]{1,0:T(8,128)}, f32[128,1024]{1,0:T(8,128)}, f32[128,256]{1,0:T(8,128)}) custom-call(bf16[8,32,1024]{2,1,0:T(8,128)(2,1)} %all-to-all-done.4.parts, bf16[128,1024]{1,0:T(8,128)(2,1)S(1)} %copy-done.3, bf16[128,1024]{1,0:T(8,128)(2,1)} %collective-permute-done.8.refs_1_, ...), custom_call_target="tpu_custom_call" | custom-call | flops 851968 | bytes 3014656 | tf_op jit(solution)/shard_map/pallas_call | solution.py:100
  (76 shorter events, 20.3 us)
Async XLA Ops:
  0.6 49.4 %copy-start = (bf16[1,1024,1024]{2,1,0:T(8,128)(2,1)S(1)}, bf16[1,1024,1024]{2,1,0:T(8,128)(2,1)}, u32[]{:S(2)}) copy-start(bf16[1,1024,1024]{2,1,0:T(8,128)(2,1)} %param.17) | copy-start | bytes 6291460
  0.6 14.2 %copy-start.15 = (bf16[512,256]{1,0:T(8,128)(2,1)S(1)}, bf16[512,256]{1,0:T(8,128)(2,1)}, u32[]{:S(2)}) copy-start(bf16[512,256]{1,0:T(8,128)(2,1)} %param.15) | copy-start | bytes 786436
  0.7 14.2 %copy-start.11 = (bf16[1,1024,256]{2,1,0:T(8,128)(2,1)S(1)}, bf16[1,1024,256]{2,1,0:T(8,128)(2,1)}, u32[]{:S(2)}) copy-start(bf16[1,1024,256]{2,1,0:T(8,128)(2,1)} %param.19) | copy-start | bytes 1572868
  3.4 42.0 %all-to-all-start = ((bf16[32,32,512]{2,1,0:T(8,128)(2,1)}), bf16[32,32,512]{2,1,0:T(8,128)(2,1)}, u32[]{:S(2)}, u32[]{:S(2)}) async-start(bf16[32,32,512]{2,1,0:T(8,128)(2,1)} %bitcast.2), calls=%async_computation | async-start | bytes 2097152 | tf_op jit(solution)/shard_map/all_to_all | solution.py:24
  14.9 35.0 %copy-start.7 = (bf16[512,256]{1,0:T(8,128)(2,1)S(1)}, bf16[512,256]{1,0:T(8,128)(2,1)}, u32[]{:S(2)}) copy-start(bf16[512,256]{1,0:T(8,128)(2,1)} %param.14) | copy-start | bytes 786436
  45.4 34.5 %all-to-all-start.1 = ((bf16[32,32,512]{2,1,0:T(8,128)(2,1)}), bf16[32,32,512]{2,1,0:T(8,128)(2,1)}, u32[]{:S(2)}, u32[]{:S(2)}) async-start(bf16[32,32,512]{2,1,0:T(8,128)(2,1)} %bitcast.4), calls=%async_computation.1 | async-start | bytes 2097152 | tf_op jit(solution)/shard_map/all_to_all | solution.py:24
  50.1 5.6 %copy-start.16 = (bf16[1,1024,1024]{2,1,0:T(8,128)(2,1)S(1)}, bf16[1,1024,1024]{2,1,0:T(8,128)(2,1)}, u32[]{:S(2)}) copy-start(bf16[1,1024,1024]{2,1,0:T(8,128)(2,1)} %param.18) | copy-start | bytes 6291460
  79.9 34.0 %all-to-all-start.2 = ((bf16[32,32,512]{2,1,0:T(8,128)(2,1)}), bf16[32,32,512]{2,1,0:T(8,128)(2,1)S(1)}, u32[]{:S(2)}, u32[]{:S(2)}) async-start(bf16[32,32,512]{2,1,0:T(8,128)(2,1)} %bitcast.175), calls=%async_computation.2 | async-start | bytes 2097152 | tf_op jit(solution)/shard_map/all_to_all | solution.py:24
  86.5 6.5 %copy-start.17 = (bf16[1,1024,1024]{2,1,0:T(8,128)(2,1)S(1)}, bf16[1,1024,1024]{2,1,0:T(8,128)(2,1)}, u32[]{:S(2)}) copy-start(bf16[1,1024,1024]{2,1,0:T(8,128)(2,1)} %param.18) | copy-start | bytes 6291460
  86.6 6.5 %copy-start.18 = (f32[1024,512]{0,1:T(8,128)S(1)}, f32[1024,512]{0,1:T(8,128)}, u32[]{:S(2)}) copy-start(f32[1024,512]{0,1:T(8,128)} %get-tuple-element.90) | copy-start | bytes 6291460
  87.8 17.8 %collective-permute-start = (bf16[128,1024]{1,0:T(8,128)(2,1)S(1)}, bf16[128,1024]{1,0:T(8,128)(2,1)S(1)}, u32[]{:S(2)}, u32[]{:S(2)}) collective-permute-start(bf16[128,1024]{1,0:T(8,128)(2,1)S(1)} %get-tuple-element.93), channel_id=1, source_target_pairs={{0,64},{32,96},{64,128},{96,160},{128,192},{160,224},{192,0},{224,... | collective-permute-start | bytes 786440 | tf_op jit(solution)/shard_map/ppermute | solution.py:56
  89.3 16.4 %collective-permute-start.1 = (bf16[128,1024]{1,0:T(8,128)(2,1)S(1)}, bf16[128,1024]{1,0:T(8,128)(2,1)S(1)}, u32[]{:S(2)}, u32[]{:S(2)}) collective-permute-start(bf16[128,1024]{1,0:T(8,128)(2,1)S(1)} %get-tuple-element.94), channel_id=1, source_target_pairs={{0,192},{32,224},{64,0},{96,32},{128,64},{160,96},{192,128},{224,1... | collective-permute-start | bytes 786440 | tf_op jit(solution)/shard_map/ppermute | solution.py:56
  98.1 5.3 %copy-start.4 = (bf16[1024,1024]{1,0:T(8,128)(2,1)}, bf16[1024,1024]{1,0:T(8,128)(2,1)S(1)}, u32[]{:S(2)}) copy-start(bf16[1024,1024]{1,0:T(8,128)(2,1)S(1)} %multiply_convert_fusion) | copy-start | bytes 6291460
  99.0 14.9 %collective-permute-start.2 = (bf16[128,1024]{1,0:T(8,128)(2,1)}, bf16[128,1024]{1,0:T(8,128)(2,1)}, u32[]{:S(2)}, u32[]{:S(2)}) collective-permute-start(bf16[128,1024]{1,0:T(8,128)(2,1)} %get-tuple-element.119), channel_id=1, source_target_pairs={{0,64},{32,96},{64,128},{96,160},{128,192},{160,224},{192,0},{224,... | collective-permute-start | bytes 786440 | tf_op jit(solution)/shard_map/ppermute | solution.py:56
  99.3 14.6 %collective-permute-start.3 = (bf16[128,1024]{1,0:T(8,128)(2,1)}, bf16[128,1024]{1,0:T(8,128)(2,1)}, u32[]{:S(2)}, u32[]{:S(2)}) collective-permute-start(bf16[128,1024]{1,0:T(8,128)(2,1)} %get-tuple-element.118), channel_id=1, source_target_pairs={{0,192},{32,224},{64,0},{96,32},{128,64},{160,96},{192,128},{224,1... | collective-permute-start | bytes 786440 | tf_op jit(solution)/shard_map/ppermute | solution.py:56
  106.4 23.9 %collective-permute-start.7 = (bf16[2,128,1024]{2,1,0:T(8,128)(2,1)}, bf16[2,128,1024]{2,1,0:T(8,128)(2,1)}, u32[]{:S(2)}, u32[]{:S(2)}) collective-permute-start(bf16[2,128,1024]{2,1,0:T(8,128)(2,1)} %fusion.39), channel_id=1, source_target_pairs={{0,192},{32,224},{64,0},{96,32},{128,64},{160,96},{192,128},{224,1... | collective-permute-start | bytes 1572872 | tf_op jit(solution)/shard_map/ppermute | solution.py:56
  107.6 22.7 %collective-permute-start.6 = (bf16[2,128,1024]{2,1,0:T(8,128)(2,1)}, bf16[2,128,1024]{2,1,0:T(8,128)(2,1)}, u32[]{:S(2)}, u32[]{:S(2)}) collective-permute-start(bf16[2,128,1024]{2,1,0:T(8,128)(2,1)} %fusion.37), channel_id=1, source_target_pairs={{0,64},{32,96},{64,128},{96,160},{128,192},{160,224},{192,0},{224,... | collective-permute-start | bytes 1572872 | tf_op jit(solution)/shard_map/ppermute | solution.py:56
  114.8 35.4 %all-to-all-start.3 = ((bf16[32,32,512]{2,1,0:T(8,128)(2,1)}), bf16[32,32,512]{2,1,0:T(8,128)(2,1)S(1)}, u32[]{:S(2)}, u32[]{:S(2)}) async-start(bf16[32,32,512]{2,1,0:T(8,128)(2,1)} %bitcast.172), calls=%async_computation.3 | async-start | bytes 2097152 | tf_op jit(solution)/shard_map/all_to_all | solution.py:24
  119.8 9.3 %copy-start.9 = (bf16[32,32,512]{2,1,0:T(8,128)(2,1)S(1)}, bf16[32,32,512]{2,1,0:T(8,128)(2,1)}, u32[]{:S(2)}) copy-start(bf16[32,32,512]{2,1,0:T(8,128)(2,1)} %copy-done.8) | copy-start | bytes 3145732
  119.8 9.3 %copy-start.12 = (bf16[1,1024,256]{2,1,0:T(8,128)(2,1)S(1)}, bf16[1,1024,256]{2,1,0:T(8,128)(2,1)}, u32[]{:S(2)}) copy-start(bf16[1,1024,256]{2,1,0:T(8,128)(2,1)} %param.19) | copy-start | bytes 1572868
  122.1 8.2 %copy-start.5 = (bf16[2,128,1024]{2,1,0:T(8,128)(2,1)S(1)}, bf16[2,128,1024]{2,1,0:T(8,128)(2,1)}, u32[]{:S(2)}) copy-start(bf16[2,128,1024]{2,1,0:T(8,128)(2,1)} %get-tuple-element.91) | copy-start | bytes 1572868
  124.0 10.8 %collective-permute-start.10 = (bf16[2,2,128,256]{3,2,1,0:T(8,128)(2,1)S(1)}, bf16[2,2,128,256]{3,2,1,0:T(8,128)(2,1)S(1)}, u32[]{:S(2)}, u32[]{:S(2)}) collective-permute-start(bf16[2,2,128,256]{3,2,1,0:T(8,128)(2,1)S(1)} %dynamic-slice_bitcast_fusion.12), channel_id=1, source_target_pairs={{0,128},{32,160},{64,192},{96,224},{128,0},{160,32},{192,64},{224,... | collective-permute-start | bytes 786440 | tf_op jit(solution)/shard_map/ppermute | solution.py:40
  125.9 19.3 %collective-permute-start.4 = (bf16[2,128,1024]{2,1,0:T(8,128)(2,1)S(1)}, bf16[2,128,1024]{2,1,0:T(8,128)(2,1)S(1)}, u32[]{:S(2)}, u32[]{:S(2)}) collective-permute-start(bf16[2,128,1024]{2,1,0:T(8,128)(2,1)S(1)} %copy-done.14), channel_id=1, source_target_pairs={{0,64},{32,96},{64,128},{96,160},{128,192},{160,224},{192,0},{224,... | collective-permute-start | bytes 1572872 | tf_op jit(solution)/shard_map/ppermute | solution.py:56
  127.2 18.4 %collective-permute-start.5 = (bf16[2,128,1024]{2,1,0:T(8,128)(2,1)S(1)}, bf16[2,128,1024]{2,1,0:T(8,128)(2,1)S(1)}, u32[]{:S(2)}, u32[]{:S(2)}) collective-permute-start(bf16[2,128,1024]{2,1,0:T(8,128)(2,1)S(1)} %copy-done.13), channel_id=1, source_target_pairs={{0,192},{32,224},{64,0},{96,32},{128,64},{160,96},{192,128},{224,1... | collective-permute-start | bytes 1572872 | tf_op jit(solution)/shard_map/ppermute | solution.py:56
  130.3 15.3 %copy-start.6 = (bf16[2,128,1024]{2,1,0:T(8,128)(2,1)S(1)}, bf16[2,128,1024]{2,1,0:T(8,128)(2,1)}, u32[]{:S(2)}) copy-start(bf16[2,128,1024]{2,1,0:T(8,128)(2,1)} %get-tuple-element.103) | copy-start | bytes 1572868
  132.7 32.4 %collective-permute-start.9 = (bf16[128,1024]{1,0:T(8,128)(2,1)}, bf16[128,1024]{1,0:T(8,128)(2,1)}, u32[]{:S(2)}, u32[]{:S(2)}) collective-permute-start(bf16[128,1024]{1,0:T(8,128)(2,1)} %get-tuple-element.132), channel_id=1, source_target_pairs={{0,32},{32,0},{64,96},{96,64},{128,160},{160,128},{192,224},{224,1... | collective-permute-start | bytes 786440 | tf_op jit(solution)/shard_map/ppermute | solution.py:40
  134.8 10.3 %copy-start.10 = (bf16[2,2,128,256]{3,2,1,0:T(8,128)(2,1)}, bf16[2,2,128,256]{3,2,1,0:T(8,128)(2,1)S(1)}, u32[]{:S(2)}) copy-start(bf16[2,2,128,256]{3,2,1,0:T(8,128)(2,1)S(1)} %fusion.27) | copy-start | bytes 786436
  135.6 20.3 %collective-permute-start.11 = (bf16[2,128,256]{2,1,0:T(8,128)(2,1)}, bf16[2,128,256]{2,1,0:T(8,128)(2,1)S(1)}, u32[]{:S(2)}, u32[]{:S(2)}) collective-permute-start(bf16[2,128,256]{2,1,0:T(8,128)(2,1)} %dynamic-slice_bitcast_fusion.17), channel_id=1, source_target_pairs={{0,64},{32,96},{64,0},{96,32},{128,192},{160,224},{192,128},{224,1... | collective-permute-start | bytes 393224 | tf_op jit(solution)/shard_map/ppermute | solution.py:40
  146.7 18.4 %collective-permute-start.8 = (bf16[128,1024]{1,0:T(8,128)(2,1)}, bf16[128,1024]{1,0:T(8,128)(2,1)}, u32[]{:S(2)}, u32[]{:S(2)}) collective-permute-start(bf16[128,1024]{1,0:T(8,128)(2,1)} %get-tuple-element.130), channel_id=1, source_target_pairs={{0,32},{32,0},{64,96},{96,64},{128,160},{160,128},{192,224},{224,1... | collective-permute-start | bytes 786440 | tf_op jit(solution)/shard_map/ppermute | solution.py:40
  151.6 13.6 %copy-start.2 = (bf16[128,1024]{1,0:T(8,128)(2,1)S(1)}, bf16[128,1024]{1,0:T(8,128)(2,1)}, u32[]{:S(2)}) copy-start(bf16[128,1024]{1,0:T(8,128)(2,1)} %get-tuple-element.133.refs_2_) | copy-start | bytes 786436
  151.6 13.6 %all-to-all-start.4 = ((bf16[8,32,1024]{2,1,0:T(8,128)(2,1)}), bf16[8,32,1024]{2,1,0:T(8,128)(2,1)}, u32[]{:S(2)}, u32[]{:S(2)}) async-start(bf16[8,32,1024]{2,1,0:T(8,128)(2,1)} %bitcast.165), calls=%async_computation.4 | async-start | bytes 1048576 | tf_op jit(solution)/shard_map/all_to_all | solution.py:29
  156.8 8.3 %collective-permute-start.12 = (bf16[128,256]{1,0:T(8,128)(2,1)S(1)}, bf16[128,256]{1,0:T(8,128)(2,1)S(1)}, u32[]{:S(2)}, u32[]{:S(2)}) collective-permute-start(bf16[128,256]{1,0:T(8,128)(2,1)S(1)} %get-tuple-element.134), channel_id=1, source_target_pairs={{0,32},{32,0},{64,96},{96,64},{128,160},{160,128},{192,224},{224,1... | collective-permute-start | bytes 196616 | tf_op jit(solution)/shard_map/ppermute | solution.py:40
  (6 other events, 12.6 us)
